TPU v7x, 32 devices: a whole 2x2x4 slice. The times are simulated.
32 devices in a mesh: dp: 16 (over z, y, core), tensor: 2 (over x).
Axes of the slice: x: 2, y: 2, z: 4, core: 2. Of those that a mesh axis runs over, the one named last changes fastest.
Arguments:
- tokens: bfloat16 [8192, 2048], P(('dp', 'tensor')), may hold values from -6 to 6
- group_of_device: int32 [16], P('dp'), may hold values from 0 to 15, each once
- segment_ids: int32 [16, 512], replicated, may hold values from 0 to 2, as said below
- start_pos: int32 [16, 2], replicated, may hold values from 512 to 1023
- attn_gain: float32 [2048], P('dp'), may hold values from 0.25 to 1.75
- q_down: float32 [2048, 1024], P('dp'), may hold values from -0.125 to 0.125
- q_gain: float32 [1024], P('dp'), may hold values from 0.25 to 1.75
- q_up: float32 [1024, 4096], P('dp', 'tensor'), may hold values from -0.25 to 0.25
- key_proj: float32 [2048, 256], P('dp'), may hold values from -0.125 to 0.125
- value_proj: float32 [2048, 256], P('dp'), may hold values from -0.125 to 0.125
- out_proj: float32 [4096, 2048], P('tensor', 'dp'), may hold values from -0.375 to 0.375
- ffn_gain: float32 [2048], P('dp'), may hold values from 0.25 to 1.75
- gate_proj: float32 [2048, 5632], P('dp', 'tensor'), may hold values from -0.125 to 0.125
- up_proj: float32 [2048, 5632], P('dp', 'tensor'), may hold values from -0.125 to 0.125
- down_proj: float32 [5632, 2048], P('tensor', 'dp'), may hold values from -0.078125 to 0.078125
- out_grad: bfloat16 [8192, 2048], P(('dp', 'tensor')), may hold values from -6 to 6
Outputs:
- output: bfloat16 [8192, 2048], P(('dp', 'tensor'))
- in_grad: bfloat16 [8192, 2048], P(('dp', 'tensor'))
- grad_attn_gain: float32 [2048], P('dp')
- grad_q_down: float32 [2048, 1024], P('dp')
- grad_q_gain: float32 [1024], P('dp')
- grad_q_up: float32 [1024, 4096], P('dp', 'tensor')
- grad_key_proj: float32 [2048, 256], P('dp')
- grad_value_proj: float32 [2048, 256], P('dp')
- grad_out_proj: float32 [4096, 2048], P('tensor', 'dp')
- grad_ffn_gain: float32 [2048], P('dp')
- grad_gate_proj: float32 [2048, 5632], P('dp', 'tensor')
- grad_up_proj: float32 [2048, 5632], P('dp', 'tensor')
- grad_down_proj: float32 [5632, 2048], P('tensor', 'dp')
Inputs may be any that keep to these rules, and one draw needn't show every extreme that they name: `segment_ids`: each row holds the prompt (segment 0) first, then continuations 1 to 2 in order; each continuation has 64 to 128 tokens, and one of each group has exactly 128.
All inputs are finite; a program needn't handle non-finite values.
Results may differ from a plain program's by a relative error of at most 0.019.
The roundings to bfloat16 on the way count: a program that leaves them out, or rounds other values in their place, can miss the bound.
Values may be sent and summed in bfloat16 or wider, within the bound.
A program may use at most 256 MiB of HBM per device.

v0:
```python
import math

import jax
import jax.numpy as jnp
from jax import lax
from jax.sharding import PartitionSpec as P

norm_eps = 1e-05
masked_score = -1e30


def matmul(left, right):
    return jnp.dot(left, right, preferred_element_type=jnp.float32)


def matmul_nt(left, right):
    return lax.dot_general(
        left, right, (((1,), (1,)), ((), ())), preferred_element_type=jnp.float32
    )


def matmul_tn(left, right):
    return lax.dot_general(
        left, right, (((0,), (0,)), ((), ())), preferred_element_type=jnp.float32
    )


def inv_rms(values):
    return lax.rsqrt(jnp.mean(values * values, axis=-1, keepdims=True) + norm_eps)


def norm_back(grad_out, unit_vals, inverse, gain_vals):
    scaled = grad_out * gain_vals
    return inverse * (scaled - unit_vals * jnp.mean(scaled * unit_vals, axis=-1, keepdims=True))


def rotate(values, cos_tab, sin_tab):
    half_dim = values.shape[-1] // 2
    first_half = values[..., :half_dim]
    second_half = values[..., half_dim:]
    return jnp.concatenate(
        [
            first_half * cos_tab - second_half * sin_tab,
            second_half * cos_tab + first_half * sin_tab,
        ],
        axis=-1,
    )


def unrotate(values, cos_tab, sin_tab):
    half_dim = values.shape[-1] // 2
    first_half = values[..., :half_dim]
    second_half = values[..., half_dim:]
    return jnp.concatenate(
        [
            first_half * cos_tab + second_half * sin_tab,
            second_half * cos_tab - first_half * sin_tab,
        ],
        axis=-1,
    )


def rope_tables(positions, head_dim):
    half_dim = head_dim // 2
    frequency = jnp.exp(
        jnp.arange(half_dim, dtype=jnp.float32) * (-2.0 * math.log(10000.0) / head_dim)
    )
    angles = positions.astype(jnp.float32)[:, None] * frequency[None, :]
    return (jnp.cos(angles), jnp.sin(angles))


def token_positions(segments, starts):
    token_index = jnp.arange(segments.shape[0], dtype=jnp.int32)
    labels = jnp.arange(1, starts.shape[0] + 1, dtype=jnp.int32)
    inside = segments[:, None] == labels[None, :]
    firsts = jnp.sum((segments[:, None] < labels[None, :]).astype(jnp.int32), axis=0)
    shifts = jnp.sum(jnp.where(inside, (starts - firsts)[None, :], 0), axis=1)
    return token_index + shifts


def allowed_pairs(segments):
    token_index = jnp.arange(segments.shape[0], dtype=jnp.int32)
    causal = token_index[None, :] <= token_index[:, None]
    visible = (segments[None, :] == segments[:, None]) | (segments[None, :] == 0)
    return causal & visible


def local(
    tokens,
    group_of_device,
    segment_ids,
    start_pos,
    attn_gain,
    q_down,
    q_gain,
    q_up,
    key_proj,
    value_proj,
    out_proj,
    ffn_gain,
    gate_proj,
    up_proj,
    down_proj,
    out_grad,
):
    own_rows = tokens.shape[0]
    row_start = lax.axis_index("tensor") * own_rows
    head_dim = key_proj.shape[1]
    scale = 1.0 / math.sqrt(head_dim)
    group_id = group_of_device[0]
    segments = lax.dynamic_index_in_dim(segment_ids, group_id, 0, keepdims=False)
    starts = lax.dynamic_index_in_dim(start_pos, group_id, 0, keepdims=False)
    cos_tab, sin_tab = rope_tables(token_positions(segments, starts), head_dim)
    cos_head = cos_tab[:, None, :]
    sin_head = sin_tab[:, None, :]
    allowed = allowed_pairs(segments)[None, :, :]
    attn_parts = (
        attn_gain.astype(jnp.bfloat16),
        q_down.astype(jnp.bfloat16),
        q_gain.astype(jnp.bfloat16),
        q_up.astype(jnp.bfloat16),
        key_proj.astype(jnp.bfloat16),
        value_proj.astype(jnp.bfloat16),
        out_proj.astype(jnp.bfloat16),
    )
    ffn_parts = (
        ffn_gain.astype(jnp.bfloat16),
        gate_proj.astype(jnp.bfloat16),
        up_proj.astype(jnp.bfloat16),
        down_proj.astype(jnp.bfloat16),
    )
    attn_set = (
        lax.all_gather(attn_parts[0], "dp", axis=0, tiled=True),
        lax.all_gather(attn_parts[1], "dp", axis=0, tiled=True),
        lax.all_gather(attn_parts[2], "dp", axis=0, tiled=True),
        lax.all_gather(attn_parts[3], "dp", axis=0, tiled=True),
        lax.all_gather(attn_parts[4], "dp", axis=0, tiled=True),
        lax.all_gather(attn_parts[5], "dp", axis=0, tiled=True),
        lax.all_gather(attn_parts[6], "dp", axis=1, tiled=True),
    )
    x_own = tokens.astype(jnp.float32)
    x_group = lax.all_gather(tokens, "tensor", axis=0, tiled=True).astype(jnp.float32)
    group_len = x_group.shape[0]
    gain_one = attn_set[0].astype(jnp.float32)
    inv_one = inv_rms(x_group)
    unit_one = x_group * inv_one
    normed = (unit_one * gain_one).astype(jnp.bfloat16)
    latent = matmul(normed, attn_set[1])
    gain_q = attn_set[2].astype(jnp.float32)
    inv_q = inv_rms(latent)
    unit_q = latent * inv_q
    latent_n = (unit_q * gain_q).astype(jnp.bfloat16)
    head_count = attn_set[3].shape[1] // head_dim
    query_raw = matmul(latent_n, attn_set[3]).reshape(group_len, head_count, head_dim)
    queries = rotate(query_raw, cos_head, sin_head).astype(jnp.bfloat16)
    keys_rot = rotate(matmul(normed, attn_set[4]), cos_tab, sin_tab).astype(jnp.bfloat16)
    values = matmul(normed, attn_set[5]).astype(jnp.bfloat16)
    raw_scores = (
        jnp.einsum("qhe,ke->hqk", queries, keys_rot, preferred_element_type=jnp.float32) * scale
    )
    raw_scores = jnp.where(allowed, raw_scores, masked_score)
    top_score = jnp.max(raw_scores, axis=-1, keepdims=True)
    expd_scores = jnp.exp(raw_scores - top_score)
    row_total = jnp.sum(expd_scores, axis=-1, keepdims=True)
    attn_probs = expd_scores / row_total
    log_total = top_score + jnp.log(row_total)
    head_mix = jnp.einsum(
        "hqk,ke->qhe", attn_probs.astype(jnp.bfloat16), values, preferred_element_type=jnp.float32
    )
    head_mix = head_mix.reshape(group_len, head_count * head_dim).astype(jnp.bfloat16)
    residual = x_own + lax.psum_scatter(
        matmul(head_mix, attn_set[6]), "tensor", scatter_dimension=0, tiled=True
    )
    ffn_set = (
        lax.all_gather(ffn_parts[0], "dp", axis=0, tiled=True),
        lax.all_gather(ffn_parts[1], "dp", axis=0, tiled=True),
        lax.all_gather(ffn_parts[2], "dp", axis=0, tiled=True),
        lax.all_gather(ffn_parts[3], "dp", axis=1, tiled=True),
    )
    gain_two = ffn_set[0].astype(jnp.float32)
    inv_two = inv_rms(residual)
    unit_two = residual * inv_two
    normed_two = lax.all_gather(
        (unit_two * gain_two).astype(jnp.bfloat16), "tensor", axis=0, tiled=True
    )
    gate_act = matmul(normed_two, ffn_set[1])
    up_act = matmul(normed_two, ffn_set[2])
    gate_sig = jax.nn.sigmoid(gate_act)
    gate_silu = gate_act * gate_sig
    hidden = (gate_silu * up_act).astype(jnp.bfloat16)
    output = (
        residual
        + lax.psum_scatter(
            matmul(hidden, ffn_set[3]).astype(jnp.bfloat16),
            "tensor",
            scatter_dimension=0,
            tiled=True,
        ).astype(jnp.float32)
    ).astype(jnp.bfloat16)
    grad_group = lax.all_gather(out_grad, "tensor", axis=0, tiled=True)
    d_down = matmul_tn(hidden, grad_group)
    d_hidden = matmul_nt(grad_group, ffn_set[3])
    d_gate_act = (d_hidden * up_act * gate_sig * (1.0 + gate_act * (1.0 - gate_sig))).astype(
        jnp.bfloat16
    )
    d_up_act = (d_hidden * gate_silu).astype(jnp.bfloat16)
    d_gate = matmul_tn(normed_two, d_gate_act)
    d_up = matmul_tn(normed_two, d_up_act)
    gate_total, up_total, down_total = (
        lax.psum_scatter(d_gate, "dp", scatter_dimension=0, tiled=True),
        lax.psum_scatter(d_up, "dp", scatter_dimension=0, tiled=True),
        lax.psum_scatter(d_down, "dp", scatter_dimension=1, tiled=True),
    )
    d_normed_two = lax.psum_scatter(
        matmul_nt(d_gate_act, ffn_set[1]) + matmul_nt(d_up_act, ffn_set[2]),
        "tensor",
        scatter_dimension=0,
        tiled=True,
    )
    d_ffn_gain_part = jnp.sum(d_normed_two * unit_two, axis=0)
    d_resid = out_grad.astype(jnp.float32) + norm_back(d_normed_two, unit_two, inv_two, gain_two)
    d_attn = lax.all_gather(d_resid.astype(jnp.bfloat16), "tensor", axis=0, tiled=True)
    d_out = matmul_tn(head_mix, d_attn)
    d_mix = (
        matmul_nt(d_attn, attn_set[6]).astype(jnp.bfloat16).reshape(group_len, head_count, head_dim)
    )
    again_scores = (
        jnp.einsum("qhe,ke->hqk", queries, keys_rot, preferred_element_type=jnp.float32) * scale
    )
    again_scores = jnp.where(allowed, again_scores, masked_score)
    probs_back = jnp.exp(again_scores - log_total)
    d_probs = jnp.einsum("qhe,ke->hqk", d_mix, values, preferred_element_type=jnp.float32)
    d_values = jnp.einsum(
        "hqk,qhe->ke", probs_back.astype(jnp.bfloat16), d_mix, preferred_element_type=jnp.float32
    )
    row_dot = jnp.sum(probs_back * d_probs, axis=-1, keepdims=True)
    d_scores = (probs_back * (d_probs - row_dot)).astype(jnp.bfloat16)
    d_queries = (
        jnp.einsum("hqk,ke->qhe", d_scores, keys_rot, preferred_element_type=jnp.float32) * scale
    )
    d_keys = (
        jnp.einsum("hqk,qhe->ke", d_scores, queries, preferred_element_type=jnp.float32) * scale
    )
    d_query_pre = (
        unrotate(d_queries, cos_head, sin_head)
        .reshape(group_len, head_count * head_dim)
        .astype(jnp.bfloat16)
    )
    d_q_up = matmul_tn(latent_n, d_query_pre)
    d_latent_part = matmul_nt(d_query_pre, attn_set[3])
    d_latent_n, d_keys_all, d_values_all, d_ffn_gain = (
        lax.psum(d_latent_part.astype(jnp.bfloat16), "tensor").astype(jnp.float32),
        lax.psum(d_keys.astype(jnp.bfloat16), "tensor").astype(jnp.float32),
        lax.psum(d_values.astype(jnp.bfloat16), "tensor").astype(jnp.float32),
        lax.psum(d_ffn_gain_part.astype(jnp.bfloat16), "tensor").astype(jnp.float32),
    )
    d_q_gain = jnp.sum(d_latent_n * unit_q, axis=0)
    d_latent = norm_back(d_latent_n, unit_q, inv_q, gain_q).astype(jnp.bfloat16)
    d_keys_pre = unrotate(d_keys_all, cos_tab, sin_tab).astype(jnp.bfloat16)
    d_values_b = d_values_all.astype(jnp.bfloat16)
    d_q_down = matmul_tn(normed, d_latent)
    d_key_proj = matmul_tn(normed, d_keys_pre)
    d_value_proj = matmul_tn(normed, d_values_b)
    d_normed = (
        matmul_nt(d_latent, attn_set[1])
        + matmul_nt(d_keys_pre, attn_set[4])
        + matmul_nt(d_values_b, attn_set[5])
    )
    d_attn_gain = jnp.sum(d_normed * unit_one, axis=0)
    d_normed_own = lax.dynamic_slice_in_dim(d_normed, row_start, own_rows, 0)
    inv_own = inv_rms(x_own)
    in_grad = (d_resid + norm_back(d_normed_own, x_own * inv_own, inv_own, gain_one)).astype(
        jnp.bfloat16
    )
    attn_grads = (
        lax.psum_scatter(d_attn_gain, "dp", scatter_dimension=0, tiled=True),
        lax.psum_scatter(d_q_down, "dp", scatter_dimension=0, tiled=True),
        lax.psum_scatter(d_q_gain, "dp", scatter_dimension=0, tiled=True),
        lax.psum_scatter(d_q_up, "dp", scatter_dimension=0, tiled=True),
        lax.psum_scatter(d_key_proj, "dp", scatter_dimension=0, tiled=True),
        lax.psum_scatter(d_value_proj, "dp", scatter_dimension=0, tiled=True),
        lax.psum_scatter(d_out, "dp", scatter_dimension=1, tiled=True),
        lax.psum_scatter(d_ffn_gain, "dp", scatter_dimension=0, tiled=True),
    )
    return (
        output,
        in_grad,
        attn_grads[0],
        attn_grads[1],
        attn_grads[2],
        attn_grads[3],
        attn_grads[4],
        attn_grads[5],
        attn_grads[6],
        attn_grads[7],
        gate_total,
        up_total,
        down_total,
    )


def solution(mesh):
    placed = (
        P(("dp", "tensor"), None),
        P("dp"),
        P(),
        P(),
        P("dp"),
        P("dp", None),
        P("dp"),
        P("dp", "tensor"),
        P("dp", None),
        P("dp", None),
        P("tensor", "dp"),
        P("dp"),
        P("dp", "tensor"),
        P("dp", "tensor"),
        P("tensor", "dp"),
        P(("dp", "tensor"), None),
    )
    return jax.shard_map(
        local,
        mesh=mesh,
        in_specs=placed,
        out_specs=(
            P(("dp", "tensor"), None),
            P(("dp", "tensor"), None),
            P("dp"),
            P("dp", None),
            P("dp"),
            P("dp", "tensor"),
            P("dp", None),
            P("dp", None),
            P("tensor", "dp"),
            P("dp"),
            P("dp", "tensor"),
            P("dp", "tensor"),
            P("tensor", "dp"),
        ),
        check_vma=False,
    )
```

profile of v0, /device:TPU:1, one launch (start us, length us, event | category | flops | bytes accessed | tf_op | source)
XLA Modules:
  0.0 2211.2 jit_solution(8606159214197567845)
XLA Ops:
  14.9 22.8 %all-gather = bf16[16,1,128]{2,1,0:T(2,128)(2,1)S(1)} all-gather(bf16[1,1,128]{2,1,0:T(2,128)(2,1)S(1)} %convert_bitcast_fusion.1), channel_id=1, replica_groups=mesh['dp'=16,'tensor'=2] {'dp'}, dimensions={0}, use_global_device_ids=true | all-gather | bytes 4352 | tf_op jit(solution)/shard_map/all_gather | solution.py:133
  39.3 29.1 %all-reduce = bf16[1024]{0:T(1024)(128)(2,1)S(1)} all-reduce(bf16[1024]{0:T(1024)(128)(2,1)S(1)} %dynamic-update-slice), channel_id=1, replica_groups=mesh['dp'=16,'tensor'=2] {'dp'}, use_global_device_ids=true, to_apply=%add | all-reduce | flops 1024 | bytes 4096
  71.2 2.3 fusion.10
  73.6 12.5 all-gather.19.cloned.1.call-done
  86.1 2.1 fusion.87
  89.9 35.8 %all-gather.17.cloned.1.call-done = bf16[2048,256]{1,0:T(8,128)(2,1)} async-done(((bf16[128,256]{1,0:T(8,128)(2,1)}), bf16[2048,256]{1,0:T(8,128)(2,1)}) %all-gather.17.cloned.1.call-update) | async-done | bytes 1048592 | tf_op jit(solution)/shard_map/all_gather | solution.py:138
  125.7 2.0 fusion.49
  127.7 50.1 %all-gather.21.cloned.1.call-done = bf16[2048,1024]{1,0:T(8,128)(2,1)} async-done(((bf16[128,1024]{1,0:T(8,128)(2,1)}), bf16[2048,1024]{1,0:T(8,128)(2,1)}) %all-gather.21.cloned.1.call-update) | async-done | bytes 4194320 | tf_op jit(solution)/shard_map/all_gather | solution.py:134
  177.8 5.3 multiply_reduce_fusion.3
  183.1 46.4 %all-gather.23.cloned.1.call-done = bf16[1024,2048]{1,0:T(8,128)(2,1)} async-done(((bf16[64,2048]{1,0:T(8,128)(2,1)}), bf16[1024,2048]{1,0:T(8,128)(2,1)}) %all-gather.23.cloned.1.call-update) | async-done | bytes 4194320 | tf_op jit(solution)/shard_map/all_gather | solution.py:136
  229.5 4.6 fusion.78
  240.3 2.1 copy-done.2
  242.5 2.0 fusion.32
  244.5 64.2 %all-gather.25.cloned.1.call-done = bf16[2048,2048]{1,0:T(8,128)(2,1)} async-done(((bf16[2048,128]{1,0:T(8,128)(2,1)}), bf16[2048,2048]{1,0:T(8,128)(2,1)}) %all-gather.25.cloned.1.call-update) | async-done | bytes 8388624 | tf_op jit(solution)/shard_map/all_gather | solution.py:139
  308.7 9.5 fusion.96
  320.5 18.8 all-gather.1
  339.3 31.0 %reduce-scatter.12.cloned.1.call-done = f32[256,2048]{1,0:T(8,128)} async-done(((f32[512,2048]{1,0:T(8,128)}), f32[256,2048]{1,0:T(8,128)}) %reduce-scatter.12.cloned.1.call-update) | async-done | bytes 2097168 | tf_op jit(solution)/shard_map/reduce_scatter | solution.py:171
  370.4 2.7 multiply_reduce_fusion.2
  374.4 2.3 convert_element_type.175
  377.5 2.3 convert_element_type.177
  379.9 88.4 %all-gather.29.cloned.1.call-done = bf16[2048,2816]{1,0:T(8,128)(2,1)} async-done(((bf16[128,2816]{1,0:T(8,128)(2,1)}), bf16[2048,2816]{1,0:T(8,128)(2,1)}) %all-gather.29.cloned.1.call-update) | async-done | bytes 11534352 | tf_op jit(solution)/shard_map/all_gather | solution.py:176
  468.3 33.1 %all-gather.27.cloned.1.call-done = bf16[512,2048]{1,0:T(8,128)(2,1)} async-done(((bf16[256,2048]{1,0:T(8,128)(2,1)}), bf16[512,2048]{1,0:T(8,128)(2,1)}) %all-gather.27.cloned.1.call-update) | async-done | bytes 2097168 | tf_op jit(solution)/shard_map/all_gather | solution.py:183
  501.4 12.5 fusion.97
  513.9 85.3 %all-gather.31.cloned.1.call-done = bf16[2048,2816]{1,0:T(8,128)(2,1)} async-done(((bf16[128,2816]{1,0:T(8,128)(2,1)}), bf16[2048,2816]{1,0:T(8,128)(2,1)}) %all-gather.31.cloned.1.call-update) | async-done | bytes 11534352 | tf_op jit(solution)/shard_map/all_gather | solution.py:177
  599.1 12.6 fusion.98
  611.7 20.0 all-gather.35.cloned.1.call-done
  631.7 100.6 %all-gather.33.cloned.1.call-done = bf16[2816,2048]{1,0:T(8,128)(2,1)} async-done(((bf16[2816,128]{1,0:T(8,128)(2,1)}), bf16[2816,2048]{1,0:T(8,128)(2,1)}) %all-gather.33.cloned.1.call-update) | async-done | bytes 11534352 | tf_op jit(solution)/shard_map/all_gather | solution.py:178
  732.3 15.6 multiply_convert_fusion
  747.9 11.1 fusion.99
  759.1 10.7 convolution_add_fusion
  769.9 52.1 %reduce-scatter.16.cloned.1.call-done = f32[256,2048]{1,0:T(8,128)} async-done(((f32[512,2048]{1,0:T(8,128)}), f32[256,2048]{1,0:T(8,128)}) %reduce-scatter.16.cloned.1.call-update) | async-done | bytes 2097168 | tf_op jit(solution)/shard_map/reduce_scatter | solution.py:214
  822.0 3.0 multiply_reduce_fusion
  827.5 32.5 %all-gather.37.cloned.1.call-done = bf16[512,2048]{1,0:T(8,128)(2,1)} async-done(((bf16[256,2048]{1,0:T(8,128)(2,1)}), bf16[512,2048]{1,0:T(8,128)(2,1)}) %all-gather.37.cloned.1.call-update) | async-done | bytes 2097168 | tf_op jit(solution)/shard_map/all_gather | solution.py:222
  860.0 8.5 convolution_convert_fusion
  868.6 4.8 fusion
  874.5 2.5 fusion.2
  878.8 2.0 fusion.48
  880.8 2.0 fusion.43
  884.9 3.9 copy.81
  888.8 6.2 convolution_convert_fusion.2
  895.1 11.1 convolution_convert_fusion.1
  906.2 40.8 %all-reduce.8.cloned.1.call-done = (bf16[512,1024]{1,0:T(8,128)(2,1)}, bf16[512,256]{0,1:T(8,128)(2,1)}, bf16[512,256]{1,0:T(8,128)(2,1)}) async-done(((bf16[512,1024]{1,0:T(8,128)(2,1)}, bf16[512,256]{0,1:T(8,128)(2,1)}, bf16[512,256]{1,0:T(8,128)(2,1)}), (bf16[512,1024]{1,0:T(8,128)(2,1)}, bf16[512,256]{0,1:T(8,128)(2,1)}, bf16[512,256]{1,0:T(8,128)(2,1)})) %all-reduce.8.cloned.1.call-update) | async-done | bytes 1572880 | tf_op jit(solution)/shard_map/psum | solution.py:252
  949.3 3.9 fusion.67
  954.1 3.9 fusion.80
  958.8 8.2 fusion.77
  968.2 2.3 fusion.27
  970.5 7.7 fusion.83
  978.2 13.5 fusion.101
  991.8 13.4 fusion.102
  1005.3 13.0 fusion.103
  1018.6 12.7 fusion.100
  1032.6 3.8 psum.31
  1036.4 2.1 fusion.68
  1038.6 4.9 fusion.94
  1043.5 3.1 fusion.9
  1046.6 57.6 %all-reduce.4 = (f32[2048]{0:T(1024)S(1)}, f32[1024]{0:T(1024)S(1)}, f32[2048]{0:T(1024)S(1)}) all-reduce(f32[2048]{0:T(1024)S(1)} %get-tuple-element.53, f32[1024]{0:T(1024)S(1)} %get-tuple-element.15, bf16[2048]{0:T(1024)(128)(2,1)S(1)} %psum.31), channel_id=5, replica_groups=mesh['dp'=16,'tensor'=2] {'dp'}, use_global_device_ids=true, to_apply=%region_19.20.clone | all-reduce | flops 5120 | bytes 36864
  1105.9 2.1 fusion.19
  1108.1 5.4 fusion.23
  1113.5 106.9 %reduce-scatter.20.cloned.1.call-done = f32[64,2048]{1,0:T(8,128)} async-done(((f32[1024,2048]{1,0:T(8,128)}), f32[64,2048]{1,0:T(8,128)}) %reduce-scatter.20.cloned.1.call-update) | async-done | bytes 524304 | tf_op jit(solution)/shard_map/reduce_scatter | solution.py:279
  1220.5 108.9 %reduce-scatter.18.cloned.1.call-done = f32[128,1024]{1,0:T(8,128)} async-done(((f32[2048,1024]{1,0:T(8,128)}), f32[128,1024]{1,0:T(8,128)}) %reduce-scatter.18.cloned.1.call-update) | async-done | bytes 524304 | tf_op jit(solution)/shard_map/reduce_scatter | solution.py:277
  1329.3 231.3 %reduce-scatter.28.cloned.1.call-done = f32[128,2816]{1,0:T(8,128)} async-done(((f32[2048,2816]{1,0:T(8,128)}), f32[128,2816]{1,0:T(8,128)}) %reduce-scatter.28.cloned.1.call-update) | async-done | bytes 1441808 | tf_op jit(solution)/shard_map/reduce_scatter | solution.py:210
  1560.7 230.6 %reduce-scatter.30.cloned.1.call-done = f32[128,2816]{1,0:T(8,128)} async-done(((f32[2048,2816]{1,0:T(8,128)}), f32[128,2816]{1,0:T(8,128)}) %reduce-scatter.30.cloned.1.call-update) | async-done | bytes 1441808 | tf_op jit(solution)/shard_map/reduce_scatter | solution.py:211
  1791.3 230.7 %reduce-scatter.32.cloned.1.call-done = f32[2816,128]{1,0:T(8,128)} async-done(((f32[2816,2048]{1,0:T(8,128)}), f32[2816,128]{1,0:T(8,128)}) %reduce-scatter.32.cloned.1.call-update) | async-done | bytes 1441808 | tf_op jit(solution)/shard_map/reduce_scatter | solution.py:212
  2022.0 182.2 %reduce-scatter.26.cloned.1.call-done = f32[2048,128]{1,0:T(8,128)} async-done(((f32[2048,2048]{1,0:T(8,128)}), f32[2048,128]{1,0:T(8,128)}) %reduce-scatter.26.cloned.1.call-update) | async-done | bytes 1048592 | tf_op jit(solution)/shard_map/reduce_scatter | solution.py:282
  (217 shorter events, 37.6 us)
Async XLA Ops:
  7.2 61.9 %copy-start = (s32[16,2]{0,1:T(2,128)S(1)}, s32[16,2]{0,1:T(2,128)}, u32[]{:S(2)}) copy-start(s32[16,2]{0,1:T(2,128)} %param.19) | copy-start | bytes 388
  7.2 5.9 copy-start.24
  7.2 6.7 copy-start.16
  7.2 64.0 %all-gather.15.cloned.1.call-start = ((), (), s32[]{:S(2)}) async-start(), calls=%async_computation.11 | async-start | bytes 3145728 | tf_op jit(solution)/shard_map/all_gather | solution.py:142
  8.0 78.1 %all-gather.19.cloned.1.call-start = ((), (), s32[]{:S(2)}) async-start(), calls=%async_computation.13 | async-start | bytes 1114112 | tf_op jit(solution)/shard_map/all_gather | solution.py:137
  9.6 116.1 %all-gather.17.cloned.1.call-start = ((), (), s32[]{:S(2)}) async-start(), calls=%async_computation.12 | async-start | bytes 1114112 | tf_op jit(solution)/shard_map/all_gather | solution.py:138
  11.2 3.7 copy-start.49
  11.2 26.6 %copy-start.50 = (f32[64]{0:T(128)S(1)}, f32[64]{0:T(128)}, u32[]{:S(2)}) copy-start(f32[64]{0:T(128)} %param.22) | copy-start | bytes 772
  11.2 26.6 %copy-start.46 = (u32[32]{0:T(128)S(1)}, u32[32]{0:T(128)}, u32[]{:S(2)}) copy-start(u32[32]{0:T(128)} %constant.54) | copy-start | bytes 388
  11.2 166.6 %all-gather.21.cloned.1.call-start = ((), (), s32[]{:S(2)}) async-start(), calls=%async_computation.14 | async-start | bytes 4456448 | tf_op jit(solution)/shard_map/all_gather | solution.py:134
  13.1 216.4 %all-gather.23.cloned.1.call-start = ((), (), s32[]{:S(2)}) async-start(), calls=%async_computation.15 | async-start | bytes 4456448 | tf_op jit(solution)/shard_map/all_gather | solution.py:136
  13.9 294.8 %all-gather.25.cloned.1.call-start = ((), (), s32[]{:S(2)}) async-start(), calls=%async_computation.16 | async-start | bytes 8912896 | tf_op jit(solution)/shard_map/all_gather | solution.py:139
  14.8 355.6 %reduce-scatter.12.cloned.1.call-start = ((), (), s32[]{:S(2)}) async-start(), calls=%async_computation.17 | async-start | bytes 6291456 | tf_op jit(solution)/shard_map/reduce_scatter | solution.py:171
  37.8 140.0 %copy-start.30 = (f32[16,1,128]{2,1,0:T(1,128)}, f32[16,1,128]{2,1,0:T(1,128)S(1)}, u32[]{:S(2)}) copy-start(f32[16,1,128]{2,1,0:T(1,128)S(1)} %convert_element_type.198) | copy-start | bytes 24580
  68.4 161.1 %copy-start.32 = (f32[1024]{0:T(1024)}, f32[1024]{0:T(1024)S(1)}, u32[]{:S(2)}) copy-start(f32[1024]{0:T(1024)S(1)} %convert_element_type.163) | copy-start | bytes 12292
  69.3 19.0 copy-start.47
  70.3 17.9 copy-start.40
  71.2 14.8 copy-start.6
  73.6 104.2 %copy-start.38 = (f32[512]{0:T(512)}, f32[512]{0:T(512)S(1)}, u32[]{:S(2)}) copy-start(f32[512]{0:T(512)S(1)} %add_rsqrt_fusion.1) | copy-start | bytes 6148
  89.6 147.6 %copy-start.22 = (bf16[512,128]{0,1:T(8,128)(2,1)}, bf16[512,128]{0,1:T(8,128)(2,1)S(1)}, u32[]{:S(2)}) copy-start(bf16[512,128]{0,1:T(8,128)(2,1)S(1)} %get-tuple-element.42) | copy-start | bytes 393220
  89.9 146.4 %copy-start.13 = (f32[512,128]{1,0:T(8,128)}, f32[512,128]{1,0:T(8,128)S(1)}, u32[]{:S(2)}) copy-start(f32[512,128]{1,0:T(8,128)S(1)} %copy.72) | copy-start | bytes 786436
  127.7 112.6 %copy-start.25 = (bf16[512,256,1]{1,0,2:T(8,128)(2,1)}, bf16[512,256,1]{1,0,2:T(8,128)(2,1)S(1)}, u32[]{:S(2)}) copy-start(bf16[512,256,1]{1,0,2:T(8,128)(2,1)S(1)} %fusion.49) | copy-start | bytes 786436
  183.1 51.0 %copy-start.3 = (f32[512,1024]{1,0:T(8,128)}, f32[512,1024]{1,0:T(8,128)S(1)}, u32[]{:S(2)}) copy-start(f32[512,1024]{1,0:T(8,128)S(1)} %get-tuple-element.48) | copy-start | bytes 6291460
  183.1 51.0 %copy-start.36 = (f32[512]{0:T(512)}, f32[512]{0:T(512)S(1)}, u32[]{:S(2)}) copy-start(f32[512]{0:T(512)S(1)} %add_rsqrt_fusion) | copy-start | bytes 6148
  239.1 3.3 copy-start.2
  239.1 3.4 copy-start.34
  244.5 73.7 %copy-start.52 = (bf16[256,8,512]{2,0,1:T(8,128)(2,1)}, bf16[256,8,512]{2,0,1:T(8,128)(2,1)S(1)}, u32[]{:S(2)}) copy-start(bf16[256,8,512]{2,0,1:T(8,128)(2,1)S(1)} %fusion.32) | copy-start | bytes 6291460
  318.2 52.2 %copy-start.9 = (bf16[256,2048]{1,0:T(8,128)(2,1)S(1)}, bf16[256,2048]{1,0:T(8,128)(2,1)}, u32[]{:S(2)}) copy-start(bf16[256,2048]{1,0:T(8,128)(2,1)} %param.16) | copy-start | bytes 3145732
  318.2 150.1 %all-gather.29.cloned.1.call-start = ((), (), s32[]{:S(2)}) async-start(), calls=%async_computation.19 | async-start | bytes 12255232 | tf_op jit(solution)/shard_map/all_gather | solution.py:176
  320.5 180.9 %all-gather.27.cloned.1.call-start = ((), (), s32[]{:S(2)}) async-start(), calls=%async_computation.18 | async-start | bytes 3145728 | tf_op jit(solution)/shard_map/all_gather | solution.py:183
  374.3 224.8 %all-gather.31.cloned.1.call-start = ((), (), s32[]{:S(2)}) async-start(), calls=%async_computation.20 | async-start | bytes 12255232 | tf_op jit(solution)/shard_map/all_gather | solution.py:177
  376.7 255.0 %all-gather.35.cloned.1.call-start = ((), (), s32[]{:S(2)}) async-start(), calls=%async_computation.23 | async-start | bytes 3145728 | tf_op jit(solution)/shard_map/all_gather | solution.py:200
  377.4 354.8 %all-gather.33.cloned.1.call-start = ((), (), s32[]{:S(2)}) async-start(), calls=%async_computation.21 | async-start | bytes 12255232 | tf_op jit(solution)/shard_map/all_gather | solution.py:178
  379.8 442.2 %reduce-scatter.16.cloned.1.call-start = ((), (), s32[]{:S(2)}) async-start(), calls=%async_computation.24 | async-start | bytes 6291456 | tf_op jit(solution)/shard_map/reduce_scatter | solution.py:214
  747.9 11.1 copy-start.54
  747.9 11.1 copy-start.53
  769.8 55.2 %copy-start.11 = (bf16[256,2048]{1,0:T(8,128)(2,1)S(1)}, bf16[256,2048]{1,0:T(8,128)(2,1)}, u32[]{:S(2)}) copy-start(bf16[256,2048]{1,0:T(8,128)(2,1)} %param.31) | copy-start | bytes 3145732
  769.9 90.2 %all-gather.37.cloned.1.call-start = ((), (), s32[]{:S(2)}) async-start(), calls=%async_computation.25 | async-start | bytes 3145728 | tf_op jit(solution)/shard_map/all_gather | solution.py:222
  822.0 3.0 copy-start.8
  826.7 120.3 %all-reduce.8.cloned.1.call-start = ((), (), s32[]{:S(2)}) async-start(), calls=%async_computation.34 | async-start | bytes 3145728 | tf_op jit(solution)/shard_map/psum | solution.py:252
  827.5 41.1 %copy-start.26 = (bf16[512,256,1]{1,0,2:T(8,128)(2,1)S(1)}, bf16[512,256,1]{1,0,2:T(8,128)(2,1)}, u32[]{:S(2)}) copy-start(bf16[512,256,1]{1,0,2:T(8,128)(2,1)} %copy-done.25) | copy-start | bytes 786436
  868.6 4.9 slice-start
  868.6 5.9 slice-start.1
  874.5 2.5 copy-start.23
  895.0 213.1 %reduce-scatter.14.cloned.1.call-start = ((), (), s32[]{:S(2)}) async-start(), calls=%async_computation.22 | async-start | bytes 3145728 | tf_op jit(solution)/shard_map/reduce_scatter | solution.py:193
  906.2 41.9 %copy-start.41 = (f32[512]{0:T(512)S(1)}, f32[512]{0:T(512)}, u32[]{:S(2)}) copy-start(f32[512]{0:T(512)} %copy-done.40) | copy-start | bytes 6148
  906.2 41.9 %copy-start.48 = (f32[128]{0:T(128)S(1)}, f32[128]{0:T(128)}, u32[]{:S(2)}) copy-start(f32[128]{0:T(128)} %copy-done.47) | copy-start | bytes 1540
  906.2 43.1 %copy-start.31 = (f32[16,1,128]{2,1,0:T(1,128)S(1)}, f32[16,1,128]{2,1,0:T(1,128)}, u32[]{:S(2)}) copy-start(f32[16,1,128]{2,1,0:T(1,128)} %copy-done.30) | copy-start | bytes 24580
  906.2 43.1 %copy-start.39 = (f32[512]{0:T(512)S(1)}, f32[512]{0:T(512)}, u32[]{:S(2)}) copy-start(f32[512]{0:T(512)} %copy-done.38) | copy-start | bytes 6148
  906.2 207.3 %reduce-scatter.22.cloned.1.call-start = ((), (), s32[]{:S(2)}) async-start(), calls=%async_computation.28 | async-start | bytes 2228224 | tf_op jit(solution)/shard_map/reduce_scatter | solution.py:280
  953.2 160.3 %reduce-scatter.24.cloned.1.call-start = ((), (), s32[]{:S(2)}) async-start(), calls=%async_computation.29 | async-start | bytes 2228224 | tf_op jit(solution)/shard_map/reduce_scatter | solution.py:281
  958.1 262.3 %reduce-scatter.20.cloned.1.call-start = ((), (), s32[]{:S(2)}) async-start(), calls=%async_computation.27 | async-start | bytes 8912896 | tf_op jit(solution)/shard_map/reduce_scatter | solution.py:279
  967.0 362.4 %reduce-scatter.18.cloned.1.call-start = ((), (), s32[]{:S(2)}) async-start(), calls=%async_computation.26 | async-start | bytes 8912896 | tf_op jit(solution)/shard_map/reduce_scatter | solution.py:277
  967.0 3.5 copy-start.4
  978.2 582.5 %reduce-scatter.28.cloned.1.call-start = ((), (), s32[]{:S(2)}) async-start(), calls=%async_computation.31 | async-start | bytes 24510464 | tf_op jit(solution)/shard_map/reduce_scatter | solution.py:210
  991.8 799.5 %reduce-scatter.30.cloned.1.call-start = ((), (), s32[]{:S(2)}) async-start(), calls=%async_computation.32 | async-start | bytes 24510464 | tf_op jit(solution)/shard_map/reduce_scatter | solution.py:211
  1005.3 1016.7 %reduce-scatter.32.cloned.1.call-start = ((), (), s32[]{:S(2)}) async-start(), calls=%async_computation.33 | async-start | bytes 24510464 | tf_op jit(solution)/shard_map/reduce_scatter | solution.py:212
  1018.4 1185.8 %reduce-scatter.26.cloned.1.call-start = ((), (), s32[]{:S(2)}) async-start(), calls=%async_computation.30 | async-start | bytes 17825792 | tf_op jit(solution)/shard_map/reduce_scatter | solution.py:282
  1038.6 4.9 copy-start.7
  1038.6 4.9 copy-start.21
  1038.6 4.9 copy-start.28
  1043.5 62.4 %copy-start.10 = (bf16[256,2048]{1,0:T(8,128)(2,1)S(1)}, bf16[256,2048]{1,0:T(8,128)(2,1)}, u32[]{:S(2)}) copy-start(bf16[256,2048]{1,0:T(8,128)(2,1)} %param.16) | copy-start | bytes 3145732
  1046.6 61.5 %copy-start.44 = (f32[256]{0:T(256)S(1)}, f32[256]{0:T(256)}, u32[]{:S(2)}) copy-start(f32[256]{0:T(256)} %copy-done.43) | copy-start | bytes 3076
  1108.1 1096.1 %copy-start.1 = (s32[16,2]{0,1:T(2,128)S(1)}, s32[16,2]{0,1:T(2,128)}, u32[]{:S(2)}) copy-start(s32[16,2]{0,1:T(2,128)} %param.19) | copy-start | bytes 388
  (17 other events, 26.2 us)
Sparse Core Ops, SparseCore 0:
  9.6 35.1 all-gather.14
  47.6 38.4 all-gather.18
  88.8 36.8 all-gather.16
  128.3 49.4 all-gather.20
  180.4 49.0 all-gather.22
  232.0 76.5 all-gather.24
  318.3 52.0 reduce-scatter.11
  373.5 94.7 all-gather.28
  470.5 30.8 all-gather.26
  504.3 94.7 all-gather.30
  600.8 30.9 all-gather.34
  634.5 97.7 all-gather.32
  770.0 52.0 reduce-scatter.15
  826.8 33.1 all-gather.36
  895.1 51.8 all-reduce.7
  949.2 31.8 reduce-scatter.13
  985.3 59.9 reduce-scatter.21
  1049.9 60.6 reduce-scatter.23
  1115.2 105.2 reduce-scatter.19
  1224.9 104.3 reduce-scatter.17
  1334.0 226.5 reduce-scatter.27
  1565.3 225.9 reduce-scatter.29
  1796.0 225.9 reduce-scatter.31
  2026.5 177.6 reduce-scatter.25
where the time goes:
time: 2220 us; the launch traced here: 2210 us
  waiting for transfers between devices  1790 us (81%)
  matrix products  213 us (10%)
  blocking collectives  132 us (6%)
  other arithmetic  45.6 us (2%)
    reduce_scatter x1, waiting for transfers between devices, local(): lax.psum_scatter(d_gate, 'dp', scatter_dimension=0, tiled=True)  231 us
    reduce_scatter x1, waiting for transfers between devices, local(): lax.psum_scatter(d_down, 'dp', scatter_dimension=1, tiled=True)  231 us
    reduce_scatter x1, waiting for transfers between devices, local(): lax.psum_scatter(d_up, 'dp', scatter_dimension=0, tiled=True)  231 us
    reduce_scatter x1, waiting for transfers between devices, local(): lax.psum_scatter(d_out, 'dp', scatter_dimension=1, tiled=True)  182 us
    reduce_scatter x1, waiting for transfers between devices, local(): lax.psum_scatter(d_q_down, 'dp', scatter_dimension=0, tiled=True)  109 us
    reduce_scatter x1, waiting for transfers between devices, local(): lax.psum_scatter(d_q_up, 'dp', scatter_dimension=0, tiled=True)  107 us
    all_gather x1, waiting for transfers between devices, local(): lax.all_gather(ffn_parts[3], 'dp', axis=1, tiled=True)  101 us
    all_gather x1, waiting for transfers between devices, local(): lax.all_gather(ffn_parts[1], 'dp', axis=0, tiled=True)  88.4 us
  transfers between devices with their start and end apart: 24, of which 20 were waited for; matrix products, arithmetic and copies ran while one was open for 8% of the time, Pallas kernels for 0%

commit v1 on v0

v1 whole, which is shorter than its diff:
```python
import math

import jax
import jax.numpy as jnp
from jax import lax
from jax.sharding import PartitionSpec as P

norm_eps = 1e-05
masked_score = -1e30
BF = jnp.bfloat16
F32 = jnp.float32


def matmul(left, right):
    return jnp.dot(left, right, preferred_element_type=F32)


def matmul_nt(left, right):
    return lax.dot_general(left, right, (((1,), (1,)), ((), ())), preferred_element_type=F32)


def matmul_tn(left, right):
    return lax.dot_general(left, right, (((0,), (0,)), ((), ())), preferred_element_type=F32)


def inv_rms(values):
    return lax.rsqrt(jnp.mean(values * values, axis=-1, keepdims=True) + norm_eps)


def norm_back(grad_out, unit_vals, inverse, gain_vals):
    scaled = grad_out * gain_vals
    return inverse * (scaled - unit_vals * jnp.mean(scaled * unit_vals, axis=-1, keepdims=True))


def rotate(values, cos_tab, sin_tab):
    half_dim = values.shape[-1] // 2
    first_half = values[..., :half_dim]
    second_half = values[..., half_dim:]
    return jnp.concatenate(
        [
            first_half * cos_tab - second_half * sin_tab,
            second_half * cos_tab + first_half * sin_tab,
        ],
        axis=-1,
    )


def unrotate(values, cos_tab, sin_tab):
    return rotate(values, cos_tab, -sin_tab)


def rope_tables(positions, head_dim):
    half_dim = head_dim // 2
    frequency = jnp.exp(
        jnp.arange(half_dim, dtype=jnp.float32) * (-2.0 * math.log(10000.0) / head_dim)
    )
    angles = positions.astype(jnp.float32)[:, None] * frequency[None, :]
    return (jnp.cos(angles), jnp.sin(angles))


def token_positions(segments, starts):
    token_index = jnp.arange(segments.shape[0], dtype=jnp.int32)
    labels = jnp.arange(1, starts.shape[0] + 1, dtype=jnp.int32)
    inside = segments[:, None] == labels[None, :]
    firsts = jnp.sum((segments[:, None] < labels[None, :]).astype(jnp.int32), axis=0)
    shifts = jnp.sum(jnp.where(inside, (starts - firsts)[None, :], 0), axis=1)
    return token_index + shifts


def build(n):
    lines = n // 4

    def dp_of(line, side, core):
        return (line * 2 + side) * 2 + core

    every = [(a, s, c) for a in range(lines) for s in range(2) for c in range(2)]
    core_pairs = [(dp_of(a, s, c), dp_of(a, s, 1 - c)) for a, s, c in every]
    side_pairs = [(dp_of(a, s, c), dp_of(a, 1 - s, c)) for a, s, c in every]
    line_groups = [[dp_of(a, s, c) for a in range(lines)] for s in range(2) for c in range(2)]

    def core_swap(value):
        return lax.ppermute(value, "dp", core_pairs)

    def side_swap(value):
        return lax.ppermute(value, "dp", side_pairs)

    def half_swap(value):
        return lax.ppermute(value, "tensor", [(0, 1), (1, 0)])

    def line_gather(value):
        return lax.all_gather(value, "dp", axis=0, tiled=True, axis_index_groups=line_groups)

    def line_sum(value):
        return lax.psum_scatter(
            value, "dp", scatter_dimension=0, tiled=True, axis_index_groups=line_groups
        )

    def quad_gather(own):
        pair = jnp.concatenate([own, half_swap(own)], axis=0)
        return jnp.concatenate([pair, core_swap(pair)], axis=0)

    def quad_sum(part):
        half = part.shape[0] // 2
        pair = part[:half] + core_swap(part[half:].astype(BF)).astype(F32)
        own = half // 2
        return pair[:own] + half_swap(pair[own:].astype(BF)).astype(F32)

    def local(
        tokens,
        group_of_device,
        segment_ids,
        start_pos,
        attn_gain,
        q_down,
        q_gain,
        q_up,
        key_proj,
        value_proj,
        out_proj,
        ffn_gain,
        gate_proj,
        up_proj,
        down_proj,
        out_grad,
    ):
        own_rows, width = tokens.shape
        place = lax.axis_index("dp")
        core = place % 2
        side = (place // 2) % 2
        half = lax.axis_index("tensor")
        head_dim = key_proj.shape[1]
        rank = q_down.shape[1]
        scale = 1.0 / math.sqrt(head_dim)
        shard = q_down.shape[0]
        block = 2 * shard
        hid = gate_proj.shape[1] // 2
        feats = q_up.shape[1] // 2
        heads = feats // head_dim
        q_shard = q_up.shape[0]

        def order(flag, first, second, axis):
            return jnp.where(
                flag == 0,
                jnp.concatenate([first, second], axis=axis),
                jnp.concatenate([second, first], axis=axis),
            )

        def to_rel(value):
            rows = value.shape[0]
            split = value.reshape(rows, lines, 2, block)
            mine = lax.dynamic_index_in_dim(split, side, 2, keepdims=False)
            theirs = lax.dynamic_index_in_dim(split, 1 - side, 2, keepdims=False)
            return jnp.concatenate(
                [mine.reshape(rows, lines * block), theirs.reshape(rows, lines * block)], axis=1
            )

        def from_rel(value):
            rows = value.shape[0]
            mine = value[:, : lines * block].reshape(rows, lines, 1, block)
            theirs = value[:, lines * block :].reshape(rows, lines, 1, block)
            return order(side, mine, theirs, 2).reshape(rows, width)

        x_low = to_rel(tokens)
        dy_low = to_rel(out_grad)
        x_quad = quad_gather(x_low)

        mixed_cols = jnp.concatenate(
            [
                lax.dynamic_slice_in_dim(q_down, half * (rank // 2), rank // 2, 1),
                lax.dynamic_slice_in_dim(key_proj, half * (head_dim // 2), head_dim // 2, 1),
                lax.dynamic_slice_in_dim(value_proj, half * (head_dim // 2), head_dim // 2, 1),
            ],
            axis=1,
        ).astype(BF)
        qkv_cols = mixed_cols.shape[1]
        gain_row = jnp.concatenate(
            [attn_gain, ffn_gain, q_gain, jnp.zeros((qkv_cols - 2 * shard - q_shard,), F32)]
        ).astype(BF)
        gain_rows = jnp.concatenate([gain_row[None, :], jnp.zeros((15, qkv_cols), BF)], axis=0)
        qkv_piece = jnp.concatenate([mixed_cols, gain_rows], axis=0)
        qkv_mine = line_gather(qkv_piece)
        qkv_theirs = side_swap(qkv_mine)

        def spread(local_weight):
            cols = local_weight.shape[1] // 2
            low = local_weight.astype(BF)
            keep = lax.dynamic_slice_in_dim(low, core * cols, cols, 1)
            give = lax.dynamic_slice_in_dim(low, (1 - core) * cols, cols, 1)
            piece = order(core, keep, core_swap(give), 0)
            mine = line_gather(piece)
            return mine, side_swap(mine)

        q_up_mine, q_up_theirs = spread(q_up)
        out_mine, out_theirs = spread(out_proj.T)
        gate_mine, gate_theirs = spread(gate_proj)
        up_mine, up_theirs = spread(up_proj)
        down_mine, down_theirs = spread(down_proj.T)

        qkv_part = jnp.stack(
            [
                qkv_mine.reshape(lines, shard + 16, qkv_cols),
                qkv_theirs.reshape(lines, shard + 16, qkv_cols),
            ]
        )
        qkv_far = half_swap(qkv_part)
        q_c, k_c = rank // 2, rank // 2 + head_dim // 2
        qkv_wide = jnp.concatenate(
            [
                order(half, qkv_part[..., :q_c], qkv_far[..., :q_c], 3),
                order(half, qkv_part[..., q_c:k_c], qkv_far[..., q_c:k_c], 3),
                order(half, qkv_part[..., k_c:], qkv_far[..., k_c:], 3),
            ],
            axis=3,
        )
        qkv_other = core_swap(qkv_wide)
        qkv_both = order(core, qkv_wide[:, :, None], qkv_other[:, :, None], 2)
        qkv_set = qkv_both[:, :, :, :shard, :].reshape(width, rank + 2 * head_dim)
        flat_gain = qkv_part[:, :, shard, :]
        flat_far = core_swap(flat_gain)
        gain_both = order(core, flat_gain[:, :, None], flat_far[:, :, None], 2)
        gain_one = gain_both[..., :shard].reshape(width).astype(F32)
        gain_two = gain_both[..., shard : 2 * shard].reshape(width).astype(F32)
        q_gain_rel = gain_both[..., 2 * shard : 2 * shard + q_shard].reshape(
            2, lines, 2 * q_shard
        )
        gain_q = (
            order(side, q_gain_rel[0][:, None], q_gain_rel[1][:, None], 1)
            .reshape(rank)
            .astype(F32)
        )
        q_up_set = order(
            side,
            q_up_mine.reshape(lines, 1, 2 * q_shard, feats),
            q_up_theirs.reshape(lines, 1, 2 * q_shard, feats),
            1,
        ).reshape(rank, feats)

        group_pair = jnp.stack([group_of_device[0], core_swap(group_of_device)[0]])
        group_len = segment_ids.shape[1]
        token_order = jnp.concatenate(
            [
                half * own_rows + jnp.arange(own_rows, dtype=jnp.int32),
                (1 - half) * own_rows + jnp.arange(own_rows, dtype=jnp.int32),
            ]
        )

        def of_group(group_id):
            segments = lax.dynamic_index_in_dim(segment_ids, group_id, 0, keepdims=False)
            starts = lax.dynamic_index_in_dim(start_pos, group_id, 0, keepdims=False)
            positions = token_positions(segments, starts)
            split = jnp.stack([segments, positions]).reshape(2, 2, own_rows)
            near = lax.dynamic_index_in_dim(split, half, 1, keepdims=False)
            far = lax.dynamic_index_in_dim(split, 1 - half, 1, keepdims=False)
            return jnp.concatenate([near, far], axis=1)

        seg_a, pos_a = of_group(group_pair[0])
        seg_b, pos_b = of_group(group_pair[1])
        segs = jnp.stack([seg_a, seg_b])
        cos_flat, sin_flat = rope_tables(jnp.concatenate([pos_a, pos_b]), head_dim)
        all_rows = 2 * group_len
        cos_tab = cos_flat[:, None, :]
        sin_tab = sin_flat[:, None, :]
        causal = token_order[None, :] <= token_order[:, None]
        visible = (segs[:, None, :] == segs[:, :, None]) | (segs[:, None, :] == 0)
        allowed = (causal[None] & visible)[:, None]

        x_f = x_quad.astype(F32)
        normed = (x_f * inv_rms(x_f) * gain_one).astype(BF)
        first = matmul(normed, qkv_set)
        latent = first[:, :rank]
        inv_q = inv_rms(latent)
        latent_n = (latent * inv_q * gain_q).astype(BF)
        queries = rotate(
            matmul(latent_n, q_up_set).reshape(all_rows, heads, head_dim), cos_tab, sin_tab
        ).astype(BF)
        queries = queries.reshape(2, group_len, heads, head_dim)
        keys_rot = (
            rotate(first[:, rank : rank + head_dim], cos_flat, sin_flat)
            .astype(BF)
            .reshape(2, group_len, head_dim)
        )
        values = first[:, rank + head_dim :].astype(BF).reshape(2, group_len, head_dim)
        raw_scores = (
            jnp.einsum("gqhe,gke->ghqk", queries, keys_rot, preferred_element_type=F32) * scale
        )
        raw_scores = jnp.where(allowed, raw_scores, masked_score)
        top_score = jnp.max(raw_scores, axis=-1, keepdims=True)
        expd = jnp.exp(raw_scores - top_score)
        row_total = jnp.sum(expd, axis=-1, keepdims=True)
        log_total = top_score + jnp.log(row_total)
        head_mix = jnp.einsum(
            "ghqk,gke->gqhe", (expd / row_total).astype(BF), values, preferred_element_type=F32
        )
        head_mix = head_mix.reshape(all_rows, feats).astype(BF)
        edge = lines * block
        attn_out = jnp.concatenate(
            [matmul_nt(head_mix, out_mine), matmul_nt(head_mix, out_theirs)], axis=1
        )
        residual = x_low.astype(F32) + quad_sum(attn_out)

        inv_two = inv_rms(residual)
        unit_two = residual * inv_two
        normed_two = quad_gather((unit_two * gain_two).astype(BF))
        grad_quad = quad_gather(dy_low)
        gate_act = matmul(normed_two[:, :edge], gate_mine) + matmul(
            normed_two[:, edge:], gate_theirs
        )
        up_act = matmul(normed_two[:, :edge], up_mine) + matmul(normed_two[:, edge:], up_theirs)
        gate_sig = jax.nn.sigmoid(gate_act)
        gate_silu = gate_act * gate_sig
        hidden = (gate_silu * up_act).astype(BF)

        def grad_sum(lhs, rhs):
            give = matmul_tn(lhs[:, edge:], rhs).astype(BF)
            part = (matmul_tn(lhs[:, :edge], rhs) + side_swap(give).astype(F32)).astype(BF)
            mine = line_sum(part)
            rows = mine.shape[0] // 2
            keep = lax.dynamic_slice_in_dim(mine, core * rows, rows, 0)
            away = lax.dynamic_slice_in_dim(mine, (1 - core) * rows, rows, 0)
            return order(core, keep, core_swap(away), 1).astype(F32)

        down_total = grad_sum(grad_quad, hidden).T
        ffn_out = jnp.concatenate(
            [matmul_nt(hidden, down_mine), matmul_nt(hidden, down_theirs)], axis=1
        )
        output = from_rel((residual + quad_sum(ffn_out)).astype(BF))
        d_hidden = matmul(grad_quad[:, :edge], down_mine) + matmul(
            grad_quad[:, edge:], down_theirs
        )
        d_gate_act = (d_hidden * up_act * gate_sig * (1.0 + gate_act * (1.0 - gate_sig))).astype(
            BF
        )
        d_up_act = (d_hidden * gate_silu).astype(BF)
        d_normed_two = quad_sum(
            jnp.concatenate(
                [
                    matmul_nt(d_gate_act, gate_mine) + matmul_nt(d_up_act, up_mine),
                    matmul_nt(d_gate_act, gate_theirs) + matmul_nt(d_up_act, up_theirs),
                ],
                axis=1,
            )
        )
        gate_total = grad_sum(normed_two, d_gate_act)
        up_total = grad_sum(normed_two, d_up_act)
        d_ffn_gain = jnp.sum(d_normed_two * unit_two, axis=0)
        d_resid = dy_low.astype(F32) + norm_back(d_normed_two, unit_two, inv_two, gain_two)

        d_attn = quad_gather(d_resid.astype(BF))
        out_total = grad_sum(d_attn, head_mix).T
        d_mix = (
            (matmul(d_attn[:, :edge], out_mine) + matmul(d_attn[:, edge:], out_theirs))
            .astype(BF)
            .reshape(2, group_len, heads, head_dim)
        )
        again = jnp.einsum("gqhe,gke->ghqk", queries, keys_rot, preferred_element_type=F32) * scale
        again = jnp.where(allowed, again, masked_score)
        probs = jnp.exp(again - log_total)
        d_probs = jnp.einsum("gqhe,gke->ghqk", d_mix, values, preferred_element_type=F32)
        d_values = jnp.einsum(
            "ghqk,gqhe->gke", probs.astype(BF), d_mix, preferred_element_type=F32
        )
        row_dot = jnp.sum(probs * d_probs, axis=-1, keepdims=True)
        d_scores = (probs * (d_probs - row_dot)).astype(BF)
        d_queries = (
            jnp.einsum("ghqk,gke->gqhe", d_scores, keys_rot, preferred_element_type=F32) * scale
        )
        d_keys = (
            jnp.einsum("ghqk,gqhe->gke", d_scores, queries, preferred_element_type=F32) * scale
        )
        d_query_pre = (
            unrotate(d_queries.reshape(all_rows, heads, head_dim), cos_tab, sin_tab)
            .reshape(all_rows, feats)
            .astype(BF)
        )
        d_first = quad_sum(
            jnp.concatenate(
                [
                    matmul_nt(d_query_pre, q_up_set),
                    d_keys.reshape(all_rows, head_dim),
                    d_values.reshape(all_rows, head_dim),
                ],
                axis=1,
            )
        )
        d_q_up = matmul_tn(latent_n, d_query_pre).astype(BF).reshape(lines, 2, 2 * q_shard, feats)
        q_up_give = lax.dynamic_index_in_dim(d_q_up, 1 - side, 1, keepdims=False)
        q_up_keep = lax.dynamic_index_in_dim(d_q_up, side, 1, keepdims=False)
        q_up_part = (q_up_keep.astype(F32) + side_swap(q_up_give).astype(F32)).astype(BF)
        q_up_sum = line_sum(q_up_part.reshape(lines * 2 * q_shard, feats))
        q_up_near = lax.dynamic_slice_in_dim(q_up_sum, core * q_shard, q_shard, 0)
        q_up_away = lax.dynamic_slice_in_dim(q_up_sum, (1 - core) * q_shard, q_shard, 0)
        q_up_total = order(core, q_up_near, core_swap(q_up_away), 1).astype(F32)

        d_latent_n = d_first[:, :rank]
        unit_q = latent[:own_rows] * inv_q[:own_rows]
        d_q_gain = jnp.sum(d_latent_n * unit_q, axis=0)
        d_latent = norm_back(d_latent_n, unit_q, inv_q[:own_rows], gain_q).astype(BF)
        d_keys_pre = unrotate(
            d_first[:, rank : rank + head_dim], cos_flat[:own_rows], sin_flat[:own_rows]
        ).astype(BF)
        d_back = jnp.concatenate(
            [d_latent, d_keys_pre, d_first[:, rank + head_dim :].astype(BF)], axis=1
        )
        d_back_quad = quad_gather(d_back)
        d_normed = matmul_nt(d_back, qkv_set)
        inv_own = inv_rms(x_low.astype(F32))
        unit_own = x_low.astype(F32) * inv_own
        d_attn_gain = jnp.sum(d_normed * unit_own, axis=0)
        in_grad = from_rel((d_resid + norm_back(d_normed, unit_own, inv_own, gain_one)).astype(BF))

        normed_rows = lax.dynamic_index_in_dim(
            normed.reshape(all_rows, 2 * lines, 2, shard), core, 2, keepdims=False
        ).reshape(all_rows, 2 * lines * shard)
        back_cols = jnp.concatenate(
            [
                lax.dynamic_slice_in_dim(d_back_quad, half * (rank // 2), rank // 2, 1),
                lax.dynamic_slice_in_dim(
                    d_back_quad, rank + half * (head_dim // 2), head_dim // 2, 1
                ),
                lax.dynamic_slice_in_dim(
                    d_back_quad, rank + head_dim + half * (head_dim // 2), head_dim // 2, 1
                ),
            ],
            axis=1,
        )
        d_qkv = matmul_tn(normed_rows, back_cols).reshape(2, lines, shard, qkv_cols)
        q_gain_abs = d_q_gain.reshape(lines, 2, 2 * q_shard)
        q_gain_parts = jnp.stack(
            [
                lax.dynamic_index_in_dim(q_gain_abs, side, 1, keepdims=False),
                lax.dynamic_index_in_dim(q_gain_abs, 1 - side, 1, keepdims=False),
            ]
        )
        d_gain = jnp.concatenate(
            [
                d_attn_gain.reshape(2, lines, block),
                d_ffn_gain.reshape(2, lines, block),
                q_gain_parts,
                jnp.zeros((2, lines, qkv_cols - 2 * block - 2 * q_shard), F32),
            ],
            axis=2,
        )[:, :, None, :]
        d_qkv = jnp.concatenate([d_qkv, d_gain, jnp.zeros((2, lines, 15, qkv_cols), F32)], axis=2)
        d_qkv_part = (d_qkv[0] + side_swap(d_qkv[1].astype(BF)).astype(F32)).astype(BF)
        d_qkv_sum = line_sum(d_qkv_part.reshape(lines * (shard + 16), qkv_cols))
        d_qkv_far = half_swap(d_qkv_sum)
        gain_pair = d_qkv_sum[shard : shard + 1].astype(F32) + d_qkv_far[
            shard : shard + 1
        ].astype(F32)
        gain_total = (gain_pair + core_swap(gain_pair.astype(BF)).astype(F32))[0]
        near, far = d_qkv_sum[:shard], d_qkv_far[:shard]
        q_down_total = order(half, near[:, :q_c], far[:, :q_c], 1).astype(F32)
        key_total = order(half, near[:, q_c:k_c], far[:, q_c:k_c], 1).astype(F32)
        value_total = order(half, near[:, k_c:], far[:, k_c:], 1).astype(F32)
        attn_gain_total = lax.dynamic_slice_in_dim(gain_total, core * shard, shard, 0)
        ffn_gain_total = lax.dynamic_slice_in_dim(gain_total, block + core * shard, shard, 0)
        q_gain_total = lax.dynamic_slice_in_dim(gain_total, 2 * block + core * q_shard, q_shard, 0)
        return (
            output,
            in_grad,
            attn_gain_total,
            q_down_total,
            q_gain_total,
            q_up_total,
            key_total,
            value_total,
            out_total,
            ffn_gain_total,
            gate_total,
            up_total,
            down_total,
        )

    return local


def solution(mesh):
    placed = (
        P(("dp", "tensor"), None),
        P("dp"),
        P(),
        P(),
        P("dp"),
        P("dp", None),
        P("dp"),
        P("dp", "tensor"),
        P("dp", None),
        P("dp", None),
        P("tensor", "dp"),
        P("dp"),
        P("dp", "tensor"),
        P("dp", "tensor"),
        P("tensor", "dp"),
        P(("dp", "tensor"), None),
    )
    return jax.shard_map(
        build(mesh.shape["dp"]),
        mesh=mesh,
        in_specs=placed,
        out_specs=(
            P(("dp", "tensor"), None),
            P(("dp", "tensor"), None),
            P("dp"),
            P("dp", None),
            P("dp"),
            P("dp", "tensor"),
            P("dp", None),
            P("dp", None),
            P("tensor", "dp"),
            P("dp"),
            P("dp", "tensor"),
            P("dp", "tensor"),
            P("tensor", "dp"),
        ),
        check_vma=False,
    )
```

time: 2220 us -> 950 us (0.43)
  waiting for transfers between devices: 1790 us -> 429 us
  blocking collectives: 132 us -> 33.9 us
  local copies, waits for them, and re-layouts: 16.5 us -> 100 us
  other arithmetic: 45.6 us -> 127 us
  starting transfers between devices: 1.16 us -> 46.1 us
  matrix products: 213 us -> 186 us
    reduce_scatter x11 -> x6, waiting for transfers between devices: 1170 us -> 12.9 us  [line_sum(): lax.psum_scatter(value, 'dp', scatter_dimension=0, tiled=True, axis_index...]
    all_gather x12 -> x5, waiting for transfers between devices: 569 us -> 0.03 us  [line_gather(): lax.all_gather(value, 'dp', axis=0, tiled=True, axis_index_groups=line_gr...]
    ppermute x0 -> x46, waiting for transfers between devices: none -> 415 us  [the longest x12 268 us: side_swap(): return lax.ppermute(value, 'dp', side_pairs)]
    unnamed x2 -> x0, blocking collectives: 86.7 us -> none
    ppermute x0 -> x46, starting transfers between devices: none -> 45.7 us  [the longest x23 31.5 us: core_swap(): return lax.ppermute(value, 'dp', core_pairs)]
    psum x1 -> x0, waiting for transfers between devices: 40.8 us -> none  [local(): lax.psum(d_latent_part.astype(jnp.bfloat16), 'tensor').astype(jnp.float32)]
    concatenate x1 -> x21, other arithmetic: 1.53 us -> 31.9 us  [the longest x4 14.9 us: quad_gather(): return jnp.concatenate([pair, core_swap(pair)], axis=0)]
    dot_general x8 -> x10, matrix products: 76.4 us -> 49.1 us  [matmul_tn(): lax.dot_general(left, right, (((0,), (0,)), ((), ())), preferred_element_...]
  transfers between devices with their start and end apart: 24 -> 57, of which waited for: 20 -> 21; matrix products, arithmetic and copies ran while one was open for 8% -> 38% of each run, Pallas kernels for 0% -> 0%
where the time goes in v1:
time: 950 us; the launch traced here: 941 us
  waiting for transfers between devices  429 us (45%)
  matrix products  186 us (20%)
  other arithmetic  127 us (13%)
  local copies, waits for them, and re-layouts  100 us (11%)
  starting transfers between devices  46.1 us (5%)
  blocking collectives  33.9 us (4%)
  between operations  18.4 us (2%)
    ppermute x12, waiting for transfers between devices, side_swap(): return lax.ppermute(value, 'dp', side_pairs)  268 us
    ppermute x11, waiting for transfers between devices, half_swap(): return lax.ppermute(value, 'tensor', [(0, 1), (1, 0)])  144 us
    dot_general x10, matrix products, matmul(): return jnp.dot(left, right, preferred_element_type=F32)  64.3 us
    dot_general x10, matrix products, matmul_nt(): lax.dot_general(left, right, (((1,), (1,)), ((), ())), preferred_element_...  54 us
    dot_general x10, matrix products, matmul_tn(): lax.dot_general(left, right, (((0,), (0,)), ((), ())), preferred_element_...  49.1 us
    unnamed x218, local copies, waits for them, and re-layouts  34.8 us
    all_gather x1, blocking collectives, line_gather(): lax.all_gather(value, 'dp', axis=0, tiled=True, axis_index_groups=line_gr...  33.9 us
    ppermute x23, starting transfers between devices, core_swap(): return lax.ppermute(value, 'dp', core_pairs)  31.5 us
  transfers between devices with their start and end apart: 57, of which 21 were waited for; matrix products, arithmetic and copies ran while one was open for 38% of the time, Pallas kernels for 0%

profile of v1, /device:TPU:1, one launch (start us, length us, event | category | flops | bytes accessed | tf_op | source)
XLA Modules:
  0.0 940.7 jit_solution(1725074151649903338)
XLA Ops:
  17.0 33.9 %all_gather.18 = bf16[576,768]{1,0:T(8,128)(2,1)S(1)} all-gather(bf16[144,768]{1,0:T(8,128)(2,1)S(1)} %maximum_maximum_fusion.1), channel_id=1, replica_groups={{0,8,16,24},{2,10,18,26},{4,12,20,28},{6,14,22,30},{1,9,17,25},{3,11,19..., dimensions={0}, use_global_device_ids=true | all-gather | bytes 1105920 | tf_op jit(solution)/shard_map/all_gather | solution.py:91
  59.6 7.6 constant_dynamic-slice_fusion.24
  84.4 51.9 %collective-permute-done.4 = bf16[2,4,144,768]{3,2,1,0:T(8,128)(2,1)} collective-permute-done((bf16[2,4,144,768]{3,2,1,0:T(8,128)(2,1)}, bf16[2,4,144,768]{3,2,1,0:T(8,128)(2,1)}, u32[]{:S(2)}, u32[]{:S(2)}) %collective-permute-start.4) | collective-permute-done | bytes 1769504 | tf_op jit(solution)/shard_map/ppermute | solution.py:88
  139.9 3.4 fusion.127
  153.3 19.6 %collective-permute-done.8 = bf16[512,1024]{1,0:T(8,128)(2,1)} collective-permute-done((bf16[512,1024]{1,0:T(8,128)(2,1)}, bf16[512,1024]{1,0:T(8,128)(2,1)}, u32[]{:S(2)}, u32[]{:S(2)}) %collective-permute-start.8) | collective-permute-done | bytes 1048608 | tf_op jit(solution)/shard_map/ppermute | solution.py:85
  178.5 5.3 fusion
  184.2 6.2 fusion.8
  191.0 11.4 %fusion.18 = f32[1024,1536]{1,0:T(8,128)S(1)} fusion(bf16[2048,1536]{1,0:T(8,128)(2,1)S(1)} %bitcast.261, f32[2048]{0:T(1024)S(1)} %bitcast.297, f32[1024]{0:T(1024)S(1)} %add_rsqrt_fusion.1, bf16[512,2048]{0,1:T(8,128)(2,1)} %collective-permute-done.1, bf16[256,2048]{0,1:T(8,128)(2,1)} %collective-permute-done, bf16[256,1024]{0,1:T(8,128)(2,1)S(1)} %bitcast.228, ...), kind=kOutput, calls=%fused_computation.44 | convolution fusion | flops 6465519616 | bytes 16789504 | tf_op jit(solution)/shard_map/dot_general | solution.py:15
  202.9 3.6 fusion.88
  225.7 4.4 collective-permute-done.10
  230.1 4.1 fusion.140
  249.5 3.5 fusion.17
  256.7 14.0 %collective-permute-done.23 = bf16[256,2048]{0,1:T(8,128)(2,1)S(1)} collective-permute-done((bf16[256,2048]{0,1:T(8,128)(2,1)}, bf16[256,2048]{0,1:T(8,128)(2,1)S(1)}, u32[]{:S(2)}, u32[]{:S(2)}) %collective-permute-start.23) | collective-permute-done | bytes 1048608 | tf_op jit(solution)/shard_map/ppermute | solution.py:88
  274.3 18.8 %collective-permute-done.12 = bf16[256,2048]{0,1:T(8,128)(2,1)} collective-permute-done((bf16[256,2048]{0,1:T(8,128)(2,1)}, bf16[256,2048]{0,1:T(8,128)(2,1)}, u32[]{:S(2)}, u32[]{:S(2)}) %collective-permute-start.12) | collective-permute-done | bytes 1048608 | tf_op jit(solution)/shard_map/ppermute | solution.py:88
  298.3 22.3 %collective-permute-done.13 = bf16[256,2048]{0,1:T(8,128)(2,1)} collective-permute-done((bf16[256,2048]{0,1:T(8,128)(2,1)}, bf16[256,2048]{0,1:T(8,128)(2,1)}, u32[]{:S(2)}, u32[]{:S(2)}) %collective-permute-start.13) | collective-permute-done | bytes 1048608 | tf_op jit(solution)/shard_map/ppermute | solution.py:88
  325.9 6.5 pad_maximum_fusion.8
  332.7 6.1 fusion.51
  338.7 5.4 convolution_add_fusion
  346.6 35.0 %collective-permute-done.18 = bf16[1024,1408]{0,1:T(8,128)(2,1)} collective-permute-done((bf16[1024,1408]{0,1:T(8,128)(2,1)}, bf16[1024,1408]{0,1:T(8,128)(2,1)}, u32[]{:S(2)}, u32[]{:S(2)}) %collective-permute-start.18) | collective-permute-done | bytes 2883616 | tf_op jit(solution)/shard_map/ppermute | solution.py:85
  381.6 5.3 fusion.76
  386.9 5.6 convolution_add_fusion.1
  392.5 50.8 %collective-permute-done.16 = bf16[1024,1408]{0,1:T(8,128)(2,1)S(1)} collective-permute-done((bf16[1024,1408]{0,1:T(8,128)(2,1)}, bf16[1024,1408]{0,1:T(8,128)(2,1)S(1)}, u32[]{:S(2)}, u32[]{:S(2)}) %collective-permute-start.16) | collective-permute-done | bytes 2883616 | tf_op jit(solution)/shard_map/ppermute | solution.py:85
  444.9 5.3 fusion.78
  450.2 13.5 %multiply_convert_fusion.1 = (bf16[1024,1408]{1,0:T(8,128)(2,1)}, bf16[1024,1408]{1,0:T(8,128)(2,1)}, bf16[1024,1408]{1,0:T(8,128)(2,1)}) fusion(f32[1024,1408]{1,0:T(8,128)} %convolution_add_fusion, f32[1024,1408]{1,0:T(8,128)} %convolution_add_fusion.1, f32[1024,1408]{1,0:T(8,128)} %fusion.78, bf16[1024,1408]{0,1:T(8,128)(2,1)} %all-gather.10.cloned.1.call-done, ...), kind=kOutput, calls=%fused_computation.30 | convolution fusion | flops 2975858688 | bytes 30932992 | tf_op jit(solution)/shard_map/dot_general | solution.py:15
  463.6 5.6 convolution_convert_fusion
  469.6 5.4 fusion.144
  475.0 5.4 fusion.143
  480.4 5.1 convolution_add_fusion.3
  485.5 45.9 %collective-permute-done.44 = bf16[1024,1408]{1,0:T(8,128)(2,1)S(1)} collective-permute-done((bf16[1024,1408]{1,0:T(8,128)(2,1)S(1)}, bf16[1024,1408]{1,0:T(8,128)(2,1)S(1)}, u32[]{:S(2)}, u32[]{:S(2)}) %collective-permute-start.44) | collective-permute-done | bytes 2883616 | tf_op jit(solution)/shard_map/ppermute | solution.py:85
  531.4 4.7 add_convert_fusion
  536.2 7.7 convolution_add_fusion.4
  547.6 5.2 convolution_convert_fusion.1
  552.8 6.4 fusion.142
  559.2 6.9 fusion.141
  577.2 37.5 %collective-permute-done.42 = bf16[1024,1408]{1,0:T(8,128)(2,1)S(1)} collective-permute-done((bf16[1024,1408]{1,0:T(8,128)(2,1)}, bf16[1024,1408]{1,0:T(8,128)(2,1)S(1)}, u32[]{:S(2)}, u32[]{:S(2)}) %collective-permute-start.42) | collective-permute-done | bytes 2883616 | tf_op jit(solution)/shard_map/ppermute | solution.py:85
  614.7 4.7 add_convert_fusion.1
  619.5 3.7 fusion.15
  624.6 4.9 convolution_convert_fusion.2
  631.6 13.3 %collective-permute-done.22 = bf16[256,2048]{0,1:T(8,128)(2,1)S(1)} collective-permute-done((bf16[256,2048]{0,1:T(8,128)(2,1)S(1)}, bf16[256,2048]{0,1:T(8,128)(2,1)S(1)}, u32[]{:S(2)}, u32[]{:S(2)}) %collective-permute-start.22) | collective-permute-done | bytes 1048608 | tf_op jit(solution)/shard_map/ppermute | solution.py:88
  645.0 4.1 fusion.128
  650.3 19.6 %collective-permute-done.27 = bf16[256,2048]{0,1:T(8,128)(2,1)S(1)} collective-permute-done((bf16[256,2048]{0,1:T(8,128)(2,1)S(1)}, bf16[256,2048]{0,1:T(8,128)(2,1)S(1)}, u32[]{:S(2)}, u32[]{:S(2)}) %collective-permute-start.27) | collective-permute-done | bytes 1048608 | tf_op jit(solution)/shard_map/ppermute | solution.py:88
  671.5 4.8 collective-permute-start.28
  676.5 13.7 %collective-permute-done.40 = bf16[1024,1408]{1,0:T(8,128)(2,1)} collective-permute-done((bf16[1024,1408]{1,0:T(8,128)(2,1)}, bf16[1024,1408]{1,0:T(8,128)(2,1)}, u32[]{:S(2)}, u32[]{:S(2)}) %collective-permute-start.40) | collective-permute-done | bytes 2883616 | tf_op jit(solution)/shard_map/ppermute | solution.py:85
  690.2 8.3 add_convert_fusion.2
  701.6 5.5 fusion.46
  707.1 3.8 add_convert_fusion.4
  710.9 3.4 reshape.552
  714.3 5.2 fusion.3
  724.8 3.3 multiply_bitcast_fusion
  728.1 5.3 copy.135
  737.8 4.2 copy.136
  742.0 4.2 fusion.71
  746.2 4.5 fusion.145
  755.2 4.6 collective-permute-start.29
  762.9 4.9 convolution_convert_fusion.4
  773.2 3.7 convolution_convert_fusion.3
  782.2 10.8 %collective-permute-done.36 = bf16[4,128,1024]{2,1,0:T(8,128)(2,1)} collective-permute-done((bf16[4,128,1024]{2,1,0:T(8,128)(2,1)}, bf16[4,128,1024]{2,1,0:T(8,128)(2,1)}, u32[]{:S(2)}, u32[]{:S(2)}) %collective-permute-start.36) | collective-permute-done | bytes 1048608 | tf_op jit(solution)/shard_map/ppermute | solution.py:85
  804.4 33.5 %collective-permute-done.38 = bf16[1024,1024]{1,0:T(8,128)(2,1)} collective-permute-done((bf16[1024,1024]{1,0:T(8,128)(2,1)}, bf16[1024,1024]{1,0:T(8,128)(2,1)}, u32[]{:S(2)}, u32[]{:S(2)}) %collective-permute-start.38) | collective-permute-done | bytes 2097184 | tf_op jit(solution)/shard_map/ppermute | solution.py:85
  837.9 5.3 add_convert_fusion.3
  852.9 6.1 fusion.35
  859.1 4.2 pad_maximum_fusion.11
  874.1 16.9 %collective-permute-done.33 = bf16[4,144,768]{2,1,0:T(8,128)(2,1)} collective-permute-done((bf16[4,144,768]{2,1,0:T(8,128)(2,1)}, bf16[4,144,768]{2,1,0:T(8,128)(2,1)}, u32[]{:S(2)}, u32[]{:S(2)}) %collective-permute-start.33) | collective-permute-done | bytes 884768 | tf_op jit(solution)/shard_map/ppermute | solution.py:85
  907.3 12.8 %reduce-scatter.7.cloned.1.call-done = bf16[144,768]{1,0:T(8,128)(2,1)} async-done(((bf16[576,768]{1,0:T(8,128)(2,1)}), bf16[144,768]{1,0:T(8,128)(2,1)}) %reduce-scatter.7.cloned.1.call-update) | async-done | bytes 221200 | tf_op jit(solution)/shard_map/reduce_scatter | solution.py:94
  923.1 4.3 collective-permute-done.34
  (494 shorter events, 219.6 us)
Async XLA Ops:
  7.2 141.0 %all-gather.6.cloned.1.call-start = ((), (), s32[]{:S(2)}) async-start(), calls=%async_computation.6 | async-start | bytes 1310720 | tf_op jit(solution)/shard_map/all_gather | solution.py:91
  8.5 1.4 collective-permute-start.7
  10.7 173.2 %all-gather.8.cloned.1.call-start = ((), (), s32[]{:S(2)}) async-start(), calls=%async_computation.7 | async-start | bytes 2621440 | tf_op jit(solution)/shard_map/all_gather | solution.py:91
  12.1 1.6 collective-permute-start.9
  12.4 67.6 %collective-permute-start.6 = (s32[1]{0:T(128)}, s32[1]{0:T(128)}, u32[]{:S(2)}, u32[]{:S(2)}) collective-permute-start(s32[1]{0:T(128)} %param.17), channel_id=1, source_target_pairs={{0,2},{2,0},{4,6},{6,4},{8,10},{10,8},{12,14},{14,12},{16,18},{18,... | collective-permute-start | bytes 20 | tf_op jit(solution)/shard_map/ppermute | solution.py:82
  14.7 241.7 %all-gather.14.cloned.1.call-start = ((), (), s32[]{:S(2)}) async-start(), calls=%async_computation.10 | async-start | bytes 3604480 | tf_op jit(solution)/shard_map/all_gather | solution.py:91
  15.6 133.8 %collective-permute-start.17 = (bf16[128,1408]{0,1:T(8,128)(2,1)}, bf16[128,1408]{0,1:T(8,128)(2,1)}, u32[]{:S(2)}, u32[]{:S(2)}) collective-permute-start(bf16[128,1408]{0,1:T(8,128)(2,1)} %get-tuple-element.123), channel_id=1, source_target_pairs={{0,2},{2,0},{4,6},{6,4},{8,10},{10,8},{12,14},{14,12},{16,18},{18,... | collective-permute-start | bytes 1081352 | tf_op jit(solution)/shard_map/ppermute | solution.py:82
  51.0 23.5 %collective-permute-start.2 = (bf16[576,768]{1,0:T(8,128)(2,1)S(1)}, bf16[576,768]{1,0:T(8,128)(2,1)S(1)}, u32[]{:S(2)}, u32[]{:S(2)}) collective-permute-start(bf16[576,768]{1,0:T(8,128)(2,1)S(1)} %all_gather.18), channel_id=1, source_target_pairs={{0,4},{2,6},{4,0},{6,2},{8,12},{10,14},{12,8},{14,10},{16,20},{18,... | collective-permute-start | bytes 2654216 | tf_op jit(solution)/shard_map/ppermute | solution.py:85
  52.9 24.7 %collective-permute-start.19 = (bf16[128,1408]{0,1:T(8,128)(2,1)}, bf16[128,1408]{0,1:T(8,128)(2,1)}, u32[]{:S(2)}, u32[]{:S(2)}) collective-permute-start(bf16[128,1408]{0,1:T(8,128)(2,1)} %get-tuple-element.119), channel_id=1, source_target_pairs={{0,2},{2,0},{4,6},{6,4},{8,10},{10,8},{12,14},{14,12},{16,18},{18,... | collective-permute-start | bytes 1081352 | tf_op jit(solution)/shard_map/ppermute | solution.py:82
  69.6 223.6 %copy-start.3 = (bf16[256,4,1,256]{0,3,1,2:T(8,128)(2,1)}, bf16[256,4,1,256]{0,3,1,2:T(8,128)(2,1)S(1)}, u32[]{:S(2)}) copy-start(bf16[256,4,1,256]{0,3,1,2:T(8,128)(2,1)S(1)} %copy.169) | copy-start | bytes 1572868
  72.1 221.1 %copy-start.5 = (bf16[256,4,1,256]{0,3,1,2:T(8,128)(2,1)}, bf16[256,4,1,256]{0,3,1,2:T(8,128)(2,1)S(1)}, u32[]{:S(2)}) copy-start(bf16[256,4,1,256]{0,3,1,2:T(8,128)(2,1)S(1)} %copy.168) | copy-start | bytes 1572868
  73.2 70.8 %collective-permute-start = (bf16[256,2048]{0,1:T(8,128)(2,1)}, bf16[256,2048]{0,1:T(8,128)(2,1)}, u32[]{:S(2)}, u32[]{:S(2)}) collective-permute-start(bf16[256,2048]{0,1:T(8,128)(2,1)} %pad_maximum_fusion.19), channel_id=1, source_target_pairs={{0,1},{1,0},{2,3},{3,2},{4,5},{5,4},{6,7},{7,6},{8,9},{9,8},{10,11... | collective-permute-start | bytes 3145736 | tf_op jit(solution)/shard_map/ppermute | solution.py:88
  75.8 60.4 %collective-permute-start.4 = (bf16[2,4,144,768]{3,2,1,0:T(8,128)(2,1)}, bf16[2,4,144,768]{3,2,1,0:T(8,128)(2,1)}, u32[]{:S(2)}, u32[]{:S(2)}) collective-permute-start(bf16[2,4,144,768]{3,2,1,0:T(8,128)(2,1)} %pad_maximum_fusion.12), channel_id=1, source_target_pairs={{0,1},{1,0},{2,3},{3,2},{4,5},{5,4},{6,7},{7,6},{8,9},{9,8},{10,11... | collective-permute-start | bytes 5308424 | tf_op jit(solution)/shard_map/ppermute | solution.py:88
  79.9 218.2 %all-gather.12.cloned.1.call-start = ((), (), s32[]{:S(2)}) async-start(), calls=%async_computation.9 | async-start | bytes 3604480 | tf_op jit(solution)/shard_map/all_gather | solution.py:91
  143.2 41.0 %collective-permute-start.5 = (bf16[2,4,144,1536]{3,2,1,0:T(8,128)(2,1)}, bf16[2,4,144,1536]{3,2,1,0:T(8,128)(2,1)}, u32[]{:S(2)}, u32[]{:S(2)}) collective-permute-start(bf16[2,4,144,1536]{3,2,1,0:T(8,128)(2,1)} %get-tuple-element.93), channel_id=1, source_target_pairs={{0,2},{2,0},{4,6},{6,4},{8,10},{10,8},{12,14},{14,12},{16,18},{18,... | collective-permute-start | bytes 10616840 | tf_op jit(solution)/shard_map/ppermute | solution.py:82
  146.7 31.8 %collective-permute-start.1 = (bf16[512,2048]{0,1:T(8,128)(2,1)}, bf16[512,2048]{0,1:T(8,128)(2,1)}, u32[]{:S(2)}, u32[]{:S(2)}) collective-permute-start(bf16[512,2048]{0,1:T(8,128)(2,1)} %pad_maximum_fusion.13), channel_id=1, source_target_pairs={{0,2},{2,0},{4,6},{6,4},{8,10},{10,8},{12,14},{14,12},{16,18},{18,... | collective-permute-start | bytes 6291464 | tf_op jit(solution)/shard_map/ppermute | solution.py:82
  148.2 24.6 %collective-permute-start.8 = (bf16[512,1024]{1,0:T(8,128)(2,1)}, bf16[512,1024]{1,0:T(8,128)(2,1)}, u32[]{:S(2)}, u32[]{:S(2)}) collective-permute-start(bf16[512,1024]{1,0:T(8,128)(2,1)} %all-gather.6.cloned.1.call-done), channel_id=1, source_target_pairs={{0,4},{2,6},{4,0},{6,2},{8,12},{10,14},{12,8},{14,10},{16,20},{18,... | collective-permute-start | bytes 3145736 | tf_op jit(solution)/shard_map/ppermute | solution.py:85
  148.6 4.3 collective-permute-start.3
  151.6 180.8 %all-gather.10.cloned.1.call-start = ((), (), s32[]{:S(2)}) async-start(), calls=%async_computation.8 | async-start | bytes 3604480 | tf_op jit(solution)/shard_map/all_gather | solution.py:91
  153.2 53.2 %copy-start.73 = (f32[4,2,128]{2,1,0:T(2,128)}, f32[4,2,128]{2,1,0:T(2,128)S(1)}, u32[]{:S(2)}) copy-start(f32[4,2,128]{2,1,0:T(2,128)S(1)} %copy.120) | copy-start | bytes 12292
  183.9 46.2 %collective-permute-start.10 = (bf16[1024,1024]{0,1:T(8,128)(2,1)}, bf16[1024,1024]{0,1:T(8,128)(2,1)}, u32[]{:S(2)}, u32[]{:S(2)}) collective-permute-start(bf16[1024,1024]{0,1:T(8,128)(2,1)} %all-gather.8.cloned.1.call-done), channel_id=1, source_target_pairs={{0,4},{2,6},{4,0},{6,2},{8,12},{10,14},{12,8},{14,10},{16,20},{18,... | collective-permute-start | bytes 6291464 | tf_op jit(solution)/shard_map/ppermute | solution.py:85
  236.8 12.7 %collective-permute-start.11 = (bf16[512,2048]{0,1:T(8,128)(2,1)}, bf16[512,2048]{0,1:T(8,128)(2,1)}, u32[]{:S(2)}, u32[]{:S(2)}) collective-permute-start(bf16[512,2048]{0,1:T(8,128)(2,1)} %fusion.22), channel_id=1, source_target_pairs={{0,2},{2,0},{4,6},{6,4},{8,10},{10,8},{12,14},{14,12},{16,18},{18,... | collective-permute-start | bytes 6291464 | tf_op jit(solution)/shard_map/ppermute | solution.py:82
  241.5 5.7 collective-permute-start.15
  246.1 24.6 %collective-permute-start.23 = (bf16[256,2048]{0,1:T(8,128)(2,1)}, bf16[256,2048]{0,1:T(8,128)(2,1)S(1)}, u32[]{:S(2)}, u32[]{:S(2)}) collective-permute-start(bf16[256,2048]{0,1:T(8,128)(2,1)} %pad_maximum_fusion.20), channel_id=1, source_target_pairs={{0,1},{1,0},{2,3},{3,2},{4,5},{5,4},{6,7},{7,6},{8,9},{9,8},{10,11... | collective-permute-start | bytes 3145736 | tf_op jit(solution)/shard_map/ppermute | solution.py:88
  249.5 593.9 %reduce-scatter.17.cloned.1.call-start = ((), (), s32[]{:S(2)}) async-start(), calls=%async_computation.16 | async-start | bytes 3604480 | tf_op jit(solution)/shard_map/reduce_scatter | solution.py:94
  256.2 37.0 %collective-permute-start.12 = (bf16[256,2048]{0,1:T(8,128)(2,1)}, bf16[256,2048]{0,1:T(8,128)(2,1)}, u32[]{:S(2)}, u32[]{:S(2)}) collective-permute-start(bf16[256,2048]{0,1:T(8,128)(2,1)} %slice.537), channel_id=1, source_target_pairs={{0,1},{1,0},{2,3},{3,2},{4,5},{5,4},{6,7},{7,6},{8,9},{9,8},{10,11... | collective-permute-start | bytes 3145736 | tf_op jit(solution)/shard_map/ppermute | solution.py:88
  256.5 76.2 %collective-permute-start.20 = (bf16[1024,1408]{0,1:T(8,128)(2,1)}, bf16[1024,1408]{0,1:T(8,128)(2,1)}, u32[]{:S(2)}, u32[]{:S(2)}) collective-permute-start(bf16[1024,1408]{0,1:T(8,128)(2,1)} %all-gather.14.cloned.1.call-done), channel_id=1, source_target_pairs={{0,4},{2,6},{4,0},{6,2},{8,12},{10,14},{12,8},{14,10},{16,20},{18,... | collective-permute-start | bytes 8650760 | tf_op jit(solution)/shard_map/ppermute | solution.py:85
  272.3 53.5 %collective-permute-start.24 = (bf16[512,2048]{0,1:T(8,128)(2,1)}, bf16[512,2048]{0,1:T(8,128)(2,1)}, u32[]{:S(2)}, u32[]{:S(2)}) collective-permute-start(bf16[512,2048]{0,1:T(8,128)(2,1)} %pad_maximum_fusion.16), channel_id=1, source_target_pairs={{0,2},{2,0},{4,6},{6,4},{8,10},{10,8},{12,14},{14,12},{16,18},{18,... | collective-permute-start | bytes 6291464 | tf_op jit(solution)/shard_map/ppermute | solution.py:82
  296.9 23.7 %collective-permute-start.13 = (bf16[256,2048]{0,1:T(8,128)(2,1)}, bf16[256,2048]{0,1:T(8,128)(2,1)}, u32[]{:S(2)}, u32[]{:S(2)}) collective-permute-start(bf16[256,2048]{0,1:T(8,128)(2,1)} %multiply_convert_fusion.5), channel_id=1, source_target_pairs={{0,1},{1,0},{2,3},{3,2},{4,5},{5,4},{6,7},{7,6},{8,9},{9,8},{10,11... | collective-permute-start | bytes 3145736 | tf_op jit(solution)/shard_map/ppermute | solution.py:88
  298.1 83.5 %collective-permute-start.18 = (bf16[1024,1408]{0,1:T(8,128)(2,1)}, bf16[1024,1408]{0,1:T(8,128)(2,1)}, u32[]{:S(2)}, u32[]{:S(2)}) collective-permute-start(bf16[1024,1408]{0,1:T(8,128)(2,1)} %all-gather.12.cloned.1.call-done), channel_id=1, source_target_pairs={{0,4},{2,6},{4,0},{6,2},{8,12},{10,14},{12,8},{14,10},{16,20},{18,... | collective-permute-start | bytes 8650760 | tf_op jit(solution)/shard_map/ppermute | solution.py:85
  323.7 20.5 %collective-permute-start.14 = (bf16[512,2048]{0,1:T(8,128)(2,1)}, bf16[512,2048]{0,1:T(8,128)(2,1)}, u32[]{:S(2)}, u32[]{:S(2)}) collective-permute-start(bf16[512,2048]{0,1:T(8,128)(2,1)} %pad_maximum_fusion.15), channel_id=1, source_target_pairs={{0,2},{2,0},{4,6},{6,4},{8,10},{10,8},{12,14},{14,12},{16,18},{18,... | collective-permute-start | bytes 6291464 | tf_op jit(solution)/shard_map/ppermute | solution.py:82
  332.3 110.9 %collective-permute-start.16 = (bf16[1024,1408]{0,1:T(8,128)(2,1)}, bf16[1024,1408]{0,1:T(8,128)(2,1)S(1)}, u32[]{:S(2)}, u32[]{:S(2)}) collective-permute-start(bf16[1024,1408]{0,1:T(8,128)(2,1)} %all-gather.10.cloned.1.call-done), channel_id=1, source_target_pairs={{0,4},{2,6},{4,0},{6,2},{8,12},{10,14},{12,8},{14,10},{16,20},{18,... | collective-permute-start | bytes 8650760 | tf_op jit(solution)/shard_map/ppermute | solution.py:85
  346.6 103.6 %copy-start.34 = (bf16[1024,2048]{0,1:T(8,128)(2,1)}, bf16[1024,2048]{0,1:T(8,128)(2,1)S(1)}, u32[]{:S(2)}) copy-start(bf16[1024,2048]{0,1:T(8,128)(2,1)S(1)} %pad_maximum_fusion.7) | copy-start | bytes 12582916
  346.6 40.3 %copy-start.85 = (bf16[1024,1408]{0,1:T(8,128)(2,1)S(1)}, bf16[1024,1408]{0,1:T(8,128)(2,1)}, u32[]{:S(2)}) copy-start(bf16[1024,1408]{0,1:T(8,128)(2,1)} %all-gather.12.cloned.1.call-done) | copy-start | bytes 8650756
  469.3 62.1 %collective-permute-start.44 = (bf16[1024,1408]{1,0:T(8,128)(2,1)S(1)}, bf16[1024,1408]{1,0:T(8,128)(2,1)S(1)}, u32[]{:S(2)}, u32[]{:S(2)}) collective-permute-start(bf16[1024,1408]{1,0:T(8,128)(2,1)S(1)} %convolution_convert_fusion), channel_id=1, source_target_pairs={{0,4},{2,6},{4,0},{6,2},{8,12},{10,14},{12,8},{14,10},{16,20},{18,... | collective-permute-start | bytes 8650760 | tf_op jit(solution)/shard_map/ppermute | solution.py:85
  480.4 51.0 %copy-start.94 = (bf16[1024,1408]{1,0:T(8,128)(2,1)S(1)}, bf16[1024,1408]{1,0:T(8,128)(2,1)}, u32[]{:S(2)}) copy-start(bf16[1024,1408]{1,0:T(8,128)(2,1)} %get-tuple-element.85) | copy-start | bytes 8650756
  536.2 312.3 %reduce-scatter.15.cloned.1.call-start = ((), (), s32[]{:S(2)}) async-start(), calls=%async_computation.15 | async-start | bytes 3604480 | tf_op jit(solution)/shard_map/reduce_scatter | solution.py:94
  544.3 27.7 %collective-permute-start.25 = (bf16[512,2048]{0,1:T(8,128)(2,1)S(1)}, bf16[512,2048]{0,1:T(8,128)(2,1)S(1)}, u32[]{:S(2)}, u32[]{:S(2)}) collective-permute-start(bf16[512,2048]{0,1:T(8,128)(2,1)S(1)} %fusion.20), channel_id=1, source_target_pairs={{0,2},{2,0},{4,6},{6,4},{8,10},{10,8},{12,14},{14,12},{16,18},{18,... | collective-permute-start | bytes 6291464 | tf_op jit(solution)/shard_map/ppermute | solution.py:82
  552.8 61.9 %collective-permute-start.42 = (bf16[1024,1408]{1,0:T(8,128)(2,1)}, bf16[1024,1408]{1,0:T(8,128)(2,1)S(1)}, u32[]{:S(2)}, u32[]{:S(2)}) collective-permute-start(bf16[1024,1408]{1,0:T(8,128)(2,1)} %convolution_convert_fusion.1), channel_id=1, source_target_pairs={{0,4},{2,6},{4,0},{6,2},{8,12},{10,14},{12,8},{14,10},{16,20},{18,... | collective-permute-start | bytes 8650760 | tf_op jit(solution)/shard_map/ppermute | solution.py:85
  568.9 45.8 %copy-start.93 = (bf16[1024,1408]{1,0:T(8,128)(2,1)S(1)}, bf16[1024,1408]{1,0:T(8,128)(2,1)}, u32[]{:S(2)}) copy-start(bf16[1024,1408]{1,0:T(8,128)(2,1)} %get-tuple-element.84) | copy-start | bytes 8650756
  568.9 50.6 %collective-permute-start.21 = (bf16[512,2048]{0,1:T(8,128)(2,1)}, bf16[512,2048]{0,1:T(8,128)(2,1)}, u32[]{:S(2)}, u32[]{:S(2)}) collective-permute-start(bf16[512,2048]{0,1:T(8,128)(2,1)} %fusion.21), channel_id=1, source_target_pairs={{0,2},{2,0},{4,6},{6,4},{8,10},{10,8},{12,14},{14,12},{16,18},{18,... | collective-permute-start | bytes 6291464 | tf_op jit(solution)/shard_map/ppermute | solution.py:82
  576.0 53.5 %collective-permute-start.26 = (bf16[256,2048]{0,1:T(8,128)(2,1)}, bf16[256,2048]{0,1:T(8,128)(2,1)}, u32[]{:S(2)}, u32[]{:S(2)}) collective-permute-start(bf16[256,2048]{0,1:T(8,128)(2,1)} %slice.535), channel_id=1, source_target_pairs={{0,1},{1,0},{2,3},{3,2},{4,5},{5,4},{6,7},{7,6},{8,9},{9,8},{10,11... | collective-permute-start | bytes 3145736 | tf_op jit(solution)/shard_map/ppermute | solution.py:88
  619.4 231.5 %reduce-scatter.13.cloned.1.call-start = ((), (), s32[]{:S(2)}) async-start(), calls=%async_computation.14 | async-start | bytes 3604480 | tf_op jit(solution)/shard_map/reduce_scatter | solution.py:94
  623.4 21.6 %collective-permute-start.22 = (bf16[256,2048]{0,1:T(8,128)(2,1)S(1)}, bf16[256,2048]{0,1:T(8,128)(2,1)S(1)}, u32[]{:S(2)}, u32[]{:S(2)}) collective-permute-start(bf16[256,2048]{0,1:T(8,128)(2,1)S(1)} %slice.536), channel_id=1, source_target_pairs={{0,1},{1,0},{2,3},{3,2},{4,5},{5,4},{6,7},{7,6},{8,9},{9,8},{10,11... | collective-permute-start | bytes 3145736 | tf_op jit(solution)/shard_map/ppermute | solution.py:88
  629.4 60.8 %collective-permute-start.40 = (bf16[1024,1408]{1,0:T(8,128)(2,1)}, bf16[1024,1408]{1,0:T(8,128)(2,1)}, u32[]{:S(2)}, u32[]{:S(2)}) collective-permute-start(bf16[1024,1408]{1,0:T(8,128)(2,1)} %convolution_convert_fusion.2), channel_id=1, source_target_pairs={{0,4},{2,6},{4,0},{6,2},{8,12},{10,14},{12,8},{14,10},{16,20},{18,... | collective-permute-start | bytes 8650760 | tf_op jit(solution)/shard_map/ppermute | solution.py:85
  649.1 20.8 %collective-permute-start.27 = (bf16[256,2048]{0,1:T(8,128)(2,1)S(1)}, bf16[256,2048]{0,1:T(8,128)(2,1)S(1)}, u32[]{:S(2)}, u32[]{:S(2)}) collective-permute-start(bf16[256,2048]{0,1:T(8,128)(2,1)S(1)} %get-tuple-element.75), channel_id=1, source_target_pairs={{0,1},{1,0},{2,3},{3,2},{4,5},{5,4},{6,7},{7,6},{8,9},{9,8},{10,11... | collective-permute-start | bytes 3145736 | tf_op jit(solution)/shard_map/ppermute | solution.py:88
  671.5 27.1 %collective-permute-start.28 = (bf16[512,2048]{0,1:T(8,128)(2,1)}, bf16[512,2048]{0,1:T(8,128)(2,1)}, u32[]{:S(2)}, u32[]{:S(2)}) collective-permute-start(bf16[512,2048]{0,1:T(8,128)(2,1)} %pad_maximum_fusion.17), channel_id=1, source_target_pairs={{0,2},{2,0},{4,6},{6,4},{8,10},{10,8},{12,14},{14,12},{16,18},{18,... | collective-permute-start | bytes 6291464 | tf_op jit(solution)/shard_map/ppermute | solution.py:82
  698.5 198.9 %reduce-scatter.9.cloned.1.call-start = ((), (), s32[]{:S(2)}) async-start(), calls=%async_computation.12 | async-start | bytes 1310720 | tf_op jit(solution)/shard_map/reduce_scatter | solution.py:94
  755.2 14.4 %collective-permute-start.29 = (bf16[512,1536]{1,0:T(8,128)(2,1)S(1)}, bf16[512,1536]{1,0:T(8,128)(2,1)S(1)}, u32[]{:S(2)}, u32[]{:S(2)}) collective-permute-start(bf16[512,1536]{1,0:T(8,128)(2,1)S(1)} %slice.534), channel_id=1, source_target_pairs={{0,2},{2,0},{4,6},{6,4},{8,10},{10,8},{12,14},{14,12},{16,18},{18,... | collective-permute-start | bytes 4718600 | tf_op jit(solution)/shard_map/ppermute | solution.py:82
  768.9 24.0 %collective-permute-start.36 = (bf16[4,128,1024]{2,1,0:T(8,128)(2,1)}, bf16[4,128,1024]{2,1,0:T(8,128)(2,1)}, u32[]{:S(2)}, u32[]{:S(2)}) collective-permute-start(bf16[4,128,1024]{2,1,0:T(8,128)(2,1)} %dynamic-slice_bitcast_fusion), channel_id=1, source_target_pairs={{0,4},{2,6},{4,0},{6,2},{8,12},{10,14},{12,8},{14,10},{16,20},{18,... | collective-permute-start | bytes 3145736 | tf_op jit(solution)/shard_map/ppermute | solution.py:85
  771.1 24.9 %collective-permute-start.30 = (bf16[256,1536]{1,0:T(8,128)(2,1)}, bf16[256,1536]{1,0:T(8,128)(2,1)}, u32[]{:S(2)}, u32[]{:S(2)}) collective-permute-start(bf16[256,1536]{1,0:T(8,128)(2,1)} %slice.538), channel_id=1, source_target_pairs={{0,1},{1,0},{2,3},{3,2},{4,5},{5,4},{6,7},{7,6},{8,9},{9,8},{10,11... | collective-permute-start | bytes 2359304 | tf_op jit(solution)/shard_map/ppermute | solution.py:88
  776.9 61.0 %collective-permute-start.38 = (bf16[1024,1024]{1,0:T(8,128)(2,1)}, bf16[1024,1024]{1,0:T(8,128)(2,1)}, u32[]{:S(2)}, u32[]{:S(2)}) collective-permute-start(bf16[1024,1024]{1,0:T(8,128)(2,1)} %convolution_convert_fusion.3), channel_id=1, source_target_pairs={{0,4},{2,6},{4,0},{6,2},{8,12},{10,14},{12,8},{14,10},{16,20},{18,... | collective-permute-start | bytes 6291464 | tf_op jit(solution)/shard_map/ppermute | solution.py:85
  795.9 104.0 %reduce-scatter.11.cloned.1.call-start = ((), (), s32[]{:S(2)}) async-start(), calls=%async_computation.13 | async-start | bytes 2621440 | tf_op jit(solution)/shard_map/reduce_scatter | solution.py:94
  803.3 43.8 %collective-permute-start.31 = (bf16[256,1536]{1,0:T(8,128)(2,1)}, bf16[256,1536]{1,0:T(8,128)(2,1)S(1)}, u32[]{:S(2)}, u32[]{:S(2)}) collective-permute-start(bf16[256,1536]{1,0:T(8,128)(2,1)} %pad_maximum_fusion.21), channel_id=1, source_target_pairs={{0,1},{1,0},{2,3},{3,2},{4,5},{5,4},{6,7},{7,6},{8,9},{9,8},{10,11... | collective-permute-start | bytes 2359304 | tf_op jit(solution)/shard_map/ppermute | solution.py:88
  843.3 76.9 %reduce-scatter.7.cloned.1.call-start = ((), (), s32[]{:S(2)}) async-start(), calls=%async_computation.11 | async-start | bytes 1105920 | tf_op jit(solution)/shard_map/reduce_scatter | solution.py:94
  845.2 48.6 %collective-permute-start.45 = (bf16[128,1408]{1,0:T(8,128)(2,1)}, bf16[128,1408]{1,0:T(8,128)(2,1)}, u32[]{:S(2)}, u32[]{:S(2)}) collective-permute-start(bf16[128,1408]{1,0:T(8,128)(2,1)} %get-tuple-element.113), channel_id=1, source_target_pairs={{0,2},{2,0},{4,6},{6,4},{8,10},{10,8},{12,14},{14,12},{16,18},{18,... | collective-permute-start | bytes 1081352 | tf_op jit(solution)/shard_map/ppermute | solution.py:82
  848.4 10.7 %collective-permute-start.32 = (bf16[512,1536]{1,0:T(8,128)(2,1)}, bf16[512,1536]{1,0:T(8,128)(2,1)}, u32[]{:S(2)}, u32[]{:S(2)}) collective-permute-start(bf16[512,1536]{1,0:T(8,128)(2,1)} %pad_maximum_fusion.18), channel_id=1, source_target_pairs={{0,2},{2,0},{4,6},{6,4},{8,10},{10,8},{12,14},{14,12},{16,18},{18,... | collective-permute-start | bytes 4718600 | tf_op jit(solution)/shard_map/ppermute | solution.py:82
  850.4 44.7 %collective-permute-start.43 = (bf16[128,1408]{1,0:T(8,128)(2,1)}, bf16[128,1408]{1,0:T(8,128)(2,1)}, u32[]{:S(2)}, u32[]{:S(2)}) collective-permute-start(bf16[128,1408]{1,0:T(8,128)(2,1)} %get-tuple-element.115), channel_id=1, source_target_pairs={{0,2},{2,0},{4,6},{6,4},{8,10},{10,8},{12,14},{14,12},{16,18},{18,... | collective-permute-start | bytes 1081352 | tf_op jit(solution)/shard_map/ppermute | solution.py:82
  852.9 48.2 %collective-permute-start.41 = (bf16[128,1408]{1,0:T(8,128)(2,1)}, bf16[128,1408]{1,0:T(8,128)(2,1)}, u32[]{:S(2)}, u32[]{:S(2)}) collective-permute-start(bf16[128,1408]{1,0:T(8,128)(2,1)} %get-tuple-element.117), channel_id=1, source_target_pairs={{0,2},{2,0},{4,6},{6,4},{8,10},{10,8},{12,14},{14,12},{16,18},{18,... | collective-permute-start | bytes 1081352 | tf_op jit(solution)/shard_map/ppermute | solution.py:82
  870.0 21.0 %collective-permute-start.33 = (bf16[4,144,768]{2,1,0:T(8,128)(2,1)}, bf16[4,144,768]{2,1,0:T(8,128)(2,1)}, u32[]{:S(2)}, u32[]{:S(2)}) collective-permute-start(bf16[4,144,768]{2,1,0:T(8,128)(2,1)} %fusion.85), channel_id=1, source_target_pairs={{0,4},{2,6},{4,0},{6,2},{8,12},{10,14},{12,8},{14,10},{16,20},{18,... | collective-permute-start | bytes 2654216 | tf_op jit(solution)/shard_map/ppermute | solution.py:85
  898.4 6.5 collective-permute-start.37
  901.0 4.9 collective-permute-start.39
  921.0 6.4 collective-permute-start.34
  928.1 4.0 collective-permute-start.35
  (94 other events, 838.1 us)
Sparse Core Ops, SparseCore 0:
  10.8 44.2 all-gather.5
  57.3 44.6 all-gather.7
  103.5 58.1 all-gather.13
  163.1 57.3 all-gather.11
  249.6 59.3 all-gather.9
  536.3 59.1 reduce-scatter.16
  619.6 59.5 reduce-scatter.14
  698.6 60.6 reduce-scatter.12
  796.0 30.4 reduce-scatter.8
  843.4 45.7 reduce-scatter.10
  894.0 26.1 reduce-scatter.6

commit v2 on v1

--- a/solution.py
+++ b/solution.py
@@ -3,6 +3,8 @@
 import jax
 import jax.numpy as jnp
 from jax import lax
+from jax.experimental import pallas as pl
+from jax.experimental.pallas import tpu as pltpu
 from jax.sharding import PartitionSpec as P
 
 norm_eps = 1e-05
@@ -67,6 +69,472 @@
     return token_index + shifts
 
 
+ANY = pl.BlockSpec(memory_space=pl.ANY)
+vmem_bytes = 60 * 1024 * 1024
+
+
+def kernel_params():
+    return pltpu.CompilerParams(vmem_limit_bytes=vmem_bytes)
+
+
+def cost(flops, arrays, transcendentals=0):
+    moved = sum(math.prod(a.shape) * a.dtype.itemsize for a in arrays)
+    return pl.CostEstimate(flops=flops, bytes_accessed=moved, transcendentals=transcendentals)
+
+
+def stack_rows(refs, held, sems):
+    rows = refs[0].shape[0]
+    copies = [
+        pltpu.make_async_copy(ref, held.at[pl.ds(j * rows, rows)], sems.at[j])
+        for j, ref in enumerate(refs)
+    ]
+    for copy in copies:
+        copy.start()
+    return copies
+
+
+def join_lines(ref, held, sems):
+    lines, _, cols = ref.shape
+    copies = [
+        pltpu.make_async_copy(ref.at[j], held.at[:, pl.ds(j * cols, cols)], sems.at[j])
+        for j in range(lines)
+    ]
+    for copy in copies:
+        copy.start()
+    return copies
+
+
+def wait_all(copies):
+    for copy in copies:
+        copy.wait()
+
+
+def tile(index, size):
+    return pl.ds(pl.multiple_of(index * size, size), size)
+
+
+def ffn_first(normed, grads, gate_up):
+    count = len(normed)
+    rows, width = normed[0].shape
+    total = rows * count
+    lines, double, cols = gate_up.shape
+    hid = double // 2
+
+    def kernel(*refs):
+        normed_refs, grad_refs = refs[:count], refs[count : 2 * count]
+        weight_ref, hid_ref, a_ref, s_ref, down_ref = refs[2 * count : 2 * count + 5]
+        n_s, g_s, w_s, hid_s, a_s, s_s, down_s, n_sem, g_sem, w_sem, o_sem, d_sem = refs[
+            2 * count + 5 :
+        ]
+        weights = join_lines(weight_ref, w_s, w_sem)
+        stack_rows(normed_refs, n_s, n_sem)
+        grad_copies = stack_rows(grad_refs, g_s, g_sem)
+        wait_all(weights)
+
+        @pl.loop(0, count)
+        def _(i):
+            pltpu.make_async_copy(normed_refs[0], n_s.at[tile(i, rows)], n_sem.at[i]).wait()
+            acts = matmul_nt(w_s[...], n_s[tile(i, rows), :])
+            gate, up = acts[:hid], acts[hid:]
+            sig = jax.nn.sigmoid(gate)
+            silu = gate * sig
+            hid_s[:, tile(i, rows)] = (silu * up).astype(BF)
+            a_s[:, tile(i, rows)] = (up * sig * (1.0 + gate * (1.0 - sig))).astype(BF)
+            s_s[:, tile(i, rows)] = silu.astype(BF)
+
+        outs = [
+            pltpu.make_async_copy(src, dst, o_sem.at[j])
+            for j, (src, dst) in enumerate(((hid_s, hid_ref), (a_s, a_ref), (s_s, s_ref)))
+        ]
+        for copy in outs:
+            copy.start()
+        wait_all(grad_copies)
+
+        @pl.loop(0, lines)
+        def _(j):
+            down_s[j] = matmul(hid_s[...], g_s[:, tile(j, cols)]).astype(BF)
+            pltpu.make_async_copy(down_s.at[j], down_ref.at[j], d_sem.at[j]).start()
+
+        @pl.loop(0, lines)
+        def _(j):
+            pltpu.make_async_copy(down_s.at[j], down_ref.at[j], d_sem.at[j]).wait()
+
+        wait_all(outs)
+
+    acts = jax.ShapeDtypeStruct((hid, total), BF)
+    out_shape = (acts, acts, acts, jax.ShapeDtypeStruct((lines, hid, cols), BF))
+    args = (*normed, *grads, gate_up)
+    return pl.pallas_call(
+        kernel,
+        out_shape=out_shape,
+        in_specs=[ANY] * len(args),
+        out_specs=(ANY,) * 4,
+        scratch_shapes=[
+            pltpu.VMEM((total, width), BF),
+            pltpu.VMEM((total, width), BF),
+            pltpu.VMEM((double, width), BF),
+            pltpu.VMEM((hid, total), BF),
+            pltpu.VMEM((hid, total), BF),
+            pltpu.VMEM((hid, total), BF),
+            pltpu.VMEM((lines, hid, cols), BF),
+            pltpu.SemaphoreType.DMA((count,)),
+            pltpu.SemaphoreType.DMA((count,)),
+            pltpu.SemaphoreType.DMA((lines,)),
+            pltpu.SemaphoreType.DMA((3,)),
+            pltpu.SemaphoreType.DMA((lines,)),
+        ],
+        compiler_params=kernel_params(),
+        cost_estimate=cost(6 * hid * total * width, args + out_shape, hid * total),
+        name="ffn_first",
+    )(*args)
+
+
+def ffn_out_part(hidden, down, rows):
+    hid, total = hidden.shape
+    lines, _, cols = down.shape
+    width = lines * cols
+    count = total // rows
+
+    def kernel(hid_ref, down_ref, out_ref, h_s, d_s, out_s, h_sem, d_sem, o_sem):
+        copy = pltpu.make_async_copy(hid_ref, h_s, h_sem)
+        copy.start()
+        wait_all(join_lines(down_ref, d_s, d_sem))
+        copy.wait()
+
+        @pl.loop(0, count)
+        def _(i):
+            at = tile(i, rows)
+            out_s[at, :] = matmul_tn(h_s[:, at], d_s[...]).astype(BF)
+            pltpu.make_async_copy(out_s.at[at], out_ref.at[at], o_sem.at[i]).start()
+
+        @pl.loop(0, count)
+        def _(i):
+            at = tile(i, rows)
+            pltpu.make_async_copy(out_s.at[at], out_ref.at[at], o_sem.at[i]).wait()
+
+    out_shape = jax.ShapeDtypeStruct((total, width), BF)
+    return pl.pallas_call(
+        kernel,
+        out_shape=out_shape,
+        in_specs=[ANY] * 2,
+        out_specs=ANY,
+        scratch_shapes=[
+            pltpu.VMEM((hid, total), BF),
+            pltpu.VMEM((hid, width), BF),
+            pltpu.VMEM((total, width), BF),
+            pltpu.SemaphoreType.DMA,
+            pltpu.SemaphoreType.DMA((lines,)),
+            pltpu.SemaphoreType.DMA((count,)),
+        ],
+        compiler_params=kernel_params(),
+        cost_estimate=cost(2 * hid * total * width, (hidden, down, out_shape)),
+        name="ffn_out_part",
+    )(hidden, down)
+
+
+MESH = pl.DeviceIdType.MESH
+
+
+def peers():
+    place, half = lax.axis_index("dp"), lax.axis_index("tensor")
+    core, side = place % 2, (place // 2) % 2
+    return (
+        (place + 1 - 2 * core, half),
+        (place + 2 - 4 * side, half),
+        (place, 1 - half),
+    )
+
+
+def greet(targets):
+    barrier = pltpu.get_barrier_semaphore()
+    for target in targets:
+        pl.semaphore_signal(barrier, inc=1, device_id=target, device_id_type=MESH)
+    pl.semaphore_wait(barrier, len(targets))
+
+
+def remote(src, dst, send_sem, recv_sem, target):
+    return pltpu.make_async_remote_copy(
+        src_ref=src,
+        dst_ref=dst,
+        send_sem=send_sem,
+        recv_sem=recv_sem,
+        device_id=target,
+        device_id_type=MESH,
+    )
+
+
+def ffn_back(grads, down, gate_up, a_fac, s_fac, normed, residual, gain):
+    count = len(grads)
+    rows, width = grads[0].shape
+    lines, double, cols = gate_up.shape
+    hid = double // 2
+    block = cols // 2
+    near = 4 * rows
+    total = count * rows
+
+    def kernel(*refs):
+        grad_refs, normed_refs = refs[:count], refs[count : 2 * count]
+        down_in, weight_ref, a_ref, s_ref, resid_ref, gain_ref = refs[2 * count : 2 * count + 6]
+        grad_out, dres_out, dgain_out, attn_out = refs[2 * count + 6 : 2 * count + 10]
+        (
+            rows_s,
+            d_s,
+            w_s,
+            a_s,
+            s_s,
+            act_s,
+            far_s,
+            core_in,
+            acc,
+            side_s,
+            side_in,
+            half_s,
+            half_in,
+            grad_s,
+            res_s,
+            own_s,
+            attn_s,
+            rows_sem,
+            d_sem,
+            w_sem,
+            f_sem,
+            core_send,
+            core_recv,
+            side_send,
+            side_recv,
+            half_send,
+            half_recv,
+            grad_sem,
+            res_sem,
+            own_sem,
+            last_send,
+            last_recv,
+            out_sem,
+        ) = refs[2 * count + 10 :]
+        across_core, across_side, across_half = peers()
+        side = (lax.axis_index("dp") // 2) % 2
+        downs = join_lines(down_in, d_s, d_sem)
+        order = list(range(count // 2, count)) + list(range(count // 2))
+        loads = {}
+        for j in order:
+            loads[j] = pltpu.make_async_copy(
+                grad_refs[j], rows_s.at[pl.ds(j * rows, rows)], rows_sem.at[j]
+            )
+            loads[j].start()
+        factors = [
+            pltpu.make_async_copy(src, dst, f_sem.at[j])
+            for j, (src, dst) in enumerate(((a_ref, a_s), (s_ref, s_s)))
+        ]
+        for copy in factors:
+            copy.start()
+        weights = join_lines(weight_ref, w_s, w_sem)
+        res_copy = pltpu.make_async_copy(resid_ref, res_s, res_sem)
+        res_copy.start()
+        own_copy = pltpu.make_async_copy(grad_refs[0], own_s, own_sem)
+        own_copy.start()
+        greet((across_core, across_side, across_half))
+        wait_all(downs + factors)
+
+        def act_block(i):
+            at = tile(i, rows)
+            pltpu.make_async_copy(grad_refs[0], rows_s.at[at], rows_sem.at[i]).wait()
+            d_hid = matmul_nt(d_s[...], rows_s[at, :])
+            act_s[pl.ds(0, hid), at] = (d_hid * a_s[:, at].astype(F32)).astype(BF)
+            act_s[pl.ds(hid, hid), at] = (d_hid * s_s[:, at].astype(F32)).astype(BF)
+
+        def to_core(j):
+            return remote(
+                far_s.at[j], core_in.at[j], core_send.at[j], core_recv.at[j], across_core
+            )
+
+        def to_side(j):
+            return remote(
+                side_s.at[j], side_in.at[j], side_send.at[j], side_recv.at[j], across_side
+            )
+
+        def to_half(j):
+            return remote(
+                half_s.at[j], half_in.at[j], half_send.at[j], half_recv.at[j], across_half
+            )
+
+        @pl.loop(count // 2, count)
+        def _(i):
+            act_block(i)
+
+        wait_all(weights)
+
+        @pl.loop(0, lines)
+        def _(j):
+            far_s[j] = matmul_tn(act_s[:, pl.ds(near, near)], w_s[:, tile(j, cols)]).astype(BF)
+            to_core(j).start()
+
+        @pl.loop(0, count // 2)
+        def _(i):
+            act_block(i)
+
+        reload = stack_rows(normed_refs, rows_s, rows_sem)
+
+        @pl.loop(0, lines)
+        def _(j):
+            part = matmul_tn(act_s[:, pl.ds(0, near)], w_s[:, tile(j, cols)])
+            to_core(j).wait_recv()
+            part = part + core_in[j].astype(F32)
+            acc[j] = part[: 2 * rows]
+            side_s[j] = part[2 * rows :].astype(BF)
+            to_side(j).start()
+
+        wait_all(reload)
+
+        def grad_copy(j):
+            return pltpu.make_async_copy(grad_s.at[j % 2], grad_out.at[j], grad_sem.at[j % 2])
+
+        @pl.loop(0, lines)
+        def _(j):
+            @pl.when(j >= 2)
+            def _():
+                grad_copy(j - 2).wait()
+
+            grad_s[j % 2] = matmul(act_s[...], rows_s[:, tile(j, cols)]).astype(BF)
+            grad_copy(j).start()
+
+        @pl.loop(0, lines)
+        def _(j):
+            to_side(j).wait_recv()
+            part = acc[j] + side_in[j].astype(F32)
+            acc[j] = part
+            half_s[j] = part[rows:].astype(BF)
+            to_half(j).start()
+
+        res_copy.wait()
+        own_copy.wait()
+        res = res_s[...]
+        inverse = inv_rms(res)
+
+        @pl.loop(0, lines)
+        def _(j):
+            to_half(j).wait_recv()
+            acc[j, pl.ds(0, rows), :] = acc[j, pl.ds(0, rows), :] + half_in[j].astype(F32)
+
+        mean = jnp.zeros((rows, 1), F32)
+        for j in range(lines):
+            at = pl.ds(j * cols, cols)
+            grad = acc[j, pl.ds(0, rows), :]
+            unit = res_s[:, at] * inverse
+            dgain_out[:, at] = jnp.sum(grad * unit, axis=0, keepdims=True)
+            mean = mean + jnp.sum(grad * gain_ref[:, at] * unit, axis=-1, keepdims=True)
+        mean = mean * (1.0 / width)
+        for j in range(lines):
+            at = pl.ds(j * cols, cols)
+            unit = res_s[:, at] * inverse
+            grad = acc[j, pl.ds(0, rows), :] * gain_ref[:, at]
+            d_res = own_s[:, at].astype(F32) + inverse * (grad - unit * mean)
+            res_s[:, at] = d_res
+            first, second = d_res[:, :block], d_res[:, block:]
+            mine = jnp.where(side == 0, first, second).astype(BF)
+            theirs = jnp.where(side == 0, second, first).astype(BF)
+            attn_s[:, pl.ds(j * block, block)] = mine
+            attn_s[:, pl.ds((lines + j) * block, block)] = theirs
+
+        sends = [
+            remote(
+                attn_s, attn_out.at[pl.ds(rows, rows)], last_send.at[0], last_recv.at[0], across_half
+            ),
+            remote(
+                attn_s,
+                attn_out.at[pl.ds(2 * rows, rows)],
+                last_send.at[1],
+                last_recv.at[1],
+                across_core,
+            ),
+            remote(
+                attn_out.at[pl.ds(rows, rows)],
+                attn_out.at[pl.ds(3 * rows, rows)],
+                last_send.at[2],
+                last_recv.at[2],
+                across_core,
+            ),
+        ]
+        sends[0].start()
+        sends[1].start()
+        outs = [
+            pltpu.make_async_copy(res_s, dres_out, out_sem.at[0]),
+            pltpu.make_async_copy(attn_s, attn_out.at[pl.ds(0, rows)], out_sem.at[1]),
+        ]
+        for copy in outs:
+            copy.start()
+        sends[0].wait_recv()
+        sends[2].start()
+        for j in range(max(lines - 2, 0), lines):
+            grad_copy(j).wait()
+
+        @pl.loop(0, lines)
+        def _(j):
+            to_core(j).wait_send()
+            to_side(j).wait_send()
+            to_half(j).wait_send()
+
+        sends[0].wait_send()
+        sends[1].wait()
+        sends[2].wait()
+        wait_all(outs)
+
+    out_shape = (
+        jax.ShapeDtypeStruct((lines, double, cols), BF),
+        jax.ShapeDtypeStruct((rows, width), F32),
+        jax.ShapeDtypeStruct((1, width), F32),
+        jax.ShapeDtypeStruct((4 * rows, width), BF),
+    )
+    args = (*grads, *normed, down, gate_up, a_fac, s_fac, residual, gain)
+    vmem = pl.BlockSpec(memory_space=pltpu.VMEM)
+    dma = pltpu.SemaphoreType.DMA
+    return pl.pallas_call(
+        kernel,
+        out_shape=out_shape,
+        in_specs=[ANY] * (len(args) - 1) + [vmem],
+        out_specs=(ANY, ANY, vmem, ANY),
+        scratch_shapes=[
+            pltpu.VMEM((total, width), BF),
+            pltpu.VMEM((hid, width), BF),
+            pltpu.VMEM((double, width), BF),
+            pltpu.VMEM((hid, total), BF),
+            pltpu.VMEM((hid, total), BF),
+            pltpu.VMEM((double, total), BF),
+            pltpu.VMEM((lines, near, cols), BF),
+            pltpu.VMEM((lines, near, cols), BF),
+            pltpu.VMEM((lines, 2 * rows, cols), F32),
+            pltpu.VMEM((lines, 2 * rows, cols), BF),
+            pltpu.VMEM((lines, 2 * rows, cols), BF),
+            pltpu.VMEM((lines, rows, cols), BF),
+            pltpu.VMEM((lines, rows, cols), BF),
+            pltpu.VMEM((2, double, cols), BF),
+            pltpu.VMEM((rows, width), F32),
+            pltpu.VMEM((rows, width), BF),
+            pltpu.VMEM((rows, width), BF),
+            dma((count,)),
+            dma((lines,)),
+            dma((lines,)),
+            dma((2,)),
+            dma((lines,)),
+            dma((lines,)),
+            dma((lines,)),
+            dma((lines,)),
+            dma((lines,)),
+            dma((lines,)),
+            dma((2,)),
+            dma,
+            dma,
+            dma((3,)),
+            dma((3,)),
+            dma((2,)),
+        ],
+        compiler_params=pltpu.CompilerParams(
+            vmem_limit_bytes=vmem_bytes, collective_id=0, has_side_effects=True
+        ),
+        cost_estimate=cost(10 * hid * total * width, args + out_shape),
+        name="ffn_back",
+    )(*args)
+
+
 def build(n):
     lines = n // 4
 
@@ -90,14 +558,35 @@
     def line_gather(value):
         return lax.all_gather(value, "dp", axis=0, tiled=True, axis_index_groups=line_groups)
 
-    def line_sum(value):
-        return lax.psum_scatter(
-            value, "dp", scatter_dimension=0, tiled=True, axis_index_groups=line_groups
-        )
+    def after(value, earlier):
+        return value if earlier is None else lax.optimization_barrier((value, earlier))[0]
+
+    def line_sum(value, queue):
+        mine = lax.psum_scatter(
+            after(value, queue[-1] if queue else None),
+            "dp",
+            scatter_dimension=0,
+            tiled=True,
+            axis_index_groups=line_groups,
+        )
+        queue.append(mine)
+        return mine
 
     def quad_gather(own):
         pair = jnp.concatenate([own, half_swap(own)], axis=0)
         return jnp.concatenate([pair, core_swap(pair)], axis=0)
+
+    def eight_gather(own):
+        across = half_swap(own)
+        near = [own, across, side_swap(own), side_swap(across)]
+        return near + [core_swap(piece) for piece in near]
+
+    def eight_sum(near, far):
+        four = near.astype(F32) + core_swap(far).astype(F32)
+        rows = four.shape[0] // 2
+        pair = four[:rows] + side_swap(four[rows:].astype(BF)).astype(F32)
+        rows = rows // 2
+        return pair[:rows] + half_swap(pair[rows:].astype(BF)).astype(F32)
 
     def quad_sum(part):
         half = part.shape[0] // 2
@@ -133,7 +622,7 @@
         scale = 1.0 / math.sqrt(head_dim)
         shard = q_down.shape[0]
         block = 2 * shard
-        hid = gate_proj.shape[1] // 2
+        hid = gate_proj.shape[1] // 4
         feats = q_up.shape[1] // 2
         heads = feats // head_dim
         q_shard = q_up.shape[0]
@@ -161,7 +650,6 @@
             return order(side, mine, theirs, 2).reshape(rows, width)
 
         x_low = to_rel(tokens)
-        dy_low = to_rel(out_grad)
         x_quad = quad_gather(x_low)
 
         mixed_cols = jnp.concatenate(
@@ -192,9 +680,21 @@
 
         q_up_mine, q_up_theirs = spread(q_up)
         out_mine, out_theirs = spread(out_proj.T)
-        gate_mine, gate_theirs = spread(gate_proj)
-        up_mine, up_theirs = spread(up_proj)
-        down_mine, down_theirs = spread(down_proj.T)
+
+        ffn_low = jnp.stack([gate_proj.T, up_proj.T, down_proj]).astype(BF)
+        ffn_keep = lax.dynamic_slice_in_dim(ffn_low, side * 2 * hid, 2 * hid, 1)
+        ffn_give = lax.dynamic_slice_in_dim(ffn_low, (1 - side) * 2 * hid, 2 * hid, 1)
+        ffn_sides = order(side, ffn_keep[:, :, None], side_swap(ffn_give)[:, :, None], 2)
+        ffn_keep = lax.dynamic_slice_in_dim(ffn_sides, core * hid, hid, 1)
+        ffn_give = lax.dynamic_slice_in_dim(ffn_sides, (1 - core) * hid, hid, 1)
+        ffn_piece = order(
+            core, ffn_keep[:, :, :, None], core_swap(ffn_give)[:, :, :, None], 3
+        ).reshape(3, hid, 2 * block)
+
+        gate_up_w = line_gather(ffn_piece[:2].reshape(2 * hid, 2 * block)).reshape(
+            lines, 2 * hid, 2 * block
+        )
+        down_w = line_gather(ffn_piece[2]).reshape(lines, hid, 2 * block)
 
         qkv_part = jnp.stack(
             [
@@ -296,56 +796,50 @@
         attn_out = jnp.concatenate(
             [matmul_nt(head_mix, out_mine), matmul_nt(head_mix, out_theirs)], axis=1
         )
-        residual = x_low.astype(F32) + quad_sum(attn_out)
+        residual = tokens.astype(F32) + from_rel(quad_sum(attn_out))
 
         inv_two = inv_rms(residual)
         unit_two = residual * inv_two
-        normed_two = quad_gather((unit_two * gain_two).astype(BF))
-        grad_quad = quad_gather(dy_low)
-        gate_act = matmul(normed_two[:, :edge], gate_mine) + matmul(
-            normed_two[:, edge:], gate_theirs
-        )
-        up_act = matmul(normed_two[:, :edge], up_mine) + matmul(normed_two[:, edge:], up_theirs)
-        gate_sig = jax.nn.sigmoid(gate_act)
-        gate_silu = gate_act * gate_sig
-        hidden = (gate_silu * up_act).astype(BF)
+        gain_two_abs = from_rel(gain_two[None, :])
+        normed_two = eight_gather((unit_two * gain_two_abs).astype(BF))
+        grad_all = eight_gather(out_grad)
+        hidden, a_fac, s_fac, d_down = ffn_first(normed_two, grad_all, gate_up_w)
+
+        queue = []
+
+        def line_part(value):
+            count = value.shape[1] // hid
+            mine = line_sum(value.reshape(lines * count * hid, 2 * block), queue)
+            mine = mine.reshape(count, hid, 2, 2, shard)
+            keep = lax.dynamic_index_in_dim(mine, core, 3, keepdims=False)
+            give = lax.dynamic_index_in_dim(mine, 1 - core, 3, keepdims=False)
+            cores = order(core, keep[:, None], core_swap(give)[:, None], 1)
+            keep = lax.dynamic_index_in_dim(cores, side, 3, keepdims=False)
+            give = lax.dynamic_index_in_dim(cores, 1 - side, 3, keepdims=False)
+            sides = order(side, keep[:, None], side_swap(give)[:, None], 1)
+            return sides.reshape(count, 4 * hid, shard).astype(F32)
+
+        down_total = line_part(d_down)[0]
+        near_rows = 4 * own_rows
+        d_gate_up, d_resid, d_ffn_gain, d_attn = ffn_back(
+            grad_all, down_w, gate_up_w, a_fac, s_fac, normed_two, residual, gain_two_abs
+        )
+        d_ffn_gain = to_rel(d_ffn_gain)
+        gate_up_total = line_part(d_gate_up)
+        ffn_part = ffn_out_part(hidden, down_w, own_rows)
+        output = (residual + eight_sum(ffn_part[:near_rows], ffn_part[near_rows:])).astype(BF)
+        gate_total = gate_up_total[0].T
+        up_total = gate_up_total[1].T
 
         def grad_sum(lhs, rhs):
             give = matmul_tn(lhs[:, edge:], rhs).astype(BF)
             part = (matmul_tn(lhs[:, :edge], rhs) + side_swap(give).astype(F32)).astype(BF)
-            mine = line_sum(part)
+            mine = line_sum(part, queue)
             rows = mine.shape[0] // 2
             keep = lax.dynamic_slice_in_dim(mine, core * rows, rows, 0)
             away = lax.dynamic_slice_in_dim(mine, (1 - core) * rows, rows, 0)
             return order(core, keep, core_swap(away), 1).astype(F32)
 
-        down_total = grad_sum(grad_quad, hidden).T
-        ffn_out = jnp.concatenate(
-            [matmul_nt(hidden, down_mine), matmul_nt(hidden, down_theirs)], axis=1
-        )
-        output = from_rel((residual + quad_sum(ffn_out)).astype(BF))
-        d_hidden = matmul(grad_quad[:, :edge], down_mine) + matmul(
-            grad_quad[:, edge:], down_theirs
-        )
-        d_gate_act = (d_hidden * up_act * gate_sig * (1.0 + gate_act * (1.0 - gate_sig))).astype(
-            BF
-        )
-        d_up_act = (d_hidden * gate_silu).astype(BF)
-        d_normed_two = quad_sum(
-            jnp.concatenate(
-                [
-                    matmul_nt(d_gate_act, gate_mine) + matmul_nt(d_up_act, up_mine),
-                    matmul_nt(d_gate_act, gate_theirs) + matmul_nt(d_up_act, up_theirs),
-                ],
-                axis=1,
-            )
-        )
-        gate_total = grad_sum(normed_two, d_gate_act)
-        up_total = grad_sum(normed_two, d_up_act)
-        d_ffn_gain = jnp.sum(d_normed_two * unit_two, axis=0)
-        d_resid = dy_low.astype(F32) + norm_back(d_normed_two, unit_two, inv_two, gain_two)
-
-        d_attn = quad_gather(d_resid.astype(BF))
         out_total = grad_sum(d_attn, head_mix).T
         d_mix = (
             (matmul(d_attn[:, :edge], out_mine) + matmul(d_attn[:, edge:], out_theirs))
@@ -386,7 +880,7 @@
         q_up_give = lax.dynamic_index_in_dim(d_q_up, 1 - side, 1, keepdims=False)
         q_up_keep = lax.dynamic_index_in_dim(d_q_up, side, 1, keepdims=False)
         q_up_part = (q_up_keep.astype(F32) + side_swap(q_up_give).astype(F32)).astype(BF)
-        q_up_sum = line_sum(q_up_part.reshape(lines * 2 * q_shard, feats))
+        q_up_sum = line_sum(q_up_part.reshape(lines * 2 * q_shard, feats), queue)
         q_up_near = lax.dynamic_slice_in_dim(q_up_sum, core * q_shard, q_shard, 0)
         q_up_away = lax.dynamic_slice_in_dim(q_up_sum, (1 - core) * q_shard, q_shard, 0)
         q_up_total = order(core, q_up_near, core_swap(q_up_away), 1).astype(F32)
@@ -406,7 +900,7 @@
         inv_own = inv_rms(x_low.astype(F32))
         unit_own = x_low.astype(F32) * inv_own
         d_attn_gain = jnp.sum(d_normed * unit_own, axis=0)
-        in_grad = from_rel((d_resid + norm_back(d_normed, unit_own, inv_own, gain_one)).astype(BF))
+        in_grad = (d_resid + from_rel(norm_back(d_normed, unit_own, inv_own, gain_one))).astype(BF)
 
         normed_rows = lax.dynamic_index_in_dim(
             normed.reshape(all_rows, 2 * lines, 2, shard), core, 2, keepdims=False
@@ -442,7 +936,7 @@
         )[:, :, None, :]
         d_qkv = jnp.concatenate([d_qkv, d_gain, jnp.zeros((2, lines, 15, qkv_cols), F32)], axis=2)
         d_qkv_part = (d_qkv[0] + side_swap(d_qkv[1].astype(BF)).astype(F32)).astype(BF)
-        d_qkv_sum = line_sum(d_qkv_part.reshape(lines * (shard + 16), qkv_cols))
+        d_qkv_sum = line_sum(d_qkv_part.reshape(lines * (shard + 16), qkv_cols), queue)
         d_qkv_far = half_swap(d_qkv_sum)
         gain_pair = d_qkv_sum[shard : shard + 1].astype(F32) + d_qkv_far[
             shard : shard + 1

time: 950 us -> 827 us (0.87)
  waiting for transfers between devices: 429 us -> 255 us
  Pallas kernels: 0 us -> 148 us
  matrix products: 186 us -> 77.7 us
  local copies, waits for them, and re-layouts: 100 us -> 123 us
  blocking collectives: 33.9 us -> 20 us
    pallas_call x0 -> x3, Pallas kernels: none -> 148 us  [the longest x1 107 us: ffn_back(): pl.pallas_call(kernel, out_shape=out_shape, in_specs=[ANY] * (len(args) -...]
    ppermute x12 -> x14, waiting for transfers between devices: 268 us -> 134 us  [side_swap(): return lax.ppermute(value, 'dp', side_pairs)]
    ppermute x11 -> x9, waiting for transfers between devices: 144 us -> 100 us  [half_swap(): return lax.ppermute(value, 'tensor', [(0, 1), (1, 0)])]
    dot_general x10 -> x4, matrix products: 64.3 us -> 21.7 us  [matmul(): return jnp.dot(left, right, preferred_element_type=F32)]
    dot_general x10 -> x4, matrix products: 54 us -> 17 us  [matmul_nt(): lax.dot_general(left, right, (((1,), (1,)), ((), ())), preferred_element_...]
    dot_general x10 -> x4, matrix products: 49.1 us -> 18.4 us  [matmul_tn(): lax.dot_general(left, right, (((0,), (0,)), ((), ())), preferred_element_...]
    concatenate x0 -> x5, local copies, waits for them, and re-layouts: none -> 14.2 us  [the longest x4 13.4 us: quad_gather(): return jnp.concatenate([pair, core_swap(pair)], axis=0)]
    all_gather x1, blocking collectives: 33.9 us -> 20 us  [line_gather(): lax.all_gather(value, 'dp', axis=0, tiled=True, axis_index_groups=line_gr...]
  transfers between devices with their start and end apart: 57 -> 56, of which waited for: 21 -> 18; matrix products, arithmetic and copies ran while one was open for 38% -> 38% of each run, Pallas kernels for 0% -> 18%
where the time goes in v2:
time: 827 us; the launch traced here: 818 us
  waiting for transfers between devices  255 us (31%)
  Pallas kernels  148 us (18%)
  other arithmetic  124 us (15%)
  local copies, waits for them, and re-layouts  123 us (15%)
  matrix products  77.7 us (9%)
  starting transfers between devices  50.9 us (6%)
  blocking collectives  20 us (2%)
  between operations  18.5 us (2%)
    ppermute x14, waiting for transfers between devices, side_swap(): return lax.ppermute(value, 'dp', side_pairs)  134 us
    pallas_call x1, Pallas kernels, ffn_back(): pl.pallas_call(kernel, out_shape=out_shape, in_specs=[ANY] * (len(args) -...  107 us
    ppermute x9, waiting for transfers between devices, half_swap(): return lax.ppermute(value, 'tensor', [(0, 1), (1, 0)])  100 us
    ppermute x24, starting transfers between devices, core_swap(): return lax.ppermute(value, 'dp', core_pairs)  31.9 us
    select_n x16, other arithmetic, order(): jnp.where(flag == 0, jnp.concatenate([first, second], axis=axis), jnp.con...  30.3 us
    pallas_call x1, Pallas kernels, ffn_first(): pl.pallas_call(kernel, out_shape=out_shape, in_specs=[ANY] * len(args), o...  29 us
    unnamed x139, local copies, waits for them, and re-layouts  25.1 us
    dot_general x4, matrix products, matmul(): return jnp.dot(left, right, preferred_element_type=F32)  21.7 us
  transfers between devices with their start and end apart: 56, of which 18 were waited for; matrix products, arithmetic and copies ran while one was open for 38% of the time, Pallas kernels for 18%

profile of v2, /device:TPU:1, one launch (start us, length us, event | category | flops | bytes accessed | tf_op | source)
XLA Modules:
  0.0 817.6 jit_solution(15383753837490981408)
XLA Ops:
  13.0 20.0 %all_gather.15 = bf16[576,768]{1,0:T(8,128)(2,1)S(1)} all-gather(bf16[144,768]{1,0:T(8,128)(2,1)S(1)} %maximum_maximum_fusion.1), channel_id=1, replica_groups={{0,8,16,24},{2,10,18,26},{4,12,20,28},{6,14,22,30},{1,9,17,25},{3,11,19..., dimensions={0}, use_global_device_ids=true | all-gather | bytes 1105920 | tf_op jit(solution)/shard_map/all_gather | solution.py:559
  50.3 3.0 dynamic-slice_bitcast_fusion.1
  64.8 36.0 %collective-permute-done.4 = bf16[2,4,144,768]{3,2,1,0:T(8,128)(2,1)} collective-permute-done((bf16[2,4,144,768]{3,2,1,0:T(8,128)(2,1)}, bf16[2,4,144,768]{3,2,1,0:T(8,128)(2,1)}, u32[]{:S(2)}, u32[]{:S(2)}) %collective-permute-start.4) | collective-permute-done | bytes 1769504 | tf_op jit(solution)/shard_map/ppermute | solution.py:556
  104.4 3.3 fusion.101
  107.7 3.7 collective-permute-start.5
  111.5 2.9 pad_maximum_fusion.9
  122.2 2.8 maximum_select_fusion.2
  129.6 15.4 %collective-permute-done.8 = bf16[512,1024]{1,0:T(8,128)(2,1)} collective-permute-done((bf16[512,1024]{1,0:T(8,128)(2,1)}, bf16[512,1024]{1,0:T(8,128)(2,1)}, u32[]{:S(2)}, u32[]{:S(2)}) %collective-permute-start.8) | collective-permute-done | bytes 1048608 | tf_op jit(solution)/shard_map/ppermute | solution.py:553
  147.6 2.7 copy.249
  150.3 5.8 fusion
  156.8 6.3 fusion.8
  163.7 10.8 %fusion.13 = f32[1024,1536]{1,0:T(8,128)S(1)} fusion(bf16[2048,1536]{1,0:T(8,128)(2,1)S(1)} %bitcast.263, f32[2048]{0:T(1024)S(1)} %bitcast.312, f32[1024]{0:T(1024)S(1)} %add_rsqrt_fusion.1, bf16[512,2048]{1,0:T(8,128)(2,1)} %collective-permute-done.1, bf16[256,2048]{1,0:T(8,128)(2,1)} %collective-permute-done, bf16[256,1024]{1,0:T(8,128)(2,1)S(1)} %copy.246, ...), kind=kOutput, calls=%fused_computation.26 | convolution fusion | flops 6465519616 | bytes 16789504 | tf_op jit(solution)/shard_map/dot_general | solution.py:17
  175.0 3.4 fusion.62
  187.2 3.1 convert_bitcast_fusion
  190.2 3.0 copy.200
  197.6 5.4 collective-permute-done.10
  203.0 4.1 fusion.114
  209.1 3.8 collective-permute-done.11
  216.6 21.8 %collective-permute-done.12 = bf16[256,2048]{0,1:T(8,128)(2,1)S(1)} collective-permute-done((bf16[256,2048]{0,1:T(8,128)(2,1)S(1)}, bf16[256,2048]{0,1:T(8,128)(2,1)S(1)}, u32[]{:S(2)}, u32[]{:S(2)}) %collective-permute-start.12) | collective-permute-done | bytes 1048608 | tf_op jit(solution)/shard_map/ppermute | solution.py:556
  242.7 6.0 maximum_select_fusion.4
  257.7 3.0 squeeze.78
  264.8 18.6 %collective-permute-done.13.refs_1_.refs_9_ = bf16[256,2048]{1,0:T(8,128)(2,1)} collective-permute-done((bf16[256,2048]{1,0:T(8,128)(2,1)}, bf16[256,2048]{1,0:T(8,128)(2,1)}, u32[]{:S(2)}, u32[]{:S(2)}) %collective-permute-start.13) | collective-permute-done | bytes 1048608 | tf_op jit(solution)/shard_map/ppermute | solution.py:556
  283.9 5.5 collective-permute-start.26
  289.9 16.4 %collective-permute-done.14.refs_2_.refs_10_ = bf16[256,2048]{1,0:T(8,128)(2,1)} collective-permute-done((bf16[256,2048]{1,0:T(8,128)(2,1)}, bf16[256,2048]{1,0:T(8,128)(2,1)}, u32[]{:S(2)}, u32[]{:S(2)}) %collective-permute-start.14) | collective-permute-done | bytes 1048608 | tf_op jit(solution)/shard_map/ppermute | solution.py:553
  306.2 5.7 collective-permute-start.18
  311.9 16.8 %collective-permute-done.15.refs_3_.refs_11_ = bf16[256,2048]{1,0:T(8,128)(2,1)} collective-permute-done((bf16[256,2048]{1,0:T(8,128)(2,1)}, bf16[256,2048]{1,0:T(8,128)(2,1)}, u32[]{:S(2)}, u32[]{:S(2)}) %collective-permute-start.15) | collective-permute-done | bytes 1048608 | tf_op jit(solution)/shard_map/ppermute | solution.py:553
  328.7 3.0 collective-permute-start.19
  334.4 29.0 %ffn_first.1 = (bf16[704,2048]{1,0:T(8,128)(2,1)}, bf16[704,2048]{1,0:T(8,128)(2,1)}, bf16[704,2048]{1,0:T(8,128)(2,1)}, bf16[4,704,512]{2,1,0:T(8,128)(2,1)}) custom-call(bf16[256,2048]{1,0:T(8,128)(2,1)} %multiply_convert_fusion.2.refs_0_.refs_8_, bf16[256,2048]{1,0:T(8,128)(2,1)} %collective-permute-done.13.refs_1_.refs_9_, ...), custom_call_target="tpu_custom_call" | custom-call | flops 17716740096 | bytes 34078720 | tf_op jit(solution)/shard_map/ffn_first/pallas_call | solution.py:167
  368.3 4.5 concatenate.363
  372.8 4.7 copy.226
  380.2 107.2 %ffn_back.1 = (bf16[4,1408,512]{2,1,0:T(8,128)(2,1)}, f32[256,2048]{1,0:T(8,128)}, f32[1,2048]{1,0:T(1,128)}, bf16[1024,2048]{1,0:T(8,128)(2,1)}) custom-call(bf16[256,2048]{1,0:T(8,128)(2,1)} %refs_0_.1, bf16[256,2048]{1,0:T(8,128)(2,1)} %collective-permute-done.20.refs_9_.refs_1_, bf16[256,2048]{1,0:T(8,128)(2,1)} %collective-permute-done.21.refs_10_.refs_2_, ...), custom_call_target="tpu_custom_call" | custom-call | flops 29527900160 | bytes 45367296 | tf_op jit(solution)/shard_map/ffn_back/pallas_call | solution.py:490
  487.5 4.7 fusion.42
  492.2 3.7 add_convert_fusion.1
  495.9 3.3 reshape.734
  499.3 6.7 fusion.3
  506.1 7.1 fusion.5
  515.3 3.3 multiply_bitcast_fusion
  518.6 5.2 copy.216
  523.8 3.1 multiply_subtract_fusion
  528.5 4.4 copy.217
  532.9 4.2 fusion.57
  537.1 4.5 fusion.115
  543.0 2.9 pad_maximum_fusion.2
  549.0 5.6 convolution_convert_fusion
  557.0 5.5 convolution_convert_fusion.1
  564.0 12.0 %ffn_out_part.1 = bf16[2048,2048]{1,0:T(8,128)(2,1)} custom-call(bf16[704,2048]{1,0:T(8,128)(2,1)} %get-tuple-element.25.hid_ref, bf16[4,704,512]{2,1,0:T(8,128)(2,1)} %bitcast.348), custom_call_target="tpu_custom_call" | custom-call | flops 5905580032 | bytes 14155776 | tf_op jit(solution)/shard_map/ffn_out_part/pallas_call | solution.py:216
  576.0 4.8 slice.325
  581.6 3.0 slice_add_fusion.1
  586.8 39.0 %collective-permute-done.37 = bf16[4,128,1024]{2,1,0:T(8,128)(2,1)} collective-permute-done((bf16[4,128,1024]{2,1,0:T(8,128)(2,1)}, bf16[4,128,1024]{2,1,0:T(8,128)(2,1)}, u32[]{:S(2)}, u32[]{:S(2)}) %collective-permute-start.37) | collective-permute-done | bytes 1048608 | tf_op jit(solution)/shard_map/ppermute | solution.py:553
  628.4 5.4 add_convert_fusion
  641.1 6.0 fusion.26
  647.1 10.8 %collective-permute-done.34 = bf16[256,1536]{1,0:T(8,128)(2,1)S(1)} collective-permute-done((bf16[256,1536]{1,0:T(8,128)(2,1)S(1)}, bf16[256,1536]{1,0:T(8,128)(2,1)S(1)}, u32[]{:S(2)}, u32[]{:S(2)}) %collective-permute-start.34) | collective-permute-done | bytes 786464 | tf_op jit(solution)/shard_map/ppermute | solution.py:556
  666.8 5.4 convert_add_fusion
  674.8 4.8 pad_maximum_fusion.6
  686.8 4.0 maximum_select_fusion.5
  690.8 3.0 select_n.414
  699.3 41.0 %collective-permute-done.36 = bf16[4,144,768]{2,1,0:T(8,128)(2,1)} collective-permute-done((bf16[4,144,768]{2,1,0:T(8,128)(2,1)}, bf16[4,144,768]{2,1,0:T(8,128)(2,1)}, u32[]{:S(2)}, u32[]{:S(2)}) %collective-permute-start.36) | collective-permute-done | bytes 884768 | tf_op jit(solution)/shard_map/ppermute | solution.py:553
  745.3 3.0 constant_dynamic-slice_fusion.7
  749.6 3.7 slice_add_fusion
  759.9 11.4 %reduce-scatter.12.cloned.1.call-done = bf16[128,1024]{1,0:T(8,128)(2,1)} async-done(((bf16[512,1024]{1,0:T(8,128)(2,1)}), bf16[128,1024]{1,0:T(8,128)(2,1)}) %reduce-scatter.12.cloned.1.call-update) | async-done | bytes 262160 | tf_op jit(solution)/shard_map/reduce_scatter | solution.py:565
  771.3 8.3 %collective-permute-done.31 = bf16[256,2048]{1,0:T(8,128)(2,1)} collective-permute-done((bf16[256,2048]{1,0:T(8,128)(2,1)}, bf16[256,2048]{1,0:T(8,128)(2,1)}, u32[]{:S(2)}, u32[]{:S(2)}) %collective-permute-start.31) | collective-permute-done | bytes 1048608 | tf_op jit(solution)/shard_map/ppermute | solution.py:556
  779.6 3.3 fusion.31
  793.7 3.1 reduce-scatter.14.cloned.1.call-done
  799.8 4.3 collective-permute-done.39
  (419 shorter events, 180.9 us)
Async XLA Ops:
  7.2 112.6 %all-gather.5.cloned.1.call-start = ((), (), s32[]{:S(2)}) async-start(), calls=%async_computation.5 | async-start | bytes 1310720 | tf_op jit(solution)/shard_map/all_gather | solution.py:559
  7.3 50.8 %collective-permute-start.6 = (s32[1]{0:T(128)}, s32[1]{0:T(128)}, u32[]{:S(2)}, u32[]{:S(2)}) collective-permute-start(s32[1]{0:T(128)} %param.17), channel_id=1, source_target_pairs={{0,2},{2,0},{4,6},{6,4},{8,10},{10,8},{12,14},{14,12},{16,18},{18,... | collective-permute-start | bytes 20 | tf_op jit(solution)/shard_map/ppermute | solution.py:550
  9.2 25.1 %copy-start.20 = (bf16[256,2048]{1,0:T(8,128)(2,1)S(1)}, bf16[256,2048]{1,0:T(8,128)(2,1)}, u32[]{:S(2)}) copy-start(bf16[256,2048]{1,0:T(8,128)(2,1)} %param.16) | copy-start | bytes 3145732
  9.2 44.4 %collective-permute-start.7 = (bf16[64,1024]{1,0:T(8,128)(2,1)}, bf16[64,1024]{1,0:T(8,128)(2,1)}, u32[]{:S(2)}, u32[]{:S(2)}) collective-permute-start(bf16[64,1024]{1,0:T(8,128)(2,1)} %get-tuple-element.159), channel_id=1, source_target_pairs={{0,2},{2,0},{4,6},{6,4},{8,10},{10,8},{12,14},{14,12},{16,18},{18,... | collective-permute-start | bytes 393224 | tf_op jit(solution)/shard_map/ppermute | solution.py:550
  11.7 50.8 %collective-permute-start.9 = (bf16[128,1024]{0,1:T(8,128)(2,1)}, bf16[128,1024]{0,1:T(8,128)(2,1)}, u32[]{:S(2)}, u32[]{:S(2)}) collective-permute-start(bf16[128,1024]{0,1:T(8,128)(2,1)} %get-tuple-element.155), channel_id=1, source_target_pairs={{0,2},{2,0},{4,6},{6,4},{8,10},{10,8},{12,14},{14,12},{16,18},{18,... | collective-permute-start | bytes 786440 | tf_op jit(solution)/shard_map/ppermute | solution.py:550
  33.0 22.7 %collective-permute-start.2 = (bf16[576,768]{1,0:T(8,128)(2,1)S(1)}, bf16[576,768]{1,0:T(8,128)(2,1)S(1)}, u32[]{:S(2)}, u32[]{:S(2)}) collective-permute-start(bf16[576,768]{1,0:T(8,128)(2,1)S(1)} %all_gather.15), channel_id=1, source_target_pairs={{0,4},{2,6},{4,0},{6,2},{8,12},{10,14},{12,8},{14,10},{16,20},{18,... | collective-permute-start | bytes 2654216 | tf_op jit(solution)/shard_map/ppermute | solution.py:553
  40.7 70.8 %collective-permute-start = (bf16[256,2048]{1,0:T(8,128)(2,1)}, bf16[256,2048]{1,0:T(8,128)(2,1)}, u32[]{:S(2)}, u32[]{:S(2)}) collective-permute-start(bf16[256,2048]{1,0:T(8,128)(2,1)} %pad_maximum_fusion.12), channel_id=1, source_target_pairs={{0,1},{1,0},{2,3},{3,2},{4,5},{5,4},{6,7},{7,6},{8,9},{9,8},{10,11... | collective-permute-start | bytes 3145736 | tf_op jit(solution)/shard_map/ppermute | solution.py:556
  53.5 60.9 %collective-permute-start.27 = (bf16[3,1408,128]{2,1,0:T(8,128)(2,1)}, bf16[3,1408,128]{2,1,0:T(8,128)(2,1)}, u32[]{:S(2)}, u32[]{:S(2)}) collective-permute-start(bf16[3,1408,128]{2,1,0:T(8,128)(2,1)} %get-tuple-element.133), channel_id=1, source_target_pairs={{0,4},{2,6},{4,0},{6,2},{8,12},{10,14},{12,8},{14,10},{16,20},{18,... | collective-permute-start | bytes 3244040 | tf_op jit(solution)/shard_map/ppermute | solution.py:553
  55.6 100.6 %all-gather.7.cloned.1.call-start = ((), (), s32[]{:S(2)}) async-start(), calls=%async_computation.6 | async-start | bytes 2621440 | tf_op jit(solution)/shard_map/all_gather | solution.py:559
  57.1 43.7 %collective-permute-start.4 = (bf16[2,4,144,768]{3,2,1,0:T(8,128)(2,1)}, bf16[2,4,144,768]{3,2,1,0:T(8,128)(2,1)}, u32[]{:S(2)}, u32[]{:S(2)}) collective-permute-start(bf16[2,4,144,768]{3,2,1,0:T(8,128)(2,1)} %pad_maximum_fusion.7), channel_id=1, source_target_pairs={{0,1},{1,0},{2,3},{3,2},{4,5},{5,4},{6,7},{7,6},{8,9},{9,8},{10,11... | collective-permute-start | bytes 5308424 | tf_op jit(solution)/shard_map/ppermute | solution.py:556
  64.6 268.2 %all-gather.9.cloned.1.call-start = ((), (), s32[]{:S(2)}) async-start(), calls=%async_computation.7 | async-start | bytes 7208960 | tf_op jit(solution)/shard_map/all_gather | solution.py:559
  107.7 49.0 %collective-permute-start.5 = (bf16[2,4,144,1536]{3,2,1,0:T(8,128)(2,1)}, bf16[2,4,144,1536]{3,2,1,0:T(8,128)(2,1)}, u32[]{:S(2)}, u32[]{:S(2)}) collective-permute-start(bf16[2,4,144,1536]{3,2,1,0:T(8,128)(2,1)} %get-tuple-element.123), channel_id=1, source_target_pairs={{0,2},{2,0},{4,6},{6,4},{8,10},{10,8},{12,14},{14,12},{16,18},{18,... | collective-permute-start | bytes 10616840 | tf_op jit(solution)/shard_map/ppermute | solution.py:550
  114.4 35.9 %collective-permute-start.1 = (bf16[512,2048]{1,0:T(8,128)(2,1)}, bf16[512,2048]{1,0:T(8,128)(2,1)}, u32[]{:S(2)}, u32[]{:S(2)}) collective-permute-start(bf16[512,2048]{1,0:T(8,128)(2,1)} %pad_maximum_fusion.9), channel_id=1, source_target_pairs={{0,2},{2,0},{4,6},{6,4},{8,10},{10,8},{12,14},{14,12},{16,18},{18,... | collective-permute-start | bytes 6291464 | tf_op jit(solution)/shard_map/ppermute | solution.py:550
  118.0 4.1 collective-permute-start.28
  119.8 25.1 %collective-permute-start.8 = (bf16[512,1024]{1,0:T(8,128)(2,1)}, bf16[512,1024]{1,0:T(8,128)(2,1)}, u32[]{:S(2)}, u32[]{:S(2)}) collective-permute-start(bf16[512,1024]{1,0:T(8,128)(2,1)} %all-gather.5.cloned.1.call-done), channel_id=1, source_target_pairs={{0,4},{2,6},{4,0},{6,2},{8,12},{10,14},{12,8},{14,10},{16,20},{18,... | collective-permute-start | bytes 3145736 | tf_op jit(solution)/shard_map/ppermute | solution.py:553
  120.1 1.7 collective-permute-start.3
  122.2 56.2 %copy-start.46 = (f32[4,2,128]{2,1,0:T(2,128)}, f32[4,2,128]{2,1,0:T(2,128)S(1)}, u32[]{:S(2)}) copy-start(f32[4,2,128]{2,1,0:T(2,128)S(1)} %copy.194) | copy-start | bytes 12292
  129.4 250.9 %all-gather.11.cloned.1.call-start = ((), (), s32[]{:S(2)}) async-start(), calls=%async_computation.8 | async-start | bytes 3604480 | tf_op jit(solution)/shard_map/all_gather | solution.py:559
  156.2 46.8 %collective-permute-start.10 = (bf16[1024,1024]{0,1:T(8,128)(2,1)}, bf16[1024,1024]{0,1:T(8,128)(2,1)}, u32[]{:S(2)}, u32[]{:S(2)}) collective-permute-start(bf16[1024,1024]{0,1:T(8,128)(2,1)} %all-gather.7.cloned.1.call-done), channel_id=1, source_target_pairs={{0,4},{2,6},{4,0},{6,2},{8,12},{10,14},{12,8},{14,10},{16,20},{18,... | collective-permute-start | bytes 6291464 | tf_op jit(solution)/shard_map/ppermute | solution.py:553
  207.4 5.5 collective-permute-start.11
  213.9 24.5 %collective-permute-start.12 = (bf16[256,2048]{0,1:T(8,128)(2,1)S(1)}, bf16[256,2048]{0,1:T(8,128)(2,1)S(1)}, u32[]{:S(2)}, u32[]{:S(2)}) collective-permute-start(bf16[256,2048]{0,1:T(8,128)(2,1)S(1)} %slice.483), channel_id=1, source_target_pairs={{0,1},{1,0},{2,3},{3,2},{4,5},{5,4},{6,7},{7,6},{8,9},{9,8},{10,11... | collective-permute-start | bytes 3145736 | tf_op jit(solution)/shard_map/ppermute | solution.py:556
  215.2 48.5 %collective-permute-start.23 = (bf16[256,2048]{1,0:T(8,128)(2,1)}, bf16[256,2048]{1,0:T(8,128)(2,1)}, u32[]{:S(2)}, u32[]{:S(2)}) collective-permute-start(bf16[256,2048]{1,0:T(8,128)(2,1)} %refs_0_.1), channel_id=1, source_target_pairs={{0,2},{2,0},{4,6},{6,4},{8,10},{10,8},{12,14},{14,12},{16,18},{18,... | collective-permute-start | bytes 3145736 | tf_op jit(solution)/shard_map/ppermute | solution.py:550
  215.9 45.5 %collective-permute-start.21 = (bf16[256,2048]{1,0:T(8,128)(2,1)}, bf16[256,2048]{1,0:T(8,128)(2,1)}, u32[]{:S(2)}, u32[]{:S(2)}) collective-permute-start(bf16[256,2048]{1,0:T(8,128)(2,1)} %refs_0_.1), channel_id=1, source_target_pairs={{0,4},{2,6},{4,0},{6,2},{8,12},{10,14},{12,8},{14,10},{16,20},{18,... | collective-permute-start | bytes 3145736 | tf_op jit(solution)/shard_map/ppermute | solution.py:553
  216.3 44.6 %collective-permute-start.20 = (bf16[256,2048]{1,0:T(8,128)(2,1)}, bf16[256,2048]{1,0:T(8,128)(2,1)}, u32[]{:S(2)}, u32[]{:S(2)}) collective-permute-start(bf16[256,2048]{1,0:T(8,128)(2,1)} %refs_0_.1), channel_id=1, source_target_pairs={{0,1},{1,0},{2,3},{3,2},{4,5},{5,4},{6,7},{7,6},{8,9},{9,8},{10,11... | collective-permute-start | bytes 3145736 | tf_op jit(solution)/shard_map/ppermute | solution.py:556
  254.8 28.5 %collective-permute-start.13 = (bf16[256,2048]{1,0:T(8,128)(2,1)}, bf16[256,2048]{1,0:T(8,128)(2,1)}, u32[]{:S(2)}, u32[]{:S(2)}) collective-permute-start(bf16[256,2048]{1,0:T(8,128)(2,1)} %multiply_convert_fusion.2.refs_0_.refs_8_), channel_id=1, source_target_pairs={{0,1},{1,0},{2,3},{3,2},{4,5},{5,4},{6,7},{7,6},{8,9},{9,8},{10,11... | collective-permute-start | bytes 3145736 | tf_op jit(solution)/shard_map/ppermute | solution.py:556
  260.7 245.3 %reduce-scatter.6.cloned.1.call-start = ((), (), s32[]{:S(2)}) async-start(), calls=%async_computation.9 | async-start | bytes 3604480 | tf_op jit(solution)/shard_map/reduce_scatter | solution.py:565
  260.9 23.0 %collective-permute-start.22 = (bf16[256,2048]{1,0:T(8,128)(2,1)}, bf16[256,2048]{1,0:T(8,128)(2,1)S(1)}, u32[]{:S(2)}, u32[]{:S(2)}) collective-permute-start(bf16[256,2048]{1,0:T(8,128)(2,1)} %collective-permute-done.20.refs_9_.refs_1_), channel_id=1, source_target_pairs={{0,4},{2,6},{4,0},{6,2},{8,12},{10,14},{12,8},{14,10},{16,20},{18,... | collective-permute-start | bytes 3145736 | tf_op jit(solution)/shard_map/ppermute | solution.py:553
  261.4 28.0 %collective-permute-start.25 = (bf16[256,2048]{1,0:T(8,128)(2,1)}, bf16[256,2048]{1,0:T(8,128)(2,1)S(1)}, u32[]{:S(2)}, u32[]{:S(2)}) collective-permute-start(bf16[256,2048]{1,0:T(8,128)(2,1)} %collective-permute-done.21.refs_10_.refs_2_), channel_id=1, source_target_pairs={{0,2},{2,0},{4,6},{6,4},{8,10},{10,8},{12,14},{14,12},{16,18},{18,... | collective-permute-start | bytes 3145736 | tf_op jit(solution)/shard_map/ppermute | solution.py:550
  263.7 25.7 %collective-permute-start.24 = (bf16[256,2048]{1,0:T(8,128)(2,1)}, bf16[256,2048]{1,0:T(8,128)(2,1)}, u32[]{:S(2)}, u32[]{:S(2)}) collective-permute-start(bf16[256,2048]{1,0:T(8,128)(2,1)} %collective-permute-done.20.refs_9_.refs_1_), channel_id=1, source_target_pairs={{0,2},{2,0},{4,6},{6,4},{8,10},{10,8},{12,14},{14,12},{16,18},{18,... | collective-permute-start | bytes 3145736 | tf_op jit(solution)/shard_map/ppermute | solution.py:550
  263.8 42.5 %collective-permute-start.14 = (bf16[256,2048]{1,0:T(8,128)(2,1)}, bf16[256,2048]{1,0:T(8,128)(2,1)}, u32[]{:S(2)}, u32[]{:S(2)}) collective-permute-start(bf16[256,2048]{1,0:T(8,128)(2,1)} %multiply_convert_fusion.2.refs_0_.refs_8_), channel_id=1, source_target_pairs={{0,4},{2,6},{4,0},{6,2},{8,12},{10,14},{12,8},{14,10},{16,20},{18,... | collective-permute-start | bytes 3145736 | tf_op jit(solution)/shard_map/ppermute | solution.py:553
  283.4 45.3 %collective-permute-start.15 = (bf16[256,2048]{1,0:T(8,128)(2,1)}, bf16[256,2048]{1,0:T(8,128)(2,1)}, u32[]{:S(2)}, u32[]{:S(2)}) collective-permute-start(bf16[256,2048]{1,0:T(8,128)(2,1)} %collective-permute-done.13.refs_1_.refs_9_), channel_id=1, source_target_pairs={{0,4},{2,6},{4,0},{6,2},{8,12},{10,14},{12,8},{14,10},{16,20},{18,... | collective-permute-start | bytes 3145736 | tf_op jit(solution)/shard_map/ppermute | solution.py:553
  283.9 50.5 %copy-start.55 = (bf16[256,2048]{1,0:T(8,128)(2,1)}, bf16[256,2048]{1,0:T(8,128)(2,1)S(1)}, u32[]{:S(2)}) copy-start(bf16[256,2048]{1,0:T(8,128)(2,1)S(1)} %collective-permute-done.22.refs_11_.refs_3_) | copy-start | bytes 3145732
  283.9 48.8 %collective-permute-start.26 = (bf16[256,2048]{1,0:T(8,128)(2,1)S(1)}, bf16[256,2048]{1,0:T(8,128)(2,1)}, u32[]{:S(2)}, u32[]{:S(2)}) collective-permute-start(bf16[256,2048]{1,0:T(8,128)(2,1)S(1)} %collective-permute-done.22.refs_11_.refs_3_), channel_id=1, source_target_pairs={{0,2},{2,0},{4,6},{6,4},{8,10},{10,8},{12,14},{14,12},{16,18},{18,... | collective-permute-start | bytes 3145736 | tf_op jit(solution)/shard_map/ppermute | solution.py:550
  289.3 45.0 %copy-start.56 = (bf16[256,2048]{1,0:T(8,128)(2,1)}, bf16[256,2048]{1,0:T(8,128)(2,1)S(1)}, u32[]{:S(2)}) copy-start(bf16[256,2048]{1,0:T(8,128)(2,1)S(1)} %collective-permute-done.25.refs_14_.refs_6_) | copy-start | bytes 3145732
  289.3 43.4 %collective-permute-start.16 = (bf16[256,2048]{1,0:T(8,128)(2,1)}, bf16[256,2048]{1,0:T(8,128)(2,1)}, u32[]{:S(2)}, u32[]{:S(2)}) collective-permute-start(bf16[256,2048]{1,0:T(8,128)(2,1)} %multiply_convert_fusion.2.refs_0_.refs_8_), channel_id=1, source_target_pairs={{0,2},{2,0},{4,6},{6,4},{8,10},{10,8},{12,14},{14,12},{16,18},{18,... | collective-permute-start | bytes 3145736 | tf_op jit(solution)/shard_map/ppermute | solution.py:550
  289.4 43.3 %collective-permute-start.17 = (bf16[256,2048]{1,0:T(8,128)(2,1)}, bf16[256,2048]{1,0:T(8,128)(2,1)}, u32[]{:S(2)}, u32[]{:S(2)}) collective-permute-start(bf16[256,2048]{1,0:T(8,128)(2,1)} %collective-permute-done.13.refs_1_.refs_9_), channel_id=1, source_target_pairs={{0,2},{2,0},{4,6},{6,4},{8,10},{10,8},{12,14},{14,12},{16,18},{18,... | collective-permute-start | bytes 3145736 | tf_op jit(solution)/shard_map/ppermute | solution.py:550
  306.2 26.5 %collective-permute-start.18 = (bf16[256,2048]{1,0:T(8,128)(2,1)}, bf16[256,2048]{1,0:T(8,128)(2,1)}, u32[]{:S(2)}, u32[]{:S(2)}) collective-permute-start(bf16[256,2048]{1,0:T(8,128)(2,1)} %collective-permute-done.14.refs_2_.refs_10_), channel_id=1, source_target_pairs={{0,2},{2,0},{4,6},{6,4},{8,10},{10,8},{12,14},{14,12},{16,18},{18,... | collective-permute-start | bytes 3145736 | tf_op jit(solution)/shard_map/ppermute | solution.py:550
  328.7 5.7 collective-permute-start.19
  363.4 303.2 %reduce-scatter.8.cloned.1.call-start = ((), (), s32[]{:S(2)}) async-start(), calls=%async_computation.10 | async-start | bytes 7208960 | tf_op jit(solution)/shard_map/reduce_scatter | solution.py:565
  506.0 236.8 %reduce-scatter.10.cloned.1.call-start = ((), (), s32[]{:S(2)}) async-start(), calls=%async_computation.11 | async-start | bytes 2621440 | tf_op jit(solution)/shard_map/reduce_scatter | solution.py:565
  547.3 34.3 %collective-permute-start.32 = (bf16[512,1536]{1,0:T(8,128)(2,1)}, bf16[512,1536]{1,0:T(8,128)(2,1)}, u32[]{:S(2)}, u32[]{:S(2)}) collective-permute-start(bf16[512,1536]{1,0:T(8,128)(2,1)} %slice.481), channel_id=1, source_target_pairs={{0,2},{2,0},{4,6},{6,4},{8,10},{10,8},{12,14},{14,12},{16,18},{18,... | collective-permute-start | bytes 4718600 | tf_op jit(solution)/shard_map/ppermute | solution.py:550
  555.9 72.5 %collective-permute-start.38 = (bf16[1024,1024]{1,0:T(8,128)(2,1)}, bf16[1024,1024]{1,0:T(8,128)(2,1)}, u32[]{:S(2)}, u32[]{:S(2)}) collective-permute-start(bf16[1024,1024]{1,0:T(8,128)(2,1)} %convolution_convert_fusion), channel_id=1, source_target_pairs={{0,4},{2,6},{4,0},{6,2},{8,12},{10,14},{12,8},{14,10},{16,20},{18,... | collective-permute-start | bytes 6291464 | tf_op jit(solution)/shard_map/ppermute | solution.py:553
  563.6 62.2 %collective-permute-start.37 = (bf16[4,128,1024]{2,1,0:T(8,128)(2,1)}, bf16[4,128,1024]{2,1,0:T(8,128)(2,1)}, u32[]{:S(2)}, u32[]{:S(2)}) collective-permute-start(bf16[4,128,1024]{2,1,0:T(8,128)(2,1)} %dynamic-slice_bitcast_fusion.2), channel_id=1, source_target_pairs={{0,4},{2,6},{4,0},{6,2},{8,12},{10,14},{12,8},{14,10},{16,20},{18,... | collective-permute-start | bytes 3145736 | tf_op jit(solution)/shard_map/ppermute | solution.py:553
  580.8 86.0 %collective-permute-start.29 = (bf16[1024,2048]{1,0:T(8,128)(2,1)}, bf16[1024,2048]{1,0:T(8,128)(2,1)}, u32[]{:S(2)}, u32[]{:S(2)}) collective-permute-start(bf16[1024,2048]{1,0:T(8,128)(2,1)} %slice.325), channel_id=1, source_target_pairs={{0,2},{2,0},{4,6},{6,4},{8,10},{10,8},{12,14},{14,12},{16,18},{18,... | collective-permute-start | bytes 12582920 | tf_op jit(solution)/shard_map/ppermute | solution.py:550
  581.6 46.8 %copy-start.59 = (bf16[1024,2048]{1,0:T(8,128)(2,1)S(1)}, bf16[1024,2048]{1,0:T(8,128)(2,1)}, u32[]{:S(2)}) copy-start(bf16[1024,2048]{1,0:T(8,128)(2,1)} %get-tuple-element.29) | copy-start | bytes 12582916
  584.5 43.9 %copy-start.12 = (f32[512,1536]{1,0:T(8,128)}, f32[512,1536]{1,0:T(8,128)S(1)}, u32[]{:S(2)}) copy-start(f32[512,1536]{1,0:T(8,128)S(1)} %slice_add_fusion.1) | copy-start | bytes 9437188
  584.5 43.9 %copy-start.29 = (bf16[128,8,4,256]{3,1,2,0:T(8,128)(2,1)S(1)}, bf16[128,8,4,256]{3,1,2,0:T(8,128)(2,1)}, u32[]{:S(2)}) copy-start(bf16[128,8,4,256]{3,1,2,0:T(8,128)(2,1)} %copy-done.27) | copy-start | bytes 6291460
  585.5 48.3 %collective-permute-start.33 = (bf16[256,1536]{1,0:T(8,128)(2,1)}, bf16[256,1536]{1,0:T(8,128)(2,1)}, u32[]{:S(2)}, u32[]{:S(2)}) collective-permute-start(bf16[256,1536]{1,0:T(8,128)(2,1)} %slice.484), channel_id=1, source_target_pairs={{0,1},{1,0},{2,3},{3,2},{4,5},{5,4},{6,7},{7,6},{8,9},{9,8},{10,11... | collective-permute-start | bytes 2359304 | tf_op jit(solution)/shard_map/ppermute | solution.py:556
  639.9 18.1 %collective-permute-start.34 = (bf16[256,1536]{1,0:T(8,128)(2,1)S(1)}, bf16[256,1536]{1,0:T(8,128)(2,1)S(1)}, u32[]{:S(2)}, u32[]{:S(2)}) collective-permute-start(bf16[256,1536]{1,0:T(8,128)(2,1)S(1)} %pad_maximum_fusion.14), channel_id=1, source_target_pairs={{0,1},{1,0},{2,3},{3,2},{4,5},{5,4},{6,7},{7,6},{8,9},{9,8},{10,11... | collective-permute-start | bytes 2359304 | tf_op jit(solution)/shard_map/ppermute | solution.py:556
  659.3 15.4 %collective-permute-start.35 = (bf16[512,1536]{1,0:T(8,128)(2,1)}, bf16[512,1536]{1,0:T(8,128)(2,1)}, u32[]{:S(2)}, u32[]{:S(2)}) collective-permute-start(bf16[512,1536]{1,0:T(8,128)(2,1)} %pad_maximum_fusion.11), channel_id=1, source_target_pairs={{0,2},{2,0},{4,6},{6,4},{8,10},{10,8},{12,14},{14,12},{16,18},{18,... | collective-permute-start | bytes 4718600 | tf_op jit(solution)/shard_map/ppermute | solution.py:550
  666.7 104.5 %reduce-scatter.12.cloned.1.call-start = ((), (), s32[]{:S(2)}) async-start(), calls=%async_computation.12 | async-start | bytes 1310720 | tf_op jit(solution)/shard_map/reduce_scatter | solution.py:565
  673.8 75.8 %collective-permute-start.30 = (bf16[512,2048]{1,0:T(8,128)(2,1)}, bf16[512,2048]{1,0:T(8,128)(2,1)}, u32[]{:S(2)}, u32[]{:S(2)}) collective-permute-start(bf16[512,2048]{1,0:T(8,128)(2,1)} %slice.480), channel_id=1, source_target_pairs={{0,4},{2,6},{4,0},{6,2},{8,12},{10,14},{12,8},{14,10},{16,20},{18,... | collective-permute-start | bytes 6291464 | tf_op jit(solution)/shard_map/ppermute | solution.py:553
  686.3 54.0 %collective-permute-start.36 = (bf16[4,144,768]{2,1,0:T(8,128)(2,1)}, bf16[4,144,768]{2,1,0:T(8,128)(2,1)}, u32[]{:S(2)}, u32[]{:S(2)}) collective-permute-start(bf16[4,144,768]{2,1,0:T(8,128)(2,1)} %fusion.61), channel_id=1, source_target_pairs={{0,4},{2,6},{4,0},{6,2},{8,12},{10,14},{12,8},{14,10},{16,20},{18,... | collective-permute-start | bytes 2654216 | tf_op jit(solution)/shard_map/ppermute | solution.py:553
  697.5 45.2 %collective-permute-start.45 = (bf16[1,704,2,128]{3,1,2,0:T(8,128)(2,1)S(1)}, bf16[1,704,2,128]{3,1,2,0:T(8,128)(2,1)S(1)}, u32[]{:S(2)}, u32[]{:S(2)}) collective-permute-start(bf16[1,704,2,128]{3,1,2,0:T(8,128)(2,1)S(1)} %bitcast.307), channel_id=1, source_target_pairs={{0,2},{2,0},{4,6},{6,4},{8,10},{10,8},{12,14},{14,12},{16,18},{18,... | collective-permute-start | bytes 1081352 | tf_op jit(solution)/shard_map/ppermute | solution.py:550
  698.1 42.3 %copy-start.10 = (f32[2,4,144,768]{3,2,1,0:T(8,128)S(1)}, f32[2,4,144,768]{3,2,1,0:T(8,128)}, u32[]{:S(2)}) copy-start(f32[2,4,144,768]{3,2,1,0:T(8,128)} %copy-done.9) | copy-start | bytes 10616836
  742.9 53.9 %reduce-scatter.14.cloned.1.call-start = ((), (), s32[]{:S(2)}) async-start(), calls=%async_computation.13 | async-start | bytes 1105920 | tf_op jit(solution)/shard_map/reduce_scatter | solution.py:565
  743.7 12.0 %collective-permute-start.46 = (bf16[1,2,704,128]{3,2,1,0:T(8,128)(2,1)}, bf16[1,2,704,128]{3,2,1,0:T(8,128)(2,1)}, u32[]{:S(2)}, u32[]{:S(2)}) collective-permute-start(bf16[1,2,704,128]{3,2,1,0:T(8,128)(2,1)} %get-tuple-element.149), channel_id=1, source_target_pairs={{0,4},{2,6},{4,0},{6,2},{8,12},{10,14},{12,8},{14,10},{16,20},{18,... | collective-permute-start | bytes 1081352 | tf_op jit(solution)/shard_map/ppermute | solution.py:553
  748.4 8.6 %collective-permute-start.43 = (bf16[2,704,2,128]{3,1,2,0:T(8,128)(2,1)S(1)}, bf16[2,704,2,128]{3,1,2,0:T(8,128)(2,1)S(1)}, u32[]{:S(2)}, u32[]{:S(2)}) collective-permute-start(bf16[2,704,2,128]{3,1,2,0:T(8,128)(2,1)S(1)} %bitcast.305), channel_id=1, source_target_pairs={{0,2},{2,0},{4,6},{6,4},{8,10},{10,8},{12,14},{14,12},{16,18},{18,... | collective-permute-start | bytes 2162696 | tf_op jit(solution)/shard_map/ppermute | solution.py:550
  754.5 25.1 %collective-permute-start.31 = (bf16[256,2048]{1,0:T(8,128)(2,1)}, bf16[256,2048]{1,0:T(8,128)(2,1)}, u32[]{:S(2)}, u32[]{:S(2)}) collective-permute-start(bf16[256,2048]{1,0:T(8,128)(2,1)} %slice.482), channel_id=1, source_target_pairs={{0,1},{1,0},{2,3},{3,2},{4,5},{5,4},{6,7},{7,6},{8,9},{9,8},{10,11... | collective-permute-start | bytes 3145736 | tf_op jit(solution)/shard_map/ppermute | solution.py:556
  758.3 24.6 %collective-permute-start.44 = (bf16[2,2,704,128]{3,2,1,0:T(8,128)(2,1)}, bf16[2,2,704,128]{3,2,1,0:T(8,128)(2,1)}, u32[]{:S(2)}, u32[]{:S(2)}) collective-permute-start(bf16[2,2,704,128]{3,2,1,0:T(8,128)(2,1)} %get-tuple-element.143), channel_id=1, source_target_pairs={{0,4},{2,6},{4,0},{6,2},{8,12},{10,14},{12,8},{14,10},{16,20},{18,... | collective-permute-start | bytes 2162696 | tf_op jit(solution)/shard_map/ppermute | solution.py:553
  785.4 4.2 collective-permute-start.42
  789.5 3.3 collective-permute-start.41
  797.7 6.4 collective-permute-start.39
  804.8 4.0 collective-permute-start.40
  (55 other events, 266.3 us)
Sparse Core Ops, SparseCore 0:
  55.7 29.4 all-gather.4
  87.4 45.1 all-gather.6
  134.7 105.8 all-gather.8
  260.8 60.2 all-gather.10
  363.6 56.2 reduce-scatter.5
  506.2 102.9 reduce-scatter.7
  666.8 44.2 reduce-scatter.9
  743.0 28.1 reduce-scatter.11
  773.6 23.2 reduce-scatter.13

commit v3 on v2

--- a/solution.py
+++ b/solution.py
@@ -32,23 +32,6 @@
 def norm_back(grad_out, unit_vals, inverse, gain_vals):
     scaled = grad_out * gain_vals
     return inverse * (scaled - unit_vals * jnp.mean(scaled * unit_vals, axis=-1, keepdims=True))
-
-
-def rotate(values, cos_tab, sin_tab):
-    half_dim = values.shape[-1] // 2
-    first_half = values[..., :half_dim]
-    second_half = values[..., half_dim:]
-    return jnp.concatenate(
-        [
-            first_half * cos_tab - second_half * sin_tab,
-            second_half * cos_tab + first_half * sin_tab,
-        ],
-        axis=-1,
-    )
-
-
-def unrotate(values, cos_tab, sin_tab):
-    return rotate(values, cos_tab, -sin_tab)
 
 
 def rope_tables(positions, head_dim):
@@ -113,23 +96,30 @@
     return pl.ds(pl.multiple_of(index * size, size), size)
 
 
-def ffn_first(normed, grads, gate_up):
-    count = len(normed)
-    rows, width = normed[0].shape
+def split_rows(ref, count):
+    rows = ref.shape[0] // count
+    return [ref.at[pl.ds(j * rows, rows)] for j in range(count)]
+
+
+def ffn_first(normed, grads, weights):
+    count = len(grads)
+    rows, width = grads[0].shape
     total = rows * count
-    lines, double, cols = gate_up.shape
-    hid = double // 2
+    lines, triple, cols = weights.shape
+    hid = triple // 3
+    double = 2 * hid
 
     def kernel(*refs):
-        normed_refs, grad_refs = refs[:count], refs[count : 2 * count]
-        weight_ref, hid_ref, a_ref, s_ref, down_ref = refs[2 * count : 2 * count + 5]
+        grad_refs = refs[:count]
+        normed_ref, weight_ref, hid_ref, a_ref, s_ref, down_ref = refs[count : count + 6]
+        normed_refs = split_rows(normed_ref, count)
         n_s, g_s, w_s, hid_s, a_s, s_s, down_s, n_sem, g_sem, w_sem, o_sem, d_sem = refs[
-            2 * count + 5 :
+            count + 6 :
         ]
-        weights = join_lines(weight_ref, w_s, w_sem)
+        parts = join_lines(weight_ref.at[:, pl.ds(0, double)], w_s, w_sem)
         stack_rows(normed_refs, n_s, n_sem)
         grad_copies = stack_rows(grad_refs, g_s, g_sem)
-        wait_all(weights)
+        wait_all(parts)
 
         @pl.loop(0, count)
         def _(i):
@@ -163,7 +153,7 @@
 
     acts = jax.ShapeDtypeStruct((hid, total), BF)
     out_shape = (acts, acts, acts, jax.ShapeDtypeStruct((lines, hid, cols), BF))
-    args = (*normed, *grads, gate_up)
+    args = (*grads, normed, weights)
     return pl.pallas_call(
         kernel,
         out_shape=out_shape,
@@ -189,49 +179,6 @@
     )(*args)
 
 
-def ffn_out_part(hidden, down, rows):
-    hid, total = hidden.shape
-    lines, _, cols = down.shape
-    width = lines * cols
-    count = total // rows
-
-    def kernel(hid_ref, down_ref, out_ref, h_s, d_s, out_s, h_sem, d_sem, o_sem):
-        copy = pltpu.make_async_copy(hid_ref, h_s, h_sem)
-        copy.start()
-        wait_all(join_lines(down_ref, d_s, d_sem))
-        copy.wait()
-
-        @pl.loop(0, count)
-        def _(i):
-            at = tile(i, rows)
-            out_s[at, :] = matmul_tn(h_s[:, at], d_s[...]).astype(BF)
-            pltpu.make_async_copy(out_s.at[at], out_ref.at[at], o_sem.at[i]).start()
-
-        @pl.loop(0, count)
-        def _(i):
-            at = tile(i, rows)
-            pltpu.make_async_copy(out_s.at[at], out_ref.at[at], o_sem.at[i]).wait()
-
-    out_shape = jax.ShapeDtypeStruct((total, width), BF)
-    return pl.pallas_call(
-        kernel,
-        out_shape=out_shape,
-        in_specs=[ANY] * 2,
-        out_specs=ANY,
-        scratch_shapes=[
-            pltpu.VMEM((hid, total), BF),
-            pltpu.VMEM((hid, width), BF),
-            pltpu.VMEM((total, width), BF),
-            pltpu.SemaphoreType.DMA,
-            pltpu.SemaphoreType.DMA((lines,)),
-            pltpu.SemaphoreType.DMA((count,)),
-        ],
-        compiler_params=kernel_params(),
-        cost_estimate=cost(2 * hid * total * width, (hidden, down, out_shape)),
-        name="ffn_out_part",
-    )(hidden, down)
-
-
 MESH = pl.DeviceIdType.MESH
 
 
@@ -263,19 +210,25 @@
     )
 
 
-def ffn_back(grads, down, gate_up, a_fac, s_fac, normed, residual, gain):
+def ffn_back(grads, weights, hidden, a_fac, s_fac, normed, residual, gain):
     count = len(grads)
     rows, width = grads[0].shape
-    lines, double, cols = gate_up.shape
-    hid = double // 2
+    lines, triple, cols = weights.shape
+    hid = triple // 3
+    double = 2 * hid
     block = cols // 2
     near = 4 * rows
     total = count * rows
 
     def kernel(*refs):
-        grad_refs, normed_refs = refs[:count], refs[count : 2 * count]
-        down_in, weight_ref, a_ref, s_ref, resid_ref, gain_ref = refs[2 * count : 2 * count + 6]
-        grad_out, dres_out, dgain_out, attn_out = refs[2 * count + 6 : 2 * count + 10]
+        grad_refs = refs[:count]
+        normed_ref, all_ref, hid_ref, a_ref, s_ref, resid_ref, gain_ref = refs[count : count + 7]
+        grad_out, dres_out, dgain_out, attn_out, near_out, away_out, away_in = refs[
+            count + 7 : count + 14
+        ]
+        normed_refs = split_rows(normed_ref, count)
+        weight_ref = all_ref.at[:, pl.ds(0, double)]
+        down_in = all_ref.at[:, pl.ds(double, hid)]
         (
             rows_s,
             d_s,
@@ -310,7 +263,11 @@
             last_send,
             last_recv,
             out_sem,
-        ) = refs[2 * count + 10 :]
+            part_sem,
+            away_send,
+            away_recv,
+            free_sem,
+        ) = refs[count + 14 :]
         across_core, across_side, across_half = peers()
         side = (lax.axis_index("dp") // 2) % 2
         downs = join_lines(down_in, d_s, d_sem)
@@ -327,7 +284,7 @@
         ]
         for copy in factors:
             copy.start()
-        weights = join_lines(weight_ref, w_s, w_sem)
+        joins = join_lines(weight_ref, w_s, w_sem)
         res_copy = pltpu.make_async_copy(resid_ref, res_s, res_sem)
         res_copy.start()
         own_copy = pltpu.make_async_copy(grad_refs[0], own_s, own_sem)
@@ -361,7 +318,7 @@
         def _(i):
             act_block(i)
 
-        wait_all(weights)
+        wait_all(joins)
 
         @pl.loop(0, lines)
         def _(j):
@@ -373,6 +330,8 @@
             act_block(i)
 
         reload = stack_rows(normed_refs, rows_s, rows_sem)
+        hid_copy = pltpu.make_async_copy(hid_ref, a_s, f_sem.at[0])
+        hid_copy.start()
 
         @pl.loop(0, lines)
         def _(j):
@@ -383,6 +342,7 @@
             side_s[j] = part[2 * rows :].astype(BF)
             to_side(j).start()
 
+        pl.semaphore_signal(free_sem, inc=1, device_id=across_core, device_id_type=MESH)
         wait_all(reload)
 
         def grad_copy(j):
@@ -396,6 +356,39 @@
 
             grad_s[j % 2] = matmul(act_s[...], rows_s[:, tile(j, cols)]).astype(BF)
             grad_copy(j).start()
+
+        hid_copy.wait()
+        pl.semaphore_wait(free_sem, 1)
+
+        @pl.loop(0, lines)
+        def _(j):
+            to_core(j).wait_send()
+            far_s[j] = matmul_tn(a_s[:, pl.ds(near, near)], d_s[:, tile(j, cols)]).astype(BF)
+            to_core(j).start()
+
+        for j in range(max(lines - 2, 0), lines):
+            grad_copy(j).wait()
+
+        def part_copies(j):
+            held = grad_s.at[j % 2]
+            return [
+                pltpu.make_async_copy(
+                    held.at[pl.ds(k * 2 * rows, 2 * rows)], ref.at[j], part_sem.at[k, j % 2]
+                )
+                for k, ref in enumerate((near_out, away_out))
+            ]
+
+        @pl.loop(0, lines)
+        def _(j):
+            @pl.when(j >= 2)
+            def _():
+                wait_all(part_copies(j - 2))
+
+            part = matmul_tn(a_s[:, pl.ds(0, near)], d_s[:, tile(j, cols)])
+            to_core(j).wait_recv()
+            grad_s[j % 2, pl.ds(0, near), :] = (part + core_in[j].astype(F32)).astype(BF)
+            for copy in part_copies(j):
+                copy.start()
 
         @pl.loop(0, lines)
         def _(j):
@@ -404,6 +397,18 @@
             acc[j] = part
             half_s[j] = part[rows:].astype(BF)
             to_half(j).start()
+
+        for j in range(max(lines - 2, 0), lines):
+            wait_all(part_copies(j))
+
+        def to_side_out(j):
+            return remote(
+                away_out.at[j], away_in.at[j], away_send.at[j], away_recv.at[j], across_side
+            )
+
+        @pl.loop(0, lines)
+        def _(j):
+            to_side_out(j).start()
 
         res_copy.wait()
         own_copy.wait()
@@ -464,13 +469,11 @@
             copy.start()
         sends[0].wait_recv()
         sends[2].start()
-        for j in range(max(lines - 2, 0), lines):
-            grad_copy(j).wait()
-
         @pl.loop(0, lines)
         def _(j):
             to_core(j).wait_send()
             to_side(j).wait_send()
+            to_side_out(j).wait()
             to_half(j).wait_send()
 
         sends[0].wait_send()
@@ -483,15 +486,18 @@
         jax.ShapeDtypeStruct((rows, width), F32),
         jax.ShapeDtypeStruct((1, width), F32),
         jax.ShapeDtypeStruct((4 * rows, width), BF),
+        jax.ShapeDtypeStruct((lines, 2 * rows, cols), BF),
+        jax.ShapeDtypeStruct((lines, 2 * rows, cols), BF),
+        jax.ShapeDtypeStruct((lines, 2 * rows, cols), BF),
     )
-    args = (*grads, *normed, down, gate_up, a_fac, s_fac, residual, gain)
+    args = (*grads, normed, weights, hidden, a_fac, s_fac, residual, gain)
     vmem = pl.BlockSpec(memory_space=pltpu.VMEM)
     dma = pltpu.SemaphoreType.DMA
     return pl.pallas_call(
         kernel,
         out_shape=out_shape,
         in_specs=[ANY] * (len(args) - 1) + [vmem],
-        out_specs=(ANY, ANY, vmem, ANY),
+        out_specs=(ANY, ANY, vmem, ANY, ANY, ANY, ANY),
         scratch_shapes=[
             pltpu.VMEM((total, width), BF),
             pltpu.VMEM((hid, width), BF),
@@ -526,12 +532,863 @@
             dma((3,)),
             dma((3,)),
             dma((2,)),
+            dma((2, 2)),
+            dma((lines,)),
+            dma((lines,)),
+            pltpu.SemaphoreType.REGULAR,
         ],
         compiler_params=pltpu.CompilerParams(
             vmem_limit_bytes=vmem_bytes, collective_id=0, has_side_effects=True
         ),
         cost_estimate=cost(10 * hid * total * width, args + out_shape),
         name="ffn_back",
+    )(*args)
+
+
+def spin(first, second, cos_vals, sin_vals):
+    return first * cos_vals - second * sin_vals, second * cos_vals + first * sin_vals
+
+
+def attn_first(
+    x_parts,
+    qkv_set,
+    q_up,
+    out_mine,
+    bias,
+    cos_tab,
+    sin_tab,
+    gain_one,
+    gain_q,
+    gain_two,
+    shard,
+    lines,
+):
+    rows, width = x_parts[0].shape
+    total = 4 * rows
+    group = 2 * rows
+    edge, feats = out_mine.shape
+    rank = q_up.shape[0]
+    wide = qkv_set.shape[1]
+    head_dim = (wide - rank) // 2
+    half_dim = head_dim // 2
+    heads = feats // head_dim
+    block = edge // lines
+    scale = 1.0 / math.sqrt(head_dim)
+    step = 256
+    cols = 512
+    tiles = width // cols
+    sends_y = edge // step
+
+    def kernel(
+        x0_ref,
+        x1_ref,
+        x2_ref,
+        x3_ref,
+        qkv_ref,
+        up_ref,
+        mine_ref,
+        bias_ref,
+        cos_ref,
+        sin_ref,
+        gain_ref,
+        gain_q_ref,
+        gain_two_ref,
+        q_out,
+        k_out,
+        v_out,
+        mixed_out,
+        lat_n_out,
+        lat_out,
+        n_out,
+        theirs_out,
+        res_out,
+        norm_out,
+        x_s,
+        n_s,
+        qkv_s,
+        w_s,
+        up_s,
+        mixed_s,
+        q_s,
+        k_s,
+        v_s,
+        bias_s,
+        cos_s,
+        sin_s,
+        lat_s,
+        lat_n_s,
+        nc_s,
+        far_s,
+        core_in,
+        half_s,
+        half_in,
+        acc,
+        res_s,
+        own_s,
+        load_sem,
+        theirs_send,
+        theirs_recv,
+        core_send,
+        core_recv,
+        half_send,
+        half_recv,
+        last_send,
+        last_recv,
+        out_sem,
+    ):
+        across_core, across_side, across_half = peers()
+        place = lax.axis_index("dp")
+        core, side = place % 2, (place // 2) % 2
+        pairs = [
+            (ref, x_s.at[pl.ds(j * rows, rows)])
+            for j, ref in enumerate((x0_ref, x1_ref, x2_ref, x3_ref))
+        ]
+        pairs += [
+            (qkv_ref, qkv_s),
+            (cos_ref, cos_s),
+            (sin_ref, sin_s),
+            (up_ref, up_s),
+            (bias_ref, bias_s),
+            (mine_ref, w_s.at[pl.ds(0, edge)]),
+        ]
+        loads = [
+            pltpu.make_async_copy(src, dst, load_sem.at[j]) for j, (src, dst) in enumerate(pairs)
+        ]
+        for copy in loads:
+            copy.start()
+        greet((across_core, across_side, across_half))
+
+        def theirs_copy(j):
+            return remote(
+                mine_ref.at[tile(j, step)],
+                w_s.at[pl.ds(pl.multiple_of(edge + j * step, step), step)],
+                theirs_send.at[j],
+                theirs_recv.at[j],
+                across_side,
+            )
+
+        @pl.loop(0, sends_y)
+        def _(j):
+            theirs_copy(j).start()
+
+        wait_all(loads[:4])
+
+        @pl.loop(0, 4)
+        def _(i):
+            at = tile(i, rows)
+            x_f = x_s[at, :].astype(F32)
+            low = (x_f * inv_rms(x_f) * gain_ref[...]).astype(BF)
+            n_s[at, :] = low
+            for j in range(2 * lines):
+                first = low[:, (2 * j) * shard : (2 * j + 1) * shard].astype(F32)
+                second = low[:, (2 * j + 1) * shard : (2 * j + 2) * shard].astype(F32)
+                nc_s[at, pl.ds(j * shard, shard)] = jnp.where(core == 0, first, second).astype(BF)
+
+        wait_all(loads[4:7])
+
+        @pl.loop(0, rank // step)
+        def _(j):
+            at = tile(j, step)
+            lat_s[:, at] = matmul(n_s[...], qkv_s[:, at])
+
+        key = matmul(n_s[...], qkv_s[:, pl.ds(rank, head_dim)])
+        turned = spin(key[:, :half_dim], key[:, half_dim:], cos_s[...], sin_s[...])
+        k_s[...] = jnp.concatenate(turned, axis=1).astype(BF)
+        v_s[...] = matmul(n_s[...], qkv_s[:, pl.ds(rank + head_dim, head_dim)]).astype(BF)
+
+        @pl.loop(0, 4)
+        def _(i):
+            at = tile(i, rows)
+            latent = lat_s[at, :]
+            lat_n_s[at, :] = (latent * inv_rms(latent) * gain_q_ref[...]).astype(BF)
+
+        wait_all(loads[7:9])
+
+        @pl.loop(0, heads)
+        def _(h):
+            lanes = tile(h, head_dim)
+            query = matmul(lat_n_s[...], up_s[:, lanes])
+            turned = spin(query[:, :half_dim], query[:, half_dim:], cos_s[...], sin_s[...])
+            q_s[:, lanes] = jnp.concatenate(turned, axis=1).astype(BF)
+
+        outs = [
+            pltpu.make_async_copy(src, dst, out_sem.at[j])
+            for j, (src, dst) in enumerate(
+                (
+                    (q_s, q_out),
+                    (k_s, k_out),
+                    (v_s, v_out),
+                    (lat_n_s, lat_n_out),
+                    (lat_s.at[pl.ds(0, rows)], lat_out),
+                    (nc_s, n_out),
+                )
+            )
+        ]
+        for copy in outs:
+            copy.start()
+
+        @pl.loop(0, 2 * heads)
+        def _(i):
+            at = tile(i // heads, group)
+            lanes = tile(i % heads, head_dim)
+            scores = matmul_nt(q_s[at, lanes], k_s[at, :]) * scale + bias_s[i // heads].astype(F32)
+            expd = jnp.exp(scores - jnp.max(scores, axis=-1, keepdims=True))
+            probs = (expd / jnp.sum(expd, axis=-1, keepdims=True)).astype(BF)
+            mixed_s[at, lanes] = matmul(probs, v_s[at, :]).astype(BF)
+
+        mixed_copy = pltpu.make_async_copy(mixed_s, mixed_out, out_sem.at[6])
+        mixed_copy.start()
+
+        def core_copy(j):
+            return remote(far_s.at[j], core_in.at[j], core_send.at[j], core_recv.at[j], across_core)
+
+        def half_copy(j):
+            return remote(half_s.at[j], half_in.at[j], half_send.at[j], half_recv.at[j], across_half)
+
+        def far_tile(j):
+            far_s[j] = matmul_nt(mixed_s[pl.ds(group, group), :], w_s[tile(j, cols), :]).astype(BF)
+            core_copy(j).start()
+
+        def near_tile(j):
+            part = matmul_nt(mixed_s[pl.ds(0, group), :], w_s[tile(j, cols), :])
+            core_copy(j).wait_recv()
+            part = part + core_in[j].astype(F32)
+            acc[:, tile(j, cols)] = part[:rows]
+            half_s[j] = part[rows:].astype(BF)
+            half_copy(j).start()
+
+        loads[9].wait()
+
+        @pl.loop(0, tiles // 2)
+        def _(j):
+            far_tile(j)
+
+        @pl.loop(0, tiles // 2)
+        def _(j):
+            near_tile(j)
+
+        @pl.loop(0, sends_y)
+        def _(j):
+            theirs_copy(j).wait()
+
+        theirs_local = pltpu.make_async_copy(w_s.at[pl.ds(edge, edge)], theirs_out, out_sem.at[7])
+        theirs_local.start()
+
+        @pl.loop(tiles // 2, tiles)
+        def _(j):
+            far_tile(j)
+
+        @pl.loop(tiles // 2, tiles)
+        def _(j):
+            near_tile(j)
+
+        @pl.loop(0, tiles)
+        def _(j):
+            half_copy(j).wait_recv()
+            at = tile(j, cols)
+            acc[:, at] = x_s[pl.ds(0, rows), at].astype(F32) + acc[:, at] + half_in[j].astype(F32)
+
+        inverse = inv_rms(acc[...])
+        for j in range(lines):
+            mine = acc[:, pl.ds(j * block, block)]
+            theirs = acc[:, pl.ds(edge + j * block, block)]
+            gain_mine = gain_two_ref[:, pl.ds(j * block, block)]
+            gain_theirs = gain_two_ref[:, pl.ds(edge + j * block, block)]
+            for s in range(2):
+                at = pl.ds((2 * j + s) * block, block)
+                picked = jnp.where(side == s, mine, theirs)
+                gain = jnp.where(side == s, gain_mine, gain_theirs)
+                res_s[:, at] = picked
+                own_s[:, at] = (picked * inverse * gain).astype(BF)
+
+        res_copy = pltpu.make_async_copy(res_s, res_out, out_sem.at[8])
+        res_copy.start()
+        own_copy = pltpu.make_async_copy(own_s, norm_out.at[pl.ds(0, rows)], out_sem.at[9])
+        own_copy.start()
+        part_rows = rows // 2
+
+        def slot(j, start=0, size=rows):
+            return norm_out.at[pl.ds(j * rows + start, size)]
+
+        def hop(j, src, dst, target):
+            return remote(src, dst, last_send.at[j], last_recv.at[j], target)
+
+        hops = [
+            hop(0, own_s, slot(1), across_half),
+            hop(1, own_s, slot(2), across_side),
+            hop(2, own_s, slot(4), across_core),
+            hop(3, slot(1, 0, part_rows), slot(3, 0, part_rows), across_side),
+            hop(4, slot(2, part_rows, part_rows), slot(3, part_rows, part_rows), across_half),
+            hop(5, slot(1), slot(5), across_core),
+            hop(6, slot(2), slot(6), across_core),
+            hop(7, slot(3), slot(7), across_core),
+        ]
+        for copy in hops[:3]:
+            copy.start()
+        hops[0].wait_recv()
+        hops[3].start()
+        hops[5].start()
+        hops[1].wait_recv()
+        hops[4].start()
+        hops[6].start()
+        hops[3].wait_recv()
+        hops[4].wait_recv()
+        hops[7].start()
+        hops[2].wait_recv()
+        for copy in hops[5:]:
+            copy.wait_recv()
+        for copy in hops:
+            copy.wait_send()
+
+        @pl.loop(0, tiles)
+        def _(j):
+            core_copy(j).wait_send()
+            half_copy(j).wait_send()
+
+        wait_all(outs)
+        mixed_copy.wait()
+        theirs_local.wait()
+        res_copy.wait()
+        own_copy.wait()
+
+    def low(*shape):
+        return jax.ShapeDtypeStruct(shape, BF)
+
+    out_shape = (
+        low(total, feats),
+        low(total, head_dim),
+        low(total, head_dim),
+        low(total, feats),
+        low(total, rank),
+        jax.ShapeDtypeStruct((rows, rank), F32),
+        low(total, edge),
+        low(edge, feats),
+        jax.ShapeDtypeStruct((rows, width), F32),
+        low(8 * rows, width),
+    )
+    args = (
+        *x_parts,
+        qkv_set,
+        q_up,
+        out_mine,
+        bias,
+        cos_tab,
+        sin_tab,
+        gain_one,
+        gain_q,
+        gain_two,
+    )
+    vmem = pl.BlockSpec(memory_space=pltpu.VMEM)
+    dma = pltpu.SemaphoreType.DMA
+    return pl.pallas_call(
+        kernel,
+        out_shape=out_shape,
+        in_specs=[vmem if a.shape[0] == 1 else ANY for a in args],
+        out_specs=(ANY,) * len(out_shape),
+        scratch_shapes=[
+            pltpu.VMEM((total, width), BF),
+            pltpu.VMEM((total, width), BF),
+            pltpu.VMEM((width, wide), BF),
+            pltpu.VMEM((width, feats), BF),
+            pltpu.VMEM((rank, feats), BF),
+            pltpu.VMEM((total, feats), BF),
+            pltpu.VMEM((total, feats), BF),
+            pltpu.VMEM((total, head_dim), BF),
+            pltpu.VMEM((total, head_dim), BF),
+            pltpu.VMEM((2, group, group), BF),
+            pltpu.VMEM((total, half_dim), F32),
+            pltpu.VMEM((total, half_dim), F32),
+            pltpu.VMEM((total, rank), F32),
+            pltpu.VMEM((total, rank), BF),
+            pltpu.VMEM((total, edge), BF),
+            pltpu.VMEM((tiles, group, cols), BF),
+            pltpu.VMEM((tiles, group, cols), BF),
+            pltpu.VMEM((tiles, rows, cols), BF),
+            pltpu.VMEM((tiles, rows, cols), BF),
+            pltpu.VMEM((rows, width), F32),
+            pltpu.VMEM((rows, width), F32),
+            pltpu.VMEM((rows, width), BF),
+            dma((10,)),
+            dma((sends_y,)),
+            dma((sends_y,)),
+            dma((tiles,)),
+            dma((tiles,)),
+            dma((tiles,)),
+            dma((tiles,)),
+            dma((8,)),
+            dma((8,)),
+            dma((10,)),
+        ],
+        compiler_params=pltpu.CompilerParams(
+            vmem_limit_bytes=vmem_bytes, collective_id=2, has_side_effects=True
+        ),
+        cost_estimate=cost(14 * total * width * feats // 2, args + out_shape),
+        name="attn_first",
+    )(*args)
+
+
+def attn_back(
+    d_attn,
+    out_mine,
+    out_theirs,
+    mixed,
+    queries,
+    keys,
+    values,
+    bias,
+    cos_tab,
+    sin_tab,
+    q_up,
+    latent_n,
+    latent_own,
+    gain_q,
+    normed_rows,
+    qkv_set,
+    x_own,
+    gain_one,
+    d_resid,
+    d_ffn_gain,
+    lines,
+):
+    total, width = d_attn.shape
+    rows = total // 4
+    group = total // 2
+    feats = mixed.shape[1]
+    head_dim = keys.shape[1]
+    heads = feats // head_dim
+    rank = q_up.shape[0]
+    wide = rank + 2 * head_dim
+    edge = width // 2
+    block = edge // lines
+    q_block = rank // (2 * lines)
+    part_cols = wide // 2
+    shard_rows = normed_rows.shape[1] // 2
+    shard = shard_rows // lines
+    scale = 1.0 / math.sqrt(head_dim)
+    step = 256
+    tiles = edge // step
+    half_dim = head_dim // 2
+
+    def kernel(
+        attn_ref,
+        mine_ref,
+        theirs_ref,
+        mixed_ref,
+        q_ref,
+        k_ref,
+        v_ref,
+        bias_ref,
+        cos_ref,
+        sin_ref,
+        up_ref,
+        lat_n_ref,
+        lat_ref,
+        gain_q_ref,
+        n_ref,
+        qkv_ref,
+        x_ref,
+        gain_ref,
+        res_ref,
+        ffn_gain_ref,
+        sums_out,
+        in_out,
+        attn_s,
+        w_s,
+        mixed_s,
+        q_s,
+        k_s,
+        v_s,
+        bias_s,
+        cos_s,
+        sin_s,
+        up_s,
+        lat_n_s,
+        lat_s,
+        x_s,
+        res_s,
+        mix_s,
+        give_s,
+        give_in,
+        dqu_s,
+        dqu_in,
+        kv_s,
+        first_s,
+        far_s,
+        core_in,
+        half_s,
+        half_in,
+        back_s,
+        cols_s,
+        dn_s,
+        dqkv_in,
+        gain_s,
+        q_gain_s,
+        load_sem,
+        give_send,
+        give_recv,
+        dqu_send,
+        dqu_recv,
+        pair_send,
+        pair_recv,
+        last_send,
+        last_recv,
+        out_sem,
+        last_out,
+    ):
+        across_core, across_side, across_half = peers()
+        place, half = lax.axis_index("dp"), lax.axis_index("tensor")
+        side = (place // 2) % 2
+        pairs = (
+            (attn_ref, attn_s),
+            (mixed_ref, mixed_s),
+            (mine_ref, w_s.at[pl.ds(0, edge), pl.ds(0, feats)]),
+            (theirs_ref, w_s.at[pl.ds(edge, edge), pl.ds(0, feats)]),
+            (q_ref, q_s),
+            (k_ref, k_s),
+            (v_ref, v_s),
+            (bias_ref, bias_s),
+            (cos_ref, cos_s),
+            (sin_ref, sin_s),
+            (up_ref, up_s),
+            (lat_n_ref, lat_n_s),
+            (lat_ref, lat_s),
+            (x_ref, x_s),
+            (res_ref, res_s),
+            (qkv_ref, w_s),
+            (n_ref, q_s),
+        )
+        loads = [
+            pltpu.make_async_copy(src, dst, load_sem.at[j]) for j, (src, dst) in enumerate(pairs)
+        ]
+        for copy in loads[:15]:
+            copy.start()
+        greet((across_core, across_side, across_half))
+
+        def give_copy(j):
+            return remote(give_s.at[j], give_in.at[j], give_send.at[j], give_recv.at[j], across_side)
+
+        def dqu_copy(j):
+            return remote(
+                dqu_s.at[j * 2 + 1 - side], dqu_in.at[j], dqu_send.at[j], dqu_recv.at[j], across_side
+            )
+
+        wait_all(loads[:2])
+
+        @pl.loop(0, tiles)
+        def _(j):
+            at = pl.ds(pl.multiple_of(edge + j * step, step), step)
+            give_s[j] = matmul_tn(attn_s[:, at], mixed_s[...]).astype(BF)
+            give_copy(j).start()
+
+        wait_all(loads[2:4])
+
+        @pl.loop(0, feats // step)
+        def _(j):
+            at = tile(j, step)
+            mix_s[:, at] = matmul(attn_s[...], w_s[:, at]).astype(BF)
+
+        loads[15].start()
+        wait_all(loads[4:10])
+        kv_s[...] = jnp.zeros((total, 2 * head_dim), F32)
+
+        @pl.loop(0, 2 * heads)
+        def _(i):
+            at = tile(i // heads, group)
+            lanes = tile(i % heads, head_dim)
+            key, value = k_s[at, :], v_s[at, :]
+            query, d_mix = q_s[at, lanes], mix_s[at, lanes]
+            scores = matmul_nt(query, key) * scale + bias_s[i // heads].astype(F32)
+            expd = jnp.exp(scores - jnp.max(scores, axis=-1, keepdims=True))
+            probs = expd / jnp.sum(expd, axis=-1, keepdims=True)
+            d_probs = matmul_nt(d_mix, value)
+            dot = jnp.sum(probs * d_probs, axis=-1, keepdims=True)
+            d_scores = (probs * (d_probs - dot)).astype(BF)
+            kv = pl.ds(0, head_dim), pl.ds(head_dim, head_dim)
+            kv_s[at, kv[0]] = kv_s[at, kv[0]] + matmul_tn(d_scores, query) * scale
+            kv_s[at, kv[1]] = kv_s[at, kv[1]] + matmul_tn(probs.astype(BF), d_mix)
+            d_query = matmul(d_scores, key) * scale
+            back = spin(d_query[:, :half_dim], d_query[:, half_dim:], cos_s[at, :], -sin_s[at, :])
+            mix_s[at, lanes] = jnp.concatenate(back, axis=1).astype(BF)
+
+        loads[16].start()
+        wait_all(loads[10:12])
+        away, kv_cols = pl.ds(group, group), pl.ds(rank, 2 * head_dim)
+
+        @pl.loop(0, rank // step)
+        def _(j):
+            at = tile(j, step)
+            far_s[:, at] = matmul_nt(mix_s[away, :], up_s[at, :]).astype(BF)
+
+        def core_copy():
+            return remote(far_s, core_in, pair_send.at[0], pair_recv.at[0], across_core)
+
+        def half_copy():
+            return remote(half_s, half_in, pair_send.at[1], pair_recv.at[1], across_half)
+
+        far_s[:, kv_cols] = kv_s[away, :].astype(BF)
+        core_copy().start()
+
+        @pl.loop(0, rank // step)
+        def _(j):
+            at = tile(j, step)
+            first_s[:, at] = matmul_nt(mix_s[pl.ds(0, group), :], up_s[at, :])
+
+        first_s[:, kv_cols] = kv_s[pl.ds(0, group), :]
+        core_copy().wait_recv()
+        first_s[pl.ds(rows, rows), :] = first_s[pl.ds(rows, rows), :] + core_in[
+            pl.ds(rows, rows), :
+        ].astype(F32)
+        half_s[...] = first_s[pl.ds(rows, rows), :].astype(BF)
+        half_copy().start()
+
+        per = step // q_block
+
+        @pl.loop(0, rank // step)
+        def _(j):
+            grad = matmul_tn(lat_n_s[:, tile(j, step)], mix_s[...]).astype(BF)
+            dqu_s[pl.ds(j * per, per)] = grad.reshape(per, q_block, feats)
+
+        @pl.loop(0, lines)
+        def _(j):
+            dqu_copy(j).start()
+
+        wait_all(loads[12:])
+        first_s[pl.ds(0, rows), :] = first_s[pl.ds(0, rows), :] + core_in[pl.ds(0, rows), :].astype(
+            F32
+        )
+        half_copy().wait_recv()
+        own = first_s[pl.ds(0, rows), :] + half_in[...].astype(F32)
+        latent = lat_s[...]
+        inv_q = inv_rms(latent)
+        unit_q = latent * inv_q
+        d_latent_n = own[:, :rank]
+        q_gain_s[...] = jnp.sum(d_latent_n * unit_q, axis=0, keepdims=True)
+        back_s[0, :, pl.ds(0, rank)] = norm_back(d_latent_n, unit_q, inv_q, gain_q_ref[...]).astype(
+            BF
+        )
+        turned = spin(
+            own[:, rank : rank + half_dim],
+            own[:, rank + half_dim : rank + head_dim],
+            cos_s[pl.ds(0, rows), :],
+            -sin_s[pl.ds(0, rows), :],
+        )
+        back_s[0, :, pl.ds(rank, head_dim)] = jnp.concatenate(turned, axis=1).astype(BF)
+        back_s[0, :, pl.ds(rank + head_dim, head_dim)] = own[:, rank + head_dim :].astype(BF)
+        sends = [
+            remote(back_s.at[0], back_s.at[1], last_send.at[0], last_recv.at[0], across_half),
+            remote(back_s.at[0], back_s.at[2], last_send.at[1], last_recv.at[1], across_core),
+            remote(back_s.at[1], back_s.at[3], last_send.at[2], last_recv.at[2], across_core),
+        ]
+        sends[0].start()
+        sends[1].start()
+
+        @pl.loop(0, width // (2 * step))
+        def _(j):
+            at = tile(j, 2 * step)
+            dn_s[:, at] = matmul_nt(back_s[0], w_s[at, :])
+
+        x_f = x_s[...].astype(F32)
+        inverse = inv_rms(x_f)
+        unit = x_f * inverse
+        d_normed = dn_s[...]
+        gain_s[...] = jnp.sum(d_normed * unit, axis=0, keepdims=True)
+        dn_s[...] = norm_back(d_normed, unit, inverse, gain_ref[...])
+        for j in range(lines):
+            mine = dn_s[:, pl.ds(j * block, block)]
+            theirs = dn_s[:, pl.ds(edge + j * block, block)]
+            for s in range(2):
+                at = pl.ds((2 * j + s) * block, block)
+                picked = jnp.where(side == s, mine, theirs)
+                x_s[:, at] = (res_s[:, at] + picked).astype(BF)
+        in_copy = pltpu.make_async_copy(x_s, in_out, out_sem.at[0])
+        in_copy.start()
+
+        @pl.loop(0, tiles)
+        def _(j):
+            part = matmul_tn(attn_s[:, tile(j, step)], mixed_s[...])
+            give_copy(j).wait()
+            give_s[j] = (part + give_in[j].astype(F32)).astype(BF)
+
+        per_line = step // block
+
+        @pl.loop(0, lines)
+        def _(j):
+            dqu_copy(j).wait_recv()
+            dqu_in[j] = (dqu_s[j * 2 + side].astype(F32) + dqu_in[j].astype(F32)).astype(BF)
+
+        outs = []
+        for j in range(lines):
+            src = give_s.at[j // per_line, pl.ds((j % per_line) * block, block)]
+            outs.append(
+                pltpu.make_async_copy(src, sums_out.at[j, pl.ds(0, block)], out_sem.at[1 + j])
+            )
+        outs.append(
+            pltpu.make_async_copy(
+                dqu_in, sums_out.at[:, pl.ds(block, q_block)], out_sem.at[1 + lines]
+            )
+        )
+        for copy in outs:
+            copy.start()
+
+        sends[0].wait_recv()
+        sends[2].start()
+        sends[1].wait_recv()
+        sends[2].wait_recv()
+        for j in range(4):
+            at = pl.ds(j * rows, rows)
+            cols_s[at, pl.ds(0, rank // 2)] = back_s[
+                j, :, pl.ds(pl.multiple_of(half * (rank // 2), 128), rank // 2)
+            ]
+            for k in range(2):
+                start = rank + k * head_dim + half * half_dim
+                cols_s[at, pl.ds(rank // 2 + k * half_dim, half_dim)] = back_s[
+                    j, :, pl.ds(pl.multiple_of(start, 128), half_dim)
+                ]
+        row_index = lax.broadcasted_iota(jnp.int32, (16, feats), 0)
+        idle = feats - 2 * block - q_block
+
+        def gain_rows(r, j):
+            def pick(ref, size):
+                first = ref[:, pl.ds(2 * j * size, size)]
+                second = ref[:, pl.ds((2 * j + 1) * size, size)]
+                return jnp.where(side == r, first, second)
+
+            row = jnp.concatenate(
+                [
+                    gain_s[:, pl.ds((r * lines + j) * block, block)],
+                    pick(ffn_gain_ref, block),
+                    pick(q_gain_s, q_block),
+                    jnp.zeros((1, idle), F32),
+                ],
+                axis=1,
+            )
+            return jnp.where(row_index == 0, row, 0.0).astype(BF)
+
+        high = shard + 16
+        stacked = pl.ds(0, lines * high)
+
+        def qkv_copy():
+            return remote(
+                up_s.at[stacked], dqkv_in, pair_send.at[2], pair_recv.at[2], across_side
+            )
+
+        used, spare = pl.ds(0, part_cols), pl.ds(part_cols, feats - part_cols)
+        for r, held in ((1, up_s), (0, lat_n_s)):
+            grad = matmul_tn(q_s[:, pl.ds(r * shard_rows, shard_rows)], cols_s[...]).astype(BF)
+            for j in range(lines):
+                at = pl.ds(j * high, shard)
+                held[at, used] = grad[j * shard : (j + 1) * shard]
+                held[at, spare] = jnp.zeros((shard, feats - part_cols), BF)
+                held[pl.ds(j * high + shard, 16), :] = gain_rows(r, j)
+            if r == 1:
+                qkv_copy().start()
+        qkv_copy().wait()
+        dqkv_in[...] = (lat_n_s[stacked, :].astype(F32) + dqkv_in[...].astype(F32)).astype(BF)
+        lasts = [
+            pltpu.make_async_copy(
+                dqkv_in.at[pl.ds(j * high, high)],
+                sums_out.at[j, pl.ds(block + q_block, high)],
+                last_out.at[j],
+            )
+            for j in range(lines)
+        ]
+        for copy in lasts:
+            copy.start()
+
+        @pl.loop(0, lines)
+        def _(j):
+            dqu_copy(j).wait_send()
+
+        core_copy().wait_send()
+        half_copy().wait_send()
+        for copy in sends:
+            copy.wait_send()
+        in_copy.wait()
+        wait_all(outs)
+        wait_all(lasts)
+
+    out_shape = (
+        jax.ShapeDtypeStruct((lines, block + q_block + shard + 16, feats), BF),
+        jax.ShapeDtypeStruct((rows, width), BF),
+    )
+    args = (
+        d_attn,
+        out_mine,
+        out_theirs,
+        mixed,
+        queries,
+        keys,
+        values,
+        bias,
+        cos_tab,
+        sin_tab,
+        q_up,
+        latent_n,
+        latent_own,
+        gain_q,
+        normed_rows,
+        qkv_set,
+        x_own,
+        gain_one,
+        d_resid,
+        d_ffn_gain,
+    )
+    vmem = pl.BlockSpec(memory_space=pltpu.VMEM)
+    dma = pltpu.SemaphoreType.DMA
+    return pl.pallas_call(
+        kernel,
+        out_shape=out_shape,
+        in_specs=[vmem if a.shape[0] == 1 else ANY for a in args],
+        out_specs=(ANY, ANY),
+        scratch_shapes=[
+            pltpu.VMEM((total, width), BF),
+            pltpu.VMEM((width, wide), BF),
+            pltpu.VMEM((total, feats), BF),
+            pltpu.VMEM((total, feats), BF),
+            pltpu.VMEM((total, head_dim), BF),
+            pltpu.VMEM((total, head_dim), BF),
+            pltpu.VMEM((2, group, group), BF),
+            pltpu.VMEM((total, half_dim), F32),
+            pltpu.VMEM((total, half_dim), F32),
+            pltpu.VMEM((rank, feats), BF),
+            pltpu.VMEM((total, rank), BF),
+            pltpu.VMEM((rows, rank), F32),
+            pltpu.VMEM((rows, width), BF),
+            pltpu.VMEM((rows, width), F32),
+            pltpu.VMEM((total, feats), BF),
+            pltpu.VMEM((tiles, step, feats), BF),
+            pltpu.VMEM((tiles, step, feats), BF),
+            pltpu.VMEM((2 * lines, q_block, feats), BF),
+            pltpu.VMEM((lines, q_block, feats), BF),
+            pltpu.VMEM((total, 2 * head_dim), F32),
+            pltpu.VMEM((group, wide), F32),
+            pltpu.VMEM((group, wide), BF),
+            pltpu.VMEM((group, wide), BF),
+            pltpu.VMEM((rows, wide), BF),
+            pltpu.VMEM((rows, wide), BF),
+            pltpu.VMEM((4, rows, wide), BF),
+            pltpu.VMEM((total, part_cols), BF),
+            pltpu.VMEM((rows, width), F32),
+            pltpu.VMEM((lines * (shard + 16), feats), BF),
+            pltpu.VMEM((1, width), F32),
+            pltpu.VMEM((1, rank), F32),
+            dma((17,)),
+            dma((tiles,)),
+            dma((tiles,)),
+            dma((lines,)),
+            dma((lines,)),
+            dma((3,)),
+            dma((3,)),
+            dma((3,)),
+            dma((3,)),
+            dma((lines + 3,)),
+            dma((lines,)),
+        ],
+        compiler_params=pltpu.CompilerParams(
+            vmem_limit_bytes=vmem_bytes, collective_id=1, has_side_effects=True
+        ),
+        cost_estimate=cost(40 * total * width * feats // 4, args + out_shape),
+        name="attn_back",
     )(*args)
 
 
@@ -572,27 +1429,10 @@
         queue.append(mine)
         return mine
 
-    def quad_gather(own):
-        pair = jnp.concatenate([own, half_swap(own)], axis=0)
-        return jnp.concatenate([pair, core_swap(pair)], axis=0)
-
     def eight_gather(own):
         across = half_swap(own)
         near = [own, across, side_swap(own), side_swap(across)]
         return near + [core_swap(piece) for piece in near]
-
-    def eight_sum(near, far):
-        four = near.astype(F32) + core_swap(far).astype(F32)
-        rows = four.shape[0] // 2
-        pair = four[:rows] + side_swap(four[rows:].astype(BF)).astype(F32)
-        rows = rows // 2
-        return pair[:rows] + half_swap(pair[rows:].astype(BF)).astype(F32)
-
-    def quad_sum(part):
-        half = part.shape[0] // 2
-        pair = part[:half] + core_swap(part[half:].astype(BF)).astype(F32)
-        own = half // 2
-        return pair[:own] + half_swap(pair[own:].astype(BF)).astype(F32)
 
     def local(
         tokens,
@@ -619,12 +1459,10 @@
         half = lax.axis_index("tensor")
         head_dim = key_proj.shape[1]
         rank = q_down.shape[1]
-        scale = 1.0 / math.sqrt(head_dim)
         shard = q_down.shape[0]
         block = 2 * shard
         hid = gate_proj.shape[1] // 4
         feats = q_up.shape[1] // 2
-        heads = feats // head_dim
         q_shard = q_up.shape[0]
 
         def order(flag, first, second, axis):
@@ -650,7 +1488,8 @@
             return order(side, mine, theirs, 2).reshape(rows, width)
 
         x_low = to_rel(tokens)
-        x_quad = quad_gather(x_low)
+        x_half = half_swap(x_low)
+        x_parts = (x_low, x_half, core_swap(x_low), core_swap(x_half))
 
         mixed_cols = jnp.concatenate(
             [
@@ -669,17 +1508,17 @@
         qkv_mine = line_gather(qkv_piece)
         qkv_theirs = side_swap(qkv_mine)
 
-        def spread(local_weight):
+        def spread(local_weight, swap):
             cols = local_weight.shape[1] // 2
             low = local_weight.astype(BF)
             keep = lax.dynamic_slice_in_dim(low, core * cols, cols, 1)
             give = lax.dynamic_slice_in_dim(low, (1 - core) * cols, cols, 1)
             piece = order(core, keep, core_swap(give), 0)
             mine = line_gather(piece)
-            return mine, side_swap(mine)
-
-        q_up_mine, q_up_theirs = spread(q_up)
-        out_mine, out_theirs = spread(out_proj.T)
+            return mine, side_swap(mine) if swap else None
+
+        q_up_mine, q_up_theirs = spread(q_up, True)
+        out_mine, _ = spread(out_proj.T, False)
 
         ffn_low = jnp.stack([gate_proj.T, up_proj.T, down_proj]).astype(BF)
         ffn_keep = lax.dynamic_slice_in_dim(ffn_low, side * 2 * hid, 2 * hid, 1)
@@ -691,10 +1530,9 @@
             core, ffn_keep[:, :, :, None], core_swap(ffn_give)[:, :, :, None], 3
         ).reshape(3, hid, 2 * block)
 
-        gate_up_w = line_gather(ffn_piece[:2].reshape(2 * hid, 2 * block)).reshape(
-            lines, 2 * hid, 2 * block
+        ffn_w = line_gather(ffn_piece.reshape(3 * hid, 2 * block)).reshape(
+            lines, 3 * hid, 2 * block
         )
-        down_w = line_gather(ffn_piece[2]).reshape(lines, hid, 2 * block)
 
         qkv_part = jnp.stack(
             [
@@ -757,53 +1595,39 @@
         seg_b, pos_b = of_group(group_pair[1])
         segs = jnp.stack([seg_a, seg_b])
         cos_flat, sin_flat = rope_tables(jnp.concatenate([pos_a, pos_b]), head_dim)
-        all_rows = 2 * group_len
-        cos_tab = cos_flat[:, None, :]
-        sin_tab = sin_flat[:, None, :]
         causal = token_order[None, :] <= token_order[:, None]
         visible = (segs[:, None, :] == segs[:, :, None]) | (segs[:, None, :] == 0)
-        allowed = (causal[None] & visible)[:, None]
-
-        x_f = x_quad.astype(F32)
-        normed = (x_f * inv_rms(x_f) * gain_one).astype(BF)
-        first = matmul(normed, qkv_set)
-        latent = first[:, :rank]
-        inv_q = inv_rms(latent)
-        latent_n = (latent * inv_q * gain_q).astype(BF)
-        queries = rotate(
-            matmul(latent_n, q_up_set).reshape(all_rows, heads, head_dim), cos_tab, sin_tab
-        ).astype(BF)
-        queries = queries.reshape(2, group_len, heads, head_dim)
-        keys_rot = (
-            rotate(first[:, rank : rank + head_dim], cos_flat, sin_flat)
-            .astype(BF)
-            .reshape(2, group_len, head_dim)
+        bias = jnp.where(causal[None] & visible, 0.0, masked_score)
+
+        (
+            queries,
+            keys_rot,
+            values,
+            head_mix,
+            latent_n,
+            latent_own,
+            normed_rows,
+            out_theirs,
+            residual,
+            normed_two,
+        ) = attn_first(
+            x_parts,
+            qkv_set,
+            q_up_set,
+            out_mine,
+            bias.astype(BF),
+            cos_flat,
+            sin_flat,
+            gain_one[None, :],
+            gain_q[None, :],
+            gain_two[None, :],
+            shard,
+            lines,
         )
-        values = first[:, rank + head_dim :].astype(BF).reshape(2, group_len, head_dim)
-        raw_scores = (
-            jnp.einsum("gqhe,gke->ghqk", queries, keys_rot, preferred_element_type=F32) * scale
-        )
-        raw_scores = jnp.where(allowed, raw_scores, masked_score)
-        top_score = jnp.max(raw_scores, axis=-1, keepdims=True)
-        expd = jnp.exp(raw_scores - top_score)
-        row_total = jnp.sum(expd, axis=-1, keepdims=True)
-        log_total = top_score + jnp.log(row_total)
-        head_mix = jnp.einsum(
-            "ghqk,gke->gqhe", (expd / row_total).astype(BF), values, preferred_element_type=F32
-        )
-        head_mix = head_mix.reshape(all_rows, feats).astype(BF)
-        edge = lines * block
-        attn_out = jnp.concatenate(
-            [matmul_nt(head_mix, out_mine), matmul_nt(head_mix, out_theirs)], axis=1
-        )
-        residual = tokens.astype(F32) + from_rel(quad_sum(attn_out))
-
-        inv_two = inv_rms(residual)
-        unit_two = residual * inv_two
+
         gain_two_abs = from_rel(gain_two[None, :])
-        normed_two = eight_gather((unit_two * gain_two_abs).astype(BF))
         grad_all = eight_gather(out_grad)
-        hidden, a_fac, s_fac, d_down = ffn_first(normed_two, grad_all, gate_up_w)
+        hidden, a_fac, s_fac, d_down = ffn_first(normed_two, grad_all, ffn_w)
 
         queue = []
 
@@ -820,123 +1644,53 @@
             return sides.reshape(count, 4 * hid, shard).astype(F32)
 
         down_total = line_part(d_down)[0]
-        near_rows = 4 * own_rows
-        d_gate_up, d_resid, d_ffn_gain, d_attn = ffn_back(
-            grad_all, down_w, gate_up_w, a_fac, s_fac, normed_two, residual, gain_two_abs
+        d_gate_up, d_resid, d_ffn_gain, d_attn, ffn_near, _, ffn_away = ffn_back(
+            grad_all, ffn_w, hidden, a_fac, s_fac, normed_two, residual, gain_two_abs
         )
-        d_ffn_gain = to_rel(d_ffn_gain)
         gate_up_total = line_part(d_gate_up)
-        ffn_part = ffn_out_part(hidden, down_w, own_rows)
-        output = (residual + eight_sum(ffn_part[:near_rows], ffn_part[near_rows:])).astype(BF)
         gate_total = gate_up_total[0].T
         up_total = gate_up_total[1].T
 
-        def grad_sum(lhs, rhs):
-            give = matmul_tn(lhs[:, edge:], rhs).astype(BF)
-            part = (matmul_tn(lhs[:, :edge], rhs) + side_swap(give).astype(F32)).astype(BF)
-            mine = line_sum(part, queue)
-            rows = mine.shape[0] // 2
-            keep = lax.dynamic_slice_in_dim(mine, core * rows, rows, 0)
-            away = lax.dynamic_slice_in_dim(mine, (1 - core) * rows, rows, 0)
+        sums, in_grad = attn_back(
+            d_attn,
+            out_mine,
+            out_theirs,
+            head_mix,
+            queries,
+            keys_rot,
+            values,
+            bias.astype(BF),
+            cos_flat,
+            sin_flat,
+            q_up_set,
+            latent_n,
+            latent_own,
+            gain_q[None, :],
+            normed_rows,
+            qkv_set,
+            x_low,
+            gain_one[None, :],
+            d_resid,
+            d_ffn_gain,
+            lines,
+        )
+        ffn_away, ffn_near = after((ffn_away, ffn_near), in_grad)
+        ffn_pair = ffn_near.astype(F32) + ffn_away.astype(F32)
+        ffn_give = ffn_pair[:, own_rows:].astype(BF)
+        ffn_own = ffn_pair[:, :own_rows] + half_swap(ffn_give).astype(F32)
+        output = (residual + ffn_own.transpose(1, 0, 2).reshape(own_rows, width)).astype(BF)
+        rows_sum = block + 2 * q_shard + shard + 16
+        mine = line_sum(sums.reshape(lines * rows_sum, feats), queue)
+
+        def core_rows(value):
+            rows = value.shape[0] // 2
+            keep = lax.dynamic_slice_in_dim(value, core * rows, rows, 0)
+            away = lax.dynamic_slice_in_dim(value, (1 - core) * rows, rows, 0)
             return order(core, keep, core_swap(away), 1).astype(F32)
 
-        out_total = grad_sum(d_attn, head_mix).T
-        d_mix = (
-            (matmul(d_attn[:, :edge], out_mine) + matmul(d_attn[:, edge:], out_theirs))
-            .astype(BF)
-            .reshape(2, group_len, heads, head_dim)
-        )
-        again = jnp.einsum("gqhe,gke->ghqk", queries, keys_rot, preferred_element_type=F32) * scale
-        again = jnp.where(allowed, again, masked_score)
-        probs = jnp.exp(again - log_total)
-        d_probs = jnp.einsum("gqhe,gke->ghqk", d_mix, values, preferred_element_type=F32)
-        d_values = jnp.einsum(
-            "ghqk,gqhe->gke", probs.astype(BF), d_mix, preferred_element_type=F32
-        )
-        row_dot = jnp.sum(probs * d_probs, axis=-1, keepdims=True)
-        d_scores = (probs * (d_probs - row_dot)).astype(BF)
-        d_queries = (
-            jnp.einsum("ghqk,gke->gqhe", d_scores, keys_rot, preferred_element_type=F32) * scale
-        )
-        d_keys = (
-            jnp.einsum("ghqk,gqhe->gke", d_scores, queries, preferred_element_type=F32) * scale
-        )
-        d_query_pre = (
-            unrotate(d_queries.reshape(all_rows, heads, head_dim), cos_tab, sin_tab)
-            .reshape(all_rows, feats)
-            .astype(BF)
-        )
-        d_first = quad_sum(
-            jnp.concatenate(
-                [
-                    matmul_nt(d_query_pre, q_up_set),
-                    d_keys.reshape(all_rows, head_dim),
-                    d_values.reshape(all_rows, head_dim),
-                ],
-                axis=1,
-            )
-        )
-        d_q_up = matmul_tn(latent_n, d_query_pre).astype(BF).reshape(lines, 2, 2 * q_shard, feats)
-        q_up_give = lax.dynamic_index_in_dim(d_q_up, 1 - side, 1, keepdims=False)
-        q_up_keep = lax.dynamic_index_in_dim(d_q_up, side, 1, keepdims=False)
-        q_up_part = (q_up_keep.astype(F32) + side_swap(q_up_give).astype(F32)).astype(BF)
-        q_up_sum = line_sum(q_up_part.reshape(lines * 2 * q_shard, feats), queue)
-        q_up_near = lax.dynamic_slice_in_dim(q_up_sum, core * q_shard, q_shard, 0)
-        q_up_away = lax.dynamic_slice_in_dim(q_up_sum, (1 - core) * q_shard, q_shard, 0)
-        q_up_total = order(core, q_up_near, core_swap(q_up_away), 1).astype(F32)
-
-        d_latent_n = d_first[:, :rank]
-        unit_q = latent[:own_rows] * inv_q[:own_rows]
-        d_q_gain = jnp.sum(d_latent_n * unit_q, axis=0)
-        d_latent = norm_back(d_latent_n, unit_q, inv_q[:own_rows], gain_q).astype(BF)
-        d_keys_pre = unrotate(
-            d_first[:, rank : rank + head_dim], cos_flat[:own_rows], sin_flat[:own_rows]
-        ).astype(BF)
-        d_back = jnp.concatenate(
-            [d_latent, d_keys_pre, d_first[:, rank + head_dim :].astype(BF)], axis=1
-        )
-        d_back_quad = quad_gather(d_back)
-        d_normed = matmul_nt(d_back, qkv_set)
-        inv_own = inv_rms(x_low.astype(F32))
-        unit_own = x_low.astype(F32) * inv_own
-        d_attn_gain = jnp.sum(d_normed * unit_own, axis=0)
-        in_grad = (d_resid + from_rel(norm_back(d_normed, unit_own, inv_own, gain_one))).astype(BF)
-
-        normed_rows = lax.dynamic_index_in_dim(
-            normed.reshape(all_rows, 2 * lines, 2, shard), core, 2, keepdims=False
-        ).reshape(all_rows, 2 * lines * shard)
-        back_cols = jnp.concatenate(
-            [
-                lax.dynamic_slice_in_dim(d_back_quad, half * (rank // 2), rank // 2, 1),
-                lax.dynamic_slice_in_dim(
-                    d_back_quad, rank + half * (head_dim // 2), head_dim // 2, 1
-                ),
-                lax.dynamic_slice_in_dim(
-                    d_back_quad, rank + head_dim + half * (head_dim // 2), head_dim // 2, 1
-                ),
-            ],
-            axis=1,
-        )
-        d_qkv = matmul_tn(normed_rows, back_cols).reshape(2, lines, shard, qkv_cols)
-        q_gain_abs = d_q_gain.reshape(lines, 2, 2 * q_shard)
-        q_gain_parts = jnp.stack(
-            [
-                lax.dynamic_index_in_dim(q_gain_abs, side, 1, keepdims=False),
-                lax.dynamic_index_in_dim(q_gain_abs, 1 - side, 1, keepdims=False),
-            ]
-        )
-        d_gain = jnp.concatenate(
-            [
-                d_attn_gain.reshape(2, lines, block),
-                d_ffn_gain.reshape(2, lines, block),
-                q_gain_parts,
-                jnp.zeros((2, lines, qkv_cols - 2 * block - 2 * q_shard), F32),
-            ],
-            axis=2,
-        )[:, :, None, :]
-        d_qkv = jnp.concatenate([d_qkv, d_gain, jnp.zeros((2, lines, 15, qkv_cols), F32)], axis=2)
-        d_qkv_part = (d_qkv[0] + side_swap(d_qkv[1].astype(BF)).astype(F32)).astype(BF)
-        d_qkv_sum = line_sum(d_qkv_part.reshape(lines * (shard + 16), qkv_cols), queue)
+        out_total = core_rows(mine[:block]).T
+        q_up_total = core_rows(mine[block : block + 2 * q_shard])
+        d_qkv_sum = mine[block + 2 * q_shard :, :qkv_cols]
         d_qkv_far = half_swap(d_qkv_sum)
         gain_pair = d_qkv_sum[shard : shard + 1].astype(F32) + d_qkv_far[
             shard : shard + 1

time: 827 us -> 721 us (0.87)
  Pallas kernels: 148 us -> 361 us
  waiting for transfers between devices: 255 us -> 165 us
  other arithmetic: 124 us -> 40.1 us
  matrix products: 77.7 us -> 0 us
  local copies, waits for them, and re-layouts: 123 us -> 63.7 us
  starting transfers between devices: 50.9 us -> 34.7 us
  blocking collectives: 20 us -> 33.3 us
    pallas_call x1 -> x2, Pallas kernels: 12 us -> 212 us  [the longest x1 107 us: attn_first(): pl.pallas_call(kernel, out_shape=out_shape, in_specs=[vmem if a.shape[0]...]
    dot_general x18 -> x0, matrix products: 77.7 us -> none  [the longest x4 21.7 us: matmul(): return jnp.dot(left, right, preferred_element_type=F32)]
    ppermute x14 -> x7, waiting for transfers between devices: 134 us -> 90.9 us  [side_swap(): return lax.ppermute(value, 'dp', side_pairs)]
    ppermute x9 -> x5, waiting for transfers between devices: 100 us -> 67.1 us  [half_swap(): return lax.ppermute(value, 'tensor', [(0, 1), (1, 0)])]
    convert_element_type x10 -> x3, other arithmetic: 24.3 us -> 3.95 us  [the longest x1 1.51 us: local(): bias.astype(BF)]
    select_n x16 -> x14, other arithmetic: 30.3 us -> 14.5 us  [order(): jnp.where(flag == 0, jnp.concatenate([first, second], axis=axis), jnp.con...]
    reduce_scatter x5 -> x2, waiting for transfers between devices: 14.5 us -> 0.04 us  [line_sum(): lax.psum_scatter(after(value, queue[-1] if queue else None), 'dp', scatte...]
    concatenate x9 -> x0, other arithmetic: 13.5 us -> none  [the longest x1 4.79 us: quad_gather(): return jnp.concatenate([pair, core_swap(pair)], axis=0)]
  transfers between devices with their start and end apart: 56 -> 35, of which waited for: 18 -> 14; matrix products, arithmetic and copies ran while one was open for 38% -> 13% of each run, Pallas kernels for 18% -> 46%
where the time goes in v3:
time: 721 us; the launch traced here: 715 us
  Pallas kernels  361 us (50%)
  waiting for transfers between devices  165 us (23%)
  local copies, waits for them, and re-layouts  63.7 us (9%)
  other arithmetic  40.1 us (6%)
  starting transfers between devices  34.7 us (5%)
  blocking collectives  33.3 us (5%)
  between operations  17.9 us (2%)
    pallas_call x1, Pallas kernels, ffn_back(): pl.pallas_call(kernel, out_shape=out_shape, in_specs=[ANY] * (len(args) -...  120 us
    pallas_call x1, Pallas kernels, attn_first(): pl.pallas_call(kernel, out_shape=out_shape, in_specs=[vmem if a.shape[0]...  107 us
    pallas_call x1, Pallas kernels, attn_back(): pl.pallas_call(kernel, out_shape=out_shape, in_specs=[vmem if a.shape[0]...  105 us
    ppermute x7, waiting for transfers between devices, side_swap(): return lax.ppermute(value, 'dp', side_pairs)  90.9 us
    ppermute x5, waiting for transfers between devices, half_swap(): return lax.ppermute(value, 'tensor', [(0, 1), (1, 0)])  67.1 us
    all_gather x1, blocking collectives, line_gather(): lax.all_gather(value, 'dp', axis=0, tiled=True, axis_index_groups=line_gr...  33.3 us
    pallas_call x1, Pallas kernels, ffn_first(): pl.pallas_call(kernel, out_shape=out_shape, in_specs=[ANY] * len(args), o...  29.2 us
    unnamed x67, local copies, waits for them, and re-layouts  20.7 us
  transfers between devices with their start and end apart: 35, of which 14 were waited for; matrix products, arithmetic and copies ran while one was open for 13% of the time, Pallas kernels for 46%

profile of v3, /device:TPU:1, one launch (start us, length us, event | category | flops | bytes accessed | tf_op | source)
XLA Modules:
  0.0 715.4 jit_solution(428306632800925362)
XLA Ops:
  9.2 1.5 collective-permute-done.6
  12.8 2.5 copy.162
  15.4 2.5 copy.161
  18.9 1.6 pad_maximum_fusion.4
  20.5 1.5 dynamic-slice_bitcast_fusion.1
  22.0 2.6 collective-permute-start.18
  24.6 24.3 %collective-permute-done.18 = bf16[3,1408,128]{2,1,0:T(8,128)(2,1)S(1)} collective-permute-done((bf16[3,1408,128]{2,1,0:T(8,128)(2,1)}, bf16[3,1408,128]{2,1,0:T(8,128)(2,1)S(1)}, u32[]{:S(2)}, u32[]{:S(2)}) %collective-permute-start.18) | collective-permute-done | bytes 1081376 | tf_op jit(solution)/shard_map/ppermute | solution.py:1410
  48.9 2.0 maximum_select_fusion.1
  51.9 2.3 collective-permute-done.19
  54.6 2.2 copy.163
  56.8 2.3 select_n.361
  60.4 33.3 %all_gather.12 = bf16[576,768]{1,0:T(8,128)(2,1)S(1)} all-gather(bf16[144,768]{1,0:T(8,128)(2,1)S(1)} %maximum_maximum_fusion), channel_id=1, replica_groups={{0,8,16,24},{2,10,18,26},{4,12,20,28},{6,14,22,30},{1,9,17,25},{3,11,19..., dimensions={0}, use_global_device_ids=true | all-gather | bytes 1105920 | tf_op jit(solution)/shard_map/all_gather | solution.py:1416
  93.7 1.4 collective-permute-start.3
  95.1 18.1 %collective-permute-done.3 = bf16[576,768]{1,0:T(8,128)(2,1)S(1)} collective-permute-done((bf16[576,768]{1,0:T(8,128)(2,1)S(1)}, bf16[576,768]{1,0:T(8,128)(2,1)S(1)}, u32[]{:S(2)}, u32[]{:S(2)}) %collective-permute-start.3) | collective-permute-done | bytes 884768 | tf_op jit(solution)/shard_map/ppermute | solution.py:1410
  113.2 1.4 pad_maximum_fusion.3
  114.6 1.4 collective-permute-start.4
  116.0 1.9 reshape.461
  117.9 6.5 dynamic-slice_reduce_fusion
  126.3 3.1 collective-permute-start.9
  129.4 1.3 collective-permute-start.11
  131.1 21.3 %collective-permute-done.4 = bf16[2,4,144,768]{3,2,1,0:T(8,128)(2,1)} collective-permute-done((bf16[2,4,144,768]{3,2,1,0:T(8,128)(2,1)}, bf16[2,4,144,768]{3,2,1,0:T(8,128)(2,1)}, u32[]{:S(2)}, u32[]{:S(2)}) %collective-permute-start.4) | collective-permute-done | bytes 1769504 | tf_op jit(solution)/shard_map/ppermute | solution.py:1413
  152.5 1.4 slice.136
  156.1 3.3 fusion.31
  159.4 6.5 collective-permute-start.5
  169.8 1.5 select_convert_fusion.bias_ref
  171.3 1.4 collective-permute-start.7
  173.0 3.4 multiply_sine_fusion
  178.4 19.0 %collective-permute-done.11.refs_1_ = bf16[256,2048]{1,0:T(8,128)(2,1)} collective-permute-done((bf16[256,2048]{1,0:T(8,128)(2,1)}, bf16[256,2048]{1,0:T(8,128)(2,1)}, u32[]{:S(2)}, u32[]{:S(2)}) %collective-permute-start.11) | collective-permute-done | bytes 1048608 | tf_op jit(solution)/shard_map/ppermute | solution.py:1413
  197.4 3.5 collective-permute-start.2
  200.9 1.5 collective-permute-start.13
  202.4 3.3 maximum_select_fusion.3
  206.0 4.3 fusion
  210.4 3.3 copy.150
  213.8 5.0 collective-permute-done.12.refs_2_
  219.9 21.4 %collective-permute-done.13.refs_3_ = bf16[256,2048]{1,0:T(8,128)(2,1)} collective-permute-done((bf16[256,2048]{1,0:T(8,128)(2,1)}, bf16[256,2048]{1,0:T(8,128)(2,1)}, u32[]{:S(2)}, u32[]{:S(2)}) %collective-permute-start.13) | collective-permute-done | bytes 1048608 | tf_op jit(solution)/shard_map/ppermute | solution.py:1410
  242.1 107.3 %attn_first.1 = (bf16[1024,1024]{1,0:T(8,128)(2,1)}, bf16[1024,256]{1,0:T(8,128)(2,1)}, bf16[1024,256]{1,0:T(8,128)(2,1)}, bf16[1024,1024]{1,0:T(8,128)(2,1)}, b...) custom-call(bf16[256,2048]{1,0:T(8,128)(2,1)} %constant_dynamic-upda, ...), custom_call_target="tpu_custom_call" | custom-call | flops 15032385536 | bytes 39866368 | tf_op jit(solution)/shard_map/attn_first/pallas_call | solution.py:883
  350.4 29.2 %ffn_first.1 = (bf16[704,2048]{1,0:T(8,128)(2,1)}, bf16[704,2048]{1,0:T(8,128)(2,1)}, bf16[704,2048]{1,0:T(8,128)(2,1)}, bf16[4,704,512]{2,1,0:T(8,128)(2,1)}) custom-call(bf16[256,2048]{1,0:T(8,128)(2,1)} %refs_0_.3, bf16[256,2048]{1,0:T(8,128)(2,1)} %collective-permute-done.11.refs_1_, bf16[256,2048]{1,0:T(8,128)(2,1)} %copy-done.18, ...), custom_call_target="tpu_custom_call" | custom-call | flops 17716740096 | bytes 36962304 | tf_op jit(solution)/shard_map/ffn_first/pallas_call | solution.py:157
  380.9 119.5 %ffn_back.1 = (bf16[4,1408,512]{2,1,0:T(8,128)(2,1)}, f32[256,2048]{1,0:T(8,128)}, f32[1,2048]{1,0:T(1,128)}, bf16[1024,2048]{1,0:T(8,128)(2,1)}, bf16[4,512,512...) custom-call(bf16[256,2048]{1,0:T(8,128)(2,1)} %refs_0_.3, ...), custom_call_target="tpu_custom_call" | custom-call | flops 29527900160 | bytes 54542336 | tf_op jit(solution)/shard_map/ffn_back/pallas_call | solution.py:496
  500.5 105.2 %attn_back.1 = (bf16[4,528,1024]{2,1,0:T(8,128)(2,1)}, bf16[256,2048]{1,0:T(8,128)(2,1)}) custom-call(bf16[1024,2048]{1,0:T(8,128)(2,1)} %get-tuple-element.46.attn_ref, bf16[1024,1024]{1,0:T(8,128)(2,1)} %all-gather.6.cloned.1.call-done.mine_ref, bf16[1024,1024]{1,0:T(8,128)(2,1)} %get-tuple-element.47.theirs_ref, ...), custom_call_target="tpu_custom_call" | custom-call | flops 21474836480 | bytes 37900288 | tf_op jit(solution)/shard_map/attn_back/pallas_call | solution.py:1338
  605.8 1.6 copy-done.6
  607.4 2.2 convert_add_fusion
  609.5 2.0 copy-done.3
  611.7 1.4 collective-permute-start.20
  613.2 1.5 constant_dynamic-slice_fusion.5
  615.5 21.5 %collective-permute-done.20 = bf16[4,256,512]{2,1,0:T(8,128)(2,1)} collective-permute-done((bf16[4,256,512]{2,1,0:T(8,128)(2,1)S(1)}, bf16[4,256,512]{2,1,0:T(8,128)(2,1)}, u32[]{:S(2)}, u32[]{:S(2)}) %collective-permute-start.20) | collective-permute-done | bytes 1048608 | tf_op jit(solution)/shard_map/ppermute | solution.py:1413
  637.0 2.3 fusion.1
  639.3 1.9 copy.168
  641.2 2.9 copy.169
  644.2 1.2 maximum_select_fusion.6
  645.4 3.4 reshape.472
  648.9 3.0 constant_dynamic-slice_fusion.7
  652.5 1.3 collective-permute-start.28
  653.9 1.2 add_convert_fusion
  655.1 7.6 %collective-permute-done.28 = bf16[1,2,704,128]{3,2,1,0:T(8,128)(2,1)S(1)} collective-permute-done((bf16[1,2,704,128]{3,2,1,0:T(8,128)(2,1)S(1)}, bf16[1,2,704,128]{3,2,1,0:T(8,128)(2,1)S(1)}, u32[]{:S(2)}, u32[]{:S(2)}) %collective-permute-start.28) | collective-permute-done | bytes 360480 | tf_op jit(solution)/shard_map/ppermute | solution.py:1410
  663.3 1.3 collective-permute-start.26
  664.6 1.2 bitcast_convert_fusion
  665.9 14.5 %collective-permute-done.26 = bf16[2,2,704,128]{3,2,1,0:T(8,128)(2,1)S(1)} collective-permute-done((bf16[2,2,704,128]{3,2,1,0:T(8,128)(2,1)S(1)}, bf16[2,2,704,128]{3,2,1,0:T(8,128)(2,1)S(1)}, u32[]{:S(2)}, u32[]{:S(2)}) %collective-permute-start.26) | collective-permute-done | bytes 720928 | tf_op jit(solution)/shard_map/ppermute | solution.py:1410
  680.9 1.5 copy.179
  682.4 1.5 copy.180
  684.0 1.9 reduce-scatter.10.cloned.1.call-done
  688.3 1.2 collective-permute-start.21
  691.5 1.2 fusion.4
  693.8 5.3 collective-permute-done.21
  705.0 2.1 convert_bitcast_fusion
  (195 shorter events, 35.7 us)
Async XLA Ops:
  7.2 53.0 %copy-start = (f32[128,1024]{1,0:T(8,128)S(1)}, f32[128,1024]{1,0:T(8,128)}, u32[]{:S(2)}) copy-start(f32[128,1024]{1,0:T(8,128)} %param.21) | copy-start | bytes 1572868
  7.2 4.4 copy-start.10
  7.2 164.1 %all-gather.4.cloned.1.call-start = ((), (), s32[]{:S(2)}) async-start(), calls=%async_computation.3 | async-start | bytes 1310720 | tf_op jit(solution)/shard_map/all_gather | solution.py:1416
  8.5 4.3 copy-start.7
  9.2 1.6 collective-permute-start.6
  11.5 230.6 %all-gather.6.cloned.1.call-start = ((), (), s32[]{:S(2)}) async-start(), calls=%async_computation.4 | async-start | bytes 2621440 | tf_op jit(solution)/shard_map/all_gather | solution.py:1416
  12.6 5.3 collective-permute-start.8
  12.8 5.0 copy-start.12
  18.8 330.6 %all-gather.8.cloned.1.call-start = ((), (), s32[]{:S(2)}) async-start(), calls=%async_computation.5 | async-start | bytes 10813440 | tf_op jit(solution)/shard_map/all_gather | solution.py:1416
  22.0 26.9 %collective-permute-start.18 = (bf16[3,1408,128]{2,1,0:T(8,128)(2,1)}, bf16[3,1408,128]{2,1,0:T(8,128)(2,1)S(1)}, u32[]{:S(2)}, u32[]{:S(2)}) collective-permute-start(bf16[3,1408,128]{2,1,0:T(8,128)(2,1)} %get-tuple-element.145), channel_id=1, source_target_pairs={{0,4},{2,6},{4,0},{6,2},{8,12},{10,14},{12,8},{14,10},{16,20},{18,... | collective-permute-start | bytes 3244040 | tf_op jit(solution)/shard_map/ppermute | solution.py:1410
  51.1 3.2 collective-permute-start.19
  59.1 1.1 copy-start.20
  59.1 1.1 copy-start.16
  59.1 1.1 copy-start.17
  59.2 441.3 %reduce-scatter.6.cloned.1.call-start = ((), (), s32[]{:S(2)}) async-start(), calls=%async_computation.6 | async-start | bytes 3604480 | tf_op jit(solution)/shard_map/reduce_scatter | solution.py:1422
  93.7 19.5 %collective-permute-start.3 = (bf16[576,768]{1,0:T(8,128)(2,1)S(1)}, bf16[576,768]{1,0:T(8,128)(2,1)S(1)}, u32[]{:S(2)}, u32[]{:S(2)}) collective-permute-start(bf16[576,768]{1,0:T(8,128)(2,1)S(1)} %all_gather.12), channel_id=1, source_target_pairs={{0,4},{2,6},{4,0},{6,2},{8,12},{10,14},{12,8},{14,10},{16,20},{18,... | collective-permute-start | bytes 2654216 | tf_op jit(solution)/shard_map/ppermute | solution.py:1410
  114.6 37.9 %collective-permute-start.4 = (bf16[2,4,144,768]{3,2,1,0:T(8,128)(2,1)}, bf16[2,4,144,768]{3,2,1,0:T(8,128)(2,1)}, u32[]{:S(2)}, u32[]{:S(2)}) collective-permute-start(bf16[2,4,144,768]{3,2,1,0:T(8,128)(2,1)} %pad_maximum_fusion.3), channel_id=1, source_target_pairs={{0,1},{1,0},{2,3},{3,2},{4,5},{5,4},{6,7},{7,6},{8,9},{9,8},{10,11... | collective-permute-start | bytes 5308424 | tf_op jit(solution)/shard_map/ppermute | solution.py:1413
  126.3 52.0 %collective-permute-start = (bf16[256,2048]{1,0:T(8,128)(2,1)}, bf16[256,2048]{1,0:T(8,128)(2,1)}, u32[]{:S(2)}, u32[]{:S(2)}) collective-permute-start(bf16[256,2048]{1,0:T(8,128)(2,1)} %constant_dynamic-update-slice_fusion.x0_ref.x_ref), channel_id=1, source_target_pairs={{0,1},{1,0},{2,3},{3,2},{4,5},{5,4},{6,7},{7,6},{8,9},{9,8},{10,11... | collective-permute-start | bytes 3145736 | tf_op jit(solution)/shard_map/ppermute | solution.py:1413
  126.3 40.2 %collective-permute-start.9 = (s32[1]{0:T(128)}, s32[1]{0:T(128)}, u32[]{:S(2)}, u32[]{:S(2)}) collective-permute-start(s32[1]{0:T(128)} %param.17), channel_id=1, source_target_pairs={{0,2},{2,0},{4,6},{6,4},{8,10},{10,8},{12,14},{14,12},{16,18},{18,... | collective-permute-start | bytes 20 | tf_op jit(solution)/shard_map/ppermute | solution.py:1407
  129.4 68.0 %collective-permute-start.11 = (bf16[256,2048]{1,0:T(8,128)(2,1)}, bf16[256,2048]{1,0:T(8,128)(2,1)}, u32[]{:S(2)}, u32[]{:S(2)}) collective-permute-start(bf16[256,2048]{1,0:T(8,128)(2,1)} %refs_0_.3), channel_id=1, source_target_pairs={{0,1},{1,0},{2,3},{3,2},{4,5},{5,4},{6,7},{7,6},{8,9},{9,8},{10,11... | collective-permute-start | bytes 3145736 | tf_op jit(solution)/shard_map/ppermute | solution.py:1413
  156.1 12.2 %copy-start.15 = (s32[16,2]{0,1:T(2,128)S(1)}, s32[16,2]{0,1:T(2,128)}, u32[]{:S(2)}) copy-start(s32[16,2]{0,1:T(2,128)} %param.19) | copy-start | bytes 388
  159.4 46.3 %collective-permute-start.5 = (bf16[2,4,144,1536]{3,2,1,0:T(8,128)(2,1)}, bf16[2,4,144,1536]{3,2,1,0:T(8,128)(2,1)}, u32[]{:S(2)}, u32[]{:S(2)}) collective-permute-start(bf16[2,4,144,1536]{3,2,1,0:T(8,128)(2,1)} %get-tuple-element.139), channel_id=1, source_target_pairs={{0,2},{2,0},{4,6},{6,4},{8,10},{10,8},{12,14},{14,12},{16,18},{18,... | collective-permute-start | bytes 10616840 | tf_op jit(solution)/shard_map/ppermute | solution.py:1407
  171.3 31.1 %copy-start.9 = (bf16[512,1024]{1,0:T(8,128)(2,1)S(1)}, bf16[512,1024]{1,0:T(8,128)(2,1)}, u32[]{:S(2)}) copy-start(bf16[512,1024]{1,0:T(8,128)(2,1)} %all-gather.4.cloned.1.call-done) | copy-start | bytes 3145732
  171.3 29.6 %collective-permute-start.7 = (bf16[512,1024]{1,0:T(8,128)(2,1)}, bf16[512,1024]{1,0:T(8,128)(2,1)}, u32[]{:S(2)}, u32[]{:S(2)}) collective-permute-start(bf16[512,1024]{1,0:T(8,128)(2,1)} %all-gather.4.cloned.1.call-done), channel_id=1, source_target_pairs={{0,4},{2,6},{4,0},{6,2},{8,12},{10,14},{12,8},{14,10},{16,20},{18,... | collective-permute-start | bytes 3145736 | tf_op jit(solution)/shard_map/ppermute | solution.py:1410
  172.7 3.8 collective-permute-start.10
  176.5 37.1 %collective-permute-start.1 = (bf16[256,2048]{1,0:T(8,128)(2,1)}, bf16[256,2048]{1,0:T(8,128)(2,1)}, u32[]{:S(2)}, u32[]{:S(2)}) collective-permute-start(bf16[256,2048]{1,0:T(8,128)(2,1)} %constant_dynamic-update-slice_fusion.x0_ref.x_ref), channel_id=1, source_target_pairs={{0,2},{2,0},{4,6},{6,4},{8,10},{10,8},{12,14},{14,12},{16,18},{18,... | collective-permute-start | bytes 3145736 | tf_op jit(solution)/shard_map/ppermute | solution.py:1407
  178.3 40.5 %collective-permute-start.12 = (bf16[256,2048]{1,0:T(8,128)(2,1)}, bf16[256,2048]{1,0:T(8,128)(2,1)S(1)}, u32[]{:S(2)}, u32[]{:S(2)}) collective-permute-start(bf16[256,2048]{1,0:T(8,128)(2,1)} %refs_0_.3), channel_id=1, source_target_pairs={{0,4},{2,6},{4,0},{6,2},{8,12},{10,14},{12,8},{14,10},{16,20},{18,... | collective-permute-start | bytes 3145736 | tf_op jit(solution)/shard_map/ppermute | solution.py:1410
  197.4 44.7 %collective-permute-start.2 = (bf16[256,2048]{1,0:T(8,128)(2,1)}, bf16[256,2048]{1,0:T(8,128)(2,1)}, u32[]{:S(2)}, u32[]{:S(2)}) collective-permute-start(bf16[256,2048]{1,0:T(8,128)(2,1)} %collective-permute-done.x1_ref), channel_id=1, source_target_pairs={{0,2},{2,0},{4,6},{6,4},{8,10},{10,8},{12,14},{14,12},{16,18},{18,... | collective-permute-start | bytes 3145736 | tf_op jit(solution)/shard_map/ppermute | solution.py:1407
  200.9 40.5 %collective-permute-start.13 = (bf16[256,2048]{1,0:T(8,128)(2,1)}, bf16[256,2048]{1,0:T(8,128)(2,1)}, u32[]{:S(2)}, u32[]{:S(2)}) collective-permute-start(bf16[256,2048]{1,0:T(8,128)(2,1)} %collective-permute-done.11.refs_1_), channel_id=1, source_target_pairs={{0,4},{2,6},{4,0},{6,2},{8,12},{10,14},{12,8},{14,10},{16,20},{18,... | collective-permute-start | bytes 3145736 | tf_op jit(solution)/shard_map/ppermute | solution.py:1410
  202.4 3.6 copy-start.2
  205.7 143.7 %collective-permute-start.14 = (bf16[256,2048]{1,0:T(8,128)(2,1)}, bf16[256,2048]{1,0:T(8,128)(2,1)S(1)}, u32[]{:S(2)}, u32[]{:S(2)}) collective-permute-start(bf16[256,2048]{1,0:T(8,128)(2,1)} %refs_0_.3), channel_id=1, source_target_pairs={{0,2},{2,0},{4,6},{6,4},{8,10},{10,8},{12,14},{14,12},{16,18},{18,... | collective-permute-start | bytes 3145736 | tf_op jit(solution)/shard_map/ppermute | solution.py:1407
  213.6 135.8 %collective-permute-start.15 = (bf16[256,2048]{1,0:T(8,128)(2,1)}, bf16[256,2048]{1,0:T(8,128)(2,1)}, u32[]{:S(2)}, u32[]{:S(2)}) collective-permute-start(bf16[256,2048]{1,0:T(8,128)(2,1)} %collective-permute-done.11.refs_1_), channel_id=1, source_target_pairs={{0,2},{2,0},{4,6},{6,4},{8,10},{10,8},{12,14},{14,12},{16,18},{18,... | collective-permute-start | bytes 3145736 | tf_op jit(solution)/shard_map/ppermute | solution.py:1407
  218.8 130.5 %copy-start.18 = (bf16[256,2048]{1,0:T(8,128)(2,1)}, bf16[256,2048]{1,0:T(8,128)(2,1)S(1)}, u32[]{:S(2)}) copy-start(bf16[256,2048]{1,0:T(8,128)(2,1)S(1)} %collective-permute-done.12.refs_2_) | copy-start | bytes 3145732
  218.9 130.6 %collective-permute-start.16 = (bf16[256,2048]{1,0:T(8,128)(2,1)S(1)}, bf16[256,2048]{1,0:T(8,128)(2,1)}, u32[]{:S(2)}, u32[]{:S(2)}) collective-permute-start(bf16[256,2048]{1,0:T(8,128)(2,1)S(1)} %collective-permute-done.12.refs_2_), channel_id=1, source_target_pairs={{0,2},{2,0},{4,6},{6,4},{8,10},{10,8},{12,14},{14,12},{16,18},{18,... | collective-permute-start | bytes 3145736 | tf_op jit(solution)/shard_map/ppermute | solution.py:1407
  241.3 108.1 %collective-permute-start.17 = (bf16[256,2048]{1,0:T(8,128)(2,1)}, bf16[256,2048]{1,0:T(8,128)(2,1)}, u32[]{:S(2)}, u32[]{:S(2)}) collective-permute-start(bf16[256,2048]{1,0:T(8,128)(2,1)} %collective-permute-done.13.refs_3_), channel_id=1, source_target_pairs={{0,2},{2,0},{4,6},{6,4},{8,10},{10,8},{12,14},{14,12},{16,18},{18,... | collective-permute-start | bytes 3145736 | tf_op jit(solution)/shard_map/ppermute | solution.py:1407
  349.4 1.0 copy-start.19
  379.6 0.7 copy-start.14
  379.6 226.1 %reduce-scatter.8.cloned.1.call-start = ((), (), s32[]{:S(2)}) async-start(), calls=%async_computation.7 | async-start | bytes 7208960 | tf_op jit(solution)/shard_map/reduce_scatter | solution.py:1422
  500.5 185.3 %reduce-scatter.10.cloned.1.call-start = ((), (), s32[]{:S(2)}) async-start(), calls=%async_computation.8 | async-start | bytes 5406720
  605.8 1.6 copy-start.6
  609.5 2.0 copy-start.3
  611.6 1.5 copy-start.13
  611.7 25.3 %collective-permute-start.20 = (bf16[4,256,512]{2,1,0:T(8,128)(2,1)S(1)}, bf16[4,256,512]{2,1,0:T(8,128)(2,1)}, u32[]{:S(2)}, u32[]{:S(2)}) collective-permute-start(bf16[4,256,512]{2,1,0:T(8,128)(2,1)S(1)} %slice.198), channel_id=1, source_target_pairs={{0,1},{1,0},{2,3},{3,2},{4,5},{5,4},{6,7},{7,6},{8,9},{9,8},{10,11... | collective-permute-start | bytes 3145736 | tf_op jit(solution)/shard_map/ppermute | solution.py:1413
  615.5 28.7 %collective-permute-start.27 = (bf16[1,704,2,128]{3,1,2,0:T(8,128)(2,1)}, bf16[1,704,2,128]{3,1,2,0:T(8,128)(2,1)}, u32[]{:S(2)}, u32[]{:S(2)}) collective-permute-start(bf16[1,704,2,128]{3,1,2,0:T(8,128)(2,1)} %bitcast.124), channel_id=1, source_target_pairs={{0,2},{2,0},{4,6},{6,4},{8,10},{10,8},{12,14},{14,12},{16,18},{18,... | collective-permute-start | bytes 1081352 | tf_op jit(solution)/shard_map/ppermute | solution.py:1407
  648.8 5.0 copy-start.5
  651.8 2.0 copy-start.4
  652.0 11.0 %collective-permute-start.25 = (bf16[2,704,2,128]{3,1,2,0:T(8,128)(2,1)S(1)}, bf16[2,704,2,128]{3,1,2,0:T(8,128)(2,1)S(1)}, u32[]{:S(2)}, u32[]{:S(2)}) collective-permute-start(bf16[2,704,2,128]{3,1,2,0:T(8,128)(2,1)S(1)} %bitcast.160), channel_id=1, source_target_pairs={{0,2},{2,0},{4,6},{6,4},{8,10},{10,8},{12,14},{14,12},{16,18},{18,... | collective-permute-start | bytes 2162696 | tf_op jit(solution)/shard_map/ppermute | solution.py:1407
  652.5 10.2 %collective-permute-start.28 = (bf16[1,2,704,128]{3,2,1,0:T(8,128)(2,1)S(1)}, bf16[1,2,704,128]{3,2,1,0:T(8,128)(2,1)S(1)}, u32[]{:S(2)}, u32[]{:S(2)}) collective-permute-start(bf16[1,2,704,128]{3,2,1,0:T(8,128)(2,1)S(1)} %get-tuple-element.157), channel_id=1, source_target_pairs={{0,4},{2,6},{4,0},{6,2},{8,12},{10,14},{12,8},{14,10},{16,20},{18,... | collective-permute-start | bytes 1081352 | tf_op jit(solution)/shard_map/ppermute | solution.py:1410
  663.3 17.1 %collective-permute-start.26 = (bf16[2,2,704,128]{3,2,1,0:T(8,128)(2,1)S(1)}, bf16[2,2,704,128]{3,2,1,0:T(8,128)(2,1)S(1)}, u32[]{:S(2)}, u32[]{:S(2)}) collective-permute-start(bf16[2,2,704,128]{3,2,1,0:T(8,128)(2,1)S(1)} %get-tuple-element.151), channel_id=1, source_target_pairs={{0,4},{2,6},{4,0},{6,2},{8,12},{10,14},{12,8},{14,10},{16,20},{18,... | collective-permute-start | bytes 2162696 | tf_op jit(solution)/shard_map/ppermute | solution.py:1410
  685.8 2.3 copy-start.8
  687.0 2.5 slice-start
  687.2 17.8 %collective-permute-start.24 = (bf16[128,1024]{0,1:T(8,128)(2,1)S(1)}, bf16[128,1024]{0,1:T(8,128)(2,1)}, u32[]{:S(2)}, u32[]{:S(2)}) collective-permute-start(bf16[128,1024]{0,1:T(8,128)(2,1)S(1)} %copy.198), channel_id=1, source_target_pairs={{0,2},{2,0},{4,6},{6,4},{8,10},{10,8},{12,14},{14,12},{16,18},{18,... | collective-permute-start | bytes 786440 | tf_op jit(solution)/shard_map/ppermute | solution.py:1407
  688.3 10.8 %collective-permute-start.21 = (bf16[144,768]{0,1:T(8,128)(2,1)S(1)}, bf16[144,768]{0,1:T(8,128)(2,1)S(1)}, u32[]{:S(2)}, u32[]{:S(2)}) collective-permute-start(bf16[144,768]{0,1:T(8,128)(2,1)S(1)} %copy.189), channel_id=1, source_target_pairs={{0,1},{1,0},{2,3},{3,2},{4,5},{5,4},{6,7},{7,6},{8,9},{9,8},{10,11... | collective-permute-start | bytes 663560 | tf_op jit(solution)/shard_map/ppermute | solution.py:1413
  689.7 1.7 collective-permute-start.23
  699.2 3.5 collective-permute-start.22
  700.1 7.0 copy-start.11
  702.7 5.4 copy-start.1
Sparse Core Ops, SparseCore 0:
  11.6 29.8 all-gather.3
  43.7 59.6 all-gather.5
  104.9 152.9 all-gather.7
  379.7 56.1 reduce-scatter.5
  500.6 103.5 reduce-scatter.7
  606.4 79.3 reduce-scatter.9

commit v4 on v3

--- a/solution.py
+++ b/solution.py
@@ -101,21 +101,24 @@
     return [ref.at[pl.ds(j * rows, rows)] for j in range(count)]
 
 
-def ffn_first(normed, grads, weights):
-    count = len(grads)
-    rows, width = grads[0].shape
-    total = rows * count
+def zip_rows(ref, far, count):
+    pairs = zip(split_rows(ref, count // 2), split_rows(far, count // 2))
+    return [one for pair in pairs for one in pair]
+
+
+def ffn_first(normed, grads, grads_far, weights):
+    count = 8
+    total, width = normed.shape
+    rows = total // count
     lines, triple, cols = weights.shape
     hid = triple // 3
     double = 2 * hid
 
     def kernel(*refs):
-        grad_refs = refs[:count]
-        normed_ref, weight_ref, hid_ref, a_ref, s_ref, down_ref = refs[count : count + 6]
+        grad_ref, grad_far, normed_ref, weight_ref, hid_ref, a_ref, s_ref, down_ref = refs[:8]
+        grad_refs = zip_rows(grad_ref, grad_far, count)
         normed_refs = split_rows(normed_ref, count)
-        n_s, g_s, w_s, hid_s, a_s, s_s, down_s, n_sem, g_sem, w_sem, o_sem, d_sem = refs[
-            count + 6 :
-        ]
+        n_s, g_s, w_s, hid_s, a_s, s_s, down_s, n_sem, g_sem, w_sem, o_sem, d_sem = refs[8:]
         parts = join_lines(weight_ref.at[:, pl.ds(0, double)], w_s, w_sem)
         stack_rows(normed_refs, n_s, n_sem)
         grad_copies = stack_rows(grad_refs, g_s, g_sem)
@@ -153,7 +156,7 @@
 
     acts = jax.ShapeDtypeStruct((hid, total), BF)
     out_shape = (acts, acts, acts, jax.ShapeDtypeStruct((lines, hid, cols), BF))
-    args = (*grads, normed, weights)
+    args = (grads, grads_far, normed, weights)
     return pl.pallas_call(
         kernel,
         out_shape=out_shape,
@@ -210,22 +213,20 @@
     )
 
 
-def ffn_back(grads, weights, hidden, a_fac, s_fac, normed, residual, gain):
-    count = len(grads)
-    rows, width = grads[0].shape
+def ffn_back(grads, grads_far, weights, hidden, a_fac, s_fac, normed, residual, gain):
+    count = 8
+    total, width = normed.shape
+    rows = total // count
     lines, triple, cols = weights.shape
     hid = triple // 3
     double = 2 * hid
     block = cols // 2
     near = 4 * rows
-    total = count * rows
 
     def kernel(*refs):
-        grad_refs = refs[:count]
-        normed_ref, all_ref, hid_ref, a_ref, s_ref, resid_ref, gain_ref = refs[count : count + 7]
-        grad_out, dres_out, dgain_out, attn_out, near_out, away_out, away_in = refs[
-            count + 7 : count + 14
-        ]
+        grad_ref, grad_far, normed_ref, all_ref, hid_ref, a_ref, s_ref, resid_ref, gain_ref = refs[:9]
+        grad_out, dres_out, dgain_out, attn_out, near_out, away_out, away_in = refs[9:16]
+        grad_refs = zip_rows(grad_ref, grad_far, count)
         normed_refs = split_rows(normed_ref, count)
         weight_ref = all_ref.at[:, pl.ds(0, double)]
         down_in = all_ref.at[:, pl.ds(double, hid)]
@@ -267,7 +268,7 @@
             away_send,
             away_recv,
             free_sem,
-        ) = refs[count + 14 :]
+        ) = refs[16:]
         across_core, across_side, across_half = peers()
         side = (lax.axis_index("dp") // 2) % 2
         downs = join_lines(down_in, d_s, d_sem)
@@ -490,7 +491,7 @@
         jax.ShapeDtypeStruct((lines, 2 * rows, cols), BF),
         jax.ShapeDtypeStruct((lines, 2 * rows, cols), BF),
     )
-    args = (*grads, normed, weights, hidden, a_fac, s_fac, residual, gain)
+    args = (grads, grads_far, normed, weights, hidden, a_fac, s_fac, residual, gain)
     vmem = pl.BlockSpec(memory_space=pltpu.VMEM)
     dma = pltpu.SemaphoreType.DMA
     return pl.pallas_call(
@@ -549,10 +550,293 @@
     return first * cos_vals - second * sin_vals, second * cos_vals + first * sin_vals
 
 
+def gather_first(x_own, grad_own, piece, gain_piece, ffn_low, lines):
+    rows, width = x_own.shape
+    hid = ffn_low.shape[1] // 4
+    shard, part_cols = piece.shape
+
+    def kernel(
+        x_ref,
+        dy_ref,
+        piece_ref,
+        gain_ref,
+        ffn_ref,
+        x_out,
+        dy_out,
+        w_out,
+        g_out,
+        ffn_out,
+        local_sem,
+        up_send,
+        up_recv,
+        down_send,
+        down_recv,
+        side_send,
+        side_recv,
+        half_send,
+        half_recv,
+        core_send,
+        core_recv,
+        row_send,
+        row_recv,
+        ffn_send,
+        ffn_recv,
+    ):
+        across_core, across_side, across_half = peers()
+        place, half = lax.axis_index("dp"), lax.axis_index("tensor")
+        core, side, line = place % 2, (place // 2) % 2, place // 4
+        across_both = (line * 4 + (1 - side) * 2 + 1 - core, half)
+        above = ((place + 4) % (4 * lines), half)
+        below = ((place + 4 * lines - 4) % (4 * lines), half)
+
+        def weight(r, at, far):
+            column = pl.multiple_of(jnp.where(far, 1 - half, half) * part_cols, 128)
+            return w_out.at[r, at, core, :, pl.ds(column, part_cols)]
+
+        def gain(r, at):
+            return g_out.at[r, at, core]
+
+        def both(r, at, to_r, sends, recvs, where, target):
+            return [
+                remote(
+                    weight(r, at, False),
+                    weight(to_r, at, False),
+                    sends.at[where, 0],
+                    recvs.at[where, 0],
+                    target,
+                ),
+                remote(
+                    gain(r, at), gain(to_r, at), sends.at[where, 1], recvs.at[where, 1], target
+                ),
+            ]
+
+        def upward(step):
+            return both(0, line - step, 0, up_send, up_recv, step, above)
+
+        def arrived_below(step):
+            return both(0, line - step, 0, up_send, up_recv, step - 1, above)
+
+        def downward(step):
+            return both(0, line + step, 0, down_send, down_recv, step, below)
+
+        def arrived_above(step):
+            return both(0, line + step, 0, down_send, down_recv, step - 1, below)
+
+        def to_side(at):
+            return both(0, at, 1, side_send, side_recv, at, across_side)
+
+        def to_half(r, at):
+            ref = weight(r, at, False)
+            return remote(ref, ref, half_send.at[r, at], half_recv.at[r, at], across_half)
+
+        def from_half(r, at):
+            ref = weight(r, at, True)
+            return remote(ref, ref, half_send.at[r, at], half_recv.at[r, at], across_half)
+
+        def to_core(r, at, kind):
+            ref = gain(r, at) if kind == 2 else weight(r, at, kind == 1)
+            return remote(
+                ref, ref, core_send.at[r, at, kind], core_recv.at[r, at, kind], across_core
+            )
+
+        def from_core(r, at, kind):
+            if kind == 2:
+                ref = g_out.at[r, at, 1 - core]
+            else:
+                column = (1 - half if kind == 1 else half) * part_cols
+                ref = w_out.at[
+                    r, at, 1 - core, :, pl.ds(pl.multiple_of(column, 128), part_cols)
+                ]
+            return remote(
+                ref, ref, core_send.at[r, at, kind], core_recv.at[r, at, kind], across_core
+            )
+
+        def start(copies):
+            for copy in copies:
+                copy.start()
+
+        def spread_near(at):
+            start(to_side(at))
+            to_half(0, at).start()
+            to_core(0, at, 0).start()
+            to_core(0, at, 2).start()
+
+        def slot(ref, j):
+            return ref.at[pl.ds(j * rows, rows)]
+
+        def hop(j, src, dst, target):
+            return remote(src, dst, row_send.at[j], row_recv.at[j], target)
+
+        moves = [
+            hop(0, x_ref, slot(x_out, 1), across_half),
+            hop(1, x_ref, slot(x_out, 2), across_core),
+            hop(2, slot(x_out, 1), slot(x_out, 3), across_core),
+            hop(3, dy_ref, slot(dy_out, 1), across_side),
+            hop(4, dy_ref, slot(dy_out, 2), across_core),
+            hop(5, slot(dy_out, 1), slot(dy_out, 3), across_core),
+        ]
+
+        def units(to_side_at, to_core_at):
+            at = (to_side_at * 2 + to_core_at) * hid
+            return ffn_ref.at[:, pl.ds(pl.multiple_of(at, 16), hid)]
+
+        me = side * 2 + core
+        shares = [
+            remote(
+                units(to_side_at, to_core_at),
+                ffn_out.at[me],
+                ffn_send.at[j],
+                ffn_recv.at[j],
+                target,
+            )
+            for j, (to_side_at, to_core_at, target) in enumerate(
+                (
+                    (1 - side, 1 - core, across_both),
+                    (1 - side, core, across_side),
+                    (side, 1 - core, across_core),
+                )
+            )
+        ]
+        locals_ = [
+            pltpu.make_async_copy(piece_ref, weight(0, line, False), local_sem.at[0]),
+            pltpu.make_async_copy(gain_ref, gain(0, line), local_sem.at[1]),
+            pltpu.make_async_copy(x_ref, slot(x_out, 0), local_sem.at[2]),
+            pltpu.make_async_copy(dy_ref, slot(dy_out, 0), local_sem.at[3]),
+            pltpu.make_async_copy(units(side, core), ffn_out.at[me], local_sem.at[4]),
+        ]
+        start(locals_)
+        greet((across_core, across_side, across_half, above, below, across_both))
+        wait_all(locals_[:2])
+
+        @pl.when(line < lines - 1)
+        def _():
+            start(upward(0))
+
+        @pl.when(line > 0)
+        def _():
+            start(downward(0))
+
+        spread_near(line)
+        start(moves[:2])
+        start(shares)
+        for step in range(1, lines):
+
+            @pl.when(line >= step)
+            def _():
+                for copy in arrived_below(step):
+                    copy.wait_recv()
+                if step < lines - 1:
+
+                    @pl.when(line < lines - 1)
+                    def _():
+                        start(upward(step))
+
+                spread_near(line - step)
+
+            @pl.when(line + step < lines)
+            def _():
+                for copy in arrived_above(step):
+                    copy.wait_recv()
+                if step < lines - 1:
+
+                    @pl.when(line > 0)
+                    def _():
+                        start(downward(step))
+
+                spread_near(line + step)
+
+        moves[3].start()
+        moves[4].start()
+        for at in range(lines):
+            for copy in to_side(at):
+                copy.wait_recv()
+            to_half(1, at).start()
+            to_core(1, at, 0).start()
+            to_core(1, at, 2).start()
+        moves[0].wait_recv()
+        moves[2].start()
+        for r in range(2):
+            for at in range(lines):
+                from_half(r, at).wait_recv()
+                to_core(r, at, 1).start()
+        moves[3].wait_recv()
+        moves[5].start()
+        for j in (1, 2, 4, 5):
+            moves[j].wait_recv()
+        for copy in shares:
+            copy.wait_recv()
+        for r in range(2):
+            for at in range(lines):
+                for kind in range(3):
+                    from_core(r, at, kind).wait_recv()
+
+        for step in range(lines - 1):
+
+            @pl.when((line >= step) & (line < lines - 1))
+            def _():
+                for copy in upward(step):
+                    copy.wait_send()
+
+            @pl.when((line + step < lines) & (line > 0))
+            def _():
+                for copy in downward(step):
+                    copy.wait_send()
+
+        for at in range(lines):
+            for copy in to_side(at):
+                copy.wait_send()
+            for r in range(2):
+                to_half(r, at).wait_send()
+                for kind in range(3):
+                    to_core(r, at, kind).wait_send()
+        for copy in moves + shares:
+            copy.wait_send()
+        wait_all(locals_[2:])
+
+    out_shape = (
+        jax.ShapeDtypeStruct((4 * rows, width), BF),
+        jax.ShapeDtypeStruct((4 * rows, width), BF),
+        jax.ShapeDtypeStruct((2, lines, 2, shard, 2 * part_cols), BF),
+        jax.ShapeDtypeStruct((2, lines, 2, 16, part_cols), BF),
+        jax.ShapeDtypeStruct((4, 3, hid, shard), BF),
+    )
+    args = (x_own, grad_own, piece, gain_piece, ffn_low)
+    dma = pltpu.SemaphoreType.DMA
+    return pl.pallas_call(
+        kernel,
+        out_shape=out_shape,
+        in_specs=[ANY] * 5,
+        out_specs=(ANY,) * 5,
+        scratch_shapes=[
+            dma((5,)),
+            dma((lines, 2)),
+            dma((lines, 2)),
+            dma((lines, 2)),
+            dma((lines, 2)),
+            dma((lines, 2)),
+            dma((lines, 2)),
+            dma((2, lines)),
+            dma((2, lines)),
+            dma((2, lines, 3)),
+            dma((2, lines, 3)),
+            dma((6,)),
+            dma((6,)),
+            dma((3,)),
+            dma((3,)),
+        ],
+        compiler_params=pltpu.CompilerParams(
+            vmem_limit_bytes=vmem_bytes, collective_id=3, has_side_effects=True
+        ),
+        cost_estimate=cost(1, args + out_shape),
+        name="gather_first",
+    )(*args)
+
+
 def attn_first(
-    x_parts,
+    x_all,
+    grad_near,
     qkv_set,
-    q_up,
+    q_up_mine,
     out_mine,
     bias,
     cos_tab,
@@ -563,11 +847,12 @@
     shard,
     lines,
 ):
-    rows, width = x_parts[0].shape
-    total = 4 * rows
+    total, width = x_all.shape
+    rows = total // 4
     group = 2 * rows
     edge, feats = out_mine.shape
-    rank = q_up.shape[0]
+    rank = 2 * q_up_mine.shape[0]
+    q_block = rank // (2 * lines)
     wide = qkv_set.shape[1]
     head_dim = (wide - rank) // 2
     half_dim = head_dim // 2
@@ -580,10 +865,8 @@
     sends_y = edge // step
 
     def kernel(
-        x0_ref,
-        x1_ref,
-        x2_ref,
-        x3_ref,
+        x_ref,
+        dy_ref,
         qkv_ref,
         up_ref,
         mine_ref,
@@ -603,6 +886,8 @@
         theirs_out,
         res_out,
         norm_out,
+        dy_out,
+        up_out,
         x_s,
         n_s,
         qkv_s,
@@ -635,19 +920,23 @@
         last_send,
         last_recv,
         out_sem,
+        up_send,
+        up_recv,
+        up_sem,
+        dy_send,
+        dy_recv,
     ):
         across_core, across_side, across_half = peers()
         place = lax.axis_index("dp")
         core, side = place % 2, (place // 2) % 2
         pairs = [
             (ref, x_s.at[pl.ds(j * rows, rows)])
-            for j, ref in enumerate((x0_ref, x1_ref, x2_ref, x3_ref))
+            for j, ref in enumerate(split_rows(x_ref, 4))
         ]
         pairs += [
             (qkv_ref, qkv_s),
             (cos_ref, cos_s),
             (sin_ref, sin_s),
-            (up_ref, up_s),
             (bias_ref, bias_s),
             (mine_ref, w_s.at[pl.ds(0, edge)]),
         ]
@@ -666,6 +955,38 @@
                 theirs_recv.at[j],
                 across_side,
             )
+
+        def up_rows(j):
+            return up_s.at[pl.ds(pl.multiple_of((j * 2 + side) * q_block, 16), q_block)]
+
+        def up_copy(j):
+            src = up_ref.at[pl.ds(j * q_block, q_block)]
+            return remote(src, up_rows(j), up_send.at[j], up_recv.at[j], across_side)
+
+        def up_local(j):
+            src = up_ref.at[pl.ds(j * q_block, q_block)]
+            return pltpu.make_async_copy(src, up_rows(j), up_sem.at[j])
+
+        for j in range(lines):
+            up_copy(j).start()
+            up_local(j).start()
+
+        def slot_of(ref, j):
+            return ref.at[pl.ds(j * rows, rows)]
+
+        grad_moves = [
+            remote(slot_of(src, j), slot_of(dy_out, k), dy_send.at[k], dy_recv.at[k], target)
+            for k, (src, j, target) in enumerate(
+                (
+                    (dy_ref, 0, across_half),
+                    (dy_ref, 1, across_half),
+                    (dy_out, 0, across_core),
+                    (dy_out, 1, across_core),
+                )
+            )
+        ]
+        grad_moves[0].start()
+        grad_moves[1].start()
 
         @pl.loop(0, sends_y)
         def _(j):
@@ -686,15 +1007,24 @@
 
         wait_all(loads[4:7])
 
+        per_half = rank // 2 // step
+
         @pl.loop(0, rank // step)
         def _(j):
-            at = tile(j, step)
-            lat_s[:, at] = matmul(n_s[...], qkv_s[:, at])
-
-        key = matmul(n_s[...], qkv_s[:, pl.ds(rank, head_dim)])
-        turned = spin(key[:, :half_dim], key[:, half_dim:], cos_s[...], sin_s[...])
+            start = (j // per_half) * (wide // 2) + (j % per_half) * step
+            lat_s[:, tile(j, step)] = matmul(
+                n_s[...], qkv_s[:, pl.ds(pl.multiple_of(start, 128), step)]
+            )
+
+        pair = [
+            matmul(n_s[...], qkv_s[:, pl.ds(j * (wide // 2) + rank // 2, head_dim)])
+            for j in range(2)
+        ]
+        turned = spin(pair[0][:, :half_dim], pair[1][:, :half_dim], cos_s[...], sin_s[...])
         k_s[...] = jnp.concatenate(turned, axis=1).astype(BF)
-        v_s[...] = matmul(n_s[...], qkv_s[:, pl.ds(rank + head_dim, head_dim)]).astype(BF)
+        v_s[...] = jnp.concatenate(
+            [pair[0][:, half_dim:], pair[1][:, half_dim:]], axis=1
+        ).astype(BF)
 
         @pl.loop(0, 4)
         def _(i):
@@ -702,7 +1032,10 @@
             latent = lat_s[at, :]
             lat_n_s[at, :] = (latent * inv_rms(latent) * gain_q_ref[...]).astype(BF)
 
-        wait_all(loads[7:9])
+        loads[7].wait()
+        for j in range(lines):
+            up_local(j).wait()
+            up_copy(j).wait()
 
         @pl.loop(0, heads)
         def _(h):
@@ -721,6 +1054,7 @@
                     (lat_n_s, lat_n_out),
                     (lat_s.at[pl.ds(0, rows)], lat_out),
                     (nc_s, n_out),
+                    (up_s, up_out),
                 )
             )
         ]
@@ -736,7 +1070,7 @@
             probs = (expd / jnp.sum(expd, axis=-1, keepdims=True)).astype(BF)
             mixed_s[at, lanes] = matmul(probs, v_s[at, :]).astype(BF)
 
-        mixed_copy = pltpu.make_async_copy(mixed_s, mixed_out, out_sem.at[6])
+        mixed_copy = pltpu.make_async_copy(mixed_s, mixed_out, out_sem.at[7])
         mixed_copy.start()
 
         def core_copy(j):
@@ -757,7 +1091,10 @@
             half_s[j] = part[rows:].astype(BF)
             half_copy(j).start()
 
-        loads[9].wait()
+        loads[8].wait()
+        for j in range(2):
+            grad_moves[j].wait_recv()
+            grad_moves[2 + j].start()
 
         @pl.loop(0, tiles // 2)
         def _(j):
@@ -771,7 +1108,7 @@
         def _(j):
             theirs_copy(j).wait()
 
-        theirs_local = pltpu.make_async_copy(w_s.at[pl.ds(edge, edge)], theirs_out, out_sem.at[7])
+        theirs_local = pltpu.make_async_copy(w_s.at[pl.ds(edge, edge)], theirs_out, out_sem.at[8])
         theirs_local.start()
 
         @pl.loop(tiles // 2, tiles)
@@ -801,9 +1138,9 @@
                 res_s[:, at] = picked
                 own_s[:, at] = (picked * inverse * gain).astype(BF)
 
-        res_copy = pltpu.make_async_copy(res_s, res_out, out_sem.at[8])
+        res_copy = pltpu.make_async_copy(res_s, res_out, out_sem.at[9])
         res_copy.start()
-        own_copy = pltpu.make_async_copy(own_s, norm_out.at[pl.ds(0, rows)], out_sem.at[9])
+        own_copy = pltpu.make_async_copy(own_s, norm_out.at[pl.ds(0, rows)], out_sem.at[10])
         own_copy.start()
         part_rows = rows // 2
 
@@ -837,7 +1174,9 @@
         hops[2].wait_recv()
         for copy in hops[5:]:
             copy.wait_recv()
-        for copy in hops:
+        for copy in grad_moves[2:]:
+            copy.wait_recv()
+        for copy in hops + grad_moves:
             copy.wait_send()
 
         @pl.loop(0, tiles)
@@ -865,11 +1204,14 @@
         low(edge, feats),
         jax.ShapeDtypeStruct((rows, width), F32),
         low(8 * rows, width),
+        low(4 * rows, width),
+        low(rank, feats),
     )
     args = (
-        *x_parts,
+        x_all,
+        grad_near,
         qkv_set,
-        q_up,
+        q_up_mine,
         out_mine,
         bias,
         cos_tab,
@@ -908,7 +1250,7 @@
             pltpu.VMEM((rows, width), F32),
             pltpu.VMEM((rows, width), F32),
             pltpu.VMEM((rows, width), BF),
-            dma((10,)),
+            dma((9,)),
             dma((sends_y,)),
             dma((sends_y,)),
             dma((tiles,)),
@@ -917,7 +1259,12 @@
             dma((tiles,)),
             dma((8,)),
             dma((8,)),
-            dma((10,)),
+            dma((11,)),
+            dma((lines,)),
+            dma((lines,)),
+            dma((lines,)),
+            dma((4,)),
+            dma((4,)),
         ],
         compiler_params=pltpu.CompilerParams(
             vmem_limit_bytes=vmem_bytes, collective_id=2, has_side_effects=True
@@ -1163,17 +1510,21 @@
         unit_q = latent * inv_q
         d_latent_n = own[:, :rank]
         q_gain_s[...] = jnp.sum(d_latent_n * unit_q, axis=0, keepdims=True)
-        back_s[0, :, pl.ds(0, rank)] = norm_back(d_latent_n, unit_q, inv_q, gain_q_ref[...]).astype(
-            BF
-        )
+        d_latent = norm_back(d_latent_n, unit_q, inv_q, gain_q_ref[...]).astype(BF)
         turned = spin(
             own[:, rank : rank + half_dim],
             own[:, rank + half_dim : rank + head_dim],
             cos_s[pl.ds(0, rows), :],
             -sin_s[pl.ds(0, rows), :],
         )
-        back_s[0, :, pl.ds(rank, head_dim)] = jnp.concatenate(turned, axis=1).astype(BF)
-        back_s[0, :, pl.ds(rank + head_dim, head_dim)] = own[:, rank + head_dim :].astype(BF)
+        for j in range(2):
+            at = j * part_cols
+            first_v = rank + head_dim + j * half_dim
+            back_s[0, :, pl.ds(at, rank // 2)] = d_latent[:, j * (rank // 2) : (j + 1) * (rank // 2)]
+            back_s[0, :, pl.ds(at + rank // 2, half_dim)] = turned[j].astype(BF)
+            back_s[0, :, pl.ds(at + rank // 2 + half_dim, half_dim)] = own[
+                :, first_v : first_v + half_dim
+            ].astype(BF)
         sends = [
             remote(back_s.at[0], back_s.at[1], last_send.at[0], last_recv.at[0], across_half),
             remote(back_s.at[0], back_s.at[2], last_send.at[1], last_recv.at[1], across_core),
@@ -1236,14 +1587,9 @@
         sends[2].wait_recv()
         for j in range(4):
             at = pl.ds(j * rows, rows)
-            cols_s[at, pl.ds(0, rank // 2)] = back_s[
-                j, :, pl.ds(pl.multiple_of(half * (rank // 2), 128), rank // 2)
+            cols_s[at, :] = back_s[
+                j, :, pl.ds(pl.multiple_of(half * part_cols, 128), part_cols)
             ]
-            for k in range(2):
-                start = rank + k * head_dim + half * half_dim
-                cols_s[at, pl.ds(rank // 2 + k * half_dim, half_dim)] = back_s[
-                    j, :, pl.ds(pl.multiple_of(start, 128), half_dim)
-                ]
         row_index = lax.broadcasted_iota(jnp.int32, (16, feats), 0)
         idle = feats - 2 * block - q_block
 
@@ -1266,24 +1612,30 @@
 
         high = shard + 16
         stacked = pl.ds(0, lines * high)
+        used, spare = pl.ds(0, part_cols), pl.ds(part_cols, feats - part_cols)
 
         def qkv_copy():
             return remote(
-                up_s.at[stacked], dqkv_in, pair_send.at[2], pair_recv.at[2], across_side
+                up_s.at[stacked, used],
+                dqkv_in.at[:, used],
+                pair_send.at[2],
+                pair_recv.at[2],
+                across_side,
             )
 
-        used, spare = pl.ds(0, part_cols), pl.ds(part_cols, feats - part_cols)
         for r, held in ((1, up_s), (0, lat_n_s)):
             grad = matmul_tn(q_s[:, pl.ds(r * shard_rows, shard_rows)], cols_s[...]).astype(BF)
             for j in range(lines):
                 at = pl.ds(j * high, shard)
                 held[at, used] = grad[j * shard : (j + 1) * shard]
-                held[at, spare] = jnp.zeros((shard, feats - part_cols), BF)
                 held[pl.ds(j * high + shard, 16), :] = gain_rows(r, j)
             if r == 1:
                 qkv_copy().start()
         qkv_copy().wait()
-        dqkv_in[...] = (lat_n_s[stacked, :].astype(F32) + dqkv_in[...].astype(F32)).astype(BF)
+        dqkv_in[:, used] = (
+            lat_n_s[stacked, used].astype(F32) + dqkv_in[:, used].astype(F32)
+        ).astype(BF)
+        dqkv_in[:, spare] = jnp.zeros((lines * high, feats - part_cols), BF)
         lasts = [
             pltpu.make_async_copy(
                 dqkv_in.at[pl.ds(j * high, high)],
@@ -1429,11 +1781,6 @@
         queue.append(mine)
         return mine
 
-    def eight_gather(own):
-        across = half_swap(own)
-        near = [own, across, side_swap(own), side_swap(across)]
-        return near + [core_swap(piece) for piece in near]
-
     def local(
         tokens,
         group_of_device,
@@ -1488,8 +1835,6 @@
             return order(side, mine, theirs, 2).reshape(rows, width)
 
         x_low = to_rel(tokens)
-        x_half = half_swap(x_low)
-        x_parts = (x_low, x_half, core_swap(x_low), core_swap(x_half))
 
         mixed_cols = jnp.concatenate(
             [
@@ -1504,58 +1849,29 @@
             [attn_gain, ffn_gain, q_gain, jnp.zeros((qkv_cols - 2 * shard - q_shard,), F32)]
         ).astype(BF)
         gain_rows = jnp.concatenate([gain_row[None, :], jnp.zeros((15, qkv_cols), BF)], axis=0)
-        qkv_piece = jnp.concatenate([mixed_cols, gain_rows], axis=0)
-        qkv_mine = line_gather(qkv_piece)
-        qkv_theirs = side_swap(qkv_mine)
-
-        def spread(local_weight, swap):
+
+        def spread(local_weight):
             cols = local_weight.shape[1] // 2
             low = local_weight.astype(BF)
             keep = lax.dynamic_slice_in_dim(low, core * cols, cols, 1)
             give = lax.dynamic_slice_in_dim(low, (1 - core) * cols, cols, 1)
             piece = order(core, keep, core_swap(give), 0)
-            mine = line_gather(piece)
-            return mine, side_swap(mine) if swap else None
-
-        q_up_mine, q_up_theirs = spread(q_up, True)
-        out_mine, _ = spread(out_proj.T, False)
+            return line_gather(piece)
+
+        q_up_mine = spread(q_up)
+        out_mine = spread(out_proj.T)
 
         ffn_low = jnp.stack([gate_proj.T, up_proj.T, down_proj]).astype(BF)
-        ffn_keep = lax.dynamic_slice_in_dim(ffn_low, side * 2 * hid, 2 * hid, 1)
-        ffn_give = lax.dynamic_slice_in_dim(ffn_low, (1 - side) * 2 * hid, 2 * hid, 1)
-        ffn_sides = order(side, ffn_keep[:, :, None], side_swap(ffn_give)[:, :, None], 2)
-        ffn_keep = lax.dynamic_slice_in_dim(ffn_sides, core * hid, hid, 1)
-        ffn_give = lax.dynamic_slice_in_dim(ffn_sides, (1 - core) * hid, hid, 1)
-        ffn_piece = order(
-            core, ffn_keep[:, :, :, None], core_swap(ffn_give)[:, :, :, None], 3
-        ).reshape(3, hid, 2 * block)
-
+        x_all, grad_near, qkv_set, gain_set, ffn_parts = gather_first(
+            x_low, out_grad, mixed_cols, gain_rows, ffn_low, lines
+        )
+        ffn_piece = ffn_parts.reshape(4, 3 * hid, shard).transpose(1, 0, 2)
         ffn_w = line_gather(ffn_piece.reshape(3 * hid, 2 * block)).reshape(
             lines, 3 * hid, 2 * block
         )
-
-        qkv_part = jnp.stack(
-            [
-                qkv_mine.reshape(lines, shard + 16, qkv_cols),
-                qkv_theirs.reshape(lines, shard + 16, qkv_cols),
-            ]
-        )
-        qkv_far = half_swap(qkv_part)
+        qkv_set = qkv_set.reshape(width, 2 * qkv_cols)
+        gain_both = gain_set[:, :, :, 0, :]
         q_c, k_c = rank // 2, rank // 2 + head_dim // 2
-        qkv_wide = jnp.concatenate(
-            [
-                order(half, qkv_part[..., :q_c], qkv_far[..., :q_c], 3),
-                order(half, qkv_part[..., q_c:k_c], qkv_far[..., q_c:k_c], 3),
-                order(half, qkv_part[..., k_c:], qkv_far[..., k_c:], 3),
-            ],
-            axis=3,
-        )
-        qkv_other = core_swap(qkv_wide)
-        qkv_both = order(core, qkv_wide[:, :, None], qkv_other[:, :, None], 2)
-        qkv_set = qkv_both[:, :, :, :shard, :].reshape(width, rank + 2 * head_dim)
-        flat_gain = qkv_part[:, :, shard, :]
-        flat_far = core_swap(flat_gain)
-        gain_both = order(core, flat_gain[:, :, None], flat_far[:, :, None], 2)
         gain_one = gain_both[..., :shard].reshape(width).astype(F32)
         gain_two = gain_both[..., shard : 2 * shard].reshape(width).astype(F32)
         q_gain_rel = gain_both[..., 2 * shard : 2 * shard + q_shard].reshape(
@@ -1566,13 +1882,6 @@
             .reshape(rank)
             .astype(F32)
         )
-        q_up_set = order(
-            side,
-            q_up_mine.reshape(lines, 1, 2 * q_shard, feats),
-            q_up_theirs.reshape(lines, 1, 2 * q_shard, feats),
-            1,
-        ).reshape(rank, feats)
-
         group_pair = jnp.stack([group_of_device[0], core_swap(group_of_device)[0]])
         group_len = segment_ids.shape[1]
         token_order = jnp.concatenate(
@@ -1610,10 +1919,13 @@
             out_theirs,
             residual,
             normed_two,
+            grad_far,
+            q_up_set,
         ) = attn_first(
-            x_parts,
+            x_all,
+            grad_near,
             qkv_set,
-            q_up_set,
+            q_up_mine,
             out_mine,
             bias.astype(BF),
             cos_flat,
@@ -1626,8 +1938,7 @@
         )
 
         gain_two_abs = from_rel(gain_two[None, :])
-        grad_all = eight_gather(out_grad)
-        hidden, a_fac, s_fac, d_down = ffn_first(normed_two, grad_all, ffn_w)
+        hidden, a_fac, s_fac, d_down = ffn_first(normed_two, grad_near, grad_far, ffn_w)
 
         queue = []
 
@@ -1645,7 +1956,7 @@
 
         down_total = line_part(d_down)[0]
         d_gate_up, d_resid, d_ffn_gain, d_attn, ffn_near, _, ffn_away = ffn_back(
-            grad_all, ffn_w, hidden, a_fac, s_fac, normed_two, residual, gain_two_abs
+            grad_near, grad_far, ffn_w, hidden, a_fac, s_fac, normed_two, residual, gain_two_abs
         )
         gate_up_total = line_part(d_gate_up)
         gate_total = gate_up_total[0].T

time: 721 us -> 650 us (0.902)
  Pallas kernels: 361 us -> 468 us
  waiting for transfers between devices: 165 us -> 69.8 us
  blocking collectives: 33.3 us -> 0 us
  starting transfers between devices: 34.7 us -> 10.1 us
  other arithmetic: 40.1 us -> 25.1 us
  local copies, waits for them, and re-layouts: 63.7 us -> 50 us
    pallas_call x0 -> x1, Pallas kernels: none -> 88.9 us  [gather_first(): pl.pallas_call(kernel, out_shape=out_shape, in_specs=[ANY] * 5, out_specs...]
    ppermute x7 -> x2, waiting for transfers between devices: 90.9 us -> 22.4 us  [side_swap(): return lax.ppermute(value, 'dp', side_pairs)]
    ppermute x5 -> x2, waiting for transfers between devices: 67.1 us -> 24.9 us  [half_swap(): return lax.ppermute(value, 'tensor', [(0, 1), (1, 0)])]
    all_gather x1 -> x0, blocking collectives: 33.3 us -> none  [line_gather(): lax.all_gather(value, 'dp', axis=0, tiled=True, axis_index_groups=line_gr...]
    pallas_call x1, Pallas kernels: 107 us -> 132 us  [attn_first(): pl.pallas_call(kernel, out_shape=out_shape, in_specs=[vmem if a.shape[0]...]
    ppermute x17 -> x8, starting transfers between devices: 19.5 us -> 4.93 us  [core_swap(): return lax.ppermute(value, 'dp', core_pairs)]
    all_gather x3, waiting for transfers between devices: 0.02 us -> 13.1 us  [line_gather(): lax.all_gather(value, 'dp', axis=0, tiled=True, axis_index_groups=line_gr...]
    select_n x14 -> x6, other arithmetic: 14.5 us -> 3.28 us  [order(): jnp.where(flag == 0, jnp.concatenate([first, second], axis=axis), jnp.con...]
  transfers between devices with their start and end apart: 35 -> 18, of which waited for: 14 -> 10; matrix products, arithmetic and copies ran while one was open for 13% -> 10% of each run, Pallas kernels for 46% -> 68%
where the time goes in v4:
time: 650 us; the launch traced here: 641 us
  Pallas kernels  468 us (72%)
  waiting for transfers between devices  69.8 us (11%)
  local copies, waits for them, and re-layouts  50 us (8%)
  other arithmetic  25.1 us (4%)
  between operations  17.8 us (3%)
  starting transfers between devices  10.1 us (2%)
    pallas_call x1, Pallas kernels, attn_first(): pl.pallas_call(kernel, out_shape=out_shape, in_specs=[vmem if a.shape[0]...  132 us
    pallas_call x1, Pallas kernels, ffn_back(): pl.pallas_call(kernel, out_shape=out_shape, in_specs=[ANY] * (len(args) -...  120 us
    pallas_call x1, Pallas kernels, attn_back(): pl.pallas_call(kernel, out_shape=out_shape, in_specs=[vmem if a.shape[0]...  98.8 us
    pallas_call x1, Pallas kernels, gather_first(): pl.pallas_call(kernel, out_shape=out_shape, in_specs=[ANY] * 5, out_specs...  88.9 us
    pallas_call x1, Pallas kernels, ffn_first(): pl.pallas_call(kernel, out_shape=out_shape, in_specs=[ANY] * len(args), o...  29.1 us
    ppermute x2, waiting for transfers between devices, half_swap(): return lax.ppermute(value, 'tensor', [(0, 1), (1, 0)])  24.9 us
    ppermute x2, waiting for transfers between devices, side_swap(): return lax.ppermute(value, 'dp', side_pairs)  22.4 us
    unnamed x63, local copies, waits for them, and re-layouts  16.8 us
  transfers between devices with their start and end apart: 18, of which 10 were waited for; matrix products, arithmetic and copies ran while one was open for 10% of the time, Pallas kernels for 68%

profile of v4, /device:TPU:1, one launch (start us, length us, event | category | flops | bytes accessed | tf_op | source)
XLA Modules:
  0.0 640.9 jit_solution(2136520667816230790)
XLA Ops:
  7.3 1.2 convert_element_type.124
  8.6 1.3 collective-permute-done
  9.9 0.8 maximum_select_fusion.7
  11.2 1.4 collective-permute-done.1
  12.6 0.9 maximum_select_fusion.4
  13.7 0.8 reshape.452
  14.6 6.5 %dynamic-slice_reduce_fusion = (bf16[256,4,256]{2,1,0:T(4,128)(2,1)S(1)}, bf16[256,4,256]{2,1,0:T(4,128)(2,1)S(1)}) fusion(bf16[256,4,2,256]{3,2,1,0:T(2,128)(2,1)S(1)} %reshape.452, s32[]{:T(128)S(6)} %select_n.242, s32[]{:T(128)S(6)} %select_n.241), kind=kLoop, calls=%fused_computation.12 | loop fusion | bytes 2097160 | tf_op jit(solution)/shard_map/jit(dynamic_index_in_dim)/dynamic_slice | solution.py:1826
  21.2 0.9 copy.182
  23.2 1.7 copy.135
  24.9 1.0 dynamic-slice_convert_fusion.1
  26.0 0.7 pad_maximum_fusion.1.piece_ref
  26.7 1.1 constant_dynamic-update-slice_fusion.x_ref
  27.9 1.6 pad_maximum_fusion.ffn_ref
  29.5 88.9 %gather_first.1 = (bf16[1024,2048]{1,0:T(8,128)(2,1)}, bf16[1024,2048]{1,0:T(8,128)(2,1)}, bf16[2,4,2,128,1536]{4,3,2,1,0:T(8,128)(2,1)}, bf16[2,4,2,16,768]{4,3,2,1,0:T(8,128)(2,1)}, bf16[4,3,704,128]{3,2,1,0:T(8,128)(2,1)}) custom-call(bf16[256,2048]{1,0:T(8,128)(2,1)} %copy-done.4, bf16[256,2048]{1,0:T(8,128)(2,1)} %dy_ref.1, ...), custom_call_target="tpu_custom_call" | custom-call | flops 1 | bytes 21716992 | tf_op jit(solution)/shard_map/gather_first/pallas_call | solution.py:805
  118.5 3.3 copy.189
  122.7 1.0 slice.84
  127.5 0.8 constant_dynamic-slice_fusion.15
  128.7 3.3 multiply_sine_fusion
  132.0 1.5 select_convert_fusion.bias_ref
  133.5 131.6 %attn_first.1 = (bf16[1024,1024]{1,0:T(8,128)(2,1)}, bf16[1024,256]{1,0:T(8,128)(2,1)}, bf16[1024,256]{1,0:T(8,128)(2,1)}, bf16[1024,1024]{1,0:T(8,128)(2,1)}, b...) custom-call(bf16[1024,2048]{1,0:T(8,128)(2,1)} %get-tuple-element.46, ...), custom_call_target="tpu_custom_call" | custom-call | flops 15032385536 | bytes 49303552 | tf_op jit(solution)/shard_map/attn_first/pallas_call | solution.py:1225
  265.1 13.1 %all-gather.8.cloned.1.call-done = bf16[8448,512]{1,0:T(8,128)(2,1)} async-done(((bf16[2112,512]{1,0:T(8,128)(2,1)}), bf16[8448,512]{1,0:T(8,128)(2,1)}) %all-gather.8.cloned.1.call-update) | async-done | bytes 8650768 | tf_op jit(solution)/shard_map/all_gather | solution.py:1768
  278.2 29.1 %ffn_first.1 = (bf16[704,2048]{1,0:T(8,128)(2,1)}, bf16[704,2048]{1,0:T(8,128)(2,1)}, bf16[704,2048]{1,0:T(8,128)(2,1)}, bf16[4,704,512]{2,1,0:T(8,128)(2,1)}) custom-call(bf16[1024,2048]{1,0:T(8,128)(2,1)} %get-tuple-element.47.dy_ref.refs_0_, bf16[1024,2048]{1,0:T(8,128)(2,1)} %get-tuple-element.51.refs_1_, bf16[2048,2048]{1,0:T(8,128)(2,1)} %get-tuple-element.52.refs_2_, ...), custom_call_target="tpu_custom_call" | custom-call | flops 17716740096 | bytes 36962304 | tf_op jit(solution)/shard_map/ffn_first/pallas_call | solution.py:160
  308.6 119.6 %ffn_back.1 = (bf16[4,1408,512]{2,1,0:T(8,128)(2,1)}, f32[256,2048]{1,0:T(8,128)}, f32[1,2048]{1,0:T(1,128)}, bf16[1024,2048]{1,0:T(8,128)(2,1)}, bf16[4,512,512...) custom-call(bf16[1024,2048]{1,0:T(8,128)(2,1)} %get-tuple-element.47.dy_ref.refs_0_, ...), custom_call_target="tpu_custom_call" | custom-call | flops 29527900160 | bytes 54542336 | tf_op jit(solution)/shard_map/ffn_back/pallas_call | solution.py:497
  428.3 98.8 %attn_back.1 = (bf16[4,528,1024]{2,1,0:T(8,128)(2,1)}, bf16[256,2048]{1,0:T(8,128)(2,1)}) custom-call(bf16[1024,2048]{1,0:T(8,128)(2,1)} %get-tuple-element.59.attn_ref, bf16[1024,1024]{1,0:T(8,128)(2,1)} %all-gather.6.cloned.1.call-done.mine_ref, bf16[1024,1024]{1,0:T(8,128)(2,1)} %get-tuple-element.60.theirs_ref, ...), custom_call_target="tpu_custom_call" | custom-call | flops 21474836480 | bytes 37900288 | tf_op jit(solution)/shard_map/attn_back/pallas_call | solution.py:1690
  527.2 2.6 reduce-scatter.8.cloned.1.call-done
  529.8 1.6 copy-done.6
  531.4 2.2 convert_add_fusion
  533.6 2.0 copy-done.2
  535.7 1.2 collective-permute-start.3
  537.1 1.5 constant_dynamic-slice_fusion.5
  538.6 0.8 copy.192
  539.4 0.9 collective-permute-start.10
  540.3 19.6 %collective-permute-done.3 = bf16[4,256,512]{2,1,0:T(8,128)(2,1)} collective-permute-done((bf16[4,256,512]{2,1,0:T(8,128)(2,1)S(1)}, bf16[4,256,512]{2,1,0:T(8,128)(2,1)}, u32[]{:S(2)}, u32[]{:S(2)}) %collective-permute-start.3) | collective-permute-done | bytes 1048608 | tf_op jit(solution)/shard_map/ppermute | solution.py:1765
  560.0 2.3 fusion
  562.3 1.9 copy.149
  564.1 2.9 copy.150
  567.1 1.2 maximum_select_fusion.2
  568.4 3.4 reshape.463
  571.8 3.0 constant_dynamic-slice_fusion.7
  574.9 1.6 collective-permute-start.8
  576.5 1.2 collective-permute-start.11
  577.8 1.2 add_convert_fusion
  579.0 7.7 %collective-permute-done.11 = bf16[1,2,704,128]{3,2,1,0:T(8,128)(2,1)S(1)} collective-permute-done((bf16[1,2,704,128]{3,2,1,0:T(8,128)(2,1)S(1)}, bf16[1,2,704,128]{3,2,1,0:T(8,128)(2,1)S(1)}, u32[]{:S(2)}, u32[]{:S(2)}) %collective-permute-start.11) | collective-permute-done | bytes 360480 | tf_op jit(solution)/shard_map/ppermute | solution.py:1762
  587.3 1.2 collective-permute-start.9
  588.6 1.2 bitcast_convert_fusion
  589.8 14.7 %collective-permute-done.9 = bf16[2,2,704,128]{3,2,1,0:T(8,128)(2,1)S(1)} collective-permute-done((bf16[2,2,704,128]{3,2,1,0:T(8,128)(2,1)S(1)}, bf16[2,2,704,128]{3,2,1,0:T(8,128)(2,1)S(1)}, u32[]{:S(2)}, u32[]{:S(2)}) %collective-permute-start.9) | collective-permute-done | bytes 720928 | tf_op jit(solution)/shard_map/ppermute | solution.py:1762
  605.0 1.5 copy.160
  606.5 1.5 copy.161
  608.0 3.4 reduce-scatter.10.cloned.1.call-done
  611.4 1.2 slice.124
  612.8 0.7 collective-permute-start.7
  613.9 1.3 collective-permute-start.4
  617.1 1.2 fusion.2
  618.3 1.1 copy.157
  619.4 5.3 collective-permute-done.4
  624.7 0.9 collective-permute-start.5
  625.7 0.8 copy.159
  626.5 0.8 copy.158
  627.2 1.0 copy.156
  628.2 1.1 convert_add_fusion.1
  629.3 0.6 dynamic-slice_reduce_fusion.4
  629.9 0.6 dynamic-slice_reduce_fusion.2
  630.6 2.1 convert_bitcast_fusion
  632.7 1.0 copy.198
  (138 shorter events, 10.3 us)
Async XLA Ops:
  7.2 18.8 %copy-start = (f32[128,1024]{1,0:T(8,128)S(1)}, f32[128,1024]{1,0:T(8,128)}, u32[]{:S(2)}) copy-start(f32[128,1024]{1,0:T(8,128)} %param.21) | copy-start | bytes 1572868
  7.2 3.6 copy-start.10
  7.2 126.3 %all-gather.4.cloned.1.call-start = ((), (), s32[]{:S(2)}) async-start(), calls=%async_computation.3 | async-start | bytes 1310720 | tf_op jit(solution)/shard_map/all_gather | solution.py:1768
  8.5 1.4 collective-permute-start
  10.7 3.0 copy-start.11
  10.7 122.8 %all-gather.6.cloned.1.call-start = ((), (), s32[]{:S(2)}) async-start(), calls=%async_computation.4 | async-start | bytes 2621440 | tf_op jit(solution)/shard_map/all_gather | solution.py:1768
  11.0 1.6 collective-permute-start.1
  13.6 264.6 %all-gather.8.cloned.1.call-start = ((), (), s32[]{:S(2)}) async-start(), calls=%async_computation.5 | async-start | bytes 10813440 | tf_op jit(solution)/shard_map/all_gather | solution.py:1768
  14.5 7.7 %copy-start.18 = (f32[64]{0:T(128)S(1)}, f32[64]{0:T(128)}, u32[]{:S(2)}) copy-start(f32[64]{0:T(128)} %param.22) | copy-start | bytes 772
  14.5 7.7 %copy-start.16 = (f32[128]{0:T(128)S(1)}, f32[128]{0:T(128)}, u32[]{:S(2)}) copy-start(f32[128]{0:T(128)} %param.27) | copy-start | bytes 1540
  14.5 7.7 %copy-start.17 = (f32[128]{0:T(128)S(1)}, f32[128]{0:T(128)}, u32[]{:S(2)}) copy-start(f32[128]{0:T(128)} %param.20) | copy-start | bytes 1540
  14.5 8.3 %copy-start.7 = (f32[128,2816]{1,0:T(8,128)S(1)}, f32[128,2816]{1,0:T(8,128)}, u32[]{:S(2)}) copy-start(f32[128,2816]{1,0:T(8,128)} %param.29) | copy-start | bytes 4325380
  24.9 2.9 copy-start.8
  27.8 1.7 copy-start.4
  121.8 5.4 copy-start.15
  121.8 306.5 %reduce-scatter.6.cloned.1.call-start = ((), (), s32[]{:S(2)}) async-start(), calls=%async_computation.6 | async-start | bytes 3604480 | tf_op jit(solution)/shard_map/reduce_scatter | solution.py:1774
  121.8 3.5 collective-permute-start.2
  307.3 0.7 copy-start.14
  307.3 222.5 %reduce-scatter.8.cloned.1.call-start = ((), (), s32[]{:S(2)}) async-start(), calls=%async_computation.7 | async-start | bytes 7208960 | tf_op jit(solution)/shard_map/reduce_scatter | solution.py:1774
  428.3 183.1 %reduce-scatter.10.cloned.1.call-start = ((), (), s32[]{:S(2)}) async-start(), calls=%async_computation.8 | async-start | bytes 5406720
  529.8 1.6 copy-start.6
  533.6 2.0 copy-start.2
  535.6 1.4 copy-start.13
  535.7 24.3 %collective-permute-start.3 = (bf16[4,256,512]{2,1,0:T(8,128)(2,1)S(1)}, bf16[4,256,512]{2,1,0:T(8,128)(2,1)}, u32[]{:S(2)}, u32[]{:S(2)}) collective-permute-start(bf16[4,256,512]{2,1,0:T(8,128)(2,1)S(1)} %slice.135), channel_id=1, source_target_pairs={{0,1},{1,0},{2,3},{3,2},{4,5},{5,4},{6,7},{7,6},{8,9},{9,8},{10,11... | collective-permute-start | bytes 3145736 | tf_op jit(solution)/shard_map/ppermute | solution.py:1765
  539.4 27.7 %collective-permute-start.10 = (bf16[1,704,2,128]{3,1,2,0:T(8,128)(2,1)}, bf16[1,704,2,128]{3,1,2,0:T(8,128)(2,1)}, u32[]{:S(2)}, u32[]{:S(2)}) collective-permute-start(bf16[1,704,2,128]{3,1,2,0:T(8,128)(2,1)} %bitcast.112), channel_id=1, source_target_pairs={{0,2},{2,0},{4,6},{6,4},{8,10},{10,8},{12,14},{14,12},{16,18},{18,... | collective-permute-start | bytes 1081352 | tf_op jit(solution)/shard_map/ppermute | solution.py:1759
  571.8 6.0 copy-start.5
  574.8 3.0 copy-start.3
  574.9 12.1 %collective-permute-start.8 = (bf16[2,704,2,128]{3,1,2,0:T(8,128)(2,1)S(1)}, bf16[2,704,2,128]{3,1,2,0:T(8,128)(2,1)S(1)}, u32[]{:S(2)}, u32[]{:S(2)}) collective-permute-start(bf16[2,704,2,128]{3,1,2,0:T(8,128)(2,1)S(1)} %bitcast.135), channel_id=1, source_target_pairs={{0,2},{2,0},{4,6},{6,4},{8,10},{10,8},{12,14},{14,12},{16,18},{18,... | collective-permute-start | bytes 2162696 | tf_op jit(solution)/shard_map/ppermute | solution.py:1759
  576.5 10.2 %collective-permute-start.11 = (bf16[1,2,704,128]{3,2,1,0:T(8,128)(2,1)S(1)}, bf16[1,2,704,128]{3,2,1,0:T(8,128)(2,1)S(1)}, u32[]{:S(2)}, u32[]{:S(2)}) collective-permute-start(bf16[1,2,704,128]{3,2,1,0:T(8,128)(2,1)S(1)} %get-tuple-element.161), channel_id=1, source_target_pairs={{0,4},{2,6},{4,0},{6,2},{8,12},{10,14},{12,8},{14,10},{16,20},{18,... | collective-permute-start | bytes 1081352 | tf_op jit(solution)/shard_map/ppermute | solution.py:1762
  587.3 17.1 %collective-permute-start.9 = (bf16[2,2,704,128]{3,2,1,0:T(8,128)(2,1)S(1)}, bf16[2,2,704,128]{3,2,1,0:T(8,128)(2,1)S(1)}, u32[]{:S(2)}, u32[]{:S(2)}) collective-permute-start(bf16[2,2,704,128]{3,2,1,0:T(8,128)(2,1)S(1)} %get-tuple-element.155), channel_id=1, source_target_pairs={{0,4},{2,6},{4,0},{6,2},{8,12},{10,14},{12,8},{14,10},{16,20},{18,... | collective-permute-start | bytes 2162696 | tf_op jit(solution)/shard_map/ppermute | solution.py:1762
  611.4 2.3 copy-start.9
  612.6 2.6 slice-start
  612.8 17.8 %collective-permute-start.7 = (bf16[128,1024]{0,1:T(8,128)(2,1)S(1)}, bf16[128,1024]{0,1:T(8,128)(2,1)}, u32[]{:S(2)}, u32[]{:S(2)}) collective-permute-start(bf16[128,1024]{0,1:T(8,128)(2,1)S(1)} %copy.179), channel_id=1, source_target_pairs={{0,2},{2,0},{4,6},{6,4},{8,10},{10,8},{12,14},{14,12},{16,18},{18,... | collective-permute-start | bytes 786440 | tf_op jit(solution)/shard_map/ppermute | solution.py:1759
  613.9 10.8 %collective-permute-start.4 = (bf16[144,768]{0,1:T(8,128)(2,1)S(1)}, bf16[144,768]{0,1:T(8,128)(2,1)S(1)}, u32[]{:S(2)}, u32[]{:S(2)}) collective-permute-start(bf16[144,768]{0,1:T(8,128)(2,1)S(1)} %copy.170), channel_id=1, source_target_pairs={{0,1},{1,0},{2,3},{3,2},{4,5},{5,4},{6,7},{7,6},{8,9},{9,8},{10,11... | collective-permute-start | bytes 663560 | tf_op jit(solution)/shard_map/ppermute | solution.py:1765
  615.3 1.7 collective-permute-start.6
  624.7 3.5 collective-permute-start.5
  625.7 7.0 %copy-start.12 = (bf16[256,2048]{1,0:T(8,128)(2,1)S(1)}, bf16[256,2048]{1,0:T(8,128)(2,1)}, u32[]{:S(2)}) copy-start(bf16[256,2048]{1,0:T(8,128)(2,1)} %get-tuple-element.216) | copy-start | bytes 3145732
  628.2 5.4 copy-start.1
Sparse Core Ops, SparseCore 0:
  10.8 29.8 all-gather.3
  42.9 48.8 all-gather.5
  121.9 156.2 all-gather.7
  307.4 54.0 reduce-scatter.5
  428.4 101.3 reduce-scatter.7
  532.0 79.3 reduce-scatter.9

commit v5 on v4

--- a/solution.py
+++ b/solution.py
@@ -222,6 +222,7 @@
     double = 2 * hid
     block = cols // 2
     near = 4 * rows
+    early = lines // 2
 
     def kernel(*refs):
         grad_ref, grad_far, normed_ref, all_ref, hid_ref, a_ref, s_ref, resid_ref, gain_ref = refs[:9]
@@ -305,15 +306,13 @@
                 far_s.at[j], core_in.at[j], core_send.at[j], core_recv.at[j], across_core
             )
 
-        def to_side(j):
-            return remote(
-                side_s.at[j], side_in.at[j], side_send.at[j], side_recv.at[j], across_side
-            )
-
-        def to_half(j):
-            return remote(
-                half_s.at[j], half_in.at[j], half_send.at[j], half_recv.at[j], across_half
-            )
+        def first_hop(j, odd):
+            target = across_half if odd else across_side
+            return remote(side_s.at[j], side_in.at[j], side_send.at[j], side_recv.at[j], target)
+
+        def second_hop(j, odd):
+            target = across_side if odd else across_half
+            return remote(half_s.at[j], half_in.at[j], half_send.at[j], half_recv.at[j], target)
 
         @pl.loop(count // 2, count)
         def _(i):
@@ -321,10 +320,26 @@
 
         wait_all(joins)
 
-        @pl.loop(0, lines)
-        def _(j):
+        def far_tile(j):
             far_s[j] = matmul_tn(act_s[:, pl.ds(near, near)], w_s[:, tile(j, cols)]).astype(BF)
             to_core(j).start()
+
+        def near_tile(j, odd):
+            part = matmul_tn(act_s[:, pl.ds(0, near)], w_s[:, tile(j, cols)])
+            to_core(j).wait_recv()
+            part = part + core_in[j].astype(F32)
+            order = (0, 2, 1, 3) if odd else (0, 1, 2, 3)
+            for k, at in enumerate(order):
+                piece = part[at * rows : (at + 1) * rows]
+                to = pl.ds((k % 2) * rows, rows)
+                if k < 2:
+                    acc[j, to, :] = piece
+                else:
+                    side_s[j, to, :] = piece.astype(BF)
+            first_hop(j, odd).start()
+
+        far_tile(0)
+        far_tile(1)
 
         @pl.loop(0, count // 2)
         def _(i):
@@ -334,14 +349,15 @@
         hid_copy = pltpu.make_async_copy(hid_ref, a_s, f_sem.at[0])
         hid_copy.start()
 
-        @pl.loop(0, lines)
-        def _(j):
-            part = matmul_tn(act_s[:, pl.ds(0, near)], w_s[:, tile(j, cols)])
-            to_core(j).wait_recv()
-            part = part + core_in[j].astype(F32)
-            acc[j] = part[: 2 * rows]
-            side_s[j] = part[2 * rows :].astype(BF)
-            to_side(j).start()
+        @pl.loop(0, lines // 2)
+        def _(p):
+            near_tile(2 * p, False)
+            near_tile(2 * p + 1, True)
+
+            @pl.when(p + 1 < lines // 2)
+            def _():
+                far_tile(2 * p + 2)
+                far_tile(2 * p + 3)
 
         pl.semaphore_signal(free_sem, inc=1, device_id=across_core, device_id_type=MESH)
         wait_all(reload)
@@ -391,13 +407,15 @@
             for copy in part_copies(j):
                 copy.start()
 
-        @pl.loop(0, lines)
-        def _(j):
-            to_side(j).wait_recv()
-            part = acc[j] + side_in[j].astype(F32)
-            acc[j] = part
-            half_s[j] = part[rows:].astype(BF)
-            to_half(j).start()
+        @pl.loop(0, lines // 2)
+        def _(p):
+            for odd in (False, True):
+                j = 2 * p + int(odd)
+                first_hop(j, odd).wait_recv()
+                part = acc[j] + side_in[j].astype(F32)
+                acc[j, pl.ds(0, rows), :] = part[:rows]
+                half_s[j] = part[rows:].astype(BF)
+                second_hop(j, odd).start()
 
         for j in range(max(lines - 2, 0), lines):
             wait_all(part_copies(j))
@@ -407,19 +425,21 @@
                 away_out.at[j], away_in.at[j], away_send.at[j], away_recv.at[j], across_side
             )
 
-        @pl.loop(0, lines)
-        def _(j):
-            to_side_out(j).start()
-
         res_copy.wait()
         own_copy.wait()
         res = res_s[...]
         inverse = inv_rms(res)
 
-        @pl.loop(0, lines)
-        def _(j):
-            to_half(j).wait_recv()
-            acc[j, pl.ds(0, rows), :] = acc[j, pl.ds(0, rows), :] + half_in[j].astype(F32)
+        @pl.loop(0, lines // 2)
+        def _(p):
+            for odd in (False, True):
+                j = 2 * p + int(odd)
+                second_hop(j, odd).wait_recv()
+                acc[j, pl.ds(0, rows), :] = acc[j, pl.ds(0, rows), :] + half_in[j].astype(F32)
+
+        @pl.loop(0, early)
+        def _(j):
+            to_side_out(j).start()
 
         mean = jnp.zeros((rows, 1), F32)
         for j in range(lines):
@@ -470,12 +490,18 @@
             copy.start()
         sends[0].wait_recv()
         sends[2].start()
-        @pl.loop(0, lines)
-        def _(j):
-            to_core(j).wait_send()
-            to_side(j).wait_send()
+
+        @pl.loop(0, lines // 2)
+        def _(p):
+            for odd in (False, True):
+                j = 2 * p + int(odd)
+                to_core(j).wait_send()
+                first_hop(j, odd).wait_send()
+                second_hop(j, odd).wait_send()
+
+        @pl.loop(0, early)
+        def _(j):
             to_side_out(j).wait()
-            to_half(j).wait_send()
 
         sends[0].wait_send()
         sends[1].wait()
@@ -489,7 +515,7 @@
         jax.ShapeDtypeStruct((4 * rows, width), BF),
         jax.ShapeDtypeStruct((lines, 2 * rows, cols), BF),
         jax.ShapeDtypeStruct((lines, 2 * rows, cols), BF),
-        jax.ShapeDtypeStruct((lines, 2 * rows, cols), BF),
+        jax.ShapeDtypeStruct((early, 2 * rows, cols), BF),
     )
     args = (grads, grads_far, normed, weights, hidden, a_fac, s_fac, residual, gain)
     vmem = pl.BlockSpec(memory_space=pltpu.VMEM)
@@ -534,8 +560,8 @@
             dma((3,)),
             dma((2,)),
             dma((2, 2)),
-            dma((lines,)),
-            dma((lines,)),
+            dma((early,)),
+            dma((early,)),
             pltpu.SemaphoreType.REGULAR,
         ],
         compiler_params=pltpu.CompilerParams(
@@ -550,8 +576,9 @@
     return first * cos_vals - second * sin_vals, second * cos_vals + first * sin_vals
 
 
-def gather_first(x_own, grad_own, piece, gain_piece, ffn_low, lines):
-    rows, width = x_own.shape
+def gather_first(tokens, grad_own, piece, gain_piece, ffn_low, lines):
+    rows, width = tokens.shape
+    edge, block = width // 2, width // (2 * lines)
     hid = ffn_low.shape[1] // 4
     shard, part_cols = piece.shape
 
@@ -563,9 +590,12 @@
         ffn_ref,
         x_out,
         dy_out,
+        far_out,
         w_out,
         g_out,
         ffn_out,
+        tok_s,
+        x_s,
         local_sem,
         up_send,
         up_recv,
@@ -573,8 +603,6 @@
         down_recv,
         side_send,
         side_recv,
-        half_send,
-        half_recv,
         core_send,
         core_recv,
         row_send,
@@ -589,9 +617,8 @@
         above = ((place + 4) % (4 * lines), half)
         below = ((place + 4 * lines - 4) % (4 * lines), half)
 
-        def weight(r, at, far):
-            column = pl.multiple_of(jnp.where(far, 1 - half, half) * part_cols, 128)
-            return w_out.at[r, at, core, :, pl.ds(column, part_cols)]
+        def weight(r, at):
+            return w_out.at[r, at]
 
         def gain(r, at):
             return g_out.at[r, at, core]
@@ -599,8 +626,8 @@
         def both(r, at, to_r, sends, recvs, where, target):
             return [
                 remote(
-                    weight(r, at, False),
-                    weight(to_r, at, False),
+                    weight(r, at),
+                    weight(to_r, at),
                     sends.at[where, 0],
                     recvs.at[where, 0],
                     target,
@@ -625,31 +652,13 @@
         def to_side(at):
             return both(0, at, 1, side_send, side_recv, at, across_side)
 
-        def to_half(r, at):
-            ref = weight(r, at, False)
-            return remote(ref, ref, half_send.at[r, at], half_recv.at[r, at], across_half)
-
-        def from_half(r, at):
-            ref = weight(r, at, True)
-            return remote(ref, ref, half_send.at[r, at], half_recv.at[r, at], across_half)
-
-        def to_core(r, at, kind):
-            ref = gain(r, at) if kind == 2 else weight(r, at, kind == 1)
-            return remote(
-                ref, ref, core_send.at[r, at, kind], core_recv.at[r, at, kind], across_core
-            )
-
-        def from_core(r, at, kind):
-            if kind == 2:
-                ref = g_out.at[r, at, 1 - core]
-            else:
-                column = (1 - half if kind == 1 else half) * part_cols
-                ref = w_out.at[
-                    r, at, 1 - core, :, pl.ds(pl.multiple_of(column, 128), part_cols)
-                ]
-            return remote(
-                ref, ref, core_send.at[r, at, kind], core_recv.at[r, at, kind], across_core
-            )
+        def to_core(r, at):
+            ref = gain(r, at)
+            return remote(ref, ref, core_send.at[r, at], core_recv.at[r, at], across_core)
+
+        def from_core(r, at):
+            ref = g_out.at[r, at, 1 - core]
+            return remote(ref, ref, core_send.at[r, at], core_recv.at[r, at], across_core)
 
         def start(copies):
             for copy in copies:
@@ -657,9 +666,7 @@
 
         def spread_near(at):
             start(to_side(at))
-            to_half(0, at).start()
-            to_core(0, at, 0).start()
-            to_core(0, at, 2).start()
+            to_core(0, at).start()
 
         def slot(ref, j):
             return ref.at[pl.ds(j * rows, rows)]
@@ -668,12 +675,16 @@
             return remote(src, dst, row_send.at[j], row_recv.at[j], target)
 
         moves = [
-            hop(0, x_ref, slot(x_out, 1), across_half),
-            hop(1, x_ref, slot(x_out, 2), across_core),
+            hop(0, x_s, slot(x_out, 1), across_half),
+            hop(1, x_s, slot(x_out, 2), across_core),
             hop(2, slot(x_out, 1), slot(x_out, 3), across_core),
             hop(3, dy_ref, slot(dy_out, 1), across_side),
             hop(4, dy_ref, slot(dy_out, 2), across_core),
             hop(5, slot(dy_out, 1), slot(dy_out, 3), across_core),
+            hop(6, dy_ref, slot(far_out, 0), across_half),
+            hop(7, slot(dy_out, 1), slot(far_out, 1), across_half),
+            hop(8, slot(far_out, 0), slot(far_out, 2), across_core),
+            hop(9, slot(far_out, 1), slot(far_out, 3), across_core),
         ]
 
         def units(to_side_at, to_core_at):
@@ -698,9 +709,9 @@
             )
         ]
         locals_ = [
-            pltpu.make_async_copy(piece_ref, weight(0, line, False), local_sem.at[0]),
+            pltpu.make_async_copy(piece_ref, weight(0, line), local_sem.at[0]),
             pltpu.make_async_copy(gain_ref, gain(0, line), local_sem.at[1]),
-            pltpu.make_async_copy(x_ref, slot(x_out, 0), local_sem.at[2]),
+            pltpu.make_async_copy(x_ref, tok_s, local_sem.at[2]),
             pltpu.make_async_copy(dy_ref, slot(dy_out, 0), local_sem.at[3]),
             pltpu.make_async_copy(units(side, core), ffn_out.at[me], local_sem.at[4]),
         ]
@@ -717,8 +728,19 @@
             start(downward(0))
 
         spread_near(line)
+        start(shares)
+        moves[3].start()
+        moves[6].start()
+        moves[4].start()
+        locals_[2].wait()
+        for j in range(lines):
+            first = tok_s[:, pl.ds(2 * j * block, block)].astype(F32)
+            second = tok_s[:, pl.ds((2 * j + 1) * block, block)].astype(F32)
+            x_s[:, pl.ds(j * block, block)] = jnp.where(side == 0, first, second).astype(BF)
+            x_s[:, pl.ds(edge + j * block, block)] = jnp.where(side == 0, second, first).astype(BF)
         start(moves[:2])
-        start(shares)
+        x_copy = pltpu.make_async_copy(x_s, slot(x_out, 0), local_sem.at[5])
+        x_copy.start()
         for step in range(1, lines):
 
             @pl.when(line >= step)
@@ -745,30 +767,26 @@
 
                 spread_near(line + step)
 
-        moves[3].start()
-        moves[4].start()
+        moves[0].wait_recv()
+        moves[2].start()
+        moves[3].wait_recv()
+        moves[7].start()
+        moves[5].start()
         for at in range(lines):
             for copy in to_side(at):
                 copy.wait_recv()
-            to_half(1, at).start()
-            to_core(1, at, 0).start()
-            to_core(1, at, 2).start()
-        moves[0].wait_recv()
-        moves[2].start()
-        for r in range(2):
-            for at in range(lines):
-                from_half(r, at).wait_recv()
-                to_core(r, at, 1).start()
-        moves[3].wait_recv()
-        moves[5].start()
-        for j in (1, 2, 4, 5):
+            to_core(1, at).start()
+        moves[6].wait_recv()
+        moves[8].start()
+        moves[7].wait_recv()
+        moves[9].start()
+        for j in (1, 2, 4, 5, 8, 9):
             moves[j].wait_recv()
         for copy in shares:
             copy.wait_recv()
         for r in range(2):
             for at in range(lines):
-                for kind in range(3):
-                    from_core(r, at, kind).wait_recv()
+                from_core(r, at).wait_recv()
 
         for step in range(lines - 1):
 
@@ -786,29 +804,31 @@
             for copy in to_side(at):
                 copy.wait_send()
             for r in range(2):
-                to_half(r, at).wait_send()
-                for kind in range(3):
-                    to_core(r, at, kind).wait_send()
+                to_core(r, at).wait_send()
         for copy in moves + shares:
             copy.wait_send()
-        wait_all(locals_[2:])
+        wait_all(locals_[3:])
+        x_copy.wait()
 
     out_shape = (
         jax.ShapeDtypeStruct((4 * rows, width), BF),
         jax.ShapeDtypeStruct((4 * rows, width), BF),
-        jax.ShapeDtypeStruct((2, lines, 2, shard, 2 * part_cols), BF),
+        jax.ShapeDtypeStruct((4 * rows, width), BF),
+        jax.ShapeDtypeStruct((2, lines, shard, part_cols), BF),
         jax.ShapeDtypeStruct((2, lines, 2, 16, part_cols), BF),
         jax.ShapeDtypeStruct((4, 3, hid, shard), BF),
     )
-    args = (x_own, grad_own, piece, gain_piece, ffn_low)
+    args = (tokens, grad_own, piece, gain_piece, ffn_low)
     dma = pltpu.SemaphoreType.DMA
     return pl.pallas_call(
         kernel,
         out_shape=out_shape,
         in_specs=[ANY] * 5,
-        out_specs=(ANY,) * 5,
+        out_specs=(ANY,) * 6,
         scratch_shapes=[
-            dma((5,)),
+            pltpu.VMEM((rows, width), BF),
+            pltpu.VMEM((rows, width), BF),
+            dma((6,)),
             dma((lines, 2)),
             dma((lines, 2)),
             dma((lines, 2)),
@@ -817,10 +837,8 @@
             dma((lines, 2)),
             dma((2, lines)),
             dma((2, lines)),
-            dma((2, lines, 3)),
-            dma((2, lines, 3)),
-            dma((6,)),
-            dma((6,)),
+            dma((10,)),
+            dma((10,)),
             dma((3,)),
             dma((3,)),
         ],
@@ -834,8 +852,7 @@
 
 def attn_first(
     x_all,
-    grad_near,
-    qkv_set,
+    qkv_part,
     q_up_mine,
     out_mine,
     bias,
@@ -853,7 +870,8 @@
     edge, feats = out_mine.shape
     rank = 2 * q_up_mine.shape[0]
     q_block = rank // (2 * lines)
-    wide = qkv_set.shape[1]
+    part_cols = qkv_part.shape[3]
+    wide = 2 * part_cols
     head_dim = (wide - rank) // 2
     half_dim = head_dim // 2
     heads = feats // head_dim
@@ -866,7 +884,6 @@
 
     def kernel(
         x_ref,
-        dy_ref,
         qkv_ref,
         up_ref,
         mine_ref,
@@ -886,7 +903,7 @@
         theirs_out,
         res_out,
         norm_out,
-        dy_out,
+        qkv_out,
         up_out,
         x_s,
         n_s,
@@ -923,18 +940,20 @@
         up_send,
         up_recv,
         up_sem,
-        dy_send,
-        dy_recv,
+        qkv_sem,
+        qkv_half_send,
+        qkv_half_recv,
+        qkv_core_send,
+        qkv_core_recv,
     ):
         across_core, across_side, across_half = peers()
         place = lax.axis_index("dp")
-        core, side = place % 2, (place // 2) % 2
+        core, side, half = place % 2, (place // 2) % 2, lax.axis_index("tensor")
         pairs = [
             (ref, x_s.at[pl.ds(j * rows, rows)])
             for j, ref in enumerate(split_rows(x_ref, 4))
         ]
         pairs += [
-            (qkv_ref, qkv_s),
             (cos_ref, cos_s),
             (sin_ref, sin_s),
             (bias_ref, bias_s),
@@ -971,22 +990,42 @@
             up_copy(j).start()
             up_local(j).start()
 
-        def slot_of(ref, j):
-            return ref.at[pl.ds(j * rows, rows)]
-
-        grad_moves = [
-            remote(slot_of(src, j), slot_of(dy_out, k), dy_send.at[k], dy_recv.at[k], target)
-            for k, (src, j, target) in enumerate(
-                (
-                    (dy_ref, 0, across_half),
-                    (dy_ref, 1, across_half),
-                    (dy_out, 0, across_core),
-                    (dy_out, 1, across_core),
-                )
+        def place_of(r, at, of_core, of_half):
+            row = ((r * lines + at) * 2 + of_core) * shard
+            column = pl.multiple_of(of_half * part_cols, 128)
+            return qkv_s.at[
+                pl.ds(pl.multiple_of(row, 16), shard), pl.ds(column, part_cols)
+            ]
+
+        def qkv_local(r, at):
+            return pltpu.make_async_copy(
+                qkv_ref.at[r, at], place_of(r, at, core, half), qkv_sem.at[r, at]
             )
-        ]
-        grad_moves[0].start()
-        grad_moves[1].start()
+
+        def qkv_half(r, at, of_half):
+            return remote(
+                qkv_ref.at[r, at],
+                place_of(r, at, core, of_half),
+                qkv_half_send.at[r, at],
+                qkv_half_recv.at[r, at],
+                across_half,
+            )
+
+        def qkv_core(r, at, far, of_core):
+            dst = place_of(r, at, of_core, 1 - half if far else half)
+            return remote(
+                place_of(r, at, core, 1 - half) if far else qkv_ref.at[r, at],
+                dst,
+                qkv_core_send.at[r, at, int(far)],
+                qkv_core_recv.at[r, at, int(far)],
+                across_core,
+            )
+
+        every = [(r, at) for r in range(2) for at in range(lines)]
+        for r, at in every:
+            qkv_half(r, at, half).start()
+            qkv_core(r, at, False, core).start()
+            qkv_local(r, at).start()
 
         @pl.loop(0, sends_y)
         def _(j):
@@ -1005,7 +1044,14 @@
                 second = low[:, (2 * j + 1) * shard : (2 * j + 2) * shard].astype(F32)
                 nc_s[at, pl.ds(j * shard, shard)] = jnp.where(core == 0, first, second).astype(BF)
 
-        wait_all(loads[4:7])
+        wait_all(loads[4:6])
+        for r, at in every:
+            qkv_half(r, at, 1 - half).wait_recv()
+            qkv_core(r, at, True, core).start()
+        for r, at in every:
+            qkv_local(r, at).wait()
+            qkv_core(r, at, False, 1 - core).wait_recv()
+            qkv_core(r, at, True, 1 - core).wait_recv()
 
         per_half = rank // 2 // step
 
@@ -1032,7 +1078,7 @@
             latent = lat_s[at, :]
             lat_n_s[at, :] = (latent * inv_rms(latent) * gain_q_ref[...]).astype(BF)
 
-        loads[7].wait()
+        loads[6].wait()
         for j in range(lines):
             up_local(j).wait()
             up_copy(j).wait()
@@ -1055,6 +1101,7 @@
                     (lat_s.at[pl.ds(0, rows)], lat_out),
                     (nc_s, n_out),
                     (up_s, up_out),
+                    (qkv_s, qkv_out),
                 )
             )
         ]
@@ -1070,7 +1117,7 @@
             probs = (expd / jnp.sum(expd, axis=-1, keepdims=True)).astype(BF)
             mixed_s[at, lanes] = matmul(probs, v_s[at, :]).astype(BF)
 
-        mixed_copy = pltpu.make_async_copy(mixed_s, mixed_out, out_sem.at[7])
+        mixed_copy = pltpu.make_async_copy(mixed_s, mixed_out, out_sem.at[8])
         mixed_copy.start()
 
         def core_copy(j):
@@ -1091,10 +1138,7 @@
             half_s[j] = part[rows:].astype(BF)
             half_copy(j).start()
 
-        loads[8].wait()
-        for j in range(2):
-            grad_moves[j].wait_recv()
-            grad_moves[2 + j].start()
+        loads[7].wait()
 
         @pl.loop(0, tiles // 2)
         def _(j):
@@ -1104,16 +1148,16 @@
         def _(j):
             near_tile(j)
 
-        @pl.loop(0, sends_y)
-        def _(j):
-            theirs_copy(j).wait()
-
-        theirs_local = pltpu.make_async_copy(w_s.at[pl.ds(edge, edge)], theirs_out, out_sem.at[8])
+        per_tile = cols // step
+
+        @pl.loop(tiles // 2, tiles)
+        def _(j):
+            for k in range(per_tile):
+                theirs_copy((j - tiles // 2) * per_tile + k).wait()
+            far_tile(j)
+
+        theirs_local = pltpu.make_async_copy(w_s.at[pl.ds(edge, edge)], theirs_out, out_sem.at[9])
         theirs_local.start()
-
-        @pl.loop(tiles // 2, tiles)
-        def _(j):
-            far_tile(j)
 
         @pl.loop(tiles // 2, tiles)
         def _(j):
@@ -1138,9 +1182,9 @@
                 res_s[:, at] = picked
                 own_s[:, at] = (picked * inverse * gain).astype(BF)
 
-        res_copy = pltpu.make_async_copy(res_s, res_out, out_sem.at[9])
+        res_copy = pltpu.make_async_copy(res_s, res_out, out_sem.at[10])
         res_copy.start()
-        own_copy = pltpu.make_async_copy(own_s, norm_out.at[pl.ds(0, rows)], out_sem.at[10])
+        own_copy = pltpu.make_async_copy(own_s, norm_out.at[pl.ds(0, rows)], out_sem.at[11])
         own_copy.start()
         part_rows = rows // 2
 
@@ -1174,10 +1218,12 @@
         hops[2].wait_recv()
         for copy in hops[5:]:
             copy.wait_recv()
-        for copy in grad_moves[2:]:
-            copy.wait_recv()
-        for copy in hops + grad_moves:
+        for copy in hops:
             copy.wait_send()
+        for r, at in every:
+            qkv_half(r, at, half).wait_send()
+            qkv_core(r, at, False, core).wait_send()
+            qkv_core(r, at, True, core).wait_send()
 
         @pl.loop(0, tiles)
         def _(j):
@@ -1204,13 +1250,12 @@
         low(edge, feats),
         jax.ShapeDtypeStruct((rows, width), F32),
         low(8 * rows, width),
-        low(4 * rows, width),
+        low(width, wide),
         low(rank, feats),
     )
     args = (
         x_all,
-        grad_near,
-        qkv_set,
+        qkv_part,
         q_up_mine,
         out_mine,
         bias,
@@ -1250,7 +1295,7 @@
             pltpu.VMEM((rows, width), F32),
             pltpu.VMEM((rows, width), F32),
             pltpu.VMEM((rows, width), BF),
-            dma((9,)),
+            dma((8,)),
             dma((sends_y,)),
             dma((sends_y,)),
             dma((tiles,)),
@@ -1259,12 +1304,15 @@
             dma((tiles,)),
             dma((8,)),
             dma((8,)),
-            dma((11,)),
+            dma((12,)),
             dma((lines,)),
             dma((lines,)),
             dma((lines,)),
-            dma((4,)),
-            dma((4,)),
+            dma((2, lines)),
+            dma((2, lines)),
+            dma((2, lines)),
+            dma((2, lines, 2)),
+            dma((2, lines, 2)),
         ],
         compiler_params=pltpu.CompilerParams(
             vmem_limit_bytes=vmem_bytes, collective_id=2, has_side_effects=True
@@ -1399,7 +1447,7 @@
             (up_ref, up_s),
             (lat_n_ref, lat_n_s),
             (lat_ref, lat_s),
-            (x_ref, x_s),
+            (x_ref.at[pl.ds(0, rows)], x_s),
             (res_ref, res_s),
             (qkv_ref, w_s),
             (n_ref, q_s),
@@ -1744,6 +1792,140 @@
     )(*args)
 
 
+def settle(near, given, give, residual, parts, start):
+    lines, pair_rows, cols = near.shape
+    rows, width = residual.shape
+    _, kinds, hid, shard = parts.shape
+
+    def kernel(
+        near_ref,
+        given_ref,
+        give_ref,
+        res_ref,
+        parts_ref,
+        out_ref,
+        parts_out,
+        near_s,
+        away_s,
+        half_s,
+        half_in,
+        res_s,
+        out_s,
+        load_sem,
+        near_sem,
+        away_sem,
+        late_send,
+        late_recv,
+        half_send,
+        half_recv,
+        share_send,
+        share_recv,
+    ):
+        across_core, across_side, across_half = peers()
+        place, half = lax.axis_index("dp"), lax.axis_index("tensor")
+        core, side, line = place % 2, (place // 2) % 2, place // 4
+        across_both = (line * 4 + (1 - side) * 2 + 1 - core, half)
+        me = side * 2 + core
+        nears = [
+            pltpu.make_async_copy(near_ref.at[j], near_s.at[j], near_sem.at[j])
+            for j in range(lines)
+        ]
+        aways = [
+            pltpu.make_async_copy(given_ref.at[j], away_s.at[j], away_sem.at[j])
+            for j in range(start)
+        ]
+        res_copy = pltpu.make_async_copy(res_ref, res_s, load_sem.at[0])
+        local_copy = pltpu.make_async_copy(parts_ref.at[me], parts_out.at[me], load_sem.at[1])
+        for copy in nears + aways + [res_copy, local_copy]:
+            copy.start()
+        greet((across_core, across_side, across_half, across_both))
+        lates = [
+            remote(
+                give_ref.at[j],
+                away_s.at[j],
+                late_send.at[j - start],
+                late_recv.at[j - start],
+                across_side,
+            )
+            for j in range(start, lines)
+        ]
+        shares = [
+            remote(parts_ref.at[to], parts_out.at[me], share_send.at[j], share_recv.at[j], target)
+            for j, (to, target) in enumerate(
+                (
+                    ((1 - side) * 2 + 1 - core, across_both),
+                    ((1 - side) * 2 + core, across_side),
+                    (side * 2 + 1 - core, across_core),
+                )
+            )
+        ]
+        for copy in lates + shares:
+            copy.start()
+        halves = [
+            remote(half_s.at[j], half_in.at[j], half_send.at[j], half_recv.at[j], across_half)
+            for j in range(lines)
+        ]
+        res_copy.wait()
+        for j in range(lines):
+            nears[j].wait()
+            if j < start:
+                aways[j].wait()
+            else:
+                lates[j - start].wait_recv()
+            total = near_s[j].astype(F32) + away_s[j].astype(F32)
+            half_s[j] = total[rows:].astype(BF)
+            halves[j].start()
+            at = pl.ds(j * cols, cols)
+            res_s[:, at] = res_s[:, at] + total[:rows]
+        for j in range(lines):
+            halves[j].wait_recv()
+            at = pl.ds(j * cols, cols)
+            out_s[:, at] = (res_s[:, at] + half_in[j].astype(F32)).astype(BF)
+        out_copy = pltpu.make_async_copy(out_s, out_ref, load_sem.at[0])
+        out_copy.start()
+        local_copy.wait()
+        for copy in shares:
+            copy.wait()
+        for copy in lates + halves:
+            copy.wait_send()
+        out_copy.wait()
+
+    out_shape = (
+        jax.ShapeDtypeStruct((rows, width), BF),
+        jax.ShapeDtypeStruct(parts.shape, BF),
+    )
+    args = (near, given, give, residual, parts)
+    dma = pltpu.SemaphoreType.DMA
+    return pl.pallas_call(
+        kernel,
+        out_shape=out_shape,
+        in_specs=[ANY] * 5,
+        out_specs=(ANY, ANY),
+        scratch_shapes=[
+            pltpu.VMEM((lines, pair_rows, cols), BF),
+            pltpu.VMEM((lines, pair_rows, cols), BF),
+            pltpu.VMEM((lines, rows, cols), BF),
+            pltpu.VMEM((lines, rows, cols), BF),
+            pltpu.VMEM((rows, width), F32),
+            pltpu.VMEM((rows, width), BF),
+            dma((2,)),
+            dma((lines,)),
+            dma((start,)),
+            dma((lines - start,)),
+            dma((lines - start,)),
+            dma((lines,)),
+            dma((lines,)),
+            dma((3,)),
+            dma((3,)),
+        ],
+        compiler_params=pltpu.CompilerParams(
+            vmem_limit_bytes=vmem_bytes, collective_id=4, has_side_effects=True
+        ),
+        cost_estimate=cost(1, args + out_shape),
+        name="settle",
+    )(*args)
+
+
 def build(n):
     lines = n // 4
 
@@ -1819,22 +2001,11 @@
                 jnp.concatenate([second, first], axis=axis),
             )
 
-        def to_rel(value):
-            rows = value.shape[0]
-            split = value.reshape(rows, lines, 2, block)
-            mine = lax.dynamic_index_in_dim(split, side, 2, keepdims=False)
-            theirs = lax.dynamic_index_in_dim(split, 1 - side, 2, keepdims=False)
-            return jnp.concatenate(
-                [mine.reshape(rows, lines * block), theirs.reshape(rows, lines * block)], axis=1
-            )
-
         def from_rel(value):
             rows = value.shape[0]
             mine = value[:, : lines * block].reshape(rows, lines, 1, block)
             theirs = value[:, lines * block :].reshape(rows, lines, 1, block)
             return order(side, mine, theirs, 2).reshape(rows, width)
-
-        x_low = to_rel(tokens)
 
         mixed_cols = jnp.concatenate(
             [
@@ -1862,14 +2033,13 @@
         out_mine = spread(out_proj.T)
 
         ffn_low = jnp.stack([gate_proj.T, up_proj.T, down_proj]).astype(BF)
-        x_all, grad_near, qkv_set, gain_set, ffn_parts = gather_first(
-            x_low, out_grad, mixed_cols, gain_rows, ffn_low, lines
+        x_all, grad_near, grad_far, qkv_part, gain_set, ffn_parts = gather_first(
+            tokens, out_grad, mixed_cols, gain_rows, ffn_low, lines
         )
         ffn_piece = ffn_parts.reshape(4, 3 * hid, shard).transpose(1, 0, 2)
         ffn_w = line_gather(ffn_piece.reshape(3 * hid, 2 * block)).reshape(
             lines, 3 * hid, 2 * block
         )
-        qkv_set = qkv_set.reshape(width, 2 * qkv_cols)
         gain_both = gain_set[:, :, :, 0, :]
         q_c, k_c = rank // 2, rank // 2 + head_dim // 2
         gain_one = gain_both[..., :shard].reshape(width).astype(F32)
@@ -1919,12 +2089,11 @@
             out_theirs,
             residual,
             normed_two,
-            grad_far,
+            qkv_set,
             q_up_set,
         ) = attn_first(
             x_all,
-            grad_near,
-            qkv_set,
+            qkv_part,
             q_up_mine,
             out_mine,
             bias.astype(BF),
@@ -1945,22 +2114,13 @@
         def line_part(value):
             count = value.shape[1] // hid
             mine = line_sum(value.reshape(lines * count * hid, 2 * block), queue)
-            mine = mine.reshape(count, hid, 2, 2, shard)
-            keep = lax.dynamic_index_in_dim(mine, core, 3, keepdims=False)
-            give = lax.dynamic_index_in_dim(mine, 1 - core, 3, keepdims=False)
-            cores = order(core, keep[:, None], core_swap(give)[:, None], 1)
-            keep = lax.dynamic_index_in_dim(cores, side, 3, keepdims=False)
-            give = lax.dynamic_index_in_dim(cores, 1 - side, 3, keepdims=False)
-            sides = order(side, keep[:, None], side_swap(give)[:, None], 1)
-            return sides.reshape(count, 4 * hid, shard).astype(F32)
-
-        down_total = line_part(d_down)[0]
-        d_gate_up, d_resid, d_ffn_gain, d_attn, ffn_near, _, ffn_away = ffn_back(
+            return mine.reshape(count, hid, 4, shard).transpose(2, 0, 1, 3)
+
+        down_part = line_part(d_down)
+        d_gate_up, d_resid, d_ffn_gain, d_attn, ffn_near, ffn_give, ffn_away = ffn_back(
             grad_near, grad_far, ffn_w, hidden, a_fac, s_fac, normed_two, residual, gain_two_abs
         )
-        gate_up_total = line_part(d_gate_up)
-        gate_total = gate_up_total[0].T
-        up_total = gate_up_total[1].T
+        gate_up_part = line_part(d_gate_up)
 
         sums, in_grad = attn_back(
             d_attn,
@@ -1979,17 +2139,12 @@
             gain_q[None, :],
             normed_rows,
             qkv_set,
-            x_low,
+            x_all,
             gain_one[None, :],
             d_resid,
             d_ffn_gain,
             lines,
         )
-        ffn_away, ffn_near = after((ffn_away, ffn_near), in_grad)
-        ffn_pair = ffn_near.astype(F32) + ffn_away.astype(F32)
-        ffn_give = ffn_pair[:, own_rows:].astype(BF)
-        ffn_own = ffn_pair[:, :own_rows] + half_swap(ffn_give).astype(F32)
-        output = (residual + ffn_own.transpose(1, 0, 2).reshape(own_rows, width)).astype(BF)
         rows_sum = block + 2 * q_shard + shard + 16
         mine = line_sum(sums.reshape(lines * rows_sum, feats), queue)
 
@@ -1999,6 +2154,12 @@
             away = lax.dynamic_slice_in_dim(value, (1 - core) * rows, rows, 0)
             return order(core, keep, core_swap(away), 1).astype(F32)
 
+        parts = jnp.concatenate([gate_up_part, down_part], axis=1)
+        output, parts = settle(
+            ffn_near, ffn_away, ffn_give, residual, after(parts, in_grad), ffn_away.shape[0]
+        )
+        totals = parts.transpose(1, 0, 2, 3).reshape(3, 4 * hid, shard).astype(F32)
+        gate_total, up_total, down_total = totals[0].T, totals[1].T, totals[2]
         out_total = core_rows(mine[:block]).T
         q_up_total = core_rows(mine[block : block + 2 * q_shard])
         d_qkv_sum = mine[block + 2 * q_shard :, :qkv_cols]

time: 650 us -> 611 us (0.940)
  waiting for transfers between devices: 69.8 us -> 44.1 us
  Pallas kernels: 468 us -> 492 us
  local copies, waits for them, and re-layouts: 50 us -> 28.9 us
    pallas_call x0 -> x1, Pallas kernels: none -> 48.9 us  [settle(): pl.pallas_call(kernel, out_shape=out_shape, in_specs=[ANY] * 5, out_specs...]
    ppermute x2 -> x0, waiting for transfers between devices: 22.4 us -> none  [side_swap(): return lax.ppermute(value, 'dp', side_pairs)]
    pallas_call x1, Pallas kernels: 120 us -> 97.5 us  [ffn_back(): pl.pallas_call(kernel, out_shape=out_shape, in_specs=[ANY] * (len(args) -...]
    ppermute x2 -> x1, waiting for transfers between devices: 24.9 us -> 5.24 us  [half_swap(): return lax.ppermute(value, 'tensor', [(0, 1), (1, 0)])]
    unnamed x7, waiting for transfers between devices: 3.46 us -> 19.1 us
    dynamic_slice x7 -> x0, local copies, waits for them, and re-layouts: 12.1 us -> none  [the longest x1 6.55 us: to_rel(): theirs = lax.dynamic_index_in_dim(split, 1 - side, 2, keepdims=False)]
    unnamed x63 -> x47, local copies, waits for them, and re-layouts: 16.8 us -> 10.7 us
  transfers between devices with their start and end apart: 18 -> 13, of which waited for: 10 -> 6; matrix products, arithmetic and copies ran while one was open for 10% -> 7% of each run, Pallas kernels for 68% -> 76%
where the time goes in v5:
time: 611 us; the launch traced here: 607 us
  Pallas kernels  492 us (81%)
  waiting for transfers between devices  44.1 us (7%)
  local copies, waits for them, and re-layouts  28.9 us (5%)
  other arithmetic  20.3 us (3%)
  between operations  17.3 us (3%)
    pallas_call x1, Pallas kernels, attn_first(): pl.pallas_call(kernel, out_shape=out_shape, in_specs=[vmem if a.shape[0]...  125 us
    pallas_call x1, Pallas kernels, attn_back(): pl.pallas_call(kernel, out_shape=out_shape, in_specs=[vmem if a.shape[0]...  100 us
    pallas_call x1, Pallas kernels, ffn_back(): pl.pallas_call(kernel, out_shape=out_shape, in_specs=[ANY] * (len(args) -...  97.5 us
    pallas_call x1, Pallas kernels, gather_first(): pl.pallas_call(kernel, out_shape=out_shape, in_specs=[ANY] * 5, out_specs...  90.8 us
    pallas_call x1, Pallas kernels, settle(): pl.pallas_call(kernel, out_shape=out_shape, in_specs=[ANY] * 5, out_specs...  48.9 us
    pallas_call x1, Pallas kernels, ffn_first(): pl.pallas_call(kernel, out_shape=out_shape, in_specs=[ANY] * len(args), o...  29 us
    unnamed x7, waiting for transfers between devices  19.1 us
    all_gather x3, waiting for transfers between devices, line_gather(): lax.all_gather(value, 'dp', axis=0, tiled=True, axis_index_groups=line_gr...  16.5 us
  transfers between devices with their start and end apart: 13, of which 6 were waited for; matrix products, arithmetic and copies ran while one was open for 7% of the time, Pallas kernels for 76%

profile of v5, /device:TPU:1, one launch (start us, length us, event | category | flops | bytes accessed | tf_op | source)
XLA Modules:
  0.0 606.6 jit_solution(7983567141629490452)
XLA Ops:
  7.3 1.2 convert_element_type.105
  8.6 1.3 collective-permute-done
  9.9 0.8 maximum_select_fusion.3
  10.8 0.2 copy.98
  11.1 0.2 collective-permute-start.1
  11.3 1.4 collective-permute-done.1
  12.7 0.9 maximum_select_fusion
  13.8 0.6 concatenate.120.gain_ref
  14.4 0.3 copy.97
  14.8 1.7 copy.96
  16.5 0.9 dynamic-slice_convert_fusion.1
  17.4 0.7 pad_maximum_fusion.2.piece_ref
  18.1 1.4 convert_bitcast_fusion.2
  19.6 1.6 pad_maximum_fusion.ffn_ref
  21.2 90.8 %gather_first.1 = (bf16[1024,2048]{1,0:T(8,128)(2,1)}, bf16[1024,2048]{1,0:T(8,128)(2,1)}, bf16[1024,2048]{1,0:T(8,128)(2,1)}, bf16[2,4,128,768]{3,2,1,0:T(8,128...) custom-call(bf16[256,2048]{1,0:T(8,128)(2,1)} %x_ref.1, bf16[256,2048]{1,0:T(8,128)(2,1)} %dy_ref.1, ...), custom_call_target="tpu_custom_call" | custom-call | flops 1 | bytes 21192704 | tf_op jit(solution)/shard_map/gather_first/pallas_call | solution.py:823
  112.0 3.4 copy.140
  116.2 1.0 slice.81
  117.4 0.6 fusion.9
  118.1 0.6 slice_convert_fusion
  118.7 0.2 broadcast_compare_fusion
  120.8 0.8 constant_dynamic-slice_fusion.11
  121.6 0.2 fusion.6
  122.1 3.2 multiply_sine_fusion
  125.3 1.5 select_convert_fusion.bias_ref
  126.8 125.2 %attn_first.1 = (bf16[1024,1024]{1,0:T(8,128)(2,1)}, bf16[1024,256]{1,0:T(8,128)(2,1)}, bf16[1024,256]{1,0:T(8,128)(2,1)}, bf16[1024,1024]{1,0:T(8,128)(2,1)}, b...) custom-call(bf16[1024,2048]{1,0:T(8,128)(2,1)} %get-tuple-element.51, ...), custom_call_target="tpu_custom_call" | custom-call | flops 15032385536 | bytes 42487808 | tf_op jit(solution)/shard_map/attn_first/pallas_call | solution.py:1270
  252.0 16.5 %all-gather.8.cloned.1.call-done = bf16[8448,512]{1,0:T(8,128)(2,1)} async-done(((bf16[2112,512]{1,0:T(8,128)(2,1)}), bf16[8448,512]{1,0:T(8,128)(2,1)}) %all-gather.8.cloned.1.call-update) | async-done | bytes 8650768 | tf_op jit(solution)/shard_map/all_gather | solution.py:1950
  268.5 29.0 %ffn_first.1 = (bf16[704,2048]{1,0:T(8,128)(2,1)}, bf16[704,2048]{1,0:T(8,128)(2,1)}, bf16[704,2048]{1,0:T(8,128)(2,1)}, bf16[4,704,512]{2,1,0:T(8,128)(2,1)}) custom-call(bf16[1024,2048]{1,0:T(8,128)(2,1)} %get-tuple-element.49.refs_0_, bf16[1024,2048]{1,0:T(8,128)(2,1)} %get-tuple-element.50.refs_1_, bf16[2048,2048]{1,0:T(8,128)(2,1)} %get-tuple-element.54.refs_2_, ...), custom_call_target="tpu_custom_call" | custom-call | flops 17716740096 | bytes 36962304 | tf_op jit(solution)/shard_map/ffn_first/pallas_call | solution.py:160
  297.6 0.4 reduce-scatter.8.cloned.1.call-start
  298.1 0.2 copy-done.8
  298.3 0.6 select_n.190.refs_8_
  298.9 97.5 %ffn_back.1 = (bf16[4,1408,512]{2,1,0:T(8,128)(2,1)}, f32[256,2048]{1,0:T(8,128)}, f32[1,2048]{1,0:T(1,128)}, bf16[1024,2048]{1,0:T(8,128)(2,1)}, bf16[4,512,512...) custom-call(bf16[1024,2048]{1,0:T(8,128)(2,1)} %get-tuple-element.49.refs_0_, ...), custom_call_target="tpu_custom_call" | custom-call | flops 29527900160 | bytes 53493760 | tf_op jit(solution)/shard_map/ffn_back/pallas_call | solution.py:523
  396.5 100.2 %attn_back.1 = (bf16[4,528,1024]{2,1,0:T(8,128)(2,1)}, bf16[256,2048]{1,0:T(8,128)(2,1)}) custom-call(bf16[1024,2048]{1,0:T(8,128)(2,1)} %get-tuple-element.66.attn_ref, bf16[1024,1024]{1,0:T(8,128)(2,1)} %all-gather.6.cloned.1.call-done.mine_ref, bf16[1024,1024]{1,0:T(8,128)(2,1)} %get-tuple-element.67.theirs_ref, ...), custom_call_target="tpu_custom_call" | custom-call | flops 21474836480 | bytes 41046016 | tf_op jit(solution)/shard_map/attn_back/pallas_call | solution.py:1738
  496.8 1.0 copy-done.7
  498.2 3.1 reshape.336
  501.2 0.2 copy.141
  501.4 1.6 pad_maximum_fusion.1.parts_ref
  503.0 48.9 %settle.1 = (bf16[256,2048]{1,0:T(8,128)(2,1)}, bf16[4,3,704,128]{3,2,1,0:T(8,128)(2,1)}) custom-call(bf16[4,512,512]{2,1,0:T(8,128)(2,1)} %get-tuple-element.60.near_ref, bf16[2,512,512]{2,1,0:T(8,128)(2,1)} %get-tuple-element.61.given_ref, bf16[4,512,512]{2,1,0:T(8,128)(2,1)} %get-tuple-element.62.give_ref, f32[256,2048]{1,0:T(8,128)} %get-tuple-element.59.refs_7_.res_ref, ...), custom_call_target="tpu_custom_call" | custom-call | flops 1 | bytes 12713984 | tf_op jit(solution)/shard_map/settle/pallas_call | solution.py:1899
  551.9 2.0 convert_bitcast_fusion
  553.9 1.4 fusion.24
  555.3 1.5 copy.113
  556.8 1.5 copy.114
  558.3 19.0 %reduce-scatter.10.cloned.1.call-done = bf16[528,1024]{1,0:T(8,128)(2,1)} async-done(((bf16[2112,1024]{1,0:T(8,128)(2,1)}), bf16[528,1024]{1,0:T(8,128)(2,1)}) %reduce-scatter.10.cloned.1.call-update) | async-done | bytes 1081360
  577.3 1.2 slice.118
  578.6 0.2 copy.134
  578.7 0.7 collective-permute-start.6
  579.6 0.2 copy.125
  579.8 1.3 collective-permute-start.3
  581.1 0.2 copy.129
  581.3 0.4 collective-permute-start.5
  581.9 0.2 copy.128
  582.2 0.2 copy.124
  582.4 0.6 collective-permute-done.5
  583.0 1.2 fusion
  584.2 1.1 copy.116
  585.4 5.2 collective-permute-done.3
  590.7 0.9 collective-permute-start.4
  591.7 0.8 copy.118
  592.4 0.8 copy.117
  593.2 1.0 copy.115
  594.3 0.6 dynamic-slice_reduce_fusion.2
  594.9 0.6 dynamic-slice_reduce_fusion
  595.5 2.1 convert_bitcast_fusion.1
  597.6 1.0 copy.147
  598.6 1.0 copy.148
  (97 shorter events, 2.7 us)
Async XLA Ops:
  7.2 10.2 %copy-start = (f32[128,1024]{1,0:T(8,128)S(1)}, f32[128,1024]{1,0:T(8,128)}, u32[]{:S(2)}) copy-start(f32[128,1024]{1,0:T(8,128)} %param.21) | copy-start | bytes 1572868
  7.2 3.6 copy-start.4
  7.2 119.6 %all-gather.4.cloned.1.call-start = ((), (), s32[]{:S(2)}) async-start(), calls=%async_computation.3 | async-start | bytes 1310720 | tf_op jit(solution)/shard_map/all_gather | solution.py:1950
  8.5 1.4 collective-permute-start
  10.7 3.1 copy-start.12
  10.7 3.1 copy-start.10
  10.7 3.1 copy-start.11
  10.7 3.7 copy-start.2
  10.7 116.1 %all-gather.6.cloned.1.call-start = ((), (), s32[]{:S(2)}) async-start(), calls=%async_computation.4 | async-start | bytes 2621440 | tf_op jit(solution)/shard_map/all_gather | solution.py:1950
  11.1 1.6 collective-permute-start.1
  13.6 254.9 %all-gather.8.cloned.1.call-start = ((), (), s32[]{:S(2)}) async-start(), calls=%async_computation.5 | async-start | bytes 10813440 | tf_op jit(solution)/shard_map/all_gather | solution.py:1950
  115.4 5.2 copy-start.9
  115.4 281.1 %reduce-scatter.6.cloned.1.call-start = ((), (), s32[]{:S(2)}) async-start(), calls=%async_computation.6 | async-start | bytes 3604480 | tf_op jit(solution)/shard_map/reduce_scatter | solution.py:1956
  115.4 3.5 collective-permute-start.2
  297.6 0.7 copy-start.8
  297.6 199.1 %reduce-scatter.8.cloned.1.call-start = ((), (), s32[]{:S(2)}) async-start(), calls=%async_computation.7 | async-start | bytes 7208960 | tf_op jit(solution)/shard_map/reduce_scatter | solution.py:1956
  396.5 180.8 %reduce-scatter.10.cloned.1.call-start = ((), (), s32[]{:S(2)}) async-start(), calls=%async_computation.8 | async-start | bytes 5406720
  496.8 1.1 copy-start.7
  577.3 2.3 copy-start.3
  578.5 2.6 slice-start
  578.7 16.8 %collective-permute-start.6 = (bf16[128,1024]{0,1:T(8,128)(2,1)S(1)}, bf16[128,1024]{0,1:T(8,128)(2,1)}, u32[]{:S(2)}, u32[]{:S(2)}) collective-permute-start(bf16[128,1024]{0,1:T(8,128)(2,1)S(1)} %copy.134), channel_id=1, source_target_pairs={{0,2},{2,0},{4,6},{6,4},{8,10},{10,8},{12,14},{14,12},{16,18},{18,... | collective-permute-start | bytes 786440 | tf_op jit(solution)/shard_map/ppermute | solution.py:1941
  579.8 10.8 %collective-permute-start.3 = (bf16[144,768]{0,1:T(8,128)(2,1)S(1)}, bf16[144,768]{0,1:T(8,128)(2,1)S(1)}, u32[]{:S(2)}, u32[]{:S(2)}) collective-permute-start(bf16[144,768]{0,1:T(8,128)(2,1)S(1)} %copy.125), channel_id=1, source_target_pairs={{0,1},{1,0},{2,3},{3,2},{4,5},{5,4},{6,7},{7,6},{8,9},{9,8},{10,11... | collective-permute-start | bytes 663560 | tf_op jit(solution)/shard_map/ppermute | solution.py:1947
  581.3 1.7 collective-permute-start.5
  590.7 3.5 collective-permute-start.4
  591.7 6.0 copy-start.6
  594.2 4.4 copy-start.5
  597.6 2.0 copy-start.1
Sparse Core Ops, SparseCore 0:
  10.8 32.3 all-gather.3
  45.3 47.8 all-gather.5
  115.5 152.9 all-gather.7
  297.7 54.0 reduce-scatter.5
  396.6 99.0 reduce-scatter.7
  497.9 79.3 reduce-scatter.9

commit v6 on v5

--- a/solution.py
+++ b/solution.py
@@ -54,10 +54,6 @@
 
 ANY = pl.BlockSpec(memory_space=pl.ANY)
 vmem_bytes = 60 * 1024 * 1024
-
-
-def kernel_params():
-    return pltpu.CompilerParams(vmem_limit_bytes=vmem_bytes)
 
 
 def cost(flops, arrays, transcendentals=0):
@@ -101,9 +97,9 @@
     return [ref.at[pl.ds(j * rows, rows)] for j in range(count)]
 
 
-def zip_rows(ref, far, count):
-    pairs = zip(split_rows(ref, count // 2), split_rows(far, count // 2))
-    return [one for pair in pairs for one in pair]
+def eight_rows(ref, far, last):
+    near, far, last = split_rows(ref, 4), split_rows(far, 2), split_rows(last, 2)
+    return [near[0], far[0], near[1], last[0], near[2], far[1], near[3], last[1]]
 
 
 def ffn_first(normed, grads, grads_far, weights):
@@ -115,13 +111,42 @@
     double = 2 * hid
 
     def kernel(*refs):
-        grad_ref, grad_far, normed_ref, weight_ref, hid_ref, a_ref, s_ref, down_ref = refs[:8]
-        grad_refs = zip_rows(grad_ref, grad_far, count)
+        grad_ref, grad_far, normed_ref, weight_ref, hid_ref, a_ref, s_ref, down_ref, last_ref = refs[:9]
+        grad_refs = eight_rows(grad_ref, grad_far, last_ref)
         normed_refs = split_rows(normed_ref, count)
-        n_s, g_s, w_s, hid_s, a_s, s_s, down_s, n_sem, g_sem, w_sem, o_sem, d_sem = refs[8:]
+        n_s, g_s, w_s, hid_s, a_s, s_s, down_s, n_sem, g_sem, w_sem, o_sem, d_sem, hop_send, hop_recv = refs[9:]
         parts = join_lines(weight_ref.at[:, pl.ds(0, double)], w_s, w_sem)
         stack_rows(normed_refs, n_s, n_sem)
-        grad_copies = stack_rows(grad_refs, g_s, g_sem)
+        grad_copies = [
+            pltpu.make_async_copy(ref, g_s.at[pl.ds(j * rows, rows)], g_sem.at[j])
+            for j, ref in enumerate(grad_refs)
+        ]
+        early, late = [0, 1, 2, 4, 5, 6], [3, 7]
+        for j in early:
+            grad_copies[j].start()
+        across_core, across_side, across_half = peers()
+        greet((across_core, across_side, across_half))
+        part = rows // 2
+        hops = [
+            remote(src, dst, hop_send.at[j], hop_recv.at[j], target)
+            for j, (src, dst, target) in enumerate(
+                (
+                    (
+                        grad_far.at[pl.ds(0, part)],
+                        last_ref.at[pl.ds(0, part)],
+                        across_side,
+                    ),
+                    (
+                        grad_ref.at[pl.ds(rows + part, part)],
+                        last_ref.at[pl.ds(part, part)],
+                        across_half,
+                    ),
+                    (last_ref.at[pl.ds(0, rows)], last_ref.at[pl.ds(rows, rows)], across_core),
+                )
+            )
+        ]
+        hops[0].start()
+        hops[1].start()
         wait_all(parts)
 
         @pl.loop(0, count)
@@ -141,6 +166,12 @@
         ]
         for copy in outs:
             copy.start()
+        hops[0].wait_recv()
+        hops[1].wait_recv()
+        hops[2].start()
+        hops[2].wait_recv()
+        for j in late:
+            grad_copies[j].start()
         wait_all(grad_copies)
 
         @pl.loop(0, lines)
@@ -153,15 +184,18 @@
             pltpu.make_async_copy(down_s.at[j], down_ref.at[j], d_sem.at[j]).wait()
 
         wait_all(outs)
+        for copy in hops:
+            copy.wait_send()
 
     acts = jax.ShapeDtypeStruct((hid, total), BF)
     out_shape = (acts, acts, acts, jax.ShapeDtypeStruct((lines, hid, cols), BF))
+    out_shape += (jax.ShapeDtypeStruct((2 * rows, width), BF),)
     args = (grads, grads_far, normed, weights)
     return pl.pallas_call(
         kernel,
         out_shape=out_shape,
         in_specs=[ANY] * len(args),
-        out_specs=(ANY,) * 4,
+        out_specs=(ANY,) * 5,
         scratch_shapes=[
             pltpu.VMEM((total, width), BF),
             pltpu.VMEM((total, width), BF),
@@ -175,8 +209,12 @@
             pltpu.SemaphoreType.DMA((lines,)),
             pltpu.SemaphoreType.DMA((3,)),
             pltpu.SemaphoreType.DMA((lines,)),
+            pltpu.SemaphoreType.DMA((3,)),
+            pltpu.SemaphoreType.DMA((3,)),
         ],
-        compiler_params=kernel_params(),
+        compiler_params=pltpu.CompilerParams(
+            vmem_limit_bytes=vmem_bytes, collective_id=5, has_side_effects=True
+        ),
         cost_estimate=cost(6 * hid * total * width, args + out_shape, hid * total),
         name="ffn_first",
     )(*args)
@@ -213,7 +251,7 @@
     )
 
 
-def ffn_back(grads, grads_far, weights, hidden, a_fac, s_fac, normed, residual, gain):
+def ffn_back(grads, grads_far, grads_last, weights, hidden, a_fac, s_fac, normed, residual, gain):
     count = 8
     total, width = normed.shape
     rows = total // count
@@ -225,9 +263,10 @@
     early = lines // 2
 
     def kernel(*refs):
-        grad_ref, grad_far, normed_ref, all_ref, hid_ref, a_ref, s_ref, resid_ref, gain_ref = refs[:9]
-        grad_out, dres_out, dgain_out, attn_out, near_out, away_out, away_in = refs[9:16]
-        grad_refs = zip_rows(grad_ref, grad_far, count)
+        grad_ref, grad_far, last_ref, normed_ref, all_ref, hid_ref = refs[:6]
+        a_ref, s_ref, resid_ref, gain_ref = refs[6:10]
+        grad_out, dres_out, dgain_out, attn_out, near_out, away_out, away_in = refs[10:17]
+        grad_refs = eight_rows(grad_ref, grad_far, last_ref)
         normed_refs = split_rows(normed_ref, count)
         weight_ref = all_ref.at[:, pl.ds(0, double)]
         down_in = all_ref.at[:, pl.ds(double, hid)]
@@ -269,7 +308,7 @@
             away_send,
             away_recv,
             free_sem,
-        ) = refs[16:]
+        ) = refs[17:]
         across_core, across_side, across_half = peers()
         side = (lax.axis_index("dp") // 2) % 2
         downs = join_lines(down_in, d_s, d_sem)
@@ -374,39 +413,6 @@
             grad_s[j % 2] = matmul(act_s[...], rows_s[:, tile(j, cols)]).astype(BF)
             grad_copy(j).start()
 
-        hid_copy.wait()
-        pl.semaphore_wait(free_sem, 1)
-
-        @pl.loop(0, lines)
-        def _(j):
-            to_core(j).wait_send()
-            far_s[j] = matmul_tn(a_s[:, pl.ds(near, near)], d_s[:, tile(j, cols)]).astype(BF)
-            to_core(j).start()
-
-        for j in range(max(lines - 2, 0), lines):
-            grad_copy(j).wait()
-
-        def part_copies(j):
-            held = grad_s.at[j % 2]
-            return [
-                pltpu.make_async_copy(
-                    held.at[pl.ds(k * 2 * rows, 2 * rows)], ref.at[j], part_sem.at[k, j % 2]
-                )
-                for k, ref in enumerate((near_out, away_out))
-            ]
-
-        @pl.loop(0, lines)
-        def _(j):
-            @pl.when(j >= 2)
-            def _():
-                wait_all(part_copies(j - 2))
-
-            part = matmul_tn(a_s[:, pl.ds(0, near)], d_s[:, tile(j, cols)])
-            to_core(j).wait_recv()
-            grad_s[j % 2, pl.ds(0, near), :] = (part + core_in[j].astype(F32)).astype(BF)
-            for copy in part_copies(j):
-                copy.start()
-
         @pl.loop(0, lines // 2)
         def _(p):
             for odd in (False, True):
@@ -416,6 +422,39 @@
                 acc[j, pl.ds(0, rows), :] = part[:rows]
                 half_s[j] = part[rows:].astype(BF)
                 second_hop(j, odd).start()
+
+        hid_copy.wait()
+        pl.semaphore_wait(free_sem, 1)
+
+        @pl.loop(0, lines)
+        def _(j):
+            to_core(j).wait_send()
+            far_s[j] = matmul_tn(a_s[:, pl.ds(near, near)], d_s[:, tile(j, cols)]).astype(BF)
+            to_core(j).start()
+
+        for j in range(max(lines - 2, 0), lines):
+            grad_copy(j).wait()
+
+        def part_copies(j):
+            held = grad_s.at[j % 2]
+            return [
+                pltpu.make_async_copy(
+                    held.at[pl.ds(k * 2 * rows, 2 * rows)], ref.at[j], part_sem.at[k, j % 2]
+                )
+                for k, ref in enumerate((near_out, away_out))
+            ]
+
+        @pl.loop(0, lines)
+        def _(j):
+            @pl.when(j >= 2)
+            def _():
+                wait_all(part_copies(j - 2))
+
+            part = matmul_tn(a_s[:, pl.ds(0, near)], d_s[:, tile(j, cols)])
+            to_core(j).wait_recv()
+            grad_s[j % 2, pl.ds(0, near), :] = (part + core_in[j].astype(F32)).astype(BF)
+            for copy in part_copies(j):
+                copy.start()
 
         for j in range(max(lines - 2, 0), lines):
             wait_all(part_copies(j))
@@ -517,7 +556,7 @@
         jax.ShapeDtypeStruct((lines, 2 * rows, cols), BF),
         jax.ShapeDtypeStruct((early, 2 * rows, cols), BF),
     )
-    args = (grads, grads_far, normed, weights, hidden, a_fac, s_fac, residual, gain)
+    args = (grads, grads_far, grads_last, normed, weights, hidden, a_fac, s_fac, residual, gain)
     vmem = pl.BlockSpec(memory_space=pltpu.VMEM)
     dma = pltpu.SemaphoreType.DMA
     return pl.pallas_call(
@@ -596,7 +635,12 @@
         ffn_out,
         tok_s,
         x_s,
+        dy_s,
+        piece_s,
+        gain_s,
+        unit_s,
         local_sem,
+        store_sem,
         up_send,
         up_recv,
         down_send,
@@ -682,9 +726,7 @@
             hop(4, dy_ref, slot(dy_out, 2), across_core),
             hop(5, slot(dy_out, 1), slot(dy_out, 3), across_core),
             hop(6, dy_ref, slot(far_out, 0), across_half),
-            hop(7, slot(dy_out, 1), slot(far_out, 1), across_half),
-            hop(8, slot(far_out, 0), slot(far_out, 2), across_core),
-            hop(9, slot(far_out, 1), slot(far_out, 3), across_core),
+            hop(7, slot(far_out, 0), slot(far_out, 1), across_core),
         ]
 
         def units(to_side_at, to_core_at):
@@ -709,15 +751,24 @@
             )
         ]
         locals_ = [
-            pltpu.make_async_copy(piece_ref, weight(0, line), local_sem.at[0]),
-            pltpu.make_async_copy(gain_ref, gain(0, line), local_sem.at[1]),
+            pltpu.make_async_copy(piece_ref, piece_s, local_sem.at[0]),
+            pltpu.make_async_copy(gain_ref, gain_s, local_sem.at[1]),
             pltpu.make_async_copy(x_ref, tok_s, local_sem.at[2]),
-            pltpu.make_async_copy(dy_ref, slot(dy_out, 0), local_sem.at[3]),
-            pltpu.make_async_copy(units(side, core), ffn_out.at[me], local_sem.at[4]),
+            pltpu.make_async_copy(dy_ref, dy_s, local_sem.at[3]),
+            pltpu.make_async_copy(units(side, core), unit_s, local_sem.at[4]),
+        ]
+        stores = [
+            pltpu.make_async_copy(piece_s, weight(0, line), store_sem.at[0]),
+            pltpu.make_async_copy(gain_s, gain(0, line), store_sem.at[1]),
+            pltpu.make_async_copy(dy_s, slot(dy_out, 0), store_sem.at[2]),
+            pltpu.make_async_copy(unit_s, ffn_out.at[me], store_sem.at[3]),
+            pltpu.make_async_copy(x_s, slot(x_out, 0), store_sem.at[4]),
         ]
         start(locals_)
         greet((across_core, across_side, across_half, above, below, across_both))
         wait_all(locals_[:2])
+        start(stores[:2])
+        wait_all(stores[:2])
 
         @pl.when(line < lines - 1)
         def _():
@@ -739,8 +790,8 @@
             x_s[:, pl.ds(j * block, block)] = jnp.where(side == 0, first, second).astype(BF)
             x_s[:, pl.ds(edge + j * block, block)] = jnp.where(side == 0, second, first).astype(BF)
         start(moves[:2])
-        x_copy = pltpu.make_async_copy(x_s, slot(x_out, 0), local_sem.at[5])
-        x_copy.start()
+        wait_all(locals_[3:])
+        start(stores[2:])
         for step in range(1, lines):
 
             @pl.when(line >= step)
@@ -770,17 +821,14 @@
         moves[0].wait_recv()
         moves[2].start()
         moves[3].wait_recv()
-        moves[7].start()
         moves[5].start()
         for at in range(lines):
             for copy in to_side(at):
                 copy.wait_recv()
             to_core(1, at).start()
         moves[6].wait_recv()
-        moves[8].start()
-        moves[7].wait_recv()
-        moves[9].start()
-        for j in (1, 2, 4, 5, 8, 9):
+        moves[7].start()
+        for j in (1, 2, 4, 5, 7):
             moves[j].wait_recv()
         for copy in shares:
             copy.wait_recv()
@@ -807,13 +855,12 @@
                 to_core(r, at).wait_send()
         for copy in moves + shares:
             copy.wait_send()
-        wait_all(locals_[3:])
-        x_copy.wait()
+        wait_all(stores[2:])
 
     out_shape = (
         jax.ShapeDtypeStruct((4 * rows, width), BF),
         jax.ShapeDtypeStruct((4 * rows, width), BF),
-        jax.ShapeDtypeStruct((4 * rows, width), BF),
+        jax.ShapeDtypeStruct((2 * rows, width), BF),
         jax.ShapeDtypeStruct((2, lines, shard, part_cols), BF),
         jax.ShapeDtypeStruct((2, lines, 2, 16, part_cols), BF),
         jax.ShapeDtypeStruct((4, 3, hid, shard), BF),
@@ -828,7 +875,12 @@
         scratch_shapes=[
             pltpu.VMEM((rows, width), BF),
             pltpu.VMEM((rows, width), BF),
-            dma((6,)),
+            pltpu.VMEM((rows, width), BF),
+            pltpu.VMEM((shard, part_cols), BF),
+            pltpu.VMEM((16, part_cols), BF),
+            pltpu.VMEM((3, hid, shard), BF),
+            dma((5,)),
+            dma((5,)),
             dma((lines, 2)),
             dma((lines, 2)),
             dma((lines, 2)),
@@ -837,8 +889,8 @@
             dma((lines, 2)),
             dma((2, lines)),
             dma((2, lines)),
-            dma((10,)),
-            dma((10,)),
+            dma((8,)),
+            dma((8,)),
             dma((3,)),
             dma((3,)),
         ],
@@ -1811,6 +1863,7 @@
         half_in,
         res_s,
         out_s,
+        part_s,
         load_sem,
         near_sem,
         away_sem,
@@ -1835,8 +1888,9 @@
             for j in range(start)
         ]
         res_copy = pltpu.make_async_copy(res_ref, res_s, load_sem.at[0])
-        local_copy = pltpu.make_async_copy(parts_ref.at[me], parts_out.at[me], load_sem.at[1])
-        for copy in nears + aways + [res_copy, local_copy]:
+        part_copy = pltpu.make_async_copy(parts_ref.at[me], part_s, load_sem.at[1])
+        local_copy = pltpu.make_async_copy(part_s, parts_out.at[me], load_sem.at[1])
+        for copy in nears + aways + [res_copy, part_copy]:
             copy.start()
         greet((across_core, across_side, across_half, across_both))
         lates = [
@@ -1866,6 +1920,8 @@
             for j in range(lines)
         ]
         res_copy.wait()
+        part_copy.wait()
+        local_copy.start()
         for j in range(lines):
             nears[j].wait()
             if j < start:
@@ -1908,6 +1964,7 @@
             pltpu.VMEM((lines, rows, cols), BF),
             pltpu.VMEM((rows, width), F32),
             pltpu.VMEM((rows, width), BF),
+            pltpu.VMEM(parts.shape[1:], BF),
             dma((2,)),
             dma((lines,)),
             dma((start,)),
@@ -2107,7 +2164,7 @@
         )
 
         gain_two_abs = from_rel(gain_two[None, :])
-        hidden, a_fac, s_fac, d_down = ffn_first(normed_two, grad_near, grad_far, ffn_w)
+        hidden, a_fac, s_fac, d_down, grad_last = ffn_first(normed_two, grad_near, grad_far, ffn_w)
 
         queue = []
 
@@ -2118,7 +2175,7 @@
 
         down_part = line_part(d_down)
         d_gate_up, d_resid, d_ffn_gain, d_attn, ffn_near, ffn_give, ffn_away = ffn_back(
-            grad_near, grad_far, ffn_w, hidden, a_fac, s_fac, normed_two, residual, gain_two_abs
+            grad_near, grad_far, grad_last, ffn_w, hidden, a_fac, s_fac, normed_two, residual, gain_two_abs
         )
         gate_up_part = line_part(d_gate_up)
 

time: 611 us -> 592 us (0.969)
  Pallas kernels: 492 us -> 473 us
    pallas_call x1, Pallas kernels: 90.8 us -> 76.5 us  [gather_first(): pl.pallas_call(kernel, out_shape=out_shape, in_specs=[ANY] * 5, out_specs...]
    pallas_call x1, Pallas kernels: 97.5 us -> 89.1 us  [ffn_back(): pl.pallas_call(kernel, out_shape=out_shape, in_specs=[ANY] * (len(args) -...]
  transfers between devices with their start and end apart: 13 -> 13, of which waited for: 6 -> 7; matrix products, arithmetic and copies ran while one was open for 7% -> 7% of each run, Pallas kernels for 76% -> 75%
where the time goes in v6:
time: 592 us; the launch traced here: 588 us
  Pallas kernels  473 us (80%)
  waiting for transfers between devices  44.5 us (8%)
  local copies, waits for them, and re-layouts  29 us (5%)
  other arithmetic  20.3 us (3%)
  between operations  17.3 us (3%)
    pallas_call x1, Pallas kernels, attn_first(): pl.pallas_call(kernel, out_shape=out_shape, in_specs=[vmem if a.shape[0]...  125 us
    pallas_call x1, Pallas kernels, attn_back(): pl.pallas_call(kernel, out_shape=out_shape, in_specs=[vmem if a.shape[0]...  100 us
    pallas_call x1, Pallas kernels, ffn_back(): pl.pallas_call(kernel, out_shape=out_shape, in_specs=[ANY] * (len(args) -...  89.1 us
    pallas_call x1, Pallas kernels, gather_first(): pl.pallas_call(kernel, out_shape=out_shape, in_specs=[ANY] * 5, out_specs...  76.5 us
    pallas_call x1, Pallas kernels, settle(): pl.pallas_call(kernel, out_shape=out_shape, in_specs=[ANY] * 5, out_specs...  48.7 us
    pallas_call x1, Pallas kernels, ffn_first(): pl.pallas_call(kernel, out_shape=out_shape, in_specs=[ANY] * len(args), o...  33 us
    unnamed x7, waiting for transfers between devices  20.2 us
    all_gather x3, waiting for transfers between devices, line_gather(): lax.all_gather(value, 'dp', axis=0, tiled=True, axis_index_groups=line_gr...  15.5 us
  transfers between devices with their start and end apart: 13, of which 7 were waited for; matrix products, arithmetic and copies ran while one was open for 7% of the time, Pallas kernels for 75%

profile of v6, /device:TPU:1, one launch (start us, length us, event | category | flops | bytes accessed | tf_op | source)
XLA Modules:
  0.0 588.1 jit_solution(7002827793327440425)
XLA Ops:
  7.3 1.2 convert_element_type.105
  8.6 1.3 collective-permute-done
  9.9 0.8 maximum_select_fusion.3
  10.8 0.2 copy.98
  11.1 0.2 collective-permute-start.1
  11.3 1.4 collective-permute-done.1
  12.7 0.9 maximum_select_fusion
  13.8 0.6 concatenate.120.gain_ref
  14.4 0.3 copy.97
  14.8 1.7 copy.96
  16.5 0.9 dynamic-slice_convert_fusion.1
  17.4 0.7 pad_maximum_fusion.2.piece_ref
  18.1 1.4 convert_bitcast_fusion.2
  19.6 1.6 pad_maximum_fusion.ffn_ref
  21.2 76.5 %gather_first.1 = (bf16[1024,2048]{1,0:T(8,128)(2,1)}, bf16[1024,2048]{1,0:T(8,128)(2,1)}, bf16[512,2048]{1,0:T(8,128)(2,1)}, bf16[2,4,128,768]{3,2,1,0:T(8,128)...) custom-call(bf16[256,2048]{1,0:T(8,128)(2,1)} %x_ref.1, bf16[256,2048]{1,0:T(8,128)(2,1)} %dy_ref.1, ...), custom_call_target="tpu_custom_call" | custom-call | flops 1 | bytes 19095552 | tf_op jit(solution)/shard_map/gather_first/pallas_call | solution.py:870
  97.7 3.4 copy.140
  101.9 1.0 slice.81
  103.2 0.6 fusion.9
  103.8 0.6 slice_convert_fusion
  104.4 0.2 broadcast_compare_fusion
  106.6 0.8 constant_dynamic-slice_fusion.11
  107.4 0.2 fusion.6
  107.8 3.2 multiply_sine_fusion
  111.0 1.5 select_convert_fusion.bias_ref
  112.5 125.4 %attn_first.1 = (bf16[1024,1024]{1,0:T(8,128)(2,1)}, bf16[1024,256]{1,0:T(8,128)(2,1)}, bf16[1024,256]{1,0:T(8,128)(2,1)}, bf16[1024,1024]{1,0:T(8,128)(2,1)}, b...) custom-call(bf16[1024,2048]{1,0:T(8,128)(2,1)} %get-tuple-element.52, ...), custom_call_target="tpu_custom_call" | custom-call | flops 15032385536 | bytes 42487808 | tf_op jit(solution)/shard_map/attn_first/pallas_call | solution.py:1322
  237.9 15.5 %all-gather.8.cloned.1.call-done = bf16[8448,512]{1,0:T(8,128)(2,1)} async-done(((bf16[2112,512]{1,0:T(8,128)(2,1)}), bf16[8448,512]{1,0:T(8,128)(2,1)}) %all-gather.8.cloned.1.call-update) | async-done | bytes 8650768 | tf_op jit(solution)/shard_map/all_gather | solution.py:2007
  253.4 33.0 %ffn_first.1 = (bf16[704,2048]{1,0:T(8,128)(2,1)}, bf16[704,2048]{1,0:T(8,128)(2,1)}, bf16[704,2048]{1,0:T(8,128)(2,1)}, bf16[4,704,512]{2,1,0:T(8,128)(2,1)}, bf16[512,2048]{1,0:T(8,128)(2,1)}) custom-call(bf16[1024,2048]{1,0:T(8,128)(2,1)} %get-tuple-element.50.refs_0_, bf16[512,2048]{1,0:T(8,128)(2,1)} %get-tuple-element.51.refs_1_, ...), custom_call_target="tpu_custom_call" | custom-call | flops 17716740096 | bytes 36962304 | tf_op jit(solution)/shard_map/ffn_first/pallas_call | solution.py:194
  286.5 0.4 reduce-scatter.8.cloned.1.call-start
  286.9 0.2 copy-done.8
  287.1 0.6 select_n.190.refs_9_
  287.8 89.1 %ffn_back.1 = (bf16[4,1408,512]{2,1,0:T(8,128)(2,1)}, f32[256,2048]{1,0:T(8,128)}, f32[1,2048]{1,0:T(1,128)}, bf16[1024,2048]{1,0:T(8,128)(2,1)}, bf16[4,512,512...) custom-call(bf16[1024,2048]{1,0:T(8,128)(2,1)} %get-tuple-element.50.refs_0_, ...), custom_call_target="tpu_custom_call" | custom-call | flops 29527900160 | bytes 53493760 | tf_op jit(solution)/shard_map/ffn_back/pallas_call | solution.py:562
  376.9 100.0 %attn_back.1 = (bf16[4,528,1024]{2,1,0:T(8,128)(2,1)}, bf16[256,2048]{1,0:T(8,128)(2,1)}) custom-call(bf16[1024,2048]{1,0:T(8,128)(2,1)} %get-tuple-element.68.attn_ref, bf16[1024,1024]{1,0:T(8,128)(2,1)} %all-gather.6.cloned.1.call-done.mine_ref, bf16[1024,1024]{1,0:T(8,128)(2,1)} %get-tuple-element.69.theirs_ref, ...), custom_call_target="tpu_custom_call" | custom-call | flops 21474836480 | bytes 41046016 | tf_op jit(solution)/shard_map/attn_back/pallas_call | solution.py:1790
  477.0 0.2 reduce-scatter.8.cloned.1.call-done
  477.2 1.0 copy-done.7
  478.5 3.1 reshape.336
  481.6 0.2 copy.141
  481.8 1.6 pad_maximum_fusion.1.parts_ref
  483.4 48.7 %settle.1 = (bf16[256,2048]{1,0:T(8,128)(2,1)}, bf16[4,3,704,128]{3,2,1,0:T(8,128)(2,1)}) custom-call(bf16[4,512,512]{2,1,0:T(8,128)(2,1)} %get-tuple-element.62.near_ref, bf16[2,512,512]{2,1,0:T(8,128)(2,1)} %get-tuple-element.63.given_ref, bf16[4,512,512]{2,1,0:T(8,128)(2,1)} %get-tuple-element.64.give_ref, f32[256,2048]{1,0:T(8,128)} %get-tuple-element.61.refs_8_.res_ref, ...), custom_call_target="tpu_custom_call" | custom-call | flops 1 | bytes 12713984 | tf_op jit(solution)/shard_map/settle/pallas_call | solution.py:1955
  532.1 2.0 convert_bitcast_fusion
  534.1 1.4 fusion.24
  535.5 1.5 copy.113
  537.0 1.5 copy.114
  538.6 20.1 %reduce-scatter.10.cloned.1.call-done = bf16[528,1024]{1,0:T(8,128)(2,1)} async-done(((bf16[2112,1024]{1,0:T(8,128)(2,1)}), bf16[528,1024]{1,0:T(8,128)(2,1)}) %reduce-scatter.10.cloned.1.call-update) | async-done | bytes 1081360
  558.7 1.2 slice.118
  560.0 0.2 copy.134
  560.1 0.7 collective-permute-start.6
  561.0 0.2 copy.125
  561.2 1.2 collective-permute-start.3
  562.7 0.4 collective-permute-start.5
  563.3 0.2 copy.128
  563.6 0.2 copy.124
  563.8 0.6 collective-permute-done.5
  564.4 1.2 fusion
  565.6 1.1 copy.116
  566.7 5.3 collective-permute-done.3
  572.1 0.9 collective-permute-start.4
  573.1 0.8 copy.118
  573.8 0.8 copy.117
  574.6 1.0 copy.115
  575.7 0.6 dynamic-slice_reduce_fusion.2
  576.3 0.6 dynamic-slice_reduce_fusion
  576.9 2.1 convert_bitcast_fusion.1
  579.0 1.0 copy.147
  580.0 1.0 copy.148
  (97 shorter events, 2.8 us)
Async XLA Ops:
  7.2 10.2 %copy-start = (f32[128,1024]{1,0:T(8,128)S(1)}, f32[128,1024]{1,0:T(8,128)}, u32[]{:S(2)}) copy-start(f32[128,1024]{1,0:T(8,128)} %param.21) | copy-start | bytes 1572868
  7.2 3.6 copy-start.4
  7.2 105.3 %all-gather.4.cloned.1.call-start = ((), (), s32[]{:S(2)}) async-start(), calls=%async_computation.3 | async-start | bytes 1310720 | tf_op jit(solution)/shard_map/all_gather | solution.py:2007
  8.5 1.4 collective-permute-start
  10.7 3.1 copy-start.12
  10.7 3.1 copy-start.10
  10.7 3.1 copy-start.11
  10.7 3.7 copy-start.2
  10.7 101.8 %all-gather.6.cloned.1.call-start = ((), (), s32[]{:S(2)}) async-start(), calls=%async_computation.4 | async-start | bytes 2621440 | tf_op jit(solution)/shard_map/all_gather | solution.py:2007
  11.1 1.6 collective-permute-start.1
  13.6 239.8 %all-gather.8.cloned.1.call-start = ((), (), s32[]{:S(2)}) async-start(), calls=%async_computation.5 | async-start | bytes 10813440 | tf_op jit(solution)/shard_map/all_gather | solution.py:2007
  101.1 5.2 copy-start.9
  101.1 275.8 %reduce-scatter.6.cloned.1.call-start = ((), (), s32[]{:S(2)}) async-start(), calls=%async_computation.6 | async-start | bytes 3604480 | tf_op jit(solution)/shard_map/reduce_scatter | solution.py:2013
  101.1 3.5 collective-permute-start.2
  286.4 0.7 copy-start.8
  286.5 190.7 %reduce-scatter.8.cloned.1.call-start = ((), (), s32[]{:S(2)}) async-start(), calls=%async_computation.7 | async-start | bytes 7208960 | tf_op jit(solution)/shard_map/reduce_scatter | solution.py:2013
  376.9 181.8 %reduce-scatter.10.cloned.1.call-start = ((), (), s32[]{:S(2)}) async-start(), calls=%async_computation.8 | async-start | bytes 5406720
  477.2 1.1 copy-start.7
  558.7 2.3 copy-start.3
  559.9 2.6 slice-start
  560.1 16.8 %collective-permute-start.6 = (bf16[128,1024]{0,1:T(8,128)(2,1)S(1)}, bf16[128,1024]{0,1:T(8,128)(2,1)}, u32[]{:S(2)}, u32[]{:S(2)}) collective-permute-start(bf16[128,1024]{0,1:T(8,128)(2,1)S(1)} %copy.134), channel_id=1, source_target_pairs={{0,2},{2,0},{4,6},{6,4},{8,10},{10,8},{12,14},{14,12},{16,18},{18,... | collective-permute-start | bytes 786440 | tf_op jit(solution)/shard_map/ppermute | solution.py:1998
  561.2 10.8 %collective-permute-start.3 = (bf16[144,768]{0,1:T(8,128)(2,1)S(1)}, bf16[144,768]{0,1:T(8,128)(2,1)S(1)}, u32[]{:S(2)}, u32[]{:S(2)}) collective-permute-start(bf16[144,768]{0,1:T(8,128)(2,1)S(1)} %copy.125), channel_id=1, source_target_pairs={{0,1},{1,0},{2,3},{3,2},{4,5},{5,4},{6,7},{7,6},{8,9},{9,8},{10,11... | collective-permute-start | bytes 663560 | tf_op jit(solution)/shard_map/ppermute | solution.py:2004
  562.7 1.7 collective-permute-start.5
  572.1 3.5 collective-permute-start.4
  573.1 6.0 %copy-start.6 = (bf16[256,2048]{1,0:T(8,128)(2,1)S(1)}, bf16[256,2048]{1,0:T(8,128)(2,1)}, u32[]{:S(2)}) copy-start(bf16[256,2048]{1,0:T(8,128)(2,1)} %get-tuple-element.201) | copy-start | bytes 3145732
  575.6 4.4 copy-start.5
  579.0 2.0 copy-start.1
Sparse Core Ops, SparseCore 0:
  10.8 35.0 all-gather.3
  48.1 46.8 all-gather.5
  101.2 152.1 all-gather.7
  286.6 53.9 reduce-scatter.5
  377.0 100.0 reduce-scatter.7
  479.3 79.3 reduce-scatter.9

commit v7 on v6

--- a/solution.py
+++ b/solution.py
@@ -97,12 +97,12 @@
     return [ref.at[pl.ds(j * rows, rows)] for j in range(count)]
 
 
-def eight_rows(ref, far, last):
-    near, far, last = split_rows(ref, 4), split_rows(far, 2), split_rows(last, 2)
-    return [near[0], far[0], near[1], last[0], near[2], far[1], near[3], last[1]]
-
-
-def ffn_first(normed, grads, grads_far, weights):
+def eight_rows(*refs):
+    pairs = [split_rows(ref, 2) for ref in refs]
+    return [pair[0] for pair in pairs] + [pair[1] for pair in pairs]
+
+
+def ffn_first(normed, grads, grads_far, grads_side, weights):
     count = 8
     total, width = normed.shape
     rows = total // count
@@ -111,10 +111,11 @@
     double = 2 * hid
 
     def kernel(*refs):
-        grad_ref, grad_far, normed_ref, weight_ref, hid_ref, a_ref, s_ref, down_ref, last_ref = refs[:9]
-        grad_refs = eight_rows(grad_ref, grad_far, last_ref)
+        grad_ref, grad_far, grad_side, normed_ref, weight_ref = refs[:5]
+        hid_ref, a_ref, s_ref, down_ref, last_ref = refs[5:10]
+        grad_refs = eight_rows(grad_ref, grad_far, grad_side, last_ref)
         normed_refs = split_rows(normed_ref, count)
-        n_s, g_s, w_s, hid_s, a_s, s_s, down_s, n_sem, g_sem, w_sem, o_sem, d_sem, hop_send, hop_recv = refs[9:]
+        n_s, g_s, w_s, hid_s, a_s, s_s, down_s, n_sem, g_sem, w_sem, o_sem, d_sem, hop_send, hop_recv = refs[10:]
         parts = join_lines(weight_ref.at[:, pl.ds(0, double)], w_s, w_sem)
         stack_rows(normed_refs, n_s, n_sem)
         grad_copies = [
@@ -137,7 +138,7 @@
                         across_side,
                     ),
                     (
-                        grad_ref.at[pl.ds(rows + part, part)],
+                        grad_side.at[pl.ds(part, part)],
                         last_ref.at[pl.ds(part, part)],
                         across_half,
                     ),
@@ -190,7 +191,7 @@
     acts = jax.ShapeDtypeStruct((hid, total), BF)
     out_shape = (acts, acts, acts, jax.ShapeDtypeStruct((lines, hid, cols), BF))
     out_shape += (jax.ShapeDtypeStruct((2 * rows, width), BF),)
-    args = (grads, grads_far, normed, weights)
+    args = (grads, grads_far, grads_side, normed, weights)
     return pl.pallas_call(
         kernel,
         out_shape=out_shape,
@@ -251,7 +252,7 @@
     )
 
 
-def ffn_back(grads, grads_far, grads_last, weights, hidden, a_fac, s_fac, normed, residual, gain):
+def ffn_back(grads, grads_far, grads_side, grads_last, weights, hidden, a_fac, s_fac, normed, residual, gain):
     count = 8
     total, width = normed.shape
     rows = total // count
@@ -263,10 +264,10 @@
     early = lines // 2
 
     def kernel(*refs):
-        grad_ref, grad_far, last_ref, normed_ref, all_ref, hid_ref = refs[:6]
-        a_ref, s_ref, resid_ref, gain_ref = refs[6:10]
-        grad_out, dres_out, dgain_out, attn_out, near_out, away_out, away_in = refs[10:17]
-        grad_refs = eight_rows(grad_ref, grad_far, last_ref)
+        grad_ref, grad_far, grad_side, last_ref, normed_ref, all_ref, hid_ref = refs[:7]
+        a_ref, s_ref, resid_ref, gain_ref = refs[7:11]
+        grad_out, dres_out, dgain_out, attn_out, near_out, away_out, away_in = refs[11:18]
+        grad_refs = eight_rows(grad_ref, grad_far, grad_side, last_ref)
         normed_refs = split_rows(normed_ref, count)
         weight_ref = all_ref.at[:, pl.ds(0, double)]
         down_in = all_ref.at[:, pl.ds(double, hid)]
@@ -308,7 +309,7 @@
             away_send,
             away_recv,
             free_sem,
-        ) = refs[17:]
+        ) = refs[18:]
         across_core, across_side, across_half = peers()
         side = (lax.axis_index("dp") // 2) % 2
         downs = join_lines(down_in, d_s, d_sem)
@@ -556,7 +557,7 @@
         jax.ShapeDtypeStruct((lines, 2 * rows, cols), BF),
         jax.ShapeDtypeStruct((early, 2 * rows, cols), BF),
     )
-    args = (grads, grads_far, grads_last, normed, weights, hidden, a_fac, s_fac, residual, gain)
+    args = (grads, grads_far, grads_side, grads_last, normed, weights, hidden, a_fac, s_fac, residual, gain)
     vmem = pl.BlockSpec(memory_space=pltpu.VMEM)
     dma = pltpu.SemaphoreType.DMA
     return pl.pallas_call(
@@ -658,8 +659,7 @@
         place, half = lax.axis_index("dp"), lax.axis_index("tensor")
         core, side, line = place % 2, (place // 2) % 2, place // 4
         across_both = (line * 4 + (1 - side) * 2 + 1 - core, half)
-        above = ((place + 4) % (4 * lines), half)
-        below = ((place + 4 * lines - 4) % (4 * lines), half)
+        whole_line = [((place + 4 * step) % (4 * lines), half) for step in range(1, lines)]
 
         def weight(r, at):
             return w_out.at[r, at]
@@ -682,16 +682,18 @@
             ]
 
         def upward(step):
-            return both(0, line - step, 0, up_send, up_recv, step, above)
+            target = whole_line[step - 1]
+            return both(0, line, 0, up_send, up_recv, step, target)
 
         def arrived_below(step):
-            return both(0, line - step, 0, up_send, up_recv, step - 1, above)
+            return both(0, line - step, 0, up_send, up_recv, step, whole_line[step - 1])
 
         def downward(step):
-            return both(0, line + step, 0, down_send, down_recv, step, below)
+            target = whole_line[lines - step - 1]
+            return both(0, line, 0, down_send, down_recv, step, target)
 
         def arrived_above(step):
-            return both(0, line + step, 0, down_send, down_recv, step - 1, below)
+            return both(0, line + step, 0, down_send, down_recv, step, whole_line[step - 1])
 
         def to_side(at):
             return both(0, at, 1, side_send, side_recv, at, across_side)
@@ -722,11 +724,9 @@
             hop(0, x_s, slot(x_out, 1), across_half),
             hop(1, x_s, slot(x_out, 2), across_core),
             hop(2, slot(x_out, 1), slot(x_out, 3), across_core),
-            hop(3, dy_ref, slot(dy_out, 1), across_side),
-            hop(4, dy_ref, slot(dy_out, 2), across_core),
-            hop(5, slot(dy_out, 1), slot(dy_out, 3), across_core),
-            hop(6, dy_ref, slot(far_out, 0), across_half),
-            hop(7, slot(far_out, 0), slot(far_out, 1), across_core),
+            hop(3, dy_ref, slot(dy_out, 1), across_core),
+            hop(4, dy_ref, slot(far_out, 0), across_half),
+            hop(5, slot(far_out, 0), slot(far_out, 1), across_core),
         ]
 
         def units(to_side_at, to_core_at):
@@ -765,23 +765,24 @@
             pltpu.make_async_copy(x_s, slot(x_out, 0), store_sem.at[4]),
         ]
         start(locals_)
-        greet((across_core, across_side, across_half, above, below, across_both))
+        greet((across_core, across_side, across_half, across_both, *whole_line))
         wait_all(locals_[:2])
         start(stores[:2])
         wait_all(stores[:2])
 
-        @pl.when(line < lines - 1)
-        def _():
-            start(upward(0))
-
-        @pl.when(line > 0)
-        def _():
-            start(downward(0))
+        for step in range(1, lines):
+
+            @pl.when(line + step < lines)
+            def _():
+                start(upward(step))
+
+            @pl.when(line >= step)
+            def _():
+                start(downward(step))
 
         spread_near(line)
         start(shares)
         moves[3].start()
-        moves[6].start()
         moves[4].start()
         locals_[2].wait()
         for j in range(lines):
@@ -798,37 +799,23 @@
             def _():
                 for copy in arrived_below(step):
                     copy.wait_recv()
-                if step < lines - 1:
-
-                    @pl.when(line < lines - 1)
-                    def _():
-                        start(upward(step))
-
                 spread_near(line - step)
 
             @pl.when(line + step < lines)
             def _():
                 for copy in arrived_above(step):
                     copy.wait_recv()
-                if step < lines - 1:
-
-                    @pl.when(line > 0)
-                    def _():
-                        start(downward(step))
-
                 spread_near(line + step)
 
         moves[0].wait_recv()
         moves[2].start()
-        moves[3].wait_recv()
-        moves[5].start()
         for at in range(lines):
             for copy in to_side(at):
                 copy.wait_recv()
             to_core(1, at).start()
-        moves[6].wait_recv()
-        moves[7].start()
-        for j in (1, 2, 4, 5, 7):
+        moves[4].wait_recv()
+        moves[5].start()
+        for j in (1, 2, 3, 5):
             moves[j].wait_recv()
         for copy in shares:
             copy.wait_recv()
@@ -836,14 +823,14 @@
             for at in range(lines):
                 from_core(r, at).wait_recv()
 
-        for step in range(lines - 1):
-
-            @pl.when((line >= step) & (line < lines - 1))
+        for step in range(1, lines):
+
+            @pl.when(line + step < lines)
             def _():
                 for copy in upward(step):
                     copy.wait_send()
 
-            @pl.when((line + step < lines) & (line > 0))
+            @pl.when(line >= step)
             def _():
                 for copy in downward(step):
                     copy.wait_send()
@@ -859,7 +846,7 @@
 
     out_shape = (
         jax.ShapeDtypeStruct((4 * rows, width), BF),
-        jax.ShapeDtypeStruct((4 * rows, width), BF),
+        jax.ShapeDtypeStruct((2 * rows, width), BF),
         jax.ShapeDtypeStruct((2 * rows, width), BF),
         jax.ShapeDtypeStruct((2, lines, shard, part_cols), BF),
         jax.ShapeDtypeStruct((2, lines, 2, 16, part_cols), BF),
@@ -889,8 +876,8 @@
             dma((lines, 2)),
             dma((2, lines)),
             dma((2, lines)),
-            dma((8,)),
-            dma((8,)),
+            dma((6,)),
+            dma((6,)),
             dma((3,)),
             dma((3,)),
         ],
@@ -905,8 +892,8 @@
 def attn_first(
     x_all,
     qkv_part,
-    q_up_mine,
-    out_mine,
+    grad_own,
+    both_mine,
     bias,
     cos_tab,
     sin_tab,
@@ -919,26 +906,25 @@
     total, width = x_all.shape
     rows = total // 4
     group = 2 * rows
-    edge, feats = out_mine.shape
-    rank = 2 * q_up_mine.shape[0]
-    q_block = rank // (2 * lines)
+    edge, feats = width // 2, both_mine.shape[2]
+    block = edge // lines
+    q_block = both_mine.shape[1] - block
+    rank = 2 * lines * q_block
     part_cols = qkv_part.shape[3]
     wide = 2 * part_cols
     head_dim = (wide - rank) // 2
     half_dim = head_dim // 2
     heads = feats // head_dim
-    block = edge // lines
     scale = 1.0 / math.sqrt(head_dim)
     step = 256
     cols = 512
     tiles = width // cols
-    sends_y = edge // step
 
     def kernel(
         x_ref,
         qkv_ref,
-        up_ref,
-        mine_ref,
+        dy_ref,
+        both_ref,
         bias_ref,
         cos_ref,
         sin_ref,
@@ -952,7 +938,8 @@
         lat_n_out,
         lat_out,
         n_out,
-        theirs_out,
+        full_out,
+        dy_out,
         res_out,
         norm_out,
         qkv_out,
@@ -997,6 +984,8 @@
         qkv_half_recv,
         qkv_core_send,
         qkv_core_recv,
+        dy_send,
+        dy_recv,
     ):
         across_core, across_side, across_half = peers()
         place = lax.axis_index("dp")
@@ -1009,7 +998,10 @@
             (cos_ref, cos_s),
             (sin_ref, sin_s),
             (bias_ref, bias_s),
-            (mine_ref, w_s.at[pl.ds(0, edge)]),
+        ]
+        pairs += [
+            (both_ref.at[j, pl.ds(q_block, block)], w_s.at[pl.ds(j * block, block)])
+            for j in range(lines)
         ]
         loads = [
             pltpu.make_async_copy(src, dst, load_sem.at[j]) for j, (src, dst) in enumerate(pairs)
@@ -1020,8 +1012,8 @@
 
         def theirs_copy(j):
             return remote(
-                mine_ref.at[tile(j, step)],
-                w_s.at[pl.ds(pl.multiple_of(edge + j * step, step), step)],
+                both_ref.at[j, pl.ds(q_block, block)],
+                w_s.at[pl.ds(pl.multiple_of(edge + j * block, block), block)],
                 theirs_send.at[j],
                 theirs_recv.at[j],
                 across_side,
@@ -1031,11 +1023,11 @@
             return up_s.at[pl.ds(pl.multiple_of((j * 2 + side) * q_block, 16), q_block)]
 
         def up_copy(j):
-            src = up_ref.at[pl.ds(j * q_block, q_block)]
+            src = both_ref.at[j, pl.ds(0, q_block)]
             return remote(src, up_rows(j), up_send.at[j], up_recv.at[j], across_side)
 
         def up_local(j):
-            src = up_ref.at[pl.ds(j * q_block, q_block)]
+            src = both_ref.at[j, pl.ds(0, q_block)]
             return pltpu.make_async_copy(src, up_rows(j), up_sem.at[j])
 
         for j in range(lines):
@@ -1079,7 +1071,7 @@
             qkv_core(r, at, False, core).start()
             qkv_local(r, at).start()
 
-        @pl.loop(0, sends_y)
+        @pl.loop(0, lines)
         def _(j):
             theirs_copy(j).start()
 
@@ -1190,7 +1182,7 @@
             half_s[j] = part[rows:].astype(BF)
             half_copy(j).start()
 
-        loads[7].wait()
+        wait_all(loads[7:])
 
         @pl.loop(0, tiles // 2)
         def _(j):
@@ -1200,7 +1192,7 @@
         def _(j):
             near_tile(j)
 
-        per_tile = cols // step
+        per_tile = cols // block
 
         @pl.loop(tiles // 2, tiles)
         def _(j):
@@ -1208,8 +1200,18 @@
                 theirs_copy((j - tiles // 2) * per_tile + k).wait()
             far_tile(j)
 
-        theirs_local = pltpu.make_async_copy(w_s.at[pl.ds(edge, edge)], theirs_out, out_sem.at[9])
-        theirs_local.start()
+        full_local = pltpu.make_async_copy(w_s, full_out, out_sem.at[9])
+        full_local.start()
+        grad_moves = [
+            remote(src, dst, dy_send.at[j], dy_recv.at[j], target)
+            for j, (src, dst, target) in enumerate(
+                (
+                    (dy_ref, dy_out.at[pl.ds(0, rows)], across_side),
+                    (dy_out.at[pl.ds(0, rows)], dy_out.at[pl.ds(rows, rows)], across_core),
+                )
+            )
+        ]
+        grad_moves[0].start()
 
         @pl.loop(tiles // 2, tiles)
         def _(j):
@@ -1270,7 +1272,10 @@
         hops[2].wait_recv()
         for copy in hops[5:]:
             copy.wait_recv()
-        for copy in hops:
+        grad_moves[0].wait_recv()
+        grad_moves[1].start()
+        grad_moves[1].wait_recv()
+        for copy in hops + grad_moves:
             copy.wait_send()
         for r, at in every:
             qkv_half(r, at, half).wait_send()
@@ -1284,7 +1289,7 @@
 
         wait_all(outs)
         mixed_copy.wait()
-        theirs_local.wait()
+        full_local.wait()
         res_copy.wait()
         own_copy.wait()
 
@@ -1299,7 +1304,8 @@
         low(total, rank),
         jax.ShapeDtypeStruct((rows, rank), F32),
         low(total, edge),
-        low(edge, feats),
+        low(width, feats),
+        low(2 * rows, width),
         jax.ShapeDtypeStruct((rows, width), F32),
         low(8 * rows, width),
         low(width, wide),
@@ -1308,8 +1314,8 @@
     args = (
         x_all,
         qkv_part,
-        q_up_mine,
-        out_mine,
+        grad_own,
+        both_mine,
         bias,
         cos_tab,
         sin_tab,
@@ -1347,9 +1353,9 @@
             pltpu.VMEM((rows, width), F32),
             pltpu.VMEM((rows, width), F32),
             pltpu.VMEM((rows, width), BF),
-            dma((8,)),
-            dma((sends_y,)),
-            dma((sends_y,)),
+            dma((7 + lines,)),
+            dma((lines,)),
+            dma((lines,)),
             dma((tiles,)),
             dma((tiles,)),
             dma((tiles,)),
@@ -1365,6 +1371,8 @@
             dma((2, lines)),
             dma((2, lines, 2)),
             dma((2, lines, 2)),
+            dma((2,)),
+            dma((2,)),
         ],
         compiler_params=pltpu.CompilerParams(
             vmem_limit_bytes=vmem_bytes, collective_id=2, has_side_effects=True
@@ -1376,8 +1384,7 @@
 
 def attn_back(
     d_attn,
-    out_mine,
-    out_theirs,
+    out_full,
     mixed,
     queries,
     keys,
@@ -1418,8 +1425,7 @@
 
     def kernel(
         attn_ref,
-        mine_ref,
-        theirs_ref,
+        full_ref,
         mixed_ref,
         q_ref,
         k_ref,
@@ -1488,8 +1494,8 @@
         pairs = (
             (attn_ref, attn_s),
             (mixed_ref, mixed_s),
-            (mine_ref, w_s.at[pl.ds(0, edge), pl.ds(0, feats)]),
-            (theirs_ref, w_s.at[pl.ds(edge, edge), pl.ds(0, feats)]),
+            (full_ref.at[pl.ds(0, edge)], w_s.at[pl.ds(0, edge), pl.ds(0, feats)]),
+            (full_ref.at[pl.ds(edge, edge)], w_s.at[pl.ds(edge, edge), pl.ds(0, feats)]),
             (q_ref, q_s),
             (k_ref, k_s),
             (v_ref, v_s),
@@ -1650,8 +1656,8 @@
             for s in range(2):
                 at = pl.ds((2 * j + s) * block, block)
                 picked = jnp.where(side == s, mine, theirs)
-                x_s[:, at] = (res_s[:, at] + picked).astype(BF)
-        in_copy = pltpu.make_async_copy(x_s, in_out, out_sem.at[0])
+                res_s[:, at] = res_s[:, at] + picked
+        in_copy = pltpu.make_async_copy(res_s, in_out, out_sem.at[0])
         in_copy.start()
 
         @pl.loop(0, tiles)
@@ -1761,12 +1767,11 @@
 
     out_shape = (
         jax.ShapeDtypeStruct((lines, block + q_block + shard + 16, feats), BF),
-        jax.ShapeDtypeStruct((rows, width), BF),
+        jax.ShapeDtypeStruct((rows, width), F32),
     )
     args = (
         d_attn,
-        out_mine,
-        out_theirs,
+        out_full,
         mixed,
         queries,
         keys,
@@ -1862,7 +1867,6 @@
         half_s,
         half_in,
         res_s,
-        out_s,
         part_s,
         load_sem,
         near_sem,
@@ -1936,8 +1940,8 @@
         for j in range(lines):
             halves[j].wait_recv()
             at = pl.ds(j * cols, cols)
-            out_s[:, at] = (res_s[:, at] + half_in[j].astype(F32)).astype(BF)
-        out_copy = pltpu.make_async_copy(out_s, out_ref, load_sem.at[0])
+            res_s[:, at] = res_s[:, at] + half_in[j].astype(F32)
+        out_copy = pltpu.make_async_copy(res_s, out_ref, load_sem.at[0])
         out_copy.start()
         local_copy.wait()
         for copy in shares:
@@ -1947,7 +1951,7 @@
         out_copy.wait()
 
     out_shape = (
-        jax.ShapeDtypeStruct((rows, width), BF),
+        jax.ShapeDtypeStruct((rows, width), F32),
         jax.ShapeDtypeStruct(parts.shape, BF),
     )
     args = (near, given, give, residual, parts)
@@ -1963,7 +1967,6 @@
             pltpu.VMEM((lines, rows, cols), BF),
             pltpu.VMEM((lines, rows, cols), BF),
             pltpu.VMEM((rows, width), F32),
-            pltpu.VMEM((rows, width), BF),
             pltpu.VMEM(parts.shape[1:], BF),
             dma((2,)),
             dma((lines,)),
@@ -2084,10 +2087,10 @@
             keep = lax.dynamic_slice_in_dim(low, core * cols, cols, 1)
             give = lax.dynamic_slice_in_dim(low, (1 - core) * cols, cols, 1)
             piece = order(core, keep, core_swap(give), 0)
-            return line_gather(piece)
-
-        q_up_mine = spread(q_up)
-        out_mine = spread(out_proj.T)
+            return piece
+
+        both_piece = jnp.concatenate([spread(q_up), spread(out_proj.T)], axis=0)
+        both_mine = line_gather(both_piece).reshape(lines, both_piece.shape[0], feats)
 
         ffn_low = jnp.stack([gate_proj.T, up_proj.T, down_proj]).astype(BF)
         x_all, grad_near, grad_far, qkv_part, gain_set, ffn_parts = gather_first(
@@ -2143,7 +2146,8 @@
             latent_n,
             latent_own,
             normed_rows,
-            out_theirs,
+            out_full,
+            grad_side,
             residual,
             normed_two,
             qkv_set,
@@ -2151,8 +2155,8 @@
         ) = attn_first(
             x_all,
             qkv_part,
-            q_up_mine,
-            out_mine,
+            out_grad,
+            both_mine,
             bias.astype(BF),
             cos_flat,
             sin_flat,
@@ -2164,7 +2168,9 @@
         )
 
         gain_two_abs = from_rel(gain_two[None, :])
-        hidden, a_fac, s_fac, d_down, grad_last = ffn_first(normed_two, grad_near, grad_far, ffn_w)
+        hidden, a_fac, s_fac, d_down, grad_last = ffn_first(
+            normed_two, grad_near, grad_far, grad_side, ffn_w
+        )
 
         queue = []
 
@@ -2175,14 +2181,13 @@
 
         down_part = line_part(d_down)
         d_gate_up, d_resid, d_ffn_gain, d_attn, ffn_near, ffn_give, ffn_away = ffn_back(
-            grad_near, grad_far, grad_last, ffn_w, hidden, a_fac, s_fac, normed_two, residual, gain_two_abs
+            grad_near, grad_far, grad_side, grad_last, ffn_w, hidden, a_fac, s_fac, normed_two, residual, gain_two_abs
         )
         gate_up_part = line_part(d_gate_up)
 
         sums, in_grad = attn_back(
             d_attn,
-            out_mine,
-            out_theirs,
+            out_full,
             head_mix,
             queries,
             keys_rot,
@@ -2233,8 +2238,8 @@
         ffn_gain_total = lax.dynamic_slice_in_dim(gain_total, block + core * shard, shard, 0)
         q_gain_total = lax.dynamic_slice_in_dim(gain_total, 2 * block + core * q_shard, q_shard, 0)
         return (
-            output,
-            in_grad,
+            output.astype(BF),
+            in_grad.astype(BF),
             attn_gain_total,
             q_down_total,
             q_gain_total,

time: 592 us -> 588 us (level)
  waiting for transfers between devices: 44.5 us -> 31 us
    pallas_call x1, Pallas kernels: 125 us -> 138 us  [attn_first(): pl.pallas_call(kernel, out_shape=out_shape, in_specs=[vmem if a.shape[0]...]
    pallas_call x1, Pallas kernels: 76.5 us -> 65.7 us  [gather_first(): pl.pallas_call(kernel, out_shape=out_shape, in_specs=[ANY] * 5, out_specs...]
    all_gather x3 -> x2, waiting for transfers between devices: 15.5 us -> 7.95 us  [line_gather(): lax.all_gather(value, 'dp', axis=0, tiled=True, axis_index_groups=line_gr...]
    unnamed x7 -> x6, waiting for transfers between devices: 20.2 us -> 15.8 us
  transfers between devices with their start and end apart: 13 -> 12, of which waited for: 7 -> 6; matrix products, arithmetic and copies ran while one was open for 7% -> 8% of each run, Pallas kernels for 75% -> 76%
where the time goes in v7:
time: 588 us; the launch traced here: 584 us
  Pallas kernels  475 us (81%)
  local copies, waits for them, and re-layouts  32.6 us (6%)
  waiting for transfers between devices  31 us (5%)
  other arithmetic  24.1 us (4%)
  between operations  17.2 us (3%)
    pallas_call x1, Pallas kernels, attn_first(): pl.pallas_call(kernel, out_shape=out_shape, in_specs=[vmem if a.shape[0]...  138 us
    pallas_call x1, Pallas kernels, attn_back(): pl.pallas_call(kernel, out_shape=out_shape, in_specs=[vmem if a.shape[0]...  100 us
    pallas_call x1, Pallas kernels, ffn_back(): pl.pallas_call(kernel, out_shape=out_shape, in_specs=[ANY] * (len(args) -...  89.5 us
    pallas_call x1, Pallas kernels, gather_first(): pl.pallas_call(kernel, out_shape=out_shape, in_specs=[ANY] * 5, out_specs...  65.7 us
    pallas_call x1, Pallas kernels, settle(): pl.pallas_call(kernel, out_shape=out_shape, in_specs=[ANY] * 5, out_specs...  48.8 us
    pallas_call x1, Pallas kernels, ffn_first(): pl.pallas_call(kernel, out_shape=out_shape, in_specs=[ANY] * len(args), o...  33 us
    unnamed x6, waiting for transfers between devices  15.8 us
  transfers between devices with their start and end apart: 12, of which 6 were waited for; matrix products, arithmetic and copies ran while one was open for 8% of the time, Pallas kernels for 76%

profile of v7, /device:TPU:1, one launch (start us, length us, event | category | flops | bytes accessed | tf_op | source)
XLA Modules:
  0.0 583.8 jit_solution(18132785555797949579)
XLA Ops:
  7.3 1.4 convert_element_type.112
  8.8 0.3 copy.101
  9.2 0.5 collective-permute-start
  9.7 1.2 collective-permute-done
  10.9 0.3 maximum_select_fusion.3
  11.2 0.2 maximum_select_fusion
  11.4 1.0 pad_maximum_fusion.2
  12.6 0.6 concatenate.123.gain_ref
  13.2 0.3 copy.100
  13.5 1.7 copy.99
  15.2 0.9 dynamic-slice_convert_fusion.1
  16.2 0.7 pad_maximum_fusion.3.piece_ref
  16.9 1.4 convert_bitcast_fusion.2
  18.3 1.6 pad_maximum_fusion.ffn_ref
  19.9 65.7 %gather_first.1 = (bf16[1024,2048]{1,0:T(8,128)(2,1)}, bf16[512,2048]{1,0:T(8,128)(2,1)}, bf16[512,2048]{1,0:T(8,128)(2,1)}, bf16[2,4,128,768]{3,2,1,0:T(8,128)(...) custom-call(bf16[256,2048]{1,0:T(8,128)(2,1)} %x_ref.1, bf16[256,2048]{1,0:T(8,128)(2,1)} %dy_ref.3, ...), custom_call_target="tpu_custom_call" | custom-call | flops 1 | bytes 16998400 | tf_op jit(solution)/shard_map/gather_first/pallas_call | solution.py:857
  85.6 3.3 copy.144
  89.8 1.0 slice.81
  91.0 0.6 fusion.9
  91.6 0.6 slice_convert_fusion
  92.2 0.2 broadcast_compare_fusion
  94.6 0.7 constant_dynamic-slice_fusion.11
  95.3 0.2 fusion.6
  95.8 3.2 multiply_sine_fusion
  99.0 1.5 select_convert_fusion.bias_ref
  100.5 4.7 copy.102
  105.3 137.9 %attn_first.1 = (bf16[1024,1024]{1,0:T(8,128)(2,1)}, bf16[1024,256]{1,0:T(8,128)(2,1)}, bf16[1024,256]{1,0:T(8,128)(2,1)}, bf16[1024,1024]{1,0:T(8,128)(2,1)}, b...) custom-call(bf16[1024,2048]{1,0:T(8,128)(2,1)} %get-tuple-element.53, ...), custom_call_target="tpu_custom_call" | custom-call | flops 15032385536 | bytes 47730688 | tf_op jit(solution)/shard_map/attn_first/pallas_call | solution.py:1328
  243.1 7.9 %all-gather.5.cloned.1.call-done = bf16[8448,512]{1,0:T(8,128)(2,1)} async-done(((bf16[2112,512]{1,0:T(8,128)(2,1)}), bf16[8448,512]{1,0:T(8,128)(2,1)}) %all-gather.5.cloned.1.call-update) | async-done | bytes 8650768 | tf_op jit(solution)/shard_map/all_gather | solution.py:2010
  251.1 33.0 %ffn_first.1 = (bf16[704,2048]{1,0:T(8,128)(2,1)}, bf16[704,2048]{1,0:T(8,128)(2,1)}, bf16[704,2048]{1,0:T(8,128)(2,1)}, bf16[4,704,512]{2,1,0:T(8,128)(2,1)}, bf16[512,2048]{1,0:T(8,128)(2,1)}) custom-call(bf16[512,2048]{1,0:T(8,128)(2,1)} %get-tuple-element.51.refs_0_, bf16[512,2048]{1,0:T(8,128)(2,1)} %get-tuple-element.52.refs_1_, ...), custom_call_target="tpu_custom_call" | custom-call | flops 17716740096 | bytes 36962304 | tf_op jit(solution)/shard_map/ffn_first/pallas_call | solution.py:195
  284.2 0.6 copy-done.7
  284.8 0.6 select_n.190.refs_10_
  285.4 89.5 %ffn_back.1 = (bf16[4,1408,512]{2,1,0:T(8,128)(2,1)}, f32[256,2048]{1,0:T(8,128)}, f32[1,2048]{1,0:T(1,128)}, bf16[1024,2048]{1,0:T(8,128)(2,1)}, bf16[4,512,512...) custom-call(bf16[512,2048]{1,0:T(8,128)(2,1)} %get-tuple-element.51.refs_0_, ...), custom_call_target="tpu_custom_call" | custom-call | flops 29527900160 | bytes 53493760 | tf_op jit(solution)/shard_map/ffn_back/pallas_call | solution.py:563
  375.0 100.0 %attn_back.1 = (bf16[4,528,1024]{2,1,0:T(8,128)(2,1)}, f32[256,2048]{1,0:T(8,128)}) custom-call(bf16[1024,2048]{1,0:T(8,128)(2,1)} %get-tuple-element.70.attn_ref, bf16[2048,1024]{1,0:T(8,128)(2,1)} %get-tuple-element.71.full_ref, bf16[1024,1024]{1,0:T(8,128)(2,1)} %get-tuple-element.72.mixed_ref, bf16[1024,1024]{1,0:T(8,128)(2,1)} %get-tuple-element.73.q_ref, ...), custom_call_target="tpu_custom_call" | custom-call | flops 21474836480 | bytes 42094592 | tf_op jit(solution)/shard_map/attn_back/pallas_call | solution.py:1795
  475.2 1.5 copy-done.2
  476.8 1.1 convert_element_type.124
  478.1 3.1 reshape.340
  481.2 0.2 copy.145
  481.4 1.6 pad_maximum_fusion.1.parts_ref
  483.0 48.8 %settle.1 = (f32[256,2048]{1,0:T(8,128)}, bf16[4,3,704,128]{3,2,1,0:T(8,128)(2,1)}) custom-call(bf16[4,512,512]{2,1,0:T(8,128)(2,1)} %get-tuple-element.64.near_ref, bf16[2,512,512]{2,1,0:T(8,128)(2,1)} %get-tuple-element.65.given_ref, bf16[4,512,512]{2,1,0:T(8,128)(2,1)} %get-tuple-element.66.give_ref, f32[256,2048]{1,0:T(8,128)} %get-tuple-element.63.refs_9_.res_ref, ...), custom_call_target="tpu_custom_call" | custom-call | flops 1 | bytes 13762560 | tf_op jit(solution)/shard_map/settle/pallas_call | solution.py:1959
  531.7 2.0 convert_bitcast_fusion
  533.7 1.4 fusion.24
  535.1 1.5 copy.117
  536.7 1.5 copy.118
  538.2 2.8 convert_element_type.123
  541.0 15.8 %reduce-scatter.10.cloned.1.call-done = bf16[528,1024]{1,0:T(8,128)(2,1)} async-done(((bf16[2112,1024]{1,0:T(8,128)(2,1)}), bf16[528,1024]{1,0:T(8,128)(2,1)}) %reduce-scatter.10.cloned.1.call-update) | async-done | bytes 1081360
  556.8 1.2 slice.118
  558.0 0.2 copy.138
  558.2 0.7 collective-permute-start.6
  559.1 0.2 copy.129
  559.2 1.3 collective-permute-start.3
  560.5 0.2 copy.133
  560.7 0.4 collective-permute-start.5
  561.3 0.2 copy.132
  561.7 0.2 copy.128
  561.8 0.6 collective-permute-done.5
  562.4 1.2 fusion
  563.6 1.1 copy.120
  564.7 5.3 collective-permute-done.3
  570.1 0.9 collective-permute-start.4
  571.1 0.8 copy.122
  571.8 0.8 copy.121
  572.6 1.0 copy.119
  573.7 0.6 dynamic-slice_reduce_fusion.2
  574.3 0.6 dynamic-slice_reduce_fusion
  574.9 2.1 convert_bitcast_fusion.1
  (94 shorter events, 2.8 us)
Async XLA Ops:
  7.2 9.0 %copy-start = (f32[128,1024]{1,0:T(8,128)S(1)}, f32[128,1024]{1,0:T(8,128)}, u32[]{:S(2)}) copy-start(f32[128,1024]{1,0:T(8,128)} %param.21) | copy-start | bytes 1572868
  7.2 1.6 copy-start.6
  7.2 93.3 %all-gather.3.cloned.1.call-start = ((), (), s32[]{:S(2)}) async-start(), calls=%async_computation.3 | async-start | bytes 3932160 | tf_op jit(solution)/shard_map/all_gather | solution.py:2010
  8.7 2.4 collective-permute-start.1
  9.2 1.7 collective-permute-start
  10.9 1.7 copy-start.11
  10.9 1.7 copy-start.9
  10.9 1.7 copy-start.10
  10.9 2.3 copy-start.3
  12.4 238.7 %all-gather.5.cloned.1.call-start = ((), (), s32[]{:S(2)}) async-start(), calls=%async_computation.4 | async-start | bytes 10813440 | tf_op jit(solution)/shard_map/all_gather | solution.py:2010
  88.9 5.4 copy-start.8
  89.0 286.0 %reduce-scatter.6.cloned.1.call-start = ((), (), s32[]{:S(2)}) async-start(), calls=%async_computation.5 | async-start | bytes 3604480 | tf_op jit(solution)/shard_map/reduce_scatter | solution.py:2016
  89.0 3.4 collective-permute-start.2
  284.1 0.7 copy-start.7
  284.1 191.0 %reduce-scatter.8.cloned.1.call-start = ((), (), s32[]{:S(2)}) async-start(), calls=%async_computation.6 | async-start | bytes 7208960 | tf_op jit(solution)/shard_map/reduce_scatter | solution.py:2016
  375.0 181.8 %reduce-scatter.10.cloned.1.call-start = ((), (), s32[]{:S(2)}) async-start(), calls=%async_computation.7 | async-start | bytes 5406720
  475.2 1.6 copy-start.2
  475.2 2.7 copy-start.5
  556.7 2.3 copy-start.4
  557.9 2.6 slice-start
  558.2 16.8 %collective-permute-start.6 = (bf16[128,1024]{0,1:T(8,128)(2,1)S(1)}, bf16[128,1024]{0,1:T(8,128)(2,1)}, u32[]{:S(2)}, u32[]{:S(2)}) collective-permute-start(bf16[128,1024]{0,1:T(8,128)(2,1)S(1)} %copy.138), channel_id=1, source_target_pairs={{0,2},{2,0},{4,6},{6,4},{8,10},{10,8},{12,14},{14,12},{16,18},{18,... | collective-permute-start | bytes 786440 | tf_op jit(solution)/shard_map/ppermute | solution.py:2001
  559.2 10.8 %collective-permute-start.3 = (bf16[144,768]{0,1:T(8,128)(2,1)S(1)}, bf16[144,768]{0,1:T(8,128)(2,1)S(1)}, u32[]{:S(2)}, u32[]{:S(2)}) collective-permute-start(bf16[144,768]{0,1:T(8,128)(2,1)S(1)} %copy.129), channel_id=1, source_target_pairs={{0,1},{1,0},{2,3},{3,2},{4,5},{5,4},{6,7},{7,6},{8,9},{9,8},{10,11... | collective-permute-start | bytes 663560 | tf_op jit(solution)/shard_map/ppermute | solution.py:2007
  560.7 1.7 collective-permute-start.5
  570.1 3.5 collective-permute-start.4
  571.1 6.0 %copy-start.1 = (f32[128,1024]{1,0:T(8,128)S(1)}, f32[128,1024]{1,0:T(8,128)}, u32[]{:S(2)}) copy-start(f32[128,1024]{1,0:T(8,128)} %param.21) | copy-start | bytes 1572868
Sparse Core Ops, SparseCore 0:
  12.5 84.2 all-gather.2
  98.4 152.6 all-gather.4
  284.2 53.9 reduce-scatter.5
  375.1 100.0 reduce-scatter.7
  477.3 79.3 reduce-scatter.9

commit v8 on v7

--- a/solution.py
+++ b/solution.py
@@ -319,20 +319,23 @@
             loads[j] = pltpu.make_async_copy(
                 grad_refs[j], rows_s.at[pl.ds(j * rows, rows)], rows_sem.at[j]
             )
-            loads[j].start()
         factors = [
             pltpu.make_async_copy(src, dst, f_sem.at[j])
             for j, (src, dst) in enumerate(((a_ref, a_s), (s_ref, s_s)))
         ]
         for copy in factors:
             copy.start()
-        joins = join_lines(weight_ref, w_s, w_sem)
+        for j in order[: count // 2]:
+            loads[j].start()
         res_copy = pltpu.make_async_copy(resid_ref, res_s, res_sem)
-        res_copy.start()
         own_copy = pltpu.make_async_copy(grad_refs[0], own_s, own_sem)
-        own_copy.start()
         greet((across_core, across_side, across_half))
         wait_all(downs + factors)
+        joins = join_lines(weight_ref, w_s, w_sem)
+        for j in order[count // 2 :]:
+            loads[j].start()
+        res_copy.start()
+        own_copy.start()
 
         def act_block(i):
             at = tile(i, rows)

time: 588 us -> 586 us (level)
  transfers between devices with their start and end apart: 12 -> 12, of which waited for: 6 -> 5; matrix products, arithmetic and copies ran while one was open for 8% -> 8% of each run, Pallas kernels for 76% -> 76%
where the time goes in v8:
time: 586 us; the launch traced here: 581 us
  Pallas kernels  472 us (81%)
  local copies, waits for them, and re-layouts  32.6 us (6%)
  waiting for transfers between devices  30.8 us (5%)
  other arithmetic  24.1 us (4%)
  between operations  17.2 us (3%)
    pallas_call x1, Pallas kernels, attn_first(): pl.pallas_call(kernel, out_shape=out_shape, in_specs=[vmem if a.shape[0]...  138 us
    pallas_call x1, Pallas kernels, attn_back(): pl.pallas_call(kernel, out_shape=out_shape, in_specs=[vmem if a.shape[0]...  100 us
    pallas_call x1, Pallas kernels, ffn_back(): pl.pallas_call(kernel, out_shape=out_shape, in_specs=[ANY] * (len(args) -...  86.7 us
    pallas_call x1, Pallas kernels, gather_first(): pl.pallas_call(kernel, out_shape=out_shape, in_specs=[ANY] * 5, out_specs...  65.7 us
    pallas_call x1, Pallas kernels, settle(): pl.pallas_call(kernel, out_shape=out_shape, in_specs=[ANY] * 5, out_specs...  48.8 us
    pallas_call x1, Pallas kernels, ffn_first(): pl.pallas_call(kernel, out_shape=out_shape, in_specs=[ANY] * len(args), o...  33 us
    unnamed x6, waiting for transfers between devices  15.8 us
  transfers between devices with their start and end apart: 12, of which 5 were waited for; matrix products, arithmetic and copies ran while one was open for 8% of the time, Pallas kernels for 76%

profile of v8, /device:TPU:1, one launch (start us, length us, event | category | flops | bytes accessed | tf_op | source)
XLA Modules:
  0.0 581.0 jit_solution(16111981316605229128)
XLA Ops:
  7.3 1.4 convert_element_type.112
  8.8 0.3 copy.101
  9.2 0.5 collective-permute-start
  9.7 1.2 collective-permute-done
  10.9 0.3 maximum_select_fusion.3
  11.2 0.2 maximum_select_fusion
  11.4 1.0 pad_maximum_fusion.2
  12.6 0.6 concatenate.123.gain_ref
  13.2 0.3 copy.100
  13.5 1.7 copy.99
  15.2 0.9 dynamic-slice_convert_fusion.1
  16.2 0.7 pad_maximum_fusion.3.piece_ref
  16.9 1.4 convert_bitcast_fusion.2
  18.3 1.6 pad_maximum_fusion.ffn_ref
  19.9 65.7 %gather_first.1 = (bf16[1024,2048]{1,0:T(8,128)(2,1)}, bf16[512,2048]{1,0:T(8,128)(2,1)}, bf16[512,2048]{1,0:T(8,128)(2,1)}, bf16[2,4,128,768]{3,2,1,0:T(8,128)(...) custom-call(bf16[256,2048]{1,0:T(8,128)(2,1)} %x_ref.1, bf16[256,2048]{1,0:T(8,128)(2,1)} %dy_ref.3, ...), custom_call_target="tpu_custom_call" | custom-call | flops 1 | bytes 16998400 | tf_op jit(solution)/shard_map/gather_first/pallas_call | solution.py:860
  85.6 3.3 copy.144
  89.8 1.0 slice.81
  91.0 0.6 fusion.9
  91.6 0.6 slice_convert_fusion
  92.2 0.2 broadcast_compare_fusion
  94.6 0.8 constant_dynamic-slice_fusion.11
  95.4 0.2 fusion.6
  95.8 3.2 multiply_sine_fusion
  99.1 1.5 select_convert_fusion.bias_ref
  100.6 4.7 copy.102
  105.3 137.9 %attn_first.1 = (bf16[1024,1024]{1,0:T(8,128)(2,1)}, bf16[1024,256]{1,0:T(8,128)(2,1)}, bf16[1024,256]{1,0:T(8,128)(2,1)}, bf16[1024,1024]{1,0:T(8,128)(2,1)}, b...) custom-call(bf16[1024,2048]{1,0:T(8,128)(2,1)} %get-tuple-element.53, ...), custom_call_target="tpu_custom_call" | custom-call | flops 15032385536 | bytes 47730688 | tf_op jit(solution)/shard_map/attn_first/pallas_call | solution.py:1331
  243.2 7.8 %all-gather.5.cloned.1.call-done = bf16[8448,512]{1,0:T(8,128)(2,1)} async-done(((bf16[2112,512]{1,0:T(8,128)(2,1)}), bf16[8448,512]{1,0:T(8,128)(2,1)}) %all-gather.5.cloned.1.call-update) | async-done | bytes 8650768 | tf_op jit(solution)/shard_map/all_gather | solution.py:2013
  251.1 33.0 %ffn_first.1 = (bf16[704,2048]{1,0:T(8,128)(2,1)}, bf16[704,2048]{1,0:T(8,128)(2,1)}, bf16[704,2048]{1,0:T(8,128)(2,1)}, bf16[4,704,512]{2,1,0:T(8,128)(2,1)}, bf16[512,2048]{1,0:T(8,128)(2,1)}) custom-call(bf16[512,2048]{1,0:T(8,128)(2,1)} %get-tuple-element.51.refs_0_, bf16[512,2048]{1,0:T(8,128)(2,1)} %get-tuple-element.52.refs_1_, ...), custom_call_target="tpu_custom_call" | custom-call | flops 17716740096 | bytes 36962304 | tf_op jit(solution)/shard_map/ffn_first/pallas_call | solution.py:195
  284.2 0.6 copy-done.7
  284.8 0.6 select_n.190.refs_10_
  285.4 86.7 %ffn_back.1 = (bf16[4,1408,512]{2,1,0:T(8,128)(2,1)}, f32[256,2048]{1,0:T(8,128)}, f32[1,2048]{1,0:T(1,128)}, bf16[1024,2048]{1,0:T(8,128)(2,1)}, bf16[4,512,512...) custom-call(bf16[512,2048]{1,0:T(8,128)(2,1)} %get-tuple-element.51.refs_0_, ...), custom_call_target="tpu_custom_call" | custom-call | flops 29527900160 | bytes 53493760 | tf_op jit(solution)/shard_map/ffn_back/pallas_call | solution.py:566
  372.3 100.0 %attn_back.1 = (bf16[4,528,1024]{2,1,0:T(8,128)(2,1)}, f32[256,2048]{1,0:T(8,128)}) custom-call(bf16[1024,2048]{1,0:T(8,128)(2,1)} %get-tuple-element.70.attn_ref, bf16[2048,1024]{1,0:T(8,128)(2,1)} %get-tuple-element.71.full_ref, bf16[1024,1024]{1,0:T(8,128)(2,1)} %get-tuple-element.72.mixed_ref, bf16[1024,1024]{1,0:T(8,128)(2,1)} %get-tuple-element.73.q_ref, ...), custom_call_target="tpu_custom_call" | custom-call | flops 21474836480 | bytes 42094592 | tf_op jit(solution)/shard_map/attn_back/pallas_call | solution.py:1798
  472.4 1.5 copy-done.2
  473.9 1.1 convert_element_type.124
  475.3 3.1 reshape.340
  478.4 0.2 copy.145
  478.6 1.6 pad_maximum_fusion.1.parts_ref
  480.2 48.8 %settle.1 = (f32[256,2048]{1,0:T(8,128)}, bf16[4,3,704,128]{3,2,1,0:T(8,128)(2,1)}) custom-call(bf16[4,512,512]{2,1,0:T(8,128)(2,1)} %get-tuple-element.64.near_ref, bf16[2,512,512]{2,1,0:T(8,128)(2,1)} %get-tuple-element.65.given_ref, bf16[4,512,512]{2,1,0:T(8,128)(2,1)} %get-tuple-element.66.give_ref, f32[256,2048]{1,0:T(8,128)} %get-tuple-element.63.refs_9_.res_ref, ...), custom_call_target="tpu_custom_call" | custom-call | flops 1 | bytes 13762560 | tf_op jit(solution)/shard_map/settle/pallas_call | solution.py:1962
  529.0 2.0 convert_bitcast_fusion
  530.9 1.4 fusion.24
  532.3 1.5 copy.117
  533.9 1.5 copy.118
  535.4 2.8 convert_element_type.123
  538.2 15.7 %reduce-scatter.10.cloned.1.call-done = bf16[528,1024]{1,0:T(8,128)(2,1)} async-done(((bf16[2112,1024]{1,0:T(8,128)(2,1)}), bf16[528,1024]{1,0:T(8,128)(2,1)}) %reduce-scatter.10.cloned.1.call-update) | async-done | bytes 1081360
  553.9 1.2 slice.118
  555.2 0.2 copy.138
  555.3 0.7 collective-permute-start.6
  556.2 0.2 copy.129
  556.4 1.3 collective-permute-start.3
  557.7 0.2 copy.133
  557.9 0.4 collective-permute-start.5
  558.5 0.2 copy.132
  558.8 0.2 copy.128
  559.0 0.6 collective-permute-done.5
  559.6 1.2 fusion
  560.8 1.1 copy.120
  561.9 5.3 collective-permute-done.3
  567.3 0.9 collective-permute-start.4
  568.3 0.8 copy.122
  569.0 0.8 copy.121
  569.8 1.0 copy.119
  570.9 0.6 dynamic-slice_reduce_fusion.2
  571.5 0.6 dynamic-slice_reduce_fusion
  572.1 2.1 convert_bitcast_fusion.1
  (94 shorter events, 2.7 us)
Async XLA Ops:
  7.2 9.0 %copy-start = (f32[128,1024]{1,0:T(8,128)S(1)}, f32[128,1024]{1,0:T(8,128)}, u32[]{:S(2)}) copy-start(f32[128,1024]{1,0:T(8,128)} %param.21) | copy-start | bytes 1572868
  7.2 1.6 copy-start.6
  7.2 93.4 %all-gather.3.cloned.1.call-start = ((), (), s32[]{:S(2)}) async-start(), calls=%async_computation.3 | async-start | bytes 3932160 | tf_op jit(solution)/shard_map/all_gather | solution.py:2013
  8.7 2.4 collective-permute-start.1
  9.2 1.7 collective-permute-start
  10.9 1.7 copy-start.11
  10.9 1.7 copy-start.9
  10.9 1.7 copy-start.10
  10.9 2.3 copy-start.3
  12.4 238.7 %all-gather.5.cloned.1.call-start = ((), (), s32[]{:S(2)}) async-start(), calls=%async_computation.4 | async-start | bytes 10813440 | tf_op jit(solution)/shard_map/all_gather | solution.py:2013
  88.9 5.4 copy-start.8
  89.0 283.2 %reduce-scatter.6.cloned.1.call-start = ((), (), s32[]{:S(2)}) async-start(), calls=%async_computation.5 | async-start | bytes 3604480 | tf_op jit(solution)/shard_map/reduce_scatter | solution.py:2019
  89.0 3.4 collective-permute-start.2
  284.1 0.7 copy-start.7
  284.1 188.2 %reduce-scatter.8.cloned.1.call-start = ((), (), s32[]{:S(2)}) async-start(), calls=%async_computation.6 | async-start | bytes 7208960 | tf_op jit(solution)/shard_map/reduce_scatter | solution.py:2019
  372.2 181.7 %reduce-scatter.10.cloned.1.call-start = ((), (), s32[]{:S(2)}) async-start(), calls=%async_computation.7 | async-start | bytes 5406720
  472.3 1.6 copy-start.2
  472.4 2.7 copy-start.5
  553.9 2.3 copy-start.4
  555.1 2.6 slice-start
  555.3 16.8 %collective-permute-start.6 = (bf16[128,1024]{0,1:T(8,128)(2,1)S(1)}, bf16[128,1024]{0,1:T(8,128)(2,1)}, u32[]{:S(2)}, u32[]{:S(2)}) collective-permute-start(bf16[128,1024]{0,1:T(8,128)(2,1)S(1)} %copy.138), channel_id=1, source_target_pairs={{0,2},{2,0},{4,6},{6,4},{8,10},{10,8},{12,14},{14,12},{16,18},{18,... | collective-permute-start | bytes 786440 | tf_op jit(solution)/shard_map/ppermute | solution.py:2004
  556.4 10.8 %collective-permute-start.3 = (bf16[144,768]{0,1:T(8,128)(2,1)S(1)}, bf16[144,768]{0,1:T(8,128)(2,1)S(1)}, u32[]{:S(2)}, u32[]{:S(2)}) collective-permute-start(bf16[144,768]{0,1:T(8,128)(2,1)S(1)} %copy.129), channel_id=1, source_target_pairs={{0,1},{1,0},{2,3},{3,2},{4,5},{5,4},{6,7},{7,6},{8,9},{9,8},{10,11... | collective-permute-start | bytes 663560 | tf_op jit(solution)/shard_map/ppermute | solution.py:2010
  557.9 1.7 collective-permute-start.5
  567.3 3.5 collective-permute-start.4
  568.2 6.0 %copy-start.1 = (f32[128,1024]{1,0:T(8,128)S(1)}, f32[128,1024]{1,0:T(8,128)}, u32[]{:S(2)}) copy-start(f32[128,1024]{1,0:T(8,128)} %param.21) | copy-start | bytes 1572868
Sparse Core Ops, SparseCore 0:
  12.5 84.2 all-gather.2
  98.4 152.6 all-gather.4
  284.2 53.9 reduce-scatter.5
  372.3 99.9 reduce-scatter.7
  474.5 79.3 reduce-scatter.9
